TPU v7x, 128 devices: a whole 4x4x4 slice. The times are simulated.
128 devices in a mesh: tile: 16 (over y_lo, x, core), mp: 8 (over y_hi, z).
Axes of the slice: x: 4, y: 4 (y_hi: 2, y_lo: 2; y = y_hi * 2 + y_lo), z: 4, core: 2. Of those that a mesh axis runs over, the one named last changes fastest.
Arguments:
- tokens: bfloat16 [128, 256, 1024], P('tile', 'mp'), may hold values from -6 to 6
- ln_gain_one: float32 [1024], replicated, may hold values from 0.5 to 1.5
- ln_gain_two: float32 [1024], replicated, may hold values from 0.5 to 1.5
- qkv_weight: bfloat16 [3, 1024, 1024], P(None, None, 'mp'), may hold values from -2 to 2
- out_weight: bfloat16 [1024, 1024], P('mp'), may hold values from -0.1875 to 0.1875
- in_weight: bfloat16 [4096, 1024], P('mp'), may hold values from -0.1875 to 0.1875
- mlp_out_weight: bfloat16 [4096, 1024], P('mp'), may hold values from -0.09375 to 0.09375
- proj_weight: bfloat16 [1024, 256], replicated, may hold values from -0.1875 to 0.1875
- land_mask: int32 [128], P('tile'), may hold values 0 or 1
- placement: int32 [128], replicated, may hold values from 0 to 127, as said below
- guide: bfloat16 [512, 256, 256], P(('tile', 'mp')), may hold values from -6 to 6
- conv_weights: bfloat16 [3, 3, 3, 256, 256], replicated, may hold values from -0.125 to 0.125
- conv_bias: float32 [3, 256], replicated, may hold values from -3 to 3
Outputs:
- dense_map: bfloat16 [512, 256, 256], P(('tile', 'mp'))
Inputs may be any that keep to these rules, and one draw needn't show every extreme that they name: placement is a permutation of the scene positions; the tiles of one group land in different slabs (entry // 8), so each slab receives at most one tile of each group.
All inputs are finite; a program needn't handle non-finite values. No bound on the sum of `land_mask` on one device may be relied on, other than what follows from the above.
Results may differ from a plain program's by a relative error of at most 0.018.
The roundings to bfloat16 on the way count: a program that leaves them out, or rounds other values in their place, can miss the bound.
Values may be sent and summed in bfloat16 or wider, within the bound.
No kernel may reach another device: no remote copies, remote signals or barrier semaphores. Data moves between devices by JAX's collectives and lax.ppermute only.
A program may use at most 128 MiB of HBM per device.

v0:
```python
import jax
import jax.numpy as jnp
from jax import lax
from jax.sharding import PartitionSpec as P

HEAD = 64
SIDE = 16
UP = 2
PATCHES = 256


def extended_2(block, sides, width):
    for axis, dim in sides:
        count = lax.axis_size(axis)
        forward = [(i, i + 1) for i in range(count - 1)]
        backward = [(target, source) for source, target in forward]
        low = lax.ppermute(
            lax.slice_in_dim(block, block.shape[dim] - width, None, axis=dim), axis, forward
        )
        high = lax.ppermute(lax.slice_in_dim(block, 0, width, axis=dim), axis, backward)
        block = jnp.concatenate([low, block, high], axis=dim)
    return block


def layer_norm(values, gain):
    widened = values.astype(jnp.float32)
    centre = jnp.mean(widened, axis=-1, keepdims=True)
    spread = jnp.mean((widened - centre) ** 2, axis=-1, keepdims=True)
    return ((widened - centre) * lax.rsqrt(spread + 1e-06) * gain).astype(jnp.bfloat16)


def conv_layer(extended, kernel, shift, out_count):
    width_px = extended.shape[1]
    padded = jnp.pad(extended, ((0, 0), (1, 1), (0, 0)))
    running = jnp.zeros((out_count, width_px, kernel.shape[-1]), jnp.float32) + shift
    for row_shift in range(3):
        for col_shift in range(3):
            window = padded[row_shift : row_shift + out_count, col_shift : col_shift + width_px]
            running = running + jnp.einsum(
                "rwc,cd->rwd",
                window,
                kernel[row_shift, col_shift],
                preferred_element_type=jnp.float32,
            )
    return running


def per_device(
    tokens,
    ln_gain_one,
    ln_gain_two,
    qkv_weight,
    out_weight,
    in_weight,
    mlp_out_weight,
    proj_weight,
    land_mask,
    placement,
    guide,
    conv_weights,
    conv_bias,
):
    tiles_here = tokens.shape[0]
    seg_rows = tokens.shape[1]
    groups = lax.axis_size("tile")
    normed = layer_norm(tokens, ln_gain_one)
    gathered = lax.all_gather(normed, "mp", axis=1, tiled=True)
    projected = jnp.einsum(
        "tpd,kde->ktpe", gathered, qkv_weight, preferred_element_type=jnp.float32
    ).astype(jnp.bfloat16)
    heads_local = projected.shape[-1] // HEAD
    shaped = projected.reshape(3, tiles_here, PATCHES, heads_local, HEAD)
    scores = jnp.einsum(
        "tphe,tqhe->thpq", shaped[0], shaped[1], preferred_element_type=jnp.float32
    ) * HEAD ** (-0.5)
    soft_weights = jax.nn.softmax(scores, axis=-1).astype(jnp.bfloat16)
    context = jnp.einsum(
        "thpq,tqhe->tphe", soft_weights, shaped[2], preferred_element_type=jnp.float32
    )
    context = context.astype(jnp.bfloat16).reshape(tiles_here, PATCHES, heads_local * HEAD)
    partial_value = jnp.einsum(
        "tpe,ed->tpd", context, out_weight, preferred_element_type=jnp.float32
    )
    attention = lax.psum_scatter(
        partial_value.astype(jnp.bfloat16), "mp", scatter_dimension=1, tiled=True
    ).astype(jnp.float32)
    middle = (tokens.astype(jnp.float32) + attention).astype(jnp.bfloat16)
    normed_mid = layer_norm(middle, ln_gain_two)
    gathered_mid = lax.all_gather(normed_mid, "mp", axis=1, tiled=True)
    hidden = jnp.einsum("tpd,fd->tpf", gathered_mid, in_weight, preferred_element_type=jnp.float32)
    hidden = jax.nn.gelu(hidden).astype(jnp.bfloat16)
    mlp_terms = jnp.einsum(
        "tpf,fd->tpd", hidden, mlp_out_weight, preferred_element_type=jnp.float32
    )
    mlp_part = lax.psum_scatter(
        mlp_terms.astype(jnp.bfloat16), "mp", scatter_dimension=1, tiled=True
    ).astype(jnp.float32)
    features = (middle.astype(jnp.float32) + mlp_part).astype(jnp.bfloat16)
    mask_here = land_mask.astype(jnp.bfloat16)[:, None, None]
    group_here = lax.axis_index("tile")
    slab_all = placement // tiles_here
    column_all = placement % tiles_here
    group_all = jnp.arange(placement.shape[0], dtype=jnp.int32) // tiles_here
    slab_local = lax.dynamic_slice_in_dim(slab_all, group_here * tiles_here, tiles_here, 0)
    selector = (slab_local[None, :] == jnp.arange(groups, dtype=jnp.int32)[:, None]).astype(
        jnp.bfloat16
    )
    in_slab = slab_all == group_here
    column_hot = (
        column_all[:, None] == jnp.arange(tiles_here, dtype=jnp.int32)[None, :]
    ) & in_slab[:, None]
    group_hot = group_all[:, None] == jnp.arange(groups, dtype=jnp.int32)[None, :]
    arrange = jnp.einsum(
        "tk,tg->kg", column_hot.astype(jnp.float32), group_hot.astype(jnp.float32)
    ).astype(jnp.bfloat16)
    masked = features * mask_here
    outgoing = jnp.einsum(
        "sj,jpd->spd", selector, masked, preferred_element_type=jnp.float32
    ).astype(jnp.bfloat16)
    incoming = lax.all_to_all(outgoing, "tile", split_axis=0, concat_axis=0, tiled=True)
    slab_feats = jnp.einsum(
        "kg,gpd->kpd", arrange, incoming, preferred_element_type=jnp.float32
    ).astype(jnp.bfloat16)
    slab_embed = jnp.einsum(
        "kpd,dc->kpc", slab_feats, proj_weight, preferred_element_type=jnp.float32
    )
    slab_embed = slab_embed.astype(jnp.bfloat16)
    token_rows = seg_rows // SIDE
    channels = proj_weight.shape[1]
    image = slab_embed.reshape(tiles_here, token_rows, SIDE, channels)
    image = jnp.transpose(image, (1, 0, 2, 3)).reshape(token_rows, tiles_here * SIDE, channels)
    upsampled = jnp.repeat(jnp.repeat(image, UP, axis=0), UP, axis=1)
    guided = (upsampled.astype(jnp.float32) + guide.astype(jnp.float32)).astype(jnp.bfloat16)
    row_count = guided.shape[0]

    def section(values, layer):
        widened = extended_2(values, ((("tile", "mp"), 0),), 1)
        return conv_layer(widened, conv_weights[layer], conv_bias[layer], row_count)

    first = jax.nn.gelu(section(guided, 0)).astype(jnp.bfloat16)
    second = jax.nn.gelu(section(first, 1)).astype(jnp.bfloat16)
    last_term = section(second, 2)
    return (guided.astype(jnp.float32) + last_term).astype(jnp.bfloat16)


def solution(mesh):
    in_specs = (
        P("tile", "mp", None),
        P(),
        P(),
        P(None, None, "mp"),
        P("mp", None),
        P("mp", None),
        P("mp", None),
        P(),
        P("tile"),
        P(),
        P(("tile", "mp"), None, None),
        P(),
        P(),
    )
    out_specs = P(("tile", "mp"), None, None)
    return jax.shard_map(
        per_device, mesh=mesh, in_specs=in_specs, out_specs=out_specs, check_vma=False
    )
```

profile of v0, /device:TPU:6, one launch (start us, length us, event | category | flops | bytes accessed | tf_op | source)
XLA Modules:
  0.0 428.9 jit_solution(2327485380840038039)
XLA Ops:
  9.2 2.1 fusion.61
  11.4 74.0 %all-gather.3.cloned.1.call-done = bf16[8,256,1024]{2,1,0:T(8,128)(2,1)} async-done(((bf16[8,32,1024]{2,1,0:T(8,128)(2,1)}), bf16[8,256,1024]{2,1,0:T(8,128)(2,1)}) %all-gather.3.cloned.1.call-update) | async-done | bytes 4194320 | tf_op jit(solution)/shard_map/all_gather | solution.py:67
  85.4 4.0 fusion.25
  89.6 3.5 fusion.186
  93.1 2.7 fusion.48
  95.8 3.2 convolution_convert_fusion.1
  99.2 82.6 %reduce-scatter.3.cloned.1.call-done = bf16[8,32,1024]{2,1,0:T(8,128)(2,1)} async-done(((bf16[8,256,1024]{2,1,0:T(8,128)(2,1)}), bf16[8,32,1024]{2,1,0:T(8,128)(2,1)}) %reduce-scatter.3.cloned.1.call-update) | async-done | bytes 524304 | tf_op jit(solution)/shard_map/reduce_scatter | solution.py:84
  184.5 70.4 %all-gather.5.cloned.1.call-done = bf16[8,256,1024]{2,1,0:T(8,128)(2,1)} async-done(((bf16[8,32,1024]{2,1,0:T(8,128)(2,1)}), bf16[8,256,1024]{2,1,0:T(8,128)(2,1)}) %all-gather.5.cloned.1.call-update) | async-done | bytes 4194320 | tf_op jit(solution)/shard_map/all_gather | solution.py:89
  254.9 8.2 %convolution_convert_fusion = bf16[8,256,1024]{2,1,0:T(8,128)(2,1)} fusion(bf16[8,256,1024]{2,1,0:T(8,128)(2,1)} %all-gather.5.cloned.1.call-done, bf16[512,1024]{1,0:T(8,128)(2,1)S(1)} %copy-done, bf16[512,1024]{1,0:T(8,128)(2,1)S(1)} %copy-done.8), kind=kOutput, calls=%fused_computation.16 | convolution fusion | flops 4306501632 | bytes 10485760 | tf_op jit(solution)/shard_map/tpf,fd->tpd/dot_general | solution.py:92
  263.9 81.9 %reduce-scatter.5.cloned.1.call-done = bf16[8,32,1024]{2,1,0:T(8,128)(2,1)} async-done(((bf16[8,256,1024]{2,1,0:T(8,128)(2,1)}), bf16[8,32,1024]{2,1,0:T(8,128)(2,1)}) %reduce-scatter.5.cloned.1.call-update) | async-done | bytes 524304 | tf_op jit(solution)/shard_map/reduce_scatter | solution.py:95
  349.0 5.0 %all-to-all-start = ((bf16[16,32,1024]{2,1,0:T(8,128)(2,1)}), bf16[16,32,1024]{2,1,0:T(8,128)(2,1)S(1)}, u32[]{:S(2)}, u32[]{:S(2)}) async-start(bf16[16,32,1024]{2,1,0:T(8,128)(2,1)} %copy.37), calls=%async_computation.2 | async-start | bytes 2097152 | tf_op jit(solution)/shard_map/all_to_all | solution.py:120
  354.1 3.3 slice_bitcast_fusion
  357.4 10.0 %all-to-all-done = bf16[16,32,1024]{2,1,0:T(8,128)(2,1)S(1)} async-done(((bf16[16,32,1024]{2,1,0:T(8,128)(2,1)}), bf16[16,32,1024]{2,1,0:T(8,128)(2,1)S(1)}, u32[]{:S(2)}, u32[]{:S(2)}) %all-to-all-start) | async-done | bytes 1048608 | tf_op jit(solution)/shard_map/all_to_all | solution.py:120
  369.0 1.7 convolution_convert_fusion.2
  371.1 1.7 convert_element_type.132
  374.4 3.1 collective-permute-start
  377.5 6.9 %collective-permute-start.1 = (bf16[1,256,256]{2,1,0:T(8,128)(2,1)S(1)}, bf16[1,256,256]{2,1,0:T(8,128)(2,1)S(1)}, u32[]{:S(2)}, u32[]{:S(2)}) collective-permute-start(bf16[1,256,256]{2,1,0:T(8,128)(2,1)S(1)} %get-tuple-element.20), channel_id=1, source_target_pairs={{1,0},{2,1},{3,2},{4,3},{5,4},{6,5},{7,6},{8,7},{9,8},{10,9},{11,1... | collective-permute-start | bytes 393224 | tf_op jit(solution)/shard_map/ppermute | solution.py:20
  385.3 1.7 collective-permute-done.1
  390.1 1.9 collective-permute-start.2
  392.1 8.3 %collective-permute-start.3 = (bf16[1,256,256]{2,1,0:T(8,128)(2,1)S(1)}, bf16[1,256,256]{2,1,0:T(8,128)(2,1)S(1)}, u32[]{:S(2)}, u32[]{:S(2)}) collective-permute-start(bf16[1,256,256]{2,1,0:T(8,128)(2,1)S(1)} %get-tuple-element.18), channel_id=1, source_target_pairs={{1,0},{2,1},{3,2},{4,3},{5,4},{6,5},{7,6},{8,7},{9,8},{10,9},{11,1... | collective-permute-start | bytes 393224 | tf_op jit(solution)/shard_map/ppermute | solution.py:20
  401.2 1.7 collective-permute-done.3
  406.0 2.6 collective-permute-start.4
  408.6 7.6 %collective-permute-start.5 = (bf16[1,256,256]{2,1,0:T(8,128)(2,1)S(1)}, bf16[1,256,256]{2,1,0:T(8,128)(2,1)S(1)}, u32[]{:S(2)}, u32[]{:S(2)}) collective-permute-start(bf16[1,256,256]{2,1,0:T(8,128)(2,1)S(1)} %get-tuple-element.16), channel_id=1, source_target_pairs={{1,0},{2,1},{3,2},{4,3},{5,4},{6,5},{7,6},{8,7},{9,8},{10,9},{11,1... | collective-permute-start | bytes 393224 | tf_op jit(solution)/shard_map/ppermute | solution.py:20
  417.0 1.8 collective-permute-done.5
  (89 shorter events, 25.5 us)
Async XLA Ops:
  6.5 248.3 %copy-start = (bf16[512,1024]{1,0:T(8,128)(2,1)S(1)}, bf16[512,1024]{1,0:T(8,128)(2,1)}, u32[]{:S(2)}) copy-start(bf16[512,1024]{1,0:T(8,128)(2,1)} %param.19) | copy-start | bytes 3145732
  6.5 78.9 %copy-start.9 = (bf16[3,1024,128]{2,1,0:T(8,128)(2,1)S(1)}, bf16[3,1024,128]{2,1,0:T(8,128)(2,1)}, u32[]{:S(2)}) copy-start(bf16[3,1024,128]{2,1,0:T(8,128)(2,1)} %param.16) | copy-start | bytes 2359300
  6.5 78.9 %all-gather.3.cloned.1.call-start = ((), (), s32[]{:S(2)}) async-start(), calls=%async_computation.3 | async-start | bytes 4718592 | tf_op jit(solution)/shard_map/all_gather | solution.py:67
  11.4 170.4 %reduce-scatter.3.cloned.1.call-start = ((), (), s32[]{:S(2)}) async-start(), calls=%async_computation.4 | async-start | bytes 4718592 | tf_op jit(solution)/shard_map/reduce_scatter | solution.py:84
  93.1 2.7 copy-start.4
  99.1 82.7 %copy-start.2 = (bf16[8,32,1024]{2,1,0:T(8,128)(2,1)S(1)}, bf16[8,32,1024]{2,1,0:T(8,128)(2,1)}, u32[]{:S(2)}) copy-start(bf16[8,32,1024]{2,1,0:T(8,128)(2,1)} %param.13) | copy-start | bytes 1572868
  99.1 84.2 %copy-start.5 = (f32[1024]{0:T(1024)S(1)}, f32[1024]{0:T(1024)}, u32[]{:S(2)}) copy-start(f32[1024]{0:T(1024)} %param.15) | copy-start | bytes 12292
  99.1 155.8 %copy-start.8 = (bf16[512,1024]{1,0:T(8,128)(2,1)S(1)}, bf16[512,1024]{1,0:T(8,128)(2,1)}, u32[]{:S(2)}) copy-start(bf16[512,1024]{1,0:T(8,128)(2,1)} %param.18) | copy-start | bytes 3145732
  99.1 155.7 %all-gather.5.cloned.1.call-start = ((), (), s32[]{:S(2)}) async-start(), calls=%async_computation.5 | async-start | bytes 4718592 | tf_op jit(solution)/shard_map/all_gather | solution.py:89
  184.4 161.3 %reduce-scatter.5.cloned.1.call-start = ((), (), s32[]{:S(2)}) async-start(), calls=%async_computation.6 | async-start | bytes 4718592 | tf_op jit(solution)/shard_map/reduce_scatter | solution.py:95
  263.1 0.7 copy-start.10
  263.1 0.7 copy-start.7
  349.0 5.0 %copy-start.6 = (f32[3,256]{1,0:T(4,128)S(1)}, f32[3,256]{1,0:T(4,128)}, u32[]{:S(2)}) copy-start(f32[3,256]{1,0:T(4,128)} %param.25) | copy-start | bytes 9220
  349.0 18.3 %all-to-all-start = ((bf16[16,32,1024]{2,1,0:T(8,128)(2,1)}), bf16[16,32,1024]{2,1,0:T(8,128)(2,1)S(1)}, u32[]{:S(2)}, u32[]{:S(2)}) async-start(bf16[16,32,1024]{2,1,0:T(8,128)(2,1)} %copy.37), calls=%async_computation.2 | async-start | bytes 2097152 | tf_op jit(solution)/shard_map/all_to_all | solution.py:120
  372.8 11.7 %copy-start.3 = (bf16[3,3,256,256]{3,2,1,0:T(8,128)(2,1)S(1)}, bf16[3,3,256,256]{3,2,1,0:T(8,128)(2,1)}, u32[]{:S(2)}) copy-start(bf16[3,3,256,256]{3,2,1,0:T(8,128)(2,1)} %get-tuple-element.10) | copy-start | bytes 3538948
  374.4 10.9 %collective-permute-start = (bf16[1,256,256]{2,1,0:T(8,128)(2,1)S(1)}, bf16[1,256,256]{2,1,0:T(8,128)(2,1)S(1)}, u32[]{:S(2)}, u32[]{:S(2)}) collective-permute-start(bf16[1,256,256]{2,1,0:T(8,128)(2,1)S(1)} %get-tuple-element.19), channel_id=1, source_target_pairs={{0,1},{1,2},{2,3},{3,4},{4,5},{5,6},{6,7},{7,8},{8,9},{9,10},{10,1... | collective-permute-start | bytes 393224 | tf_op jit(solution)/shard_map/ppermute | solution.py:17
  377.5 9.5 %collective-permute-start.1 = (bf16[1,256,256]{2,1,0:T(8,128)(2,1)S(1)}, bf16[1,256,256]{2,1,0:T(8,128)(2,1)S(1)}, u32[]{:S(2)}, u32[]{:S(2)}) collective-permute-start(bf16[1,256,256]{2,1,0:T(8,128)(2,1)S(1)} %get-tuple-element.20), channel_id=1, source_target_pairs={{1,0},{2,1},{3,2},{4,3},{5,4},{6,5},{7,6},{8,7},{9,8},{10,9},{11,1... | collective-permute-start | bytes 393224 | tf_op jit(solution)/shard_map/ppermute | solution.py:20
  390.1 11.1 %collective-permute-start.2 = (bf16[1,256,256]{2,1,0:T(8,128)(2,1)S(1)}, bf16[1,256,256]{2,1,0:T(8,128)(2,1)S(1)}, u32[]{:S(2)}, u32[]{:S(2)}) collective-permute-start(bf16[1,256,256]{2,1,0:T(8,128)(2,1)S(1)} %get-tuple-element.17), channel_id=1, source_target_pairs={{0,1},{1,2},{2,3},{3,4},{4,5},{5,6},{6,7},{7,8},{8,9},{9,10},{10,1... | collective-permute-start | bytes 393224 | tf_op jit(solution)/shard_map/ppermute | solution.py:17
  392.1 10.8 %collective-permute-start.3 = (bf16[1,256,256]{2,1,0:T(8,128)(2,1)S(1)}, bf16[1,256,256]{2,1,0:T(8,128)(2,1)S(1)}, u32[]{:S(2)}, u32[]{:S(2)}) collective-permute-start(bf16[1,256,256]{2,1,0:T(8,128)(2,1)S(1)} %get-tuple-element.18), channel_id=1, source_target_pairs={{1,0},{2,1},{3,2},{4,3},{5,4},{6,5},{7,6},{8,7},{9,8},{10,9},{11,1... | collective-permute-start | bytes 393224 | tf_op jit(solution)/shard_map/ppermute | solution.py:20
  406.0 10.9 %collective-permute-start.4 = (bf16[1,256,256]{2,1,0:T(8,128)(2,1)S(1)}, bf16[1,256,256]{2,1,0:T(8,128)(2,1)S(1)}, u32[]{:S(2)}, u32[]{:S(2)}) collective-permute-start(bf16[1,256,256]{2,1,0:T(8,128)(2,1)S(1)} %get-tuple-element.15), channel_id=1, source_target_pairs={{0,1},{1,2},{2,3},{3,4},{4,5},{5,6},{6,7},{7,8},{8,9},{9,10},{10,1... | collective-permute-start | bytes 393224 | tf_op jit(solution)/shard_map/ppermute | solution.py:17
  408.6 10.1 %collective-permute-start.5 = (bf16[1,256,256]{2,1,0:T(8,128)(2,1)S(1)}, bf16[1,256,256]{2,1,0:T(8,128)(2,1)S(1)}, u32[]{:S(2)}, u32[]{:S(2)}) collective-permute-start(bf16[1,256,256]{2,1,0:T(8,128)(2,1)S(1)} %get-tuple-element.16), channel_id=1, source_target_pairs={{1,0},{2,1},{3,2},{4,3},{5,4},{6,5},{7,6},{8,7},{9,8},{10,9},{11,1... | collective-permute-start | bytes 393224 | tf_op jit(solution)/shard_map/ppermute | solution.py:20
  420.8 1.6 copy-start.1
Sparse Core Ops, SparseCore 0:
  11.5 73.8 all-gather.2
  99.2 82.4 reduce-scatter.2
  184.6 70.2 all-gather.4
  263.2 82.4 reduce-scatter.4
where the time goes:
time: 433 us; the launch traced here: 429 us
  waiting for transfers between devices  325 us (75%)
  starting transfers between devices  35.7 us (8%)
  matrix products  35.5 us (8%)
  between operations  13.5 us (3%)
  other arithmetic  10.9 us (3%)
  local copies, waits for them, and re-layouts  7.92 us (2%)
    reduce_scatter x1, waiting for transfers between devices, per_device(): lax.psum_scatter(partial_value.astype(jnp.bfloat16), 'mp', scatter_dimens...  82.6 us
    reduce_scatter x1, waiting for transfers between devices, per_device(): lax.psum_scatter(mlp_terms.astype(jnp.bfloat16), 'mp', scatter_dimension=...  81.9 us
    all_gather x1, waiting for transfers between devices, per_device(): gathered = lax.all_gather(normed, 'mp', axis=1, tiled=True)  74 us
    all_gather x1, waiting for transfers between devices, per_device(): gathered_mid = lax.all_gather(normed_mid, 'mp', axis=1, tiled=True)  70.4 us
    ppermute x3, starting transfers between devices, extended_2(): lax.ppermute(lax.slice_in_dim(block, 0, width, axis=dim), axis, backward)  22.9 us
    dot_general x27, matrix products, conv_layer(): jnp.einsum('rwc,cd->rwd', window, kernel[row_shift, col_shift], preferred...  10.1 us
    all_to_all x1, waiting for transfers between devices, per_device(): lax.all_to_all(outgoing, 'tile', split_axis=0, concat_axis=0, tiled=True)  9.96 us
  transfers between devices with their start and end apart: 11, of which 11 were waited for; matrix products, arithmetic and copies ran while one was open for 1% of the time, Pallas kernels for 0%

commit v1 on v0

v1 whole, which is shorter than its diff:
```python
import jax
import jax.numpy as jnp
from jax import lax
from jax.sharding import Mesh, PartitionSpec as P

HEAD = 64
SIDE = 16
UP = 2
AXES = ("yl", "x", "c", "yh", "z")
TILE = ("yl", "x", "c")
MP = ("yh", "z")
F32 = jnp.float32
BF16 = jnp.bfloat16
FAR = 64.0


def layer_norm(values, gain):
    widened = values.astype(F32)
    centre = jnp.mean(widened, axis=-1, keepdims=True)
    spread = jnp.mean((widened - centre) ** 2, axis=-1, keepdims=True)
    return ((widened - centre) * lax.rsqrt(spread + 1e-06) * gain).astype(BF16)


def ring(axis, step):
    count = lax.axis_size(axis)
    return [(i, (i + step) % count) for i in range(count)]


def swap_cores(block):
    return lax.ppermute(block, "c", [(0, 1), (1, 0)])


def type_exchange(block):
    def at(pos, core):
        return ((pos % 2) * 2 + core) * 2 + pos // 2

    pairs = []
    for core in range(2):
        for pos in range(4):
            if pos // 2 == core:
                pairs.append((at(pos, core), at(3 - pos, core)))
    received = lax.ppermute(block, ("yl", "c", "yh"), pairs)
    mine = lax.axis_index("yh") == lax.axis_index("c")
    return jnp.where(mine, block, received)


def conv_layer(extended, kernel, shift, out_count):
    width_px = extended.shape[1]
    padded = jnp.pad(extended, ((0, 0), (1, 1), (0, 0)))
    running = jnp.zeros((out_count, width_px, kernel.shape[-1]), F32) + shift
    for row_shift in range(3):
        for col_shift in range(3):
            window = padded[row_shift : row_shift + out_count, col_shift : col_shift + width_px]
            running = running + jnp.einsum(
                "rwc,cd->rwd", window, kernel[row_shift, col_shift], preferred_element_type=F32
            )
    return running


def per_device(
    tokens,
    ln_gain_one,
    ln_gain_two,
    qkv_weight,
    out_weight,
    in_weight,
    mlp_out_weight,
    proj_weight,
    land_mask,
    placement,
    guide,
    conv_weights,
    conv_bias,
):
    tiles, seg, width = tokens.shape
    groups = lax.axis_size(TILE)
    here = lax.axis_index(TILE)
    core = lax.axis_index("c")

    parity = lax.axis_index("x") % 2
    heads_t = jnp.transpose(qkv_weight, (0, 2, 1))
    own_qkv = lax.dynamic_slice_in_dim(heads_t, parity * HEAD, HEAD, 1)
    own_out = lax.dynamic_slice_in_dim(out_weight, parity * HEAD, HEAD, 0)
    own_attn = jnp.concatenate([own_qkv.reshape(3 * HEAD, width), own_out], axis=0)
    piece = type_exchange(own_attn)
    pieces = [piece] + [lax.ppermute(piece, "z", ring("z", s)) for s in (1, 3, 2)]
    first_half = jnp.stack(pieces)
    from_above = lax.ppermute(first_half[:2], "x", ring("x", 3))
    from_below = lax.ppermute(first_half[2:], "x", ring("x", 1))
    attn_w = jnp.concatenate([first_half, from_above, from_below], axis=0)

    ff_half = in_weight.shape[0] // 2
    slice_rows = ff_half // 8
    start = core * ff_half + lax.axis_index(("x", "yl")) * slice_rows
    mlp_own = jnp.concatenate(
        [
            lax.dynamic_slice_in_dim(in_weight, start, slice_rows, 0),
            lax.dynamic_slice_in_dim(mlp_out_weight, start, slice_rows, 0),
        ],
        axis=0,
    )
    mlp_w = lax.all_gather(mlp_own, ("x", "yh", "yl", "z"), axis=0, tiled=False)
    w_in = mlp_w[:, :slice_rows].reshape(-1, width)
    w_out = mlp_w[:, slice_rows:].reshape(-1, width)

    slab_all = placement // tiles
    column_all = placement % tiles
    group_all = jnp.arange(placement.shape[0], dtype=jnp.int32) // tiles
    slab_local = lax.dynamic_slice_in_dim(slab_all, here * tiles, tiles, 0)
    selector = (slab_local[None, :] == jnp.arange(groups, dtype=jnp.int32)[:, None]).astype(BF16)
    in_slab = slab_all == here
    column_hot = (
        column_all[:, None] == jnp.arange(tiles, dtype=jnp.int32)[None, :]
    ) & in_slab[:, None]
    group_hot = group_all[:, None] == jnp.arange(groups, dtype=jnp.int32)[None, :]
    arrange = jnp.einsum(
        "tk,tg->kg", column_hot.astype(F32), group_hot.astype(F32)
    ).astype(BF16)
    marked = jnp.where((land_mask == 0)[:, None, None], jnp.asarray(FAR, BF16), tokens)
    outgoing = jnp.einsum("sj,jpd->spd", selector, marked, preferred_element_type=F32).astype(BF16)
    incoming = lax.all_to_all(outgoing, TILE, split_axis=0, concat_axis=0, tiled=True)
    slab_tokens = jnp.einsum(
        "kg,gpd->kpd", arrange, incoming, preferred_element_type=F32
    ).astype(BF16)
    land = slab_tokens[:, 0, 0] < FAR / 2
    tile_tokens = lax.all_to_all(slab_tokens, MP, split_axis=0, concat_axis=0, tiled=True)
    tile_tokens = tile_tokens.reshape(tiles * seg, width)

    count = tiles * seg
    normed = layer_norm(tile_tokens, ln_gain_one)
    pair = jnp.stack([normed, swap_cores(normed)])
    q, k, v = (
        jnp.einsum(
            "tpd,hed->thpe", pair, attn_w[:, i * HEAD : (i + 1) * HEAD], preferred_element_type=F32
        ).astype(BF16)
        for i in range(3)
    )
    scores = jnp.einsum("thpe,thqe->thpq", q, k, preferred_element_type=F32) * HEAD ** (-0.5)
    soft = jax.nn.softmax(scores, axis=-1).astype(BF16)
    context = jnp.einsum("thpq,thqe->thpe", soft, v, preferred_element_type=F32).astype(BF16)
    partial = jnp.einsum(
        "thpe,hed->tpd", context, attn_w[:, 3 * HEAD :], preferred_element_type=F32
    )
    attention = partial[0] + swap_cores(partial[1].astype(BF16)).astype(F32)
    middle = (tile_tokens.astype(F32) + attention).astype(BF16)

    middle = lax.all_to_all(
        middle.reshape(tiles, seg, width), MP, split_axis=0, concat_axis=0, tiled=True
    ).reshape(count, width)
    normed_mid = layer_norm(middle, ln_gain_two)
    pair_mid = jnp.concatenate([normed_mid, swap_cores(normed_mid)], axis=0)
    hidden = jnp.einsum("pd,fd->pf", pair_mid, w_in, preferred_element_type=F32)
    hidden = jax.nn.gelu(hidden).astype(BF16)
    mlp = jnp.einsum("pf,fd->pd", hidden, w_out, preferred_element_type=F32)
    mlp_sum = mlp[:count] + swap_cores(mlp[count:].astype(BF16)).astype(F32)
    features = (middle.astype(F32) + mlp_sum).astype(BF16)
    embed = jnp.einsum("pd,dc->pc", features, proj_weight, preferred_element_type=F32).astype(BF16)
    channels = proj_weight.shape[1]
    token_rows = seg // SIDE
    embed = embed.reshape(tiles, token_rows, SIDE, channels) * land.astype(BF16)[:, None, None, None]
    image = jnp.transpose(embed, (1, 0, 2, 3)).reshape(token_rows, tiles * SIDE, channels)

    total = lax.axis_size(AXES)
    forward = [(i, i + 1) for i in range(total - 1)]
    backward = [(b, a) for a, b in forward]
    rows = guide.shape[0]
    guide_low = lax.ppermute(guide[rows - 3 :], AXES, forward)
    guide_high = lax.ppermute(guide[:3], AXES, backward)
    image_low = lax.ppermute(image, AXES, forward)
    image_high = lax.ppermute(image, AXES, backward)
    image = jnp.concatenate([image_low, image, image_high], axis=0)
    guide = jnp.concatenate([guide_low, guide, guide_high], axis=0)
    upsampled = jnp.repeat(jnp.repeat(image, UP, axis=0), UP, axis=1)[1:-1]
    guided = (upsampled.astype(F32) + guide.astype(F32)).astype(BF16)

    first_row = lax.axis_index(AXES) * rows
    last_row = total * rows

    def inside(values, margin):
        row = first_row - margin + jnp.arange(values.shape[0], dtype=jnp.int32)
        return jnp.where(((row >= 0) & (row < last_row))[:, None, None], values, 0)

    first = jax.nn.gelu(conv_layer(guided, conv_weights[0], conv_bias[0], rows + 4))
    first = inside(first.astype(BF16), 2)
    second = jax.nn.gelu(conv_layer(first, conv_weights[1], conv_bias[1], rows + 2))
    second = inside(second.astype(BF16), 1)
    last_term = conv_layer(second, conv_weights[2], conv_bias[2], rows)
    return (guided[3:-3].astype(F32) + last_term).astype(BF16)


def solution(mesh):
    fine = Mesh(mesh.devices.reshape(2, 4, 2, 2, 4), AXES)
    in_specs = (
        P(TILE, MP, None),
        P(),
        P(),
        P(None, None, MP),
        P(MP, None),
        P(MP, None),
        P(MP, None),
        P(),
        P(TILE),
        P(),
        P(AXES, None, None),
        P(),
        P(),
    )
    return jax.shard_map(
        per_device, mesh=fine, in_specs=in_specs, out_specs=P(AXES, None, None), check_vma=False
    )
```

time: 433 us -> 201 us (0.46)
  waiting for transfers between devices: 325 us -> 45.4 us
  local copies, waits for them, and re-layouts: 7.92 us -> 34.5 us
  starting transfers between devices: 35.7 us -> 48.5 us
  other arithmetic: 10.9 us -> 18.2 us
    reduce_scatter x2 -> x0, waiting for transfers between devices: 164 us -> none  [the longest x1 82.6 us: per_device(): lax.psum_scatter(partial_value.astype(jnp.bfloat16), 'mp', scatter_dimens...]
    all_gather x2 -> x1, waiting for transfers between devices: 144 us -> 0.02 us  [per_device(): mlp_w = lax.all_gather(mlp_own, ('x', 'yh', 'yl', 'z'), axis=0, tiled=False)]
    ppermute x6 -> x14, waiting for transfers between devices: 6.59 us -> 33.7 us  [the longest x1 12.4 us: per_device(): from_above = lax.ppermute(first_half[:2], 'x', ring('x', 3))]
    all_to_all x1 -> x3, starting transfers between devices: 5 us -> 15.6 us  [the longest x1 5.59 us: per_device(): lax.all_to_all(slab_tokens, MP, split_axis=0, concat_axis=0, tiled=True)]
    slice x5 -> x4, local copies, waits for them, and re-layouts: 0.21 us -> 8.5 us  [the longest x1 6.26 us: per_device(): w_in = mlp_w[:, :slice_rows].reshape(-1, width)]
    unnamed x22 -> x36, local copies, waits for them, and re-layouts: 0.68 us -> 7.69 us
    sub x0 -> x1, other arithmetic: none -> 6.71 us  [per_device(): soft = jax.nn.softmax(scores, axis=-1).astype(BF16)]
    convert_element_type x2 -> x4, local copies, waits for them, and re-layouts: 1.71 us -> 7.43 us  [the longest x1 3.44 us: per_device(): guided = (upsampled.astype(F32) + guide.astype(F32)).astype(BF16)]
  transfers between devices with their start and end apart: 11 -> 18, of which waited for: 11 -> 9; matrix products, arithmetic and copies ran while one was open for 1% -> 37% of each run, Pallas kernels for 0% -> 0%
where the time goes in v1:
time: 201 us; the launch traced here: 198 us
  starting transfers between devices  48.5 us (24%)
  waiting for transfers between devices  45.4 us (23%)
  matrix products  37.8 us (19%)
  local copies, waits for them, and re-layouts  34.5 us (17%)
  other arithmetic  18.2 us (9%)
  between operations  14 us (7%)
    dot_general x27, matrix products, conv_layer(): jnp.einsum('rwc,cd->rwd', window, kernel[row_shift, col_shift], preferred...  13 us
    ppermute x1, waiting for transfers between devices, per_device(): from_above = lax.ppermute(first_half[:2], 'x', ring('x', 3))  12.4 us
    ppermute x3, waiting for transfers between devices, per_device(): lax.ppermute(piece, 'z', ring('z', s))  10.7 us
    dot_general x1, matrix products, per_device(): mlp = jnp.einsum('pf,fd->pd', hidden, w_out, preferred_element_type=F32)  9.45 us
    ppermute x1, starting transfers between devices, per_device(): image_high = lax.ppermute(image, AXES, backward)  8.15 us
    unnamed x36, local copies, waits for them, and re-layouts  7.69 us
    all_to_all x1, waiting for transfers between devices, per_device(): lax.all_to_all(outgoing, TILE, split_axis=0, concat_axis=0, tiled=True)  7.38 us
    sub x1, other arithmetic, per_device(): soft = jax.nn.softmax(scores, axis=-1).astype(BF16)  6.71 us
  transfers between devices with their start and end apart: 18, of which 9 were waited for; matrix products, arithmetic and copies ran while one was open for 37% of the time, Pallas kernels for 0%

profile of v1, /device:TPU:6, one launch (start us, length us, event | category | flops | bytes accessed | tf_op | source)
XLA Modules:
  0.0 198.4 jit_solution(7304096600700369495)
XLA Ops:
  8.9 5.0 %collective-permute-start = (bf16[256,1024]{1,0:T(8,128)(2,1)S(1)}, bf16[256,1024]{1,0:T(8,128)(2,1)S(1)}, u32[]{:S(2)}, u32[]{:S(2)}) collective-permute-start(bf16[256,1024]{1,0:T(8,128)(2,1)S(1)} %pad_maximum_fusion.3), channel_id=1, source_target_pairs={{0,68},{64,4},{12,72},{76,8},{1,69},{65,5},{13,73},{77,9},{2,70},{... | collective-permute-start | bytes 1572872 | tf_op jit(solution)/shard_map/ppermute | solution.py:42
  16.3 4.8 %all-to-all-start = ((bf16[16,32,1024]{2,1,0:T(8,128)(2,1)}), bf16[16,32,1024]{2,1,0:T(8,128)(2,1)S(1)}, u32[]{:S(2)}, u32[]{:S(2)}) async-start(bf16[16,32,1024]{2,1,0:T(8,128)(2,1)} %copy.56), calls=%async_computation | async-start | bytes 2097152 | tf_op jit(solution)/shard_map/all_to_all | solution.py:121
  28.1 7.4 %all-to-all-done = bf16[16,32,1024]{2,1,0:T(8,128)(2,1)S(1)} async-done(((bf16[16,32,1024]{2,1,0:T(8,128)(2,1)}), bf16[16,32,1024]{2,1,0:T(8,128)(2,1)S(1)}, u32[]{:S(2)}, u32[]{:S(2)}) %all-to-all-start) | async-done | bytes 1048608 | tf_op jit(solution)/shard_map/all_to_all | solution.py:121
  37.4 5.6 %all-to-all-start.1 = ((bf16[8,32,1024]{2,1,0:T(8,128)(2,1)}), bf16[8,32,1024]{2,1,0:T(8,128)(2,1)S(1)}, u32[]{:S(2)}, u32[]{:S(2)}) async-start(bf16[8,32,1024]{2,1,0:T(8,128)(2,1)} %copy.58), calls=%async_computation.1 | async-start | bytes 1048576 | tf_op jit(solution)/shard_map/all_to_all | solution.py:126
  44.8 8.8 %collective-permute-done.2 = bf16[256,1024]{1,0:T(8,128)(2,1)} collective-permute-done((bf16[256,1024]{1,0:T(8,128)(2,1)S(1)}, bf16[256,1024]{1,0:T(8,128)(2,1)}, u32[]{:S(2)}, u32[]{:S(2)}) %collective-permute-start.2) | collective-permute-done | bytes 524320 | tf_op jit(solution)/shard_map/ppermute | solution.py:86
  55.6 2.3 %pad_maximum_fusion.1 = bf16[2,256,1024]{2,1,0:T(8,128)(2,1)} fusion(bf16[1,256,1024]{2,1,0:T(8,128)(2,1)} %bitcast.8, bf16[1,256,1024]{2,1,0:T(8,128)(2,1)} %bitcast.7), kind=kLoop, calls=%fused_computation.82 | loop fusion | flops 524288 | bytes 2097152 | tf_op jit(solution)/shard_map/stack | solution.py:87
  64.0 12.4 %collective-permute-done.4 = bf16[2,256,1024]{2,1,0:T(8,128)(2,1)} collective-permute-done((bf16[2,256,1024]{2,1,0:T(8,128)(2,1)}, bf16[2,256,1024]{2,1,0:T(8,128)(2,1)}, u32[]{:S(2)}, u32[]{:S(2)}) %collective-permute-start.4) | collective-permute-done | bytes 1048608 | tf_op jit(solution)/shard_map/ppermute | solution.py:88
  76.4 2.3 %constant_dynamic-update-slice_fusion.1 = bf16[8,256,1024]{2,1,0:T(8,128)(2,1)} fusion(bf16[8,256,1024]{2,1,0:T(8,128)(2,1)} %constant_dynamic-update-slice_fusion.2, bf16[2,256,1024]{2,1,0:T(8,128)(2,1)} %collective-permute-done.4), kind=kLoop, calls=%fused_computation.215 | loop fusion | bytes 2097152
  78.7 6.1 %collective-permute-done.5 = bf16[2,256,1024]{2,1,0:T(8,128)(2,1)} collective-permute-done((bf16[2,256,1024]{2,1,0:T(8,128)(2,1)}, bf16[2,256,1024]{2,1,0:T(8,128)(2,1)}, u32[]{:S(2)}, u32[]{:S(2)}) %collective-permute-start.5) | collective-permute-done | bytes 1048608 | tf_op jit(solution)/shard_map/ppermute | solution.py:89
  84.9 2.4 %constant_dynamic-update-slice_fusion = bf16[8,256,1024]{2,1,0:T(8,128)(2,1)} fusion(bf16[8,256,1024]{2,1,0:T(8,128)(2,1)} %constant_dynamic-update-slice_fusion.1, bf16[2,256,1024]{2,1,0:T(8,128)(2,1)} %collective-permute-done.5), kind=kLoop, calls=%fused_computation.214 | loop fusion | bytes 2097152 | tf_op jit(solution)/shard_map/concatenate | solution.py:90
  91.3 4.5 %fusion.43 = f32[2,8,256,256]{2,3,1,0:T(8,128)} fusion(bf16[2,8,256,64]{2,3,1,0:T(8,128)(2,1)S(1)} %fusion.44, bf16[8,256,1024]{2,1,0:T(8,128)(2,1)} %constant_dynamic-update-slice_fusion, bf16[1,256,1024]{2,1,0:T(8,128)(2,1)S(1)} %bitcast.276, bf16[1,256,1024]{2,1,0:T(8,128)(2,1)S(1)} %fusion.75), kind=kOutput, calls=%fused_computation.57 | convolution fusion | flops 673447936 | bytes 6815744 | tf_op jit(solution)/shard_map/thpe,thqe->thpq/dot_general | solution.py:138
  95.8 6.7 %fusion.188 = (f32[2,8,256]{2,1,0:T(8,128)S(1)}, f32[2,8,256,256]{2,3,1,0:T(8,128)}) fusion(f32[2,8,256,256]{2,3,1,0:T(8,128)} %fusion.43), kind=kOutput, calls=%fused_computation.275 | output fusion | flops 4194559 | bytes 8404992 | tf_op jit(solution)/shard_map/sub | solution.py:139
  102.5 5.1 %convolution_bitcast_fusion = f32[2,256,1024]{2,1,0:T(8,128)} fusion(f32[2,8,256,256]{2,3,1,0:T(8,128)} %get-tuple-element.20, f32[2,8,256]{2,1,0:T(8,128)S(1)} %get-tuple-element.19, bf16[8,256,1024]{2,1,0:T(8,128)(2,1)} %constant_dynamic-update-slice_fusion, bf16[2,8,256,64]{2,3,0,1:T(8,128)(2,1)S(1)} %fusion.45), kind=kOutput, calls=%fused_computation.32 | convolution fusion | flops 673447936 | bytes 7880704 | tf_op jit(solution)/shard_map/thpe,hed->tpd/dot_general | solution.py:141
  110.9 2.3 %fusion.53 = bf16[256,1024]{1,0:T(8,128)(2,1)} fusion(f32[2,256,1024]{2,1,0:T(8,128)} %convolution_bitcast_fusion, bf16[8,32,1024]{2,1,0:T(8,128)(2,1)S(1)} %all-to-all-done.1, bf16[256,1024]{1,0:T(8,128)(2,1)S(1)} %collective-permute-done.7), kind=kLoop, calls=%fused_computation.76 | loop fusion | flops 1310720 | bytes 2621440 | tf_op jit(solution)/shard_map/convert_element_type | solution.py:145
  113.2 5.2 %all-to-all-start.2 = ((bf16[8,32,1024]{2,1,0:T(8,128)(2,1)}), bf16[8,32,1024]{2,1,0:T(8,128)(2,1)S(1)}, u32[]{:S(2)}, u32[]{:S(2)}) async-start(bf16[8,32,1024]{2,1,0:T(8,128)(2,1)} %bitcast.26), calls=%async_computation.2 | async-start | bytes 1048576 | tf_op jit(solution)/shard_map/all_to_all | solution.py:147
  119.3 4.1 %collective-permute-start.12 = (bf16[3,256,256]{2,1,0:T(8,128)(2,1)}, bf16[3,256,256]{2,1,0:T(8,128)(2,1)}, u32[]{:S(2)}, u32[]{:S(2)}) collective-permute-start(bf16[3,256,256]{2,1,0:T(8,128)(2,1)} %get-tuple-element.14), channel_id=1, source_target_pairs={{0,1},{1,2},{2,3},{3,4},{4,5},{5,6},{6,7},{7,8},{8,9},{9,10},{10,1... | collective-permute-start | bytes 1179656 | tf_op jit(solution)/shard_map/ppermute | solution.py:167
  123.4 6.0 %collective-permute-start.13 = (bf16[3,256,256]{2,1,0:T(8,128)(2,1)}, bf16[3,256,256]{2,1,0:T(8,128)(2,1)}, u32[]{:S(2)}, u32[]{:S(2)}) collective-permute-start(bf16[3,256,256]{2,1,0:T(8,128)(2,1)} %get-tuple-element.15), channel_id=1, source_target_pairs={{1,0},{2,1},{3,2},{4,3},{5,4},{6,5},{7,6},{8,7},{9,8},{10,9},{11,1... | collective-permute-start | bytes 1179656 | tf_op jit(solution)/shard_map/ppermute | solution.py:168
  129.4 4.4 %all-to-all-done.2 = bf16[8,32,1024]{2,1,0:T(8,128)(2,1)S(1)} async-done(((bf16[8,32,1024]{2,1,0:T(8,128)(2,1)}), bf16[8,32,1024]{2,1,0:T(8,128)(2,1)S(1)}, u32[]{:S(2)}, u32[]{:S(2)}) %all-to-all-start.2) | async-done | bytes 524320 | tf_op jit(solution)/shard_map/all_to_all | solution.py:147
  134.8 6.3 %fusion.185 = (bf16[64,32,1024]{2,1,0:T(8,128)(2,1)}, bf16[64,32,1024]{2,1,0:T(8,128)(2,1)}) fusion(bf16[64,64,1024]{2,1,0:T(8,128)(2,1)} %bitcast.261), kind=kLoop, calls=%fused_computation.272 | loop fusion | bytes 16777216 | tf_op jit(solution)/shard_map/slice | solution.py:103
  141.1 9.4 %fusion.20 = f32[512,1024]{1,0:T(8,128)} fusion(bf16[2048,1024]{1,0:T(8,128)(2,1)} %bitcast.264, bf16[2048,1024]{1,0:T(8,128)(2,1)} %bitcast.263, bf16[256,1024]{1,0:T(8,128)(2,1)S(1)} %collective-permute-done.8, bf16[256,1024]{1,0:T(8,128)(2,1)S(1)} %fusion.68), kind=kOutput, calls=%fused_computation.25 | convolution fusion | flops 4306501632 | bytes 11534336 | tf_op jit(solution)/shard_map/pf,fd->pd/dot_general | solution.py:154
  152.6 4.1 %slice_bitcast_fusion = (bf16[3,3,256,256]{3,2,1,0:T(8,128)(2,1)}, bf16[3,3,256,256]{3,2,1,0:T(8,128)(2,1)}, bf16[3,3,256,256]{3,2,1,0:T(8,128)(2,1)}) fusion(bf16[3,3,3,256,256]{4,3,2,1,0:T(8,128)(2,1)} %param.24), kind=kLoop, calls=%fused_computation.60 | loop fusion | bytes 7077888 | tf_op jit(solution)/shard_map/squeeze | solution.py:187
  160.0 8.2 %collective-permute-start.11 = (bf16[2,128,256]{2,1,0:T(8,128)(2,1)S(1)}, bf16[2,128,256]{2,1,0:T(8,128)(2,1)S(1)}, u32[]{:S(2)}, u32[]{:S(2)}) collective-permute-start(bf16[2,128,256]{2,1,0:T(8,128)(2,1)S(1)} %bitcast.272), channel_id=1, source_target_pairs={{1,0},{2,1},{3,2},{4,3},{5,4},{6,5},{7,6},{8,7},{9,8},{10,9},{11,1... | collective-permute-start | bytes 393224 | tf_op jit(solution)/shard_map/ppermute | solution.py:170
  170.9 2.4 %broadcast_in_dim.39 = f32[10,128,2,256]{3,2,1,0:T(2,128)} broadcast(f32[10,128,256]{2,1,0:T(8,128)S(1)} %slice_convert_fusion.2), dimensions={0,1,3} | broadcast | bytes 3932160 | tf_op jit(solution)/shard_map/broadcast_in_dim | solution.py:173
  173.4 3.4 %convert_element_type.185 = f32[10,256,256]{2,1,0:T(8,128)S(1)} reshape(f32[10,128,2,256]{3,2,1,0:T(2,128)} %broadcast_in_dim.39) | data formatting | bytes 5242880 | tf_op jit(solution)/shard_map/convert_element_type | solution.py:174
  (136 shorter events, 55.3 us)
Async XLA Ops:
  6.5 128.3 %all-gather.3.cloned.1.call-start = ((), (), s32[]{:S(2)}) async-start(), calls=%async_computation.3 | async-start | bytes 8519680 | tf_op jit(solution)/shard_map/all_gather | solution.py:102
  8.2 5.7 %copy-start.14 = (s32[128]{0:T(128)S(1)}, s32[128]{0:T(128)}, u32[]{:S(2)}) copy-start(s32[128]{0:T(128)} %param.22) | copy-start | bytes 1540
  8.2 5.8 %copy-start.15 = (s32[8]{0:T(128)S(1)}, s32[8]{0:T(128)}, u32[]{:S(2)}) copy-start(s32[8]{0:T(128)} %param.21) | copy-start | bytes 100
  8.2 5.8 %copy-start.9 = (bf16[8,32,1024]{2,1,0:T(8,128)(2,1)S(1)}, bf16[8,32,1024]{2,1,0:T(8,128)(2,1)}, u32[]{:S(2)}) copy-start(bf16[8,32,1024]{2,1,0:T(8,128)(2,1)} %param.13) | copy-start | bytes 1572868
  8.9 12.2 %collective-permute-start = (bf16[256,1024]{1,0:T(8,128)(2,1)S(1)}, bf16[256,1024]{1,0:T(8,128)(2,1)S(1)}, u32[]{:S(2)}, u32[]{:S(2)}) collective-permute-start(bf16[256,1024]{1,0:T(8,128)(2,1)S(1)} %pad_maximum_fusion.3), channel_id=1, source_target_pairs={{0,68},{64,4},{12,72},{76,8},{1,69},{65,5},{13,73},{77,9},{2,70},{... | collective-permute-start | bytes 1572872 | tf_op jit(solution)/shard_map/ppermute | solution.py:42
  16.3 19.2 %all-to-all-start = ((bf16[16,32,1024]{2,1,0:T(8,128)(2,1)}), bf16[16,32,1024]{2,1,0:T(8,128)(2,1)S(1)}, u32[]{:S(2)}, u32[]{:S(2)}) async-start(bf16[16,32,1024]{2,1,0:T(8,128)(2,1)} %copy.56), calls=%async_computation | async-start | bytes 2097152 | tf_op jit(solution)/shard_map/all_to_all | solution.py:121
  22.2 20.8 %collective-permute-start.1 = (bf16[256,1024]{1,0:T(8,128)(2,1)S(1)}, bf16[256,1024]{1,0:T(8,128)(2,1)S(1)}, u32[]{:S(2)}, u32[]{:S(2)}) collective-permute-start(bf16[256,1024]{1,0:T(8,128)(2,1)S(1)} %get-tuple-element.8), channel_id=1, source_target_pairs={{0,1},{1,2},{2,3},{3,0},{4,5},{5,6},{6,7},{7,4},{8,9},{9,10},{10,1... | collective-permute-start | bytes 1572872 | tf_op jit(solution)/shard_map/ppermute | solution.py:86
  24.1 29.5 %collective-permute-start.2 = (bf16[256,1024]{1,0:T(8,128)(2,1)S(1)}, bf16[256,1024]{1,0:T(8,128)(2,1)}, u32[]{:S(2)}, u32[]{:S(2)}) collective-permute-start(bf16[256,1024]{1,0:T(8,128)(2,1)S(1)} %get-tuple-element.8), channel_id=1, source_target_pairs={{0,3},{1,0},{2,1},{3,2},{4,7},{5,4},{6,5},{7,6},{8,11},{9,8},{10,9... | collective-permute-start | bytes 1572872 | tf_op jit(solution)/shard_map/ppermute | solution.py:86
  26.2 29.3 %collective-permute-start.3 = (bf16[256,1024]{1,0:T(8,128)(2,1)S(1)}, bf16[256,1024]{1,0:T(8,128)(2,1)}, u32[]{:S(2)}, u32[]{:S(2)}) collective-permute-start(bf16[256,1024]{1,0:T(8,128)(2,1)S(1)} %get-tuple-element.8), channel_id=1, source_target_pairs={{0,2},{1,3},{2,0},{3,1},{4,6},{5,7},{6,4},{7,5},{8,10},{9,11},{10,... | collective-permute-start | bytes 1572872 | tf_op jit(solution)/shard_map/ppermute | solution.py:86
  37.4 25.1 %all-to-all-start.1 = ((bf16[8,32,1024]{2,1,0:T(8,128)(2,1)}), bf16[8,32,1024]{2,1,0:T(8,128)(2,1)S(1)}, u32[]{:S(2)}, u32[]{:S(2)}) async-start(bf16[8,32,1024]{2,1,0:T(8,128)(2,1)} %copy.58), calls=%async_computation.1 | async-start | bytes 1048576 | tf_op jit(solution)/shard_map/all_to_all | solution.py:126
  44.1 32.3 %collective-permute-start.4 = (bf16[2,256,1024]{2,1,0:T(8,128)(2,1)}, bf16[2,256,1024]{2,1,0:T(8,128)(2,1)}, u32[]{:S(2)}, u32[]{:S(2)}) collective-permute-start(bf16[2,256,1024]{2,1,0:T(8,128)(2,1)} %pad_maximum_fusion), channel_id=1, source_target_pairs={{0,48},{16,0},{32,16},{48,32},{1,49},{17,1},{33,17},{49,33},{2,50}... | collective-permute-start | bytes 3145736 | tf_op jit(solution)/shard_map/ppermute | solution.py:88
  57.8 27.0 %collective-permute-start.5 = (bf16[2,256,1024]{2,1,0:T(8,128)(2,1)}, bf16[2,256,1024]{2,1,0:T(8,128)(2,1)}, u32[]{:S(2)}, u32[]{:S(2)}) collective-permute-start(bf16[2,256,1024]{2,1,0:T(8,128)(2,1)} %pad_maximum_fusion.1), channel_id=1, source_target_pairs={{0,16},{16,32},{32,48},{48,0},{1,17},{17,33},{33,49},{49,1},{2,18}... | collective-permute-start | bytes 3145736 | tf_op jit(solution)/shard_map/ppermute | solution.py:89
  63.4 23.9 %collective-permute-start.6 = (bf16[256,1024]{1,0:T(8,128)(2,1)S(1)}, bf16[256,1024]{1,0:T(8,128)(2,1)S(1)}, u32[]{:S(2)}, u32[]{:S(2)}) collective-permute-start(bf16[256,1024]{1,0:T(8,128)(2,1)S(1)} %fusion.78), channel_id=1, source_target_pairs={{0,8},{8,0},{1,9},{9,1},{2,10},{10,2},{3,11},{11,3},{4,12},{12,4},... | collective-permute-start | bytes 1572872 | tf_op jit(solution)/shard_map/ppermute | solution.py:30
  108.9 9.4 %copy-start.5 = (bf16[4,256,256]{2,1,0:T(8,128)(2,1)S(1)}, bf16[4,256,256]{2,1,0:T(8,128)(2,1)}, u32[]{:S(2)}) copy-start(bf16[4,256,256]{2,1,0:T(8,128)(2,1)} %param.23) | copy-start | bytes 1572868
  108.9 2.0 %collective-permute-start.7 = (bf16[256,1024]{1,0:T(8,128)(2,1)S(1)}, bf16[256,1024]{1,0:T(8,128)(2,1)S(1)}, u32[]{:S(2)}, u32[]{:S(2)}) collective-permute-start(bf16[256,1024]{1,0:T(8,128)(2,1)S(1)} %fusion.112), channel_id=1, source_target_pairs={{0,8},{8,0},{1,9},{9,1},{2,10},{10,2},{3,11},{11,3},{4,12},{12,4},... | collective-permute-start | bytes 1572872 | tf_op jit(solution)/shard_map/ppermute | solution.py:30
  113.2 21.2 %copy-start.12 = (f32[1024]{0:T(1024)S(1)}, f32[1024]{0:T(1024)}, u32[]{:S(2)}) copy-start(f32[1024]{0:T(1024)} %param.15) | copy-start | bytes 12292
  113.2 20.6 %all-to-all-start.2 = ((bf16[8,32,1024]{2,1,0:T(8,128)(2,1)}), bf16[8,32,1024]{2,1,0:T(8,128)(2,1)S(1)}, u32[]{:S(2)}, u32[]{:S(2)}) async-start(bf16[8,32,1024]{2,1,0:T(8,128)(2,1)} %bitcast.26), calls=%async_computation.2 | async-start | bytes 1048576 | tf_op jit(solution)/shard_map/all_to_all | solution.py:147
  119.3 57.5 %collective-permute-start.12 = (bf16[3,256,256]{2,1,0:T(8,128)(2,1)}, bf16[3,256,256]{2,1,0:T(8,128)(2,1)}, u32[]{:S(2)}, u32[]{:S(2)}) collective-permute-start(bf16[3,256,256]{2,1,0:T(8,128)(2,1)} %get-tuple-element.14), channel_id=1, source_target_pairs={{0,1},{1,2},{2,3},{3,4},{4,5},{5,6},{6,7},{7,8},{8,9},{9,10},{10,1... | collective-permute-start | bytes 1179656 | tf_op jit(solution)/shard_map/ppermute | solution.py:167
  123.4 53.4 %collective-permute-start.13 = (bf16[3,256,256]{2,1,0:T(8,128)(2,1)}, bf16[3,256,256]{2,1,0:T(8,128)(2,1)}, u32[]{:S(2)}, u32[]{:S(2)}) collective-permute-start(bf16[3,256,256]{2,1,0:T(8,128)(2,1)} %get-tuple-element.15), channel_id=1, source_target_pairs={{1,0},{2,1},{3,2},{4,3},{5,4},{6,5},{7,6},{8,7},{9,8},{10,9},{11,1... | collective-permute-start | bytes 1179656 | tf_op jit(solution)/shard_map/ppermute | solution.py:168
  134.7 6.4 %collective-permute-start.8 = (bf16[256,1024]{1,0:T(8,128)(2,1)S(1)}, bf16[256,1024]{1,0:T(8,128)(2,1)S(1)}, u32[]{:S(2)}, u32[]{:S(2)}) collective-permute-start(bf16[256,1024]{1,0:T(8,128)(2,1)S(1)} %fusion.68), channel_id=1, source_target_pairs={{0,8},{8,0},{1,9},{9,1},{2,10},{10,2},{3,11},{11,3},{4,12},{12,4},... | collective-permute-start | bytes 1572872 | tf_op jit(solution)/shard_map/ppermute | solution.py:30
  141.1 11.5 %copy-start.13 = (f32[3,256]{1,0:T(4,128)S(1)}, f32[3,256]{1,0:T(4,128)}, u32[]{:S(2)}) copy-start(f32[3,256]{1,0:T(4,128)} %param.25) | copy-start | bytes 9220
  151.8 5.0 %collective-permute-start.9 = (bf16[256,1024]{1,0:T(8,128)(2,1)S(1)}, bf16[256,1024]{1,0:T(8,128)(2,1)S(1)}, u32[]{:S(2)}, u32[]{:S(2)}) collective-permute-start(bf16[256,1024]{1,0:T(8,128)(2,1)S(1)} %slice.480), channel_id=1, source_target_pairs={{0,8},{8,0},{1,9},{9,1},{2,10},{10,2},{3,11},{11,3},{4,12},{12,4},... | collective-permute-start | bytes 1572872 | tf_op jit(solution)/shard_map/ppermute | solution.py:30
  158.1 10.9 %collective-permute-start.10 = (bf16[2,128,256]{2,1,0:T(8,128)(2,1)S(1)}, bf16[2,128,256]{2,1,0:T(8,128)(2,1)S(1)}, u32[]{:S(2)}, u32[]{:S(2)}) collective-permute-start(bf16[2,128,256]{2,1,0:T(8,128)(2,1)S(1)} %bitcast.271), channel_id=1, source_target_pairs={{0,1},{1,2},{2,3},{3,4},{4,5},{5,6},{6,7},{7,8},{8,9},{9,10},{10,1... | collective-permute-start | bytes 393224 | tf_op jit(solution)/shard_map/ppermute | solution.py:169
  160.0 10.7 %collective-permute-start.11 = (bf16[2,128,256]{2,1,0:T(8,128)(2,1)S(1)}, bf16[2,128,256]{2,1,0:T(8,128)(2,1)S(1)}, u32[]{:S(2)}, u32[]{:S(2)}) collective-permute-start(bf16[2,128,256]{2,1,0:T(8,128)(2,1)S(1)} %bitcast.272), channel_id=1, source_target_pairs={{1,0},{2,1},{3,2},{4,3},{5,4},{6,5},{7,6},{8,7},{9,8},{10,9},{11,1... | collective-permute-start | bytes 393224 | tf_op jit(solution)/shard_map/ppermute | solution.py:170
  (10 other events, 23.8 us)
Sparse Core Ops, SparseCore 0:
  10.2 101.0 all-gather.2

commit v2 on v1

v2 whole, which is shorter than its diff:
```python
import jax
import jax.numpy as jnp
from jax import lax
from jax.experimental import pallas as pl
from jax.experimental.pallas import tpu as pltpu
from jax.sharding import Mesh, PartitionSpec as P

HEAD = 64
SIDE = 16
AXES = ("yl", "x", "c", "yh", "z")
TILE = ("yl", "x", "c")
MP = ("yh", "z")
F32 = jnp.float32
BF16 = jnp.bfloat16
FAR = 64.0

def shift(block, axis, step):
    if axis == "y":
        def at(pos):
            return (pos % 2) * 2 + pos // 2

        pairs = [(at((pos + step) % 4), at(pos)) for pos in range(4)]
        return lax.ppermute(block, ("yl", "yh"), pairs)
    count = lax.axis_size(axis)
    return lax.ppermute(block, axis, [((i + step) % count, i) for i in range(count)])


def swap_cores(block):
    return lax.ppermute(block, "c", [(0, 1), (1, 0)])


def type_exchange(mine, sent):
    def at(pos, core):
        return ((pos % 2) * 2 + core) * 2 + pos // 2

    pairs = []
    for core in range(2):
        for pos in range(4):
            if pos // 2 == core:
                pairs.append((at(pos, core), at(3 - pos, core)))
    received = lax.ppermute(sent, ("yl", "c", "yh"), pairs)
    return jnp.where(lax.axis_index("yh") == lax.axis_index("c"), mine, received)


def along_z(piece):
    return jnp.stack([piece] + [shift(piece, "z", step) for step in (1, 3, 2)])


def across(base, one, two):
    return (
        base,
        shift(base, one, 1),
        shift(base, one, 3),
        shift(base[:2], two, 1),
        shift(base[2:], two, 3),
    )


VMEM_LIMIT = 56 * 2**20
NT = (((1,), (1,)), ((), ()))


def whole(memory):
    return pl.BlockSpec(memory_space=memory)


def normalise(values, gain):
    widened = values.astype(F32)
    centre = jnp.mean(widened, axis=-1, keepdims=True)
    spread = jnp.mean((widened - centre) ** 2, axis=-1, keepdims=True)
    return ((widened - centre) * lax.rsqrt(spread + 1e-06) * gain).astype(BF16)


def attention_kernel(
    parity, own, other, gain, base, plus, minus, two_low, two_high,
    near_out, far_out, held_base, held_plus, held_minus, held_two, normed, queries, values, context, sems
):
    copies = [
        pltpu.make_async_copy(base, held_base, sems.at[0]),
        pltpu.make_async_copy(minus, held_minus, sems.at[1]),
        pltpu.make_async_copy(plus, held_plus, sems.at[2]),
        pltpu.make_async_copy(two_low, held_two.at[0:2], sems.at[3]),
        pltpu.make_async_copy(two_high, held_two.at[2:4], sems.at[4]),
    ]
    for copy in copies:
        copy.start()
    even = parity[0] == 0
    count = own.shape[0]
    normed[0:count] = normalise(own[...], gain[...])
    normed[count:] = normalise(other[...], gain[...])
    for copy in copies:
        copy.wait()
    width = own.shape[1]
    half = 4 * HEAD

    def pick(one, two, rows):
        first = one[:, rows].reshape(-1, width)
        return jnp.where(even, first, two[:, rows].reshape(-1, width))

    everything = slice(0, 2 * HEAD)
    upper = slice(0, HEAD)
    lower = slice(HEAD, 2 * HEAD)
    sides = (
        ((held_base, held_minus), (held_plus, held_base)),
        ((held_two, held_plus), (held_minus, held_two)),
    )
    for side, (qk, vo) in enumerate(sides):
        queries[:, side * 2 * half : (side + 1) * 2 * half] = lax.dot_general(
            normed[...], pick(*qk, everything), NT, preferred_element_type=F32
        ).astype(BF16)
        values[:, side * half : (side + 1) * half] = lax.dot_general(
            normed[...], pick(*vo, upper), NT, preferred_element_type=F32
        ).astype(BF16)
    for tile in range(2):
        rows = slice(tile * count, (tile + 1) * count)
        for head in range(8):
            q = queries[rows, head * 2 * HEAD : head * 2 * HEAD + HEAD]
            k = queries[rows, head * 2 * HEAD + HEAD : (head + 1) * 2 * HEAD]
            v = values[rows, head * HEAD : (head + 1) * HEAD]
            scores = lax.dot_general(q, k, NT, preferred_element_type=F32) * HEAD ** (-0.5)
            scores = jnp.exp(scores - jnp.max(scores, axis=-1, keepdims=True))
            soft = (scores / jnp.sum(scores, axis=-1, keepdims=True)).astype(BF16)
            context[rows, head * HEAD : (head + 1) * HEAD] = jnp.dot(
                soft, v, preferred_element_type=F32
            ).astype(BF16)
    total = None
    for side, (qk, vo) in enumerate(sides):
        term = jnp.dot(
            context[:, side * half : (side + 1) * half], pick(*vo, lower), preferred_element_type=F32
        )
        total = term if total is None else total + term
    near_out[...] = total[:count]
    far_out[...] = total[count:].astype(BF16)


def attention(parity, own, other, gain, base, plus, minus, two_low, two_high):
    count, width = own.shape
    stack = pltpu.VMEM((4, 2 * HEAD, width), BF16)
    return pl.pallas_call(
        attention_kernel,
        out_shape=(
            jax.ShapeDtypeStruct((count, width), F32),
            jax.ShapeDtypeStruct((count, width), BF16),
        ),
        in_specs=[whole(pltpu.SMEM)] + [whole(pltpu.VMEM)] * 3 + [whole(pl.ANY)] * 5,
        out_specs=(whole(pltpu.VMEM), whole(pltpu.VMEM)),
        scratch_shapes=[stack] * 4
        + [
            pltpu.VMEM((2 * count, width), BF16),
            pltpu.VMEM((2 * count, 16 * HEAD), BF16),
            pltpu.VMEM((2 * count, 8 * HEAD), BF16),
            pltpu.VMEM((2 * count, 8 * HEAD), BF16),
            pltpu.SemaphoreType.DMA((5,)),
        ],
        compiler_params=pltpu.CompilerParams(vmem_limit_bytes=VMEM_LIMIT),
        cost_estimate=pl.CostEstimate(flops=3 * 10**9, bytes_accessed=7 * 10**6, transcendentals=2**20),
        name="attention",
    )(parity, own, other, gain, base, plus, minus, two_low, two_high)


def mlp_kernel(own, other, gain, *rest):
    groups = rest[:10]
    near_out, far_out, held, normed, total, sems = rest[10:]
    copies = []
    slot = 0
    for at, group in enumerate(groups):
        size = group.shape[0]
        copies.append(pltpu.make_async_copy(group, held.at[slot : slot + size], sems.at[at]))
        slot += size
    for copy in copies:
        copy.start()
    count, width = own.shape
    normed[0:count] = normalise(own[...], gain[...])
    normed[count:] = normalise(other[...], gain[...])
    slot = 0
    for at, group in enumerate(groups):
        copies[at].wait()
        size = group.shape[0]
        w_in = held[slot : slot + size, :HEAD].reshape(-1, width)
        w_out = held[slot : slot + size, HEAD:].reshape(-1, width)
        hidden = lax.dot_general(normed[...], w_in, NT, preferred_element_type=F32)
        hidden = jax.nn.gelu(hidden).astype(BF16)
        term = jnp.dot(hidden, w_out, preferred_element_type=F32)
        if at == 0:
            total[...] = term
        else:
            total[...] += term
        slot += size
    near_out[...] = total[:count]
    far_out[...] = total[count:].astype(BF16)


def mlp(own, other, gain, groups):
    count, width = own.shape
    return pl.pallas_call(
        mlp_kernel,
        out_shape=(
            jax.ShapeDtypeStruct((count, width), F32),
            jax.ShapeDtypeStruct((count, width), BF16),
        ),
        in_specs=[whole(pltpu.VMEM)] * 3 + [whole(pl.ANY)] * 10,
        out_specs=(whole(pltpu.VMEM), whole(pltpu.VMEM)),
        scratch_shapes=[
            pltpu.VMEM((32, 2 * HEAD, width), BF16),
            pltpu.VMEM((2 * count, width), BF16),
            pltpu.VMEM((2 * count, width), F32),
            pltpu.SemaphoreType.DMA((10,)),
        ],
        compiler_params=pltpu.CompilerParams(vmem_limit_bytes=VMEM_LIMIT),
        cost_estimate=pl.CostEstimate(flops=5 * 10**9, bytes_accessed=12 * 10**6, transcendentals=2**20),
        name="mlp",
    )(own, other, gain, *groups)


def conv_kernel(
    place, image_low, image, image_high, guide_low, guide, guide_high, weights, bias,
    out, guided, first, second, held, sems
):
    copies = [pltpu.make_async_copy(weights.at[k], held.at[k], sems.at[k]) for k in range(3)]
    for copy in copies:
        copy.start()
    cols = guide.shape[1]
    tokens = image.shape[1]
    channels = image.shape[2]
    pixel = lax.broadcasted_iota(jnp.int32, (cols, tokens), 0)
    token = lax.broadcasted_iota(jnp.int32, (cols, tokens), 1)
    spread = jnp.where(pixel // 2 == token, 1.0, 0.0).astype(BF16)
    rows = guide.shape[0]
    token_rows = (
        (image_low, 0), (image_low, 1), (image, 0), (image, 1), (image_high, 0), (image_high, 1)
    )
    for at, (source, row) in enumerate(token_rows):
        wide = jnp.dot(spread, source[row], preferred_element_type=F32)
        for pixel_row in (2 * at - 4, 2 * at - 3):
            if -3 <= pixel_row < 0:
                addend = guide_low[pixel_row + 3]
            elif 0 <= pixel_row < rows:
                addend = guide[pixel_row]
            elif rows <= pixel_row < rows + 3:
                addend = guide_high[pixel_row - rows]
            else:
                continue
            guided[pixel_row + 3] = (wide + addend.astype(F32)).astype(BF16)
    first_row = place[0]
    last_row = place[1]
    column = lax.broadcasted_iota(jnp.int32, (1, cols, channels), 1)
    at_left = column == 0
    at_right = column == cols - 1

    def layer(source, layer_at, start, size):
        sums = []
        for col in range(3):
            total = None
            for row in range(3):
                block = source[start + row : start + row + size].reshape(size * cols, channels)
                term = jnp.dot(block, held[layer_at, row, col], preferred_element_type=F32)
                total = term if total is None else total + term
            sums.append(total)
        left = pltpu.roll(sums[0], 1, 0).reshape(size, cols, channels)
        right = pltpu.roll(sums[2], size * cols - 1, 0).reshape(size, cols, channels)
        middle = sums[1].reshape(size, cols, channels)
        return (
            middle
            + jnp.where(at_left, 0.0, left)
            + jnp.where(at_right, 0.0, right)
            + bias[layer_at : layer_at + 1, :].reshape(1, 1, channels)
        )

    def inside(values, top):
        for row in range(values.shape[0]):
            at = first_row + top + row
            keep = jnp.logical_and(at >= 0, at < last_row)
            yield row, jnp.where(keep, values[row], 0.0).astype(BF16)

    copies[0].wait()
    for start in range(0, rows + 4, 2):
        for row, value in inside(jax.nn.gelu(layer(guided, 0, start, 2)), start - 2):
            first[start + row] = value
    copies[1].wait()
    for start in range(0, rows + 2, 2):
        for row, value in inside(jax.nn.gelu(layer(first, 1, start, 2)), start - 1):
            second[start + row] = value
    copies[2].wait()
    for start in range(0, rows, 2):
        last = layer(second, 2, start, 2) + guided[start + 3 : start + 5].astype(F32)
        out[start : start + 2] = last.astype(BF16)


def conv_stage(place, image_low, image, image_high, guide_low, guide, guide_high, weights, bias):
    rows, cols, channels = guide.shape
    return pl.pallas_call(
        conv_kernel,
        out_shape=jax.ShapeDtypeStruct(guide.shape, BF16),
        in_specs=[whole(pltpu.SMEM)] + [whole(pltpu.VMEM)] * 6 + [whole(pl.ANY), whole(pltpu.VMEM)],
        out_specs=whole(pltpu.VMEM),
        scratch_shapes=[
            pltpu.VMEM((rows + 6, cols, channels), BF16),
            pltpu.VMEM((rows + 4, cols, channels), BF16),
            pltpu.VMEM((rows + 2, cols, channels), BF16),
            pltpu.VMEM(weights.shape, BF16),
            pltpu.SemaphoreType.DMA((3,)),
        ],
        compiler_params=pltpu.CompilerParams(vmem_limit_bytes=VMEM_LIMIT),
        cost_estimate=pl.CostEstimate(flops=6 * 10**9, bytes_accessed=6 * 10**6, transcendentals=2**20),
        name="convs",
    )(place, image_low, image, image_high, guide_low, guide, guide_high, weights, bias)


def per_device(
    tokens,
    ln_gain_one,
    ln_gain_two,
    qkv_weight,
    out_weight,
    in_weight,
    mlp_out_weight,
    proj_weight,
    land_mask,
    placement,
    guide,
    conv_weights,
    conv_bias,
):
    tiles, seg, width = tokens.shape
    groups = lax.axis_size(TILE)
    here = lax.axis_index(TILE)

    x_at = lax.axis_index("x")
    y_at = lax.axis_index("yh") * 2 + lax.axis_index("yl")
    colour_x = (x_at + 2 * y_at) % 4
    colour_x_beside = (x_at + 2 * (3 - y_at)) % 4
    colour_y = (y_at + 2 * x_at) % 4
    colour_y_beside = (3 - y_at + 2 * x_at) % 4

    by_head = jnp.transpose(qkv_weight, (0, 2, 1)).reshape(3, 2, HEAD, width)
    out_heads = out_weight.reshape(2, HEAD, width)
    attn_all = jnp.stack(
        [by_head[0], by_head[1], by_head[2], out_heads], axis=1
    ).reshape(4, 2 * HEAD, width)
    attn_base = along_z(type_exchange(attn_all[colour_x], attn_all[colour_x_beside]))
    attn_w = across(attn_base, "x", "y")

    in_parts = in_weight.reshape(2, 4, HEAD, width)
    out_parts = mlp_out_weight.reshape(2, 4, HEAD, width)

    def mlp_slice(half, colour):
        return jnp.concatenate([in_parts[half, colour], out_parts[half, colour]], axis=0)

    mlp_pieces = type_exchange(
        jnp.stack([mlp_slice(0, colour_y), mlp_slice(1, colour_x)]),
        jnp.stack([mlp_slice(0, colour_y_beside), mlp_slice(1, colour_x_beside)]),
    )
    mlp_w = across(along_z(mlp_pieces[0]), "y", "x") + across(along_z(mlp_pieces[1]), "x", "y")

    slab_all = placement // tiles
    column_all = placement % tiles
    group_all = jnp.arange(placement.shape[0], dtype=jnp.int32) // tiles
    slab_local = lax.dynamic_slice_in_dim(slab_all, here * tiles, tiles, 0)
    selector = (slab_local[None, :] == jnp.arange(groups, dtype=jnp.int32)[:, None]).astype(BF16)
    in_slab = slab_all == here
    column_hot = (
        column_all[:, None] == jnp.arange(tiles, dtype=jnp.int32)[None, :]
    ) & in_slab[:, None]
    group_hot = group_all[:, None] == jnp.arange(groups, dtype=jnp.int32)[None, :]
    arrange = jnp.einsum(
        "tk,tg->kg", column_hot.astype(F32), group_hot.astype(F32)
    ).astype(BF16)
    marked = jnp.where((land_mask == 0)[:, None, None], jnp.asarray(FAR, BF16), tokens)
    outgoing = jnp.einsum("sj,jpd->spd", selector, marked, preferred_element_type=F32).astype(BF16)
    incoming = lax.all_to_all(outgoing, TILE, split_axis=0, concat_axis=0, tiled=True)
    slab_tokens = jnp.einsum(
        "kg,gpd->kpd", arrange, incoming, preferred_element_type=F32
    ).astype(BF16)
    land = slab_tokens[:, 0, 0] < FAR / 2
    tile_tokens = lax.all_to_all(slab_tokens, MP, split_axis=0, concat_axis=0, tiled=True)
    tile_tokens = tile_tokens.reshape(tiles * seg, width)

    count = tiles * seg
    near, far = attention(
        (x_at % 2).astype(jnp.int32).reshape(1),
        tile_tokens,
        swap_cores(tile_tokens),
        ln_gain_one.reshape(1, width),
        *attn_w,
    )
    summed = near + swap_cores(far).astype(F32)
    middle = (tile_tokens.astype(F32) + summed).astype(BF16)

    middle = lax.all_to_all(
        middle.reshape(tiles, seg, width), MP, split_axis=0, concat_axis=0, tiled=True
    ).reshape(count, width)
    near, far = mlp(middle, swap_cores(middle), ln_gain_two.reshape(1, width), mlp_w)
    summed = near + swap_cores(far).astype(F32)
    features = (middle.astype(F32) + summed).astype(BF16)
    embed = jnp.einsum("pd,dc->pc", features, proj_weight, preferred_element_type=F32).astype(BF16)
    channels = proj_weight.shape[1]
    token_rows = seg // SIDE
    embed = embed.reshape(tiles, token_rows, SIDE, channels) * land.astype(BF16)[:, None, None, None]
    image = jnp.transpose(embed, (1, 0, 2, 3)).reshape(token_rows, tiles * SIDE, channels)

    total = lax.axis_size(AXES)
    forward = [(i, i + 1) for i in range(total - 1)]
    backward = [(b, a) for a, b in forward]
    rows = guide.shape[0]
    guide_low = lax.ppermute(guide[rows - 3 :], AXES, forward)
    guide_high = lax.ppermute(guide[:3], AXES, backward)
    image_low = lax.ppermute(image, AXES, forward)
    image_high = lax.ppermute(image, AXES, backward)
    place = jnp.stack([lax.axis_index(AXES) * rows, jnp.int32(total * rows)])
    return conv_stage(
        place, image_low, image, image_high, guide_low, guide, guide_high, conv_weights, conv_bias
    )


def solution(mesh):
    fine = Mesh(mesh.devices.reshape(2, 4, 2, 2, 4), AXES)
    in_specs = (
        P(TILE, MP, None),
        P(),
        P(),
        P(None, None, MP),
        P(MP, None),
        P(MP, None),
        P(MP, None),
        P(),
        P(TILE),
        P(),
        P(AXES, None, None),
        P(),
        P(),
    )
    return jax.shard_map(
        per_device, mesh=fine, in_specs=in_specs, out_specs=P(AXES, None, None), check_vma=False
    )
```

time: 201 us -> 203 us (level)
  Pallas kernels: 0 us -> 36.6 us
  matrix products: 37.8 us -> 3.11 us
  starting transfers between devices: 48.5 us -> 75.9 us
  local copies, waits for them, and re-layouts: 34.5 us -> 8.45 us
  waiting for transfers between devices: 45.4 us -> 63.2 us
  between operations: 14 us -> 0.68 us
  other arithmetic: 18.2 us -> 13.1 us
    pallas_call x0 -> x3, Pallas kernels: none -> 36.6 us  [the longest x1 15.9 us: mlp(): pl.pallas_call(mlp_kernel, out_shape=(jax.ShapeDtypeStruct((count, width)...]
    dot_general x32 -> x0, matrix products: 36.1 us -> none  [the longest x27 13 us: conv_layer(): jnp.einsum('rwc,cd->rwd', window, kernel[row_shift, col_shift], preferred...]
    ppermute x6 -> x23, waiting for transfers between devices: 29.3 us -> 59 us  [the longest x6 42.3 us: shift(): return lax.ppermute(block, ('yl', 'yh'), pairs)]
    ppermute x6 -> x23, starting transfers between devices: 11.5 us -> 39.6 us  [the longest x15 25.4 us: shift(): lax.ppermute(block, axis, [((i + step) % count, i) for i in range(count)])]
    slice x4 -> x3, local copies, waits for them, and re-layouts: 8.5 us -> 1.03 us  [the longest x1 0.93 us: per_device(): mlp_pieces[1]]
    all_to_all x1, waiting for transfers between devices: 7.38 us -> 0.01 us  [per_device(): lax.all_to_all(outgoing, TILE, split_axis=0, concat_axis=0, tiled=True)]
    sub x1 -> x0, other arithmetic: 6.71 us -> none  [per_device(): soft = jax.nn.softmax(scores, axis=-1).astype(BF16)]
    unnamed x36 -> x45, local copies, waits for them, and re-layouts: 7.69 us -> 1.85 us
  transfers between devices with their start and end apart: 18 -> 34, of which waited for: 9 -> 11; matrix products, arithmetic and copies ran while one was open for 37% -> 9% of each run, Pallas kernels for 0% -> 5%
where the time goes in v2:
time: 203 us; the launch traced here: 201 us
  starting transfers between devices  75.9 us (37%)
  waiting for transfers between devices  63.2 us (31%)
  Pallas kernels  36.6 us (18%)
  other arithmetic  13.1 us (6%)
  local copies, waits for them, and re-layouts  8.45 us (4%)
  matrix products  3.11 us (2%)
    ppermute x6, waiting for transfers between devices, shift(): return lax.ppermute(block, ('yl', 'yh'), pairs)  42.3 us
    ppermute x15, starting transfers between devices, shift(): lax.ppermute(block, axis, [((i + step) % count, i) for i in range(count)])  25.4 us
    ppermute x15, waiting for transfers between devices, shift(): lax.ppermute(block, axis, [((i + step) % count, i) for i in range(count)])  16.6 us
    pallas_call x1, Pallas kernels, mlp(): pl.pallas_call(mlp_kernel, out_shape=(jax.ShapeDtypeStruct((count, width)...  15.9 us
    pallas_call x1, Pallas kernels, conv_stage(): pl.pallas_call(conv_kernel, out_shape=jax.ShapeDtypeStruct(guide.shape, B...  10.5 us
    pallas_call x1, Pallas kernels, attention(): pl.pallas_call(attention_kernel, out_shape=(jax.ShapeDtypeStruct((count,...  10.1 us
    ppermute x1, starting transfers between devices, per_device(): image_high = lax.ppermute(image, AXES, backward)  8.42 us
    ppermute x2, starting transfers between devices, type_exchange(): received = lax.ppermute(sent, ('yl', 'c', 'yh'), pairs)  7.61 us
  transfers between devices with their start and end apart: 34, of which 11 were waited for; matrix products, arithmetic and copies ran while one was open for 9% of the time, Pallas kernels for 5%

profile of v2, /device:TPU:6, one launch (start us, length us, event | category | flops | bytes accessed | tf_op | source)
XLA Modules:
  0.0 201.1 jit_solution(14721013702787470742)
XLA Ops:
  4.8 5.8 %all-to-all-start = ((bf16[16,32,1024]{2,1,0:T(8,128)(2,1)}), bf16[16,32,1024]{2,1,0:T(8,128)(2,1)S(1)}, u32[]{:S(2)}, u32[]{:S(2)}) async-start(bf16[16,32,1024]{2,1,0:T(8,128)(2,1)} %copy.29), calls=%async_computation | async-start | bytes 2097152 | tf_op jit(solution)/shard_map/all_to_all | solution.py:370
  12.0 5.5 %collective-permute-start.1 = (bf16[128,1024]{1,0:T(8,128)(2,1)}, bf16[128,1024]{1,0:T(8,128)(2,1)}, u32[]{:S(2)}, u32[]{:S(2)}) collective-permute-start(bf16[128,1024]{1,0:T(8,128)(2,1)} %dynamic-slice_bitcast_fusion), channel_id=1, source_target_pairs={{0,68},{64,4},{12,72},{76,8},{1,69},{65,5},{13,73},{77,9},{2,70},{... | collective-permute-start | bytes 786440 | tf_op jit(solution)/shard_map/ppermute | solution.py:41
  21.8 4.0 %collective-permute-start.4 = (bf16[128,1024]{1,0:T(8,128)(2,1)S(1)}, bf16[128,1024]{1,0:T(8,128)(2,1)S(1)}, u32[]{:S(2)}, u32[]{:S(2)}) collective-permute-start(bf16[128,1024]{1,0:T(8,128)(2,1)S(1)} %bitcast_select_fusion), channel_id=1, source_target_pairs={{2,0},{3,1},{0,2},{1,3},{6,4},{7,5},{4,6},{5,7},{10,8},{11,9},{8,1... | collective-permute-start | bytes 786440 | tf_op jit(solution)/shard_map/ppermute | solution.py:25
  26.8 2.2 %collective-permute-start.2 = (bf16[128,1024]{1,0:T(8,128)(2,1)S(1)}, bf16[128,1024]{1,0:T(8,128)(2,1)S(1)}, u32[]{:S(2)}, u32[]{:S(2)}) collective-permute-start(bf16[128,1024]{1,0:T(8,128)(2,1)S(1)} %bitcast_select_fusion), channel_id=1, source_target_pairs={{1,0},{2,1},{3,2},{0,3},{5,4},{6,5},{7,6},{4,7},{9,8},{10,9},{11,1... | collective-permute-start | bytes 786440 | tf_op jit(solution)/shard_map/ppermute | solution.py:25
  29.9 3.0 %collective-permute-done.4 = bf16[128,1024]{1,0:T(8,128)(2,1)S(1)} collective-permute-done((bf16[128,1024]{1,0:T(8,128)(2,1)S(1)}, bf16[128,1024]{1,0:T(8,128)(2,1)S(1)}, u32[]{:S(2)}, u32[]{:S(2)}) %collective-permute-start.4) | collective-permute-done | bytes 262176 | tf_op jit(solution)/shard_map/ppermute | solution.py:25
  32.9 5.0 %collective-permute-done.3 = bf16[128,1024]{1,0:T(8,128)(2,1)S(1)} collective-permute-done((bf16[128,1024]{1,0:T(8,128)(2,1)S(1)}, bf16[128,1024]{1,0:T(8,128)(2,1)S(1)}, u32[]{:S(2)}, u32[]{:S(2)}) %collective-permute-start.3) | collective-permute-done | bytes 262176 | tf_op jit(solution)/shard_map/ppermute | solution.py:25
  40.6 2.5 %collective-permute-start.6 = (bf16[4,128,1024]{2,1,0:T(8,128)(2,1)}, bf16[4,128,1024]{2,1,0:T(8,128)(2,1)}, u32[]{:S(2)}, u32[]{:S(2)}) collective-permute-start(bf16[4,128,1024]{2,1,0:T(8,128)(2,1)} %pad_maximum_fusion.1.base), channel_id=1, source_target_pairs={{48,0},{0,16},{16,32},{32,48},{49,1},{1,17},{17,33},{33,49},{50,2}... | collective-permute-start | bytes 3145736 | tf_op jit(solution)/shard_map/ppermute | solution.py:25
  48.2 3.8 %all-to-all-start.1 = ((bf16[8,32,1024]{2,1,0:T(8,128)(2,1)}), bf16[8,32,1024]{2,1,0:T(8,128)(2,1)S(1)}, u32[]{:S(2)}, u32[]{:S(2)}) async-start(bf16[8,32,1024]{2,1,0:T(8,128)(2,1)} %copy.31), calls=%async_computation.1 | async-start | bytes 1048576 | tf_op jit(solution)/shard_map/all_to_all | solution.py:375
  55.3 2.1 %collective-permute-start.19 = (bf16[128,1024]{1,0:T(8,128)(2,1)}, bf16[128,1024]{1,0:T(8,128)(2,1)S(1)}, u32[]{:S(2)}, u32[]{:S(2)}) collective-permute-start(bf16[128,1024]{1,0:T(8,128)(2,1)} %get-tuple-element.30), channel_id=1, source_target_pairs={{1,0},{2,1},{3,2},{0,3},{5,4},{6,5},{7,6},{4,7},{9,8},{10,9},{11,1... | collective-permute-start | bytes 786440 | tf_op jit(solution)/shard_map/ppermute | solution.py:25
  61.1 5.5 %collective-permute-done.13 = bf16[128,1024]{1,0:T(8,128)(2,1)S(1)} collective-permute-done((bf16[128,1024]{1,0:T(8,128)(2,1)}, bf16[128,1024]{1,0:T(8,128)(2,1)S(1)}, u32[]{:S(2)}, u32[]{:S(2)}) %collective-permute-start.13) | collective-permute-done | bytes 262176 | tf_op jit(solution)/shard_map/ppermute | solution.py:25
  66.6 2.5 %collective-permute-start.7 = (bf16[2,128,1024]{2,1,0:T(8,128)(2,1)}, bf16[2,128,1024]{2,1,0:T(8,128)(2,1)}, u32[]{:S(2)}, u32[]{:S(2)}) collective-permute-start(bf16[2,128,1024]{2,1,0:T(8,128)(2,1)} %pad_maximum_fusion.4), channel_id=1, source_target_pairs={{64,0},{4,64},{68,4},{0,68},{65,1},{5,65},{69,5},{1,69},{66,2},{6,... | collective-permute-start | bytes 1572872 | tf_op jit(solution)/shard_map/ppermute | solution.py:23
  69.1 2.3 %collective-permute-done.19 = bf16[128,1024]{1,0:T(8,128)(2,1)S(1)} collective-permute-done((bf16[128,1024]{1,0:T(8,128)(2,1)}, bf16[128,1024]{1,0:T(8,128)(2,1)S(1)}, u32[]{:S(2)}, u32[]{:S(2)}) %collective-permute-start.19) | collective-permute-done | bytes 262176 | tf_op jit(solution)/shard_map/ppermute | solution.py:25
  71.6 8.8 %collective-permute-done.7.two_low = bf16[2,128,1024]{2,1,0:T(8,128)(2,1)} collective-permute-done((bf16[2,128,1024]{2,1,0:T(8,128)(2,1)}, bf16[2,128,1024]{2,1,0:T(8,128)(2,1)}, u32[]{:S(2)}, u32[]{:S(2)}) %collective-permute-start.7) | collective-permute-done | bytes 524320 | tf_op jit(solution)/shard_map/ppermute | solution.py:23
  81.5 2.3 %collective-permute-done.8.two_high = bf16[2,128,1024]{2,1,0:T(8,128)(2,1)} collective-permute-done((bf16[2,128,1024]{2,1,0:T(8,128)(2,1)}, bf16[2,128,1024]{2,1,0:T(8,128)(2,1)}, u32[]{:S(2)}, u32[]{:S(2)}) %collective-permute-start.8) | collective-permute-done | bytes 524320 | tf_op jit(solution)/shard_map/ppermute | solution.py:23
  83.9 3.2 %collective-permute-start.18 = (bf16[2,128,1024]{2,1,0:T(8,128)(2,1)S(1)}, bf16[2,128,1024]{2,1,0:T(8,128)(2,1)S(1)}, u32[]{:S(2)}, u32[]{:S(2)}) collective-permute-start(bf16[2,128,1024]{2,1,0:T(8,128)(2,1)S(1)} %pad_maximum_fusion.8), channel_id=1, source_target_pairs={{48,0},{0,16},{16,32},{32,48},{49,1},{1,17},{17,33},{33,49},{50,2}... | collective-permute-start | bytes 1572872 | tf_op jit(solution)/shard_map/ppermute | solution.py:25
  88.7 10.1 %attention.1 = (f32[256,1024]{1,0:T(8,128)}, bf16[256,1024]{1,0:T(8,128)(2,1)}) custom-call(s32[1]{0:T(128)} %bitcast.4.parity, bf16[256,1024]{1,0:T(8,128)(2,1)} %bitcast.76, bf16[256,1024]{1,0:T(8,128)(2,1)} %collective-permute-done.other, f32[1,1024]{1,0:T(1,128)} %bitcast.108, bf16[4,128,1024]{2,1,0:T(8,128)(2,1)} %pad_maximum_fusion.1.base, ...), custom_call_target="tpu_custom_call" | custom-call | flops 3000000000 | bytes 7000000 | tf_op jit(solution)/shard_map/attention/pallas_call | solution.py:139
  103.3 3.2 %collective-permute-start.23 = (bf16[4,128,1024]{2,1,0:T(8,128)(2,1)}, bf16[4,128,1024]{2,1,0:T(8,128)(2,1)}, u32[]{:S(2)}, u32[]{:S(2)}) collective-permute-start(bf16[4,128,1024]{2,1,0:T(8,128)(2,1)} %pad_maximum_fusion.3.rest_5_), channel_id=1, source_target_pairs={{48,0},{0,16},{16,32},{32,48},{49,1},{1,17},{17,33},{33,49},{50,2}... | collective-permute-start | bytes 3145736 | tf_op jit(solution)/shard_map/ppermute | solution.py:25
  108.0 6.0 %all-to-all-start.2 = ((bf16[8,32,1024]{2,1,0:T(8,128)(2,1)}), bf16[8,32,1024]{2,1,0:T(8,128)(2,1)S(1)}, u32[]{:S(2)}, u32[]{:S(2)}) async-start(bf16[8,32,1024]{2,1,0:T(8,128)(2,1)} %bitcast.18), calls=%async_computation.2 | async-start | bytes 1048576 | tf_op jit(solution)/shard_map/all_to_all | solution.py:389
  114.0 31.2 %collective-permute-done.25.rest_9_ = bf16[2,128,1024]{2,1,0:T(8,128)(2,1)} collective-permute-done((bf16[2,128,1024]{2,1,0:T(8,128)(2,1)S(1)}, bf16[2,128,1024]{2,1,0:T(8,128)(2,1)}, u32[]{:S(2)}, u32[]{:S(2)}) %collective-permute-start.25) | collective-permute-done | bytes 524320 | tf_op jit(solution)/shard_map/ppermute | solution.py:23
  148.9 15.9 %mlp.1 = (f32[256,1024]{1,0:T(8,128)}, bf16[256,1024]{1,0:T(8,128)(2,1)}) custom-call(bf16[256,1024]{1,0:T(8,128)(2,1)} %bitcast.78, bf16[256,1024]{1,0:T(8,128)(2,1)} %copy-done.17, f32[1,1024]{1,0:T(1,128)} %bitcast.109, bf16[4,128,1024]{2,1,0:T(8,128)(2,1)} %pad_maximum_fusion.2.rest_0_, bf16[4,128,1024]{2,1,0:T(8,128)(2,1)} %collective-permute-done.15.rest_1_, ...), custom_call_target="tpu_custom_call" | custom-call | flops 5000000000 | bytes 12000000 | tf_op jit(solution)/shard_map/mlp/pallas_call | solution.py:195
  165.1 3.2 %collective-permute-start.29 = (bf16[3,256,256]{2,1,0:T(8,128)(2,1)S(1)}, bf16[3,256,256]{2,1,0:T(8,128)(2,1)S(1)}, u32[]{:S(2)}, u32[]{:S(2)}) collective-permute-start(bf16[3,256,256]{2,1,0:T(8,128)(2,1)S(1)} %get-tuple-element.27), channel_id=1, source_target_pairs={{0,1},{1,2},{2,3},{3,4},{4,5},{5,6},{6,7},{7,8},{8,9},{9,10},{10,1... | collective-permute-start | bytes 1179656 | tf_op jit(solution)/shard_map/ppermute | solution.py:405
  168.3 6.9 %collective-permute-start.30 = (bf16[3,256,256]{2,1,0:T(8,128)(2,1)S(1)}, bf16[3,256,256]{2,1,0:T(8,128)(2,1)S(1)}, u32[]{:S(2)}, u32[]{:S(2)}) collective-permute-start(bf16[3,256,256]{2,1,0:T(8,128)(2,1)S(1)} %get-tuple-element.26), channel_id=1, source_target_pairs={{1,0},{2,1},{3,2},{4,3},{5,4},{6,5},{7,6},{8,7},{9,8},{10,9},{11,1... | collective-permute-start | bytes 1179656 | tf_op jit(solution)/shard_map/ppermute | solution.py:406
  179.0 8.4 %collective-permute-start.28 = (bf16[2,128,256]{2,1,0:T(8,128)(2,1)S(1)}, bf16[2,128,256]{2,1,0:T(8,128)(2,1)S(1)}, u32[]{:S(2)}, u32[]{:S(2)}) collective-permute-start(bf16[2,128,256]{2,1,0:T(8,128)(2,1)S(1)} %bitcast.106), channel_id=1, source_target_pairs={{1,0},{2,1},{3,2},{4,3},{5,4},{6,5},{7,6},{8,7},{9,8},{10,9},{11,1... | collective-permute-start | bytes 393224 | tf_op jit(solution)/shard_map/ppermute | solution.py:408
  190.3 10.5 %convs.1 = bf16[4,256,256]{2,1,0:T(8,128)(2,1)} custom-call(s32[2]{0:T(128)} %pad_add_fusion.place, bf16[2,128,256]{2,1,0:T(8,128)(2,1)} %copy-done.20, bf16[2,128,256]{2,1,0:T(8,128)(2,1)} %bitcast.107, bf16[2,128,256]{2,1,0:T(8,128)(2,1)} %copy-done.21, bf16[3,256,256]{2,1,0:T(8,128)(2,1)} %copy-done.18, bf16[4,256,256]{2,1,0:T(8,128)(2,1)} %guide.1, ...), custom_call_target="tpu_custom_call" | custom-call | flops 6000000000 | bytes 6000000 | tf_op jit(solution)/shard_map/convs/pallas_call | solution.py:291
  (129 shorter events, 46.3 us)
Async XLA Ops:
  4.8 41.4 %all-to-all-start = ((bf16[16,32,1024]{2,1,0:T(8,128)(2,1)}), bf16[16,32,1024]{2,1,0:T(8,128)(2,1)S(1)}, u32[]{:S(2)}, u32[]{:S(2)}) async-start(bf16[16,32,1024]{2,1,0:T(8,128)(2,1)} %copy.29), calls=%async_computation | async-start | bytes 2097152 | tf_op jit(solution)/shard_map/all_to_all | solution.py:370
  19.6 23.5 %collective-permute-start.11 = (bf16[2,128,1024]{2,1,0:T(8,128)(2,1)S(1)}, bf16[2,128,1024]{2,1,0:T(8,128)(2,1)}, u32[]{:S(2)}, u32[]{:S(2)}) collective-permute-start(bf16[2,128,1024]{2,1,0:T(8,128)(2,1)S(1)} %pad_maximum_fusion.6), channel_id=1, source_target_pairs={{0,68},{64,4},{12,72},{76,8},{1,69},{65,5},{13,73},{77,9},{2,70},{... | collective-permute-start | bytes 1572872 | tf_op jit(solution)/shard_map/ppermute | solution.py:41
  39.9 43.9 %collective-permute-start.5 = (bf16[4,128,1024]{2,1,0:T(8,128)(2,1)}, bf16[4,128,1024]{2,1,0:T(8,128)(2,1)}, u32[]{:S(2)}, u32[]{:S(2)}) collective-permute-start(bf16[4,128,1024]{2,1,0:T(8,128)(2,1)} %pad_maximum_fusion.1.base), channel_id=1, source_target_pairs={{16,0},{32,16},{48,32},{0,48},{17,1},{33,17},{49,33},{1,49},{18,2}... | collective-permute-start | bytes 3145736 | tf_op jit(solution)/shard_map/ppermute | solution.py:25
  40.6 43.3 %collective-permute-start.6 = (bf16[4,128,1024]{2,1,0:T(8,128)(2,1)}, bf16[4,128,1024]{2,1,0:T(8,128)(2,1)}, u32[]{:S(2)}, u32[]{:S(2)}) collective-permute-start(bf16[4,128,1024]{2,1,0:T(8,128)(2,1)} %pad_maximum_fusion.1.base), channel_id=1, source_target_pairs={{48,0},{0,16},{16,32},{32,48},{49,1},{1,17},{17,33},{33,49},{50,2}... | collective-permute-start | bytes 3145736 | tf_op jit(solution)/shard_map/ppermute | solution.py:25
  48.2 23.2 %all-to-all-start.1 = ((bf16[8,32,1024]{2,1,0:T(8,128)(2,1)}), bf16[8,32,1024]{2,1,0:T(8,128)(2,1)S(1)}, u32[]{:S(2)}, u32[]{:S(2)}) async-start(bf16[8,32,1024]{2,1,0:T(8,128)(2,1)} %copy.31), calls=%async_computation.1 | async-start | bytes 1048576 | tf_op jit(solution)/shard_map/all_to_all | solution.py:375
  52.0 14.6 %collective-permute-start.13 = (bf16[128,1024]{1,0:T(8,128)(2,1)}, bf16[128,1024]{1,0:T(8,128)(2,1)S(1)}, u32[]{:S(2)}, u32[]{:S(2)}) collective-permute-start(bf16[128,1024]{1,0:T(8,128)(2,1)} %get-tuple-element.29), channel_id=1, source_target_pairs={{3,0},{0,1},{1,2},{2,3},{7,4},{4,5},{5,6},{6,7},{11,8},{8,9},{9,10... | collective-permute-start | bytes 786440 | tf_op jit(solution)/shard_map/ppermute | solution.py:25
  54.0 15.1 %collective-permute-start.12 = (bf16[128,1024]{1,0:T(8,128)(2,1)}, bf16[128,1024]{1,0:T(8,128)(2,1)S(1)}, u32[]{:S(2)}, u32[]{:S(2)}) collective-permute-start(bf16[128,1024]{1,0:T(8,128)(2,1)} %get-tuple-element.29), channel_id=1, source_target_pairs={{1,0},{2,1},{3,2},{0,3},{5,4},{6,5},{7,6},{4,7},{9,8},{10,9},{11,1... | collective-permute-start | bytes 786440 | tf_op jit(solution)/shard_map/ppermute | solution.py:25
  55.3 16.1 %collective-permute-start.19 = (bf16[128,1024]{1,0:T(8,128)(2,1)}, bf16[128,1024]{1,0:T(8,128)(2,1)S(1)}, u32[]{:S(2)}, u32[]{:S(2)}) collective-permute-start(bf16[128,1024]{1,0:T(8,128)(2,1)} %get-tuple-element.30), channel_id=1, source_target_pairs={{1,0},{2,1},{3,2},{0,3},{5,4},{6,5},{7,6},{4,7},{9,8},{10,9},{11,1... | collective-permute-start | bytes 786440 | tf_op jit(solution)/shard_map/ppermute | solution.py:25
  66.6 13.8 %collective-permute-start.7 = (bf16[2,128,1024]{2,1,0:T(8,128)(2,1)}, bf16[2,128,1024]{2,1,0:T(8,128)(2,1)}, u32[]{:S(2)}, u32[]{:S(2)}) collective-permute-start(bf16[2,128,1024]{2,1,0:T(8,128)(2,1)} %pad_maximum_fusion.4), channel_id=1, source_target_pairs={{64,0},{4,64},{68,4},{0,68},{65,1},{5,65},{69,5},{1,69},{66,2},{6,... | collective-permute-start | bytes 1572872 | tf_op jit(solution)/shard_map/ppermute | solution.py:23
  69.1 14.7 %collective-permute-start.8 = (bf16[2,128,1024]{2,1,0:T(8,128)(2,1)}, bf16[2,128,1024]{2,1,0:T(8,128)(2,1)}, u32[]{:S(2)}, u32[]{:S(2)}) collective-permute-start(bf16[2,128,1024]{2,1,0:T(8,128)(2,1)} %pad_maximum_fusion.5), channel_id=1, source_target_pairs={{68,0},{0,64},{64,4},{4,68},{69,1},{1,65},{65,5},{5,69},{70,2},{2,... | collective-permute-start | bytes 1572872 | tf_op jit(solution)/shard_map/ppermute | solution.py:23
  71.4 15.7 %collective-permute-start = (bf16[256,1024]{1,0:T(8,128)(2,1)S(1)}, bf16[256,1024]{1,0:T(8,128)(2,1)}, u32[]{:S(2)}, u32[]{:S(2)}) collective-permute-start(bf16[256,1024]{1,0:T(8,128)(2,1)S(1)} %bitcast.75), channel_id=1, source_target_pairs={{0,8},{8,0},{1,9},{9,1},{2,10},{10,2},{3,11},{11,3},{4,12},{12,4},... | collective-permute-start | bytes 1572872 | tf_op jit(solution)/shard_map/ppermute | solution.py:29
  80.4 18.4 %collective-permute-start.21 = (bf16[128,1024]{1,0:T(8,128)(2,1)}, bf16[128,1024]{1,0:T(8,128)(2,1)S(1)}, u32[]{:S(2)}, u32[]{:S(2)}) collective-permute-start(bf16[128,1024]{1,0:T(8,128)(2,1)} %get-tuple-element.30), channel_id=1, source_target_pairs={{2,0},{3,1},{0,2},{1,3},{6,4},{7,5},{4,6},{5,7},{10,8},{11,9},{8,1... | collective-permute-start | bytes 786440 | tf_op jit(solution)/shard_map/ppermute | solution.py:25
  83.8 16.3 %collective-permute-start.20 = (bf16[128,1024]{1,0:T(8,128)(2,1)}, bf16[128,1024]{1,0:T(8,128)(2,1)S(1)}, u32[]{:S(2)}, u32[]{:S(2)}) collective-permute-start(bf16[128,1024]{1,0:T(8,128)(2,1)} %get-tuple-element.30), channel_id=1, source_target_pairs={{3,0},{0,1},{1,2},{2,3},{7,4},{4,5},{5,6},{6,7},{11,8},{8,9},{9,10... | collective-permute-start | bytes 786440 | tf_op jit(solution)/shard_map/ppermute | solution.py:25
  83.8 17.5 %collective-permute-start.17 = (bf16[2,128,1024]{2,1,0:T(8,128)(2,1)S(1)}, bf16[2,128,1024]{2,1,0:T(8,128)(2,1)S(1)}, u32[]{:S(2)}, u32[]{:S(2)}) collective-permute-start(bf16[2,128,1024]{2,1,0:T(8,128)(2,1)S(1)} %pad_maximum_fusion.7), channel_id=1, source_target_pairs={{16,0},{32,16},{48,32},{0,48},{17,1},{33,17},{49,33},{1,49},{18,2}... | collective-permute-start | bytes 1572872 | tf_op jit(solution)/shard_map/ppermute | solution.py:25
  83.9 19.5 %collective-permute-start.18 = (bf16[2,128,1024]{2,1,0:T(8,128)(2,1)S(1)}, bf16[2,128,1024]{2,1,0:T(8,128)(2,1)S(1)}, u32[]{:S(2)}, u32[]{:S(2)}) collective-permute-start(bf16[2,128,1024]{2,1,0:T(8,128)(2,1)S(1)} %pad_maximum_fusion.8), channel_id=1, source_target_pairs={{48,0},{0,16},{16,32},{32,48},{49,1},{1,17},{17,33},{33,49},{50,2}... | collective-permute-start | bytes 1572872 | tf_op jit(solution)/shard_map/ppermute | solution.py:25
  87.1 16.2 %collective-permute-start.24 = (bf16[2,128,1024]{2,1,0:T(8,128)(2,1)S(1)}, bf16[2,128,1024]{2,1,0:T(8,128)(2,1)S(1)}, u32[]{:S(2)}, u32[]{:S(2)}) collective-permute-start(bf16[2,128,1024]{2,1,0:T(8,128)(2,1)S(1)} %pad_maximum_fusion.9), channel_id=1, source_target_pairs={{64,0},{4,64},{68,4},{0,68},{65,1},{5,65},{69,5},{1,69},{66,2},{6,... | collective-permute-start | bytes 1572872 | tf_op jit(solution)/shard_map/ppermute | solution.py:23
  100.1 46.0 %collective-permute-start.15 = (bf16[4,128,1024]{2,1,0:T(8,128)(2,1)}, bf16[4,128,1024]{2,1,0:T(8,128)(2,1)}, u32[]{:S(2)}, u32[]{:S(2)}) collective-permute-start(bf16[4,128,1024]{2,1,0:T(8,128)(2,1)} %pad_maximum_fusion.2.rest_0_), channel_id=1, source_target_pairs={{64,0},{4,64},{68,4},{0,68},{65,1},{5,65},{69,5},{1,69},{66,2},{6,... | collective-permute-start | bytes 3145736 | tf_op jit(solution)/shard_map/ppermute | solution.py:23
  101.3 44.8 %collective-permute-start.16 = (bf16[4,128,1024]{2,1,0:T(8,128)(2,1)}, bf16[4,128,1024]{2,1,0:T(8,128)(2,1)S(1)}, u32[]{:S(2)}, u32[]{:S(2)}) collective-permute-start(bf16[4,128,1024]{2,1,0:T(8,128)(2,1)} %pad_maximum_fusion.2.rest_0_), channel_id=1, source_target_pairs={{68,0},{0,64},{64,4},{4,68},{69,1},{1,65},{65,5},{5,69},{70,2},{2,... | collective-permute-start | bytes 3145736 | tf_op jit(solution)/shard_map/ppermute | solution.py:23
  103.3 42.8 %collective-permute-start.22 = (bf16[4,128,1024]{2,1,0:T(8,128)(2,1)}, bf16[4,128,1024]{2,1,0:T(8,128)(2,1)}, u32[]{:S(2)}, u32[]{:S(2)}) collective-permute-start(bf16[4,128,1024]{2,1,0:T(8,128)(2,1)} %pad_maximum_fusion.3.rest_5_), channel_id=1, source_target_pairs={{16,0},{32,16},{48,32},{0,48},{17,1},{33,17},{49,33},{1,49},{18,2}... | collective-permute-start | bytes 3145736 | tf_op jit(solution)/shard_map/ppermute | solution.py:25
  103.3 42.8 %collective-permute-start.23 = (bf16[4,128,1024]{2,1,0:T(8,128)(2,1)}, bf16[4,128,1024]{2,1,0:T(8,128)(2,1)}, u32[]{:S(2)}, u32[]{:S(2)}) collective-permute-start(bf16[4,128,1024]{2,1,0:T(8,128)(2,1)} %pad_maximum_fusion.3.rest_5_), channel_id=1, source_target_pairs={{48,0},{0,16},{16,32},{32,48},{49,1},{1,17},{17,33},{33,49},{50,2}... | collective-permute-start | bytes 3145736 | tf_op jit(solution)/shard_map/ppermute | solution.py:25
  106.6 38.7 %collective-permute-start.25 = (bf16[2,128,1024]{2,1,0:T(8,128)(2,1)S(1)}, bf16[2,128,1024]{2,1,0:T(8,128)(2,1)}, u32[]{:S(2)}, u32[]{:S(2)}) collective-permute-start(bf16[2,128,1024]{2,1,0:T(8,128)(2,1)S(1)} %pad_maximum_fusion.10), channel_id=1, source_target_pairs={{68,0},{0,64},{64,4},{4,68},{69,1},{1,65},{65,5},{5,69},{70,2},{2,... | collective-permute-start | bytes 1572872 | tf_op jit(solution)/shard_map/ppermute | solution.py:23
  108.0 38.1 %all-to-all-start.2 = ((bf16[8,32,1024]{2,1,0:T(8,128)(2,1)}), bf16[8,32,1024]{2,1,0:T(8,128)(2,1)S(1)}, u32[]{:S(2)}, u32[]{:S(2)}) async-start(bf16[8,32,1024]{2,1,0:T(8,128)(2,1)} %bitcast.18), calls=%async_computation.2 | async-start | bytes 1048576 | tf_op jit(solution)/shard_map/all_to_all | solution.py:389
  165.1 23.0 %collective-permute-start.29 = (bf16[3,256,256]{2,1,0:T(8,128)(2,1)S(1)}, bf16[3,256,256]{2,1,0:T(8,128)(2,1)S(1)}, u32[]{:S(2)}, u32[]{:S(2)}) collective-permute-start(bf16[3,256,256]{2,1,0:T(8,128)(2,1)S(1)} %get-tuple-element.27), channel_id=1, source_target_pairs={{0,1},{1,2},{2,3},{3,4},{4,5},{5,6},{6,7},{7,8},{8,9},{9,10},{10,1... | collective-permute-start | bytes 1179656 | tf_op jit(solution)/shard_map/ppermute | solution.py:405
  168.3 19.8 %collective-permute-start.30 = (bf16[3,256,256]{2,1,0:T(8,128)(2,1)S(1)}, bf16[3,256,256]{2,1,0:T(8,128)(2,1)S(1)}, u32[]{:S(2)}, u32[]{:S(2)}) collective-permute-start(bf16[3,256,256]{2,1,0:T(8,128)(2,1)S(1)} %get-tuple-element.26), channel_id=1, source_target_pairs={{1,0},{2,1},{3,2},{4,3},{5,4},{6,5},{7,6},{8,7},{9,8},{10,9},{11,1... | collective-permute-start | bytes 1179656 | tf_op jit(solution)/shard_map/ppermute | solution.py:406
  (32 other events, 418.6 us)

commit v3 on v2

--- a/solution.py
+++ b/solution.py
@@ -58,6 +58,7 @@
 
 VMEM_LIMIT = 56 * 2**20
 NT = (((1,), (1,)), ((), ()))
+PARTS = 4
 
 
 def whole(memory):
@@ -158,26 +159,25 @@
     )(parity, own, other, gain, base, plus, minus, two_low, two_high)
 
 
-def mlp_kernel(own, other, gain, *rest):
-    groups = rest[:10]
-    near_out, far_out, held, normed, total, sems = rest[10:]
-    copies = []
-    slot = 0
-    for at, group in enumerate(groups):
-        size = group.shape[0]
-        copies.append(pltpu.make_async_copy(group, held.at[slot : slot + size], sems.at[at]))
-        slot += size
+def mlp_kernel(own, other, gain, weights, near_out, far_out, held, normed, total, sems):
+    parts = sems.shape[0]
+    size = weights.shape[0] // parts
+    half = weights.shape[1] // 2
+    copies = [
+        pltpu.make_async_copy(
+            weights.at[at * size : (at + 1) * size], held.at[at * size : (at + 1) * size], sems.at[at]
+        )
+        for at in range(parts)
+    ]
     for copy in copies:
         copy.start()
     count, width = own.shape
     normed[0:count] = normalise(own[...], gain[...])
     normed[count:] = normalise(other[...], gain[...])
-    slot = 0
-    for at, group in enumerate(groups):
+    for at in range(parts):
         copies[at].wait()
-        size = group.shape[0]
-        w_in = held[slot : slot + size, :HEAD].reshape(-1, width)
-        w_out = held[slot : slot + size, HEAD:].reshape(-1, width)
+        w_in = held[at * size : (at + 1) * size, :half].reshape(-1, width)
+        w_out = held[at * size : (at + 1) * size, half:].reshape(-1, width)
         hidden = lax.dot_general(normed[...], w_in, NT, preferred_element_type=F32)
         hidden = jax.nn.gelu(hidden).astype(BF16)
         term = jnp.dot(hidden, w_out, preferred_element_type=F32)
@@ -185,12 +185,11 @@
             total[...] = term
         else:
             total[...] += term
-        slot += size
     near_out[...] = total[:count]
     far_out[...] = total[count:].astype(BF16)
 
 
-def mlp(own, other, gain, groups):
+def mlp(own, other, gain, weights, parts=PARTS):
     count, width = own.shape
     return pl.pallas_call(
         mlp_kernel,
@@ -198,18 +197,18 @@
             jax.ShapeDtypeStruct((count, width), F32),
             jax.ShapeDtypeStruct((count, width), BF16),
         ),
-        in_specs=[whole(pltpu.VMEM)] * 3 + [whole(pl.ANY)] * 10,
+        in_specs=[whole(pltpu.VMEM)] * 3 + [whole(pl.ANY)],
         out_specs=(whole(pltpu.VMEM), whole(pltpu.VMEM)),
         scratch_shapes=[
-            pltpu.VMEM((32, 2 * HEAD, width), BF16),
+            pltpu.VMEM(weights.shape, BF16),
             pltpu.VMEM((2 * count, width), BF16),
             pltpu.VMEM((2 * count, width), F32),
-            pltpu.SemaphoreType.DMA((10,)),
+            pltpu.SemaphoreType.DMA((parts,)),
         ],
         compiler_params=pltpu.CompilerParams(vmem_limit_bytes=VMEM_LIMIT),
         cost_estimate=pl.CostEstimate(flops=5 * 10**9, bytes_accessed=12 * 10**6, transcendentals=2**20),
         name="mlp",
-    )(own, other, gain, *groups)
+    )(own, other, gain, weights)
 
 
 def conv_kernel(
@@ -329,28 +328,26 @@
     y_at = lax.axis_index("yh") * 2 + lax.axis_index("yl")
     colour_x = (x_at + 2 * y_at) % 4
     colour_x_beside = (x_at + 2 * (3 - y_at)) % 4
-    colour_y = (y_at + 2 * x_at) % 4
-    colour_y_beside = (3 - y_at + 2 * x_at) % 4
 
     by_head = jnp.transpose(qkv_weight, (0, 2, 1)).reshape(3, 2, HEAD, width)
     out_heads = out_weight.reshape(2, HEAD, width)
     attn_all = jnp.stack(
         [by_head[0], by_head[1], by_head[2], out_heads], axis=1
     ).reshape(4, 2 * HEAD, width)
-    attn_base = along_z(type_exchange(attn_all[colour_x], attn_all[colour_x_beside]))
+    attn_piece = type_exchange(attn_all[colour_x], attn_all[colour_x_beside])
+    attn_base = along_z(attn_piece)
     attn_w = across(attn_base, "x", "y")
 
-    in_parts = in_weight.reshape(2, 4, HEAD, width)
-    out_parts = mlp_out_weight.reshape(2, 4, HEAD, width)
-
-    def mlp_slice(half, colour):
-        return jnp.concatenate([in_parts[half, colour], out_parts[half, colour]], axis=0)
-
-    mlp_pieces = type_exchange(
-        jnp.stack([mlp_slice(0, colour_y), mlp_slice(1, colour_x)]),
-        jnp.stack([mlp_slice(0, colour_y_beside), mlp_slice(1, colour_x_beside)]),
-    )
-    mlp_w = across(along_z(mlp_pieces[0]), "y", "x") + across(along_z(mlp_pieces[1]), "x", "y")
+    slice_rows = in_weight.shape[0] // 16
+    start = (lax.axis_index("c") * 8 + lax.axis_index(("x", "yl"))) * slice_rows
+    mlp_own = jnp.concatenate(
+        [
+            lax.dynamic_slice_in_dim(in_weight, start, slice_rows, 0),
+            lax.dynamic_slice_in_dim(mlp_out_weight, start, slice_rows, 0),
+        ],
+        axis=0,
+    )
+    mlp_w = lax.all_gather(mlp_own, ("x", "yh", "yl", "z"), axis=0, tiled=False)
 
     slab_all = placement // tiles
     column_all = placement % tiles
@@ -367,6 +364,7 @@
     ).astype(BF16)
     marked = jnp.where((land_mask == 0)[:, None, None], jnp.asarray(FAR, BF16), tokens)
     outgoing = jnp.einsum("sj,jpd->spd", selector, marked, preferred_element_type=F32).astype(BF16)
+    outgoing, _ = lax.optimization_barrier((outgoing, attn_piece))
     incoming = lax.all_to_all(outgoing, TILE, split_axis=0, concat_axis=0, tiled=True)
     slab_tokens = jnp.einsum(
         "kg,gpd->kpd", arrange, incoming, preferred_element_type=F32
@@ -386,9 +384,18 @@
     summed = near + swap_cores(far).astype(F32)
     middle = (tile_tokens.astype(F32) + summed).astype(BF16)
 
+    total = lax.axis_size(AXES)
+    forward = [(i, i + 1) for i in range(total - 1)]
+    backward = [(b, a) for a, b in forward]
+    rows = guide.shape[0]
+    guide_ends, _ = lax.optimization_barrier(((guide[rows - 3 :], guide[:3]), tile_tokens))
+    guide_low = lax.ppermute(guide_ends[0], AXES, forward)
+    guide_high = lax.ppermute(guide_ends[1], AXES, backward)
+
     middle = lax.all_to_all(
         middle.reshape(tiles, seg, width), MP, split_axis=0, concat_axis=0, tiled=True
     ).reshape(count, width)
+    middle, guide_low, guide_high = lax.optimization_barrier((middle, guide_low, guide_high))
     near, far = mlp(middle, swap_cores(middle), ln_gain_two.reshape(1, width), mlp_w)
     summed = near + swap_cores(far).astype(F32)
     features = (middle.astype(F32) + summed).astype(BF16)
@@ -398,12 +405,6 @@
     embed = embed.reshape(tiles, token_rows, SIDE, channels) * land.astype(BF16)[:, None, None, None]
     image = jnp.transpose(embed, (1, 0, 2, 3)).reshape(token_rows, tiles * SIDE, channels)
 
-    total = lax.axis_size(AXES)
-    forward = [(i, i + 1) for i in range(total - 1)]
-    backward = [(b, a) for a, b in forward]
-    rows = guide.shape[0]
-    guide_low = lax.ppermute(guide[rows - 3 :], AXES, forward)
-    guide_high = lax.ppermute(guide[:3], AXES, backward)
     image_low = lax.ppermute(image, AXES, forward)
     image_high = lax.ppermute(image, AXES, backward)
     place = jnp.stack([lax.axis_index(AXES) * rows, jnp.int32(total * rows)])

time: 203 us -> 168 us (0.83)
  waiting for transfers between devices: 63.2 us -> 42.7 us
  starting transfers between devices: 75.9 us -> 61.4 us
  between operations: 0.68 us -> 13.8 us
  Pallas kernels: 36.6 us -> 30.3 us
  other arithmetic: 13.1 us -> 7.3 us
    ppermute x6 -> x2, waiting for transfers between devices: 42.3 us -> 9.33 us  [shift(): return lax.ppermute(block, ('yl', 'yh'), pairs)]
    ppermute x15 -> x5, starting transfers between devices: 25.4 us -> 10.5 us  [shift(): lax.ppermute(block, axis, [((i + step) % count, i) for i in range(count)])]
    ppermute x2, waiting for transfers between devices: 0.01 us -> 6.65 us  [the longest x1 4.72 us: per_device(): guide_low = lax.ppermute(guide_ends[0], AXES, forward)]
    pallas_call x1, Pallas kernels: 15.9 us -> 9.59 us  [mlp(): pl.pallas_call(mlp_kernel, out_shape=(jax.ShapeDtypeStruct((count, width)...]
    ppermute x15 -> x5, waiting for transfers between devices: 16.6 us -> 10.4 us  [shift(): lax.ppermute(block, axis, [((i + step) % count, i) for i in range(count)])]
    all_to_all x1, waiting for transfers between devices: 0.01 us -> 6.19 us  [per_device(): lax.all_to_all(slab_tokens, MP, split_axis=0, concat_axis=0, tiled=True)]
    another operation x9 -> x3, other arithmetic: 7.33 us -> 3 us  [along_z(): return jnp.stack([piece] + [shift(piece, 'z', step) for step in (1, 3, 2)])]
    ppermute x4, starting transfers between devices: 0.31 us -> 4.6 us  [swap_cores(): return lax.ppermute(block, 'c', [(0, 1), (1, 0)])]
  transfers between devices with their start and end apart: 34 -> 20, of which waited for: 11 -> 14; matrix products, arithmetic and copies ran while one was open for 9% -> 7% of each run, Pallas kernels for 5% -> 6%
where the time goes in v3:
time: 168 us; the launch traced here: 165 us
  starting transfers between devices  61.4 us (37%)
  waiting for transfers between devices  42.7 us (25%)
  Pallas kernels  30.3 us (18%)
  between operations  13.8 us (8%)
  other arithmetic  7.3 us (4%)
  local copies, waits for them, and re-layouts  6.86 us (4%)
  matrix products  3.11 us (2%)
    pallas_call x1, Pallas kernels, conv_stage(): pl.pallas_call(conv_kernel, out_shape=jax.ShapeDtypeStruct(guide.shape, B...  10.5 us
    ppermute x5, starting transfers between devices, shift(): lax.ppermute(block, axis, [((i + step) % count, i) for i in range(count)])  10.5 us
    ppermute x5, waiting for transfers between devices, shift(): lax.ppermute(block, axis, [((i + step) % count, i) for i in range(count)])  10.4 us
    pallas_call x1, Pallas kernels, attention(): pl.pallas_call(attention_kernel, out_shape=(jax.ShapeDtypeStruct((count,...  10.2 us
    pallas_call x1, Pallas kernels, mlp(): pl.pallas_call(mlp_kernel, out_shape=(jax.ShapeDtypeStruct((count, width)...  9.59 us
    ppermute x2, waiting for transfers between devices, shift(): return lax.ppermute(block, ('yl', 'yh'), pairs)  9.33 us
    ppermute x1, starting transfers between devices, per_device(): image_high = lax.ppermute(image, AXES, backward)  8.15 us
    all_to_all x1, starting transfers between devices, per_device(): lax.all_to_all(slab_tokens, MP, split_axis=0, concat_axis=0, tiled=True)  7.57 us
  transfers between devices with their start and end apart: 20, of which 14 were waited for; matrix products, arithmetic and copies ran while one was open for 7% of the time, Pallas kernels for 6%

profile of v3, /device:TPU:6, one launch (start us, length us, event | category | flops | bytes accessed | tf_op | source)
XLA Modules:
  0.0 165.4 jit_solution(3556364650716015461)
XLA Ops:
  10.0 4.9 %collective-permute-start = (bf16[128,1024]{1,0:T(8,128)(2,1)S(1)}, bf16[128,1024]{1,0:T(8,128)(2,1)S(1)}, u32[]{:S(2)}, u32[]{:S(2)}) collective-permute-start(bf16[128,1024]{1,0:T(8,128)(2,1)S(1)} %dynamic-slice_bitcast_fusion), channel_id=1, source_target_pairs={{0,68},{64,4},{12,72},{76,8},{1,69},{65,5},{13,73},{77,9},{2,70},{... | collective-permute-start | bytes 786440 | tf_op jit(solution)/shard_map/ppermute | solution.py:41
  15.8 3.0 %collective-permute-done = bf16[128,1024]{1,0:T(8,128)(2,1)S(1)} collective-permute-done((bf16[128,1024]{1,0:T(8,128)(2,1)S(1)}, bf16[128,1024]{1,0:T(8,128)(2,1)S(1)}, u32[]{:S(2)}, u32[]{:S(2)}) %collective-permute-start) | collective-permute-done | bytes 262176 | tf_op jit(solution)/shard_map/ppermute | solution.py:41
  20.4 4.8 %all-to-all-start = ((bf16[16,32,1024]{2,1,0:T(8,128)(2,1)}), bf16[16,32,1024]{2,1,0:T(8,128)(2,1)S(1)}, u32[]{:S(2)}, u32[]{:S(2)}) async-start(bf16[16,32,1024]{2,1,0:T(8,128)(2,1)} %copy.31), calls=%async_computation | async-start | bytes 2097152 | tf_op jit(solution)/shard_map/all_to_all | solution.py:368
  25.2 3.9 %collective-permute-start.4 = (bf16[128,1024]{1,0:T(8,128)(2,1)S(1)}, bf16[128,1024]{1,0:T(8,128)(2,1)S(1)}, u32[]{:S(2)}, u32[]{:S(2)}) collective-permute-start(bf16[128,1024]{1,0:T(8,128)(2,1)S(1)} %bitcast_select_fusion), channel_id=1, source_target_pairs={{2,0},{3,1},{0,2},{1,3},{6,4},{7,5},{4,6},{5,7},{10,8},{11,9},{8,1... | collective-permute-start | bytes 786440 | tf_op jit(solution)/shard_map/ppermute | solution.py:25
  30.1 2.2 %collective-permute-start.2 = (bf16[128,1024]{1,0:T(8,128)(2,1)S(1)}, bf16[128,1024]{1,0:T(8,128)(2,1)S(1)}, u32[]{:S(2)}, u32[]{:S(2)}) collective-permute-start(bf16[128,1024]{1,0:T(8,128)(2,1)S(1)} %bitcast_select_fusion), channel_id=1, source_target_pairs={{1,0},{2,1},{3,2},{0,3},{5,4},{6,5},{7,6},{4,7},{9,8},{10,9},{11,1... | collective-permute-start | bytes 786440 | tf_op jit(solution)/shard_map/ppermute | solution.py:25
  32.3 4.7 %collective-permute-done.4 = bf16[128,1024]{1,0:T(8,128)(2,1)S(1)} collective-permute-done((bf16[128,1024]{1,0:T(8,128)(2,1)S(1)}, bf16[128,1024]{1,0:T(8,128)(2,1)S(1)}, u32[]{:S(2)}, u32[]{:S(2)}) %collective-permute-start.4) | collective-permute-done | bytes 262176 | tf_op jit(solution)/shard_map/ppermute | solution.py:25
  37.0 5.2 %collective-permute-done.3 = bf16[128,1024]{1,0:T(8,128)(2,1)S(1)} collective-permute-done((bf16[128,1024]{1,0:T(8,128)(2,1)S(1)}, bf16[128,1024]{1,0:T(8,128)(2,1)S(1)}, u32[]{:S(2)}, u32[]{:S(2)}) %collective-permute-start.3) | collective-permute-done | bytes 262176 | tf_op jit(solution)/shard_map/ppermute | solution.py:25
  43.8 2.4 %collective-permute-start.6 = (bf16[4,128,1024]{2,1,0:T(8,128)(2,1)S(1)}, bf16[4,128,1024]{2,1,0:T(8,128)(2,1)}, u32[]{:S(2)}, u32[]{:S(2)}) collective-permute-start(bf16[4,128,1024]{2,1,0:T(8,128)(2,1)S(1)} %pad_maximum_fusion.1.base), channel_id=1, source_target_pairs={{48,0},{0,16},{16,32},{32,48},{49,1},{1,17},{17,33},{33,49},{50,2}... | collective-permute-start | bytes 3145736 | tf_op jit(solution)/shard_map/ppermute | solution.py:25
  48.2 7.6 %all-to-all-start.1 = ((bf16[8,32,1024]{2,1,0:T(8,128)(2,1)}), bf16[8,32,1024]{2,1,0:T(8,128)(2,1)S(1)}, u32[]{:S(2)}, u32[]{:S(2)}) async-start(bf16[8,32,1024]{2,1,0:T(8,128)(2,1)} %copy.33), calls=%async_computation.1 | async-start | bytes 1048576 | tf_op jit(solution)/shard_map/all_to_all | solution.py:373
  58.7 3.6 %collective-permute-start.7 = (bf16[2,128,1024]{2,1,0:T(8,128)(2,1)}, bf16[2,128,1024]{2,1,0:T(8,128)(2,1)}, u32[]{:S(2)}, u32[]{:S(2)}) collective-permute-start(bf16[2,128,1024]{2,1,0:T(8,128)(2,1)} %pad_maximum_fusion.2), channel_id=1, source_target_pairs={{64,0},{4,64},{68,4},{0,68},{65,1},{5,65},{69,5},{1,69},{66,2},{6,... | collective-permute-start | bytes 1572872 | tf_op jit(solution)/shard_map/ppermute | solution.py:23
  62.2 6.2 %all-to-all-done.1 = bf16[8,32,1024]{2,1,0:T(8,128)(2,1)S(1)} async-done(((bf16[8,32,1024]{2,1,0:T(8,128)(2,1)}), bf16[8,32,1024]{2,1,0:T(8,128)(2,1)S(1)}, u32[]{:S(2)}, u32[]{:S(2)}) %all-to-all-start.1) | async-done | bytes 524320 | tf_op jit(solution)/shard_map/all_to_all | solution.py:373
  68.4 7.8 %collective-permute-done.7.two_low = bf16[2,128,1024]{2,1,0:T(8,128)(2,1)} collective-permute-done((bf16[2,128,1024]{2,1,0:T(8,128)(2,1)}, bf16[2,128,1024]{2,1,0:T(8,128)(2,1)}, u32[]{:S(2)}, u32[]{:S(2)}) %collective-permute-start.7) | collective-permute-done | bytes 524320 | tf_op jit(solution)/shard_map/ppermute | solution.py:23
  77.8 10.2 %attention.1 = (f32[256,1024]{1,0:T(8,128)}, bf16[256,1024]{1,0:T(8,128)(2,1)}) custom-call(s32[1]{0:T(128)} %bitcast.12.parity, bf16[256,1024]{1,0:T(8,128)(2,1)} %bitcast.41, bf16[256,1024]{1,0:T(8,128)(2,1)} %collective-permute-done.1.other, f32[1,1024]{1,0:T(1,128)} %bitcast.60, bf16[4,128,1024]{2,1,0:T(8,128)(2,1)} %copy-done.4, ...), custom_call_target="tpu_custom_call" | custom-call | flops 3000000000 | bytes 7000000 | tf_op jit(solution)/shard_map/attention/pallas_call | solution.py:140
  88.1 2.1 %collective-permute-done.9 = bf16[256,1024]{1,0:T(8,128)(2,1)S(1)} collective-permute-done((bf16[256,1024]{1,0:T(8,128)(2,1)}, bf16[256,1024]{1,0:T(8,128)(2,1)S(1)}, u32[]{:S(2)}, u32[]{:S(2)}) %collective-permute-start.9) | collective-permute-done | bytes 524320 | tf_op jit(solution)/shard_map/ppermute | solution.py:29
  90.2 2.5 %add_convert_fusion.1 = bf16[256,1024]{1,0:T(8,128)(2,1)} fusion(f32[256,1024]{1,0:T(8,128)} %get-tuple-element.16, bf16[256,1024]{1,0:T(8,128)(2,1)S(1)} %collective-permute-done.9, bf16[8,32,1024]{2,1,0:T(8,128)(2,1)} %copy-done.1), kind=kLoop, calls=%fused_computation.9 | loop fusion | flops 1310720 | bytes 2621440 | tf_op jit(solution)/shard_map/convert_element_type | solution.py:385
  92.7 5.3 %all-to-all-start.2 = ((bf16[8,32,1024]{2,1,0:T(8,128)(2,1)}), bf16[8,32,1024]{2,1,0:T(8,128)(2,1)S(1)}, u32[]{:S(2)}, u32[]{:S(2)}) async-start(bf16[8,32,1024]{2,1,0:T(8,128)(2,1)} %bitcast.18), calls=%async_computation.2 | async-start | bytes 1048576 | tf_op jit(solution)/shard_map/all_to_all | solution.py:395
  98.0 3.9 %collective-permute-start.10 = (bf16[3,256,256]{2,1,0:T(8,128)(2,1)S(1)}, bf16[3,256,256]{2,1,0:T(8,128)(2,1)S(1)}, u32[]{:S(2)}, u32[]{:S(2)}) collective-permute-start(bf16[3,256,256]{2,1,0:T(8,128)(2,1)S(1)} %get-tuple-element.18), channel_id=1, source_target_pairs={{0,1},{1,2},{2,3},{3,4},{4,5},{5,6},{6,7},{7,8},{8,9},{9,10},{10,1... | collective-permute-start | bytes 1179656 | tf_op jit(solution)/shard_map/ppermute | solution.py:392
  101.9 6.2 %collective-permute-start.11 = (bf16[3,256,256]{2,1,0:T(8,128)(2,1)S(1)}, bf16[3,256,256]{2,1,0:T(8,128)(2,1)S(1)}, u32[]{:S(2)}, u32[]{:S(2)}) collective-permute-start(bf16[3,256,256]{2,1,0:T(8,128)(2,1)S(1)} %get-tuple-element.19), channel_id=1, source_target_pairs={{1,0},{2,1},{3,2},{4,3},{5,4},{6,5},{7,6},{8,7},{9,8},{10,9},{11,1... | collective-permute-start | bytes 1179656 | tf_op jit(solution)/shard_map/ppermute | solution.py:393
  108.1 4.7 %collective-permute-done.10.guide_low = bf16[3,256,256]{2,1,0:T(8,128)(2,1)S(1)} collective-permute-done((bf16[3,256,256]{2,1,0:T(8,128)(2,1)S(1)}, bf16[3,256,256]{2,1,0:T(8,128)(2,1)S(1)}, u32[]{:S(2)}, u32[]{:S(2)}) %collective-permute-start.10) | collective-permute-done | bytes 393248 | tf_op jit(solution)/shard_map/ppermute | solution.py:392
  112.8 1.9 %collective-permute-done.11.guide_high = bf16[3,256,256]{2,1,0:T(8,128)(2,1)S(1)} collective-permute-done((bf16[3,256,256]{2,1,0:T(8,128)(2,1)S(1)}, bf16[3,256,256]{2,1,0:T(8,128)(2,1)S(1)}, u32[]{:S(2)}, u32[]{:S(2)}) %collective-permute-start.11) | collective-permute-done | bytes 393248 | tf_op jit(solution)/shard_map/ppermute | solution.py:393
  114.8 3.8 %collective-permute-start.12 = (bf16[256,1024]{1,0:T(8,128)(2,1)S(1)}, bf16[256,1024]{1,0:T(8,128)(2,1)S(1)}, u32[]{:S(2)}, u32[]{:S(2)}) collective-permute-start(bf16[256,1024]{1,0:T(8,128)(2,1)S(1)} %bitcast.42), channel_id=1, source_target_pairs={{0,8},{8,0},{1,9},{9,1},{2,10},{10,2},{3,11},{11,3},{4,12},{12,4},... | collective-permute-start | bytes 1572872 | tf_op jit(solution)/shard_map/ppermute | solution.py:29
  120.9 9.6 %mlp.1 = (f32[256,1024]{1,0:T(8,128)}, bf16[256,1024]{1,0:T(8,128)(2,1)}) custom-call(bf16[256,1024]{1,0:T(8,128)(2,1)} %bitcast.43, bf16[256,1024]{1,0:T(8,128)(2,1)} %copy-done.12, f32[1,1024]{1,0:T(1,128)} %bitcast.61, bf16[64,64,1024]{2,1,0:T(8,128)(2,1)} %bitcast.59), custom_call_target="tpu_custom_call" | custom-call | flops 5000000000 | bytes 12000000 | tf_op jit(solution)/shard_map/mlp/pallas_call | solution.py:194
  136.7 8.2 %collective-permute-start.15 = (bf16[2,128,256]{2,1,0:T(8,128)(2,1)S(1)}, bf16[2,128,256]{2,1,0:T(8,128)(2,1)S(1)}, u32[]{:S(2)}, u32[]{:S(2)}) collective-permute-start(bf16[2,128,256]{2,1,0:T(8,128)(2,1)S(1)} %bitcast.57), channel_id=1, source_target_pairs={{1,0},{2,1},{3,2},{4,3},{5,4},{6,5},{7,6},{8,7},{9,8},{10,9},{11,1... | collective-permute-start | bytes 393224 | tf_op jit(solution)/shard_map/ppermute | solution.py:409
  148.0 10.5 %convs.1 = bf16[4,256,256]{2,1,0:T(8,128)(2,1)} custom-call(s32[2]{0:T(128)} %pad_add_fusion.place, bf16[2,128,256]{2,1,0:T(8,128)(2,1)} %copy-done.15, bf16[2,128,256]{2,1,0:T(8,128)(2,1)} %bitcast.58, bf16[2,128,256]{2,1,0:T(8,128)(2,1)} %copy-done.16, bf16[3,256,256]{2,1,0:T(8,128)(2,1)} %copy-done.13, bf16[4,256,256]{2,1,0:T(8,128)(2,1)} %guide.1, ...), custom_call_target="tpu_custom_call" | custom-call | flops 6000000000 | bytes 6000000 | tf_op jit(solution)/shard_map/convs/pallas_call | solution.py:290
  (82 shorter events, 26.5 us)
Async XLA Ops:
  6.5 126.4 %copy-start = (bf16[1024,256]{1,0:T(8,128)(2,1)S(1)}, bf16[1024,256]{1,0:T(8,128)(2,1)}, u32[]{:S(2)}) copy-start(bf16[1024,256]{1,0:T(8,128)(2,1)} %param.20) | copy-start | bytes 1572868
  6.5 113.6 %all-gather.3.cloned.1.call-start = ((), (), s32[]{:S(2)}) async-start(), calls=%async_computation.3 | async-start | bytes 8519680 | tf_op jit(solution)/shard_map/all_gather | solution.py:350
  10.0 8.8 %collective-permute-start = (bf16[128,1024]{1,0:T(8,128)(2,1)S(1)}, bf16[128,1024]{1,0:T(8,128)(2,1)S(1)}, u32[]{:S(2)}, u32[]{:S(2)}) collective-permute-start(bf16[128,1024]{1,0:T(8,128)(2,1)S(1)} %dynamic-slice_bitcast_fusion), channel_id=1, source_target_pairs={{0,68},{64,4},{12,72},{76,8},{1,69},{65,5},{13,73},{77,9},{2,70},{... | collective-permute-start | bytes 786440 | tf_op jit(solution)/shard_map/ppermute | solution.py:41
  20.4 25.9 %all-to-all-start = ((bf16[16,32,1024]{2,1,0:T(8,128)(2,1)}), bf16[16,32,1024]{2,1,0:T(8,128)(2,1)S(1)}, u32[]{:S(2)}, u32[]{:S(2)}) async-start(bf16[16,32,1024]{2,1,0:T(8,128)(2,1)} %copy.31), calls=%async_computation | async-start | bytes 2097152 | tf_op jit(solution)/shard_map/all_to_all | solution.py:368
  25.2 11.8 %collective-permute-start.4 = (bf16[128,1024]{1,0:T(8,128)(2,1)S(1)}, bf16[128,1024]{1,0:T(8,128)(2,1)S(1)}, u32[]{:S(2)}, u32[]{:S(2)}) collective-permute-start(bf16[128,1024]{1,0:T(8,128)(2,1)S(1)} %bitcast_select_fusion), channel_id=1, source_target_pairs={{2,0},{3,1},{0,2},{1,3},{6,4},{7,5},{4,6},{5,7},{10,8},{11,9},{8,1... | collective-permute-start | bytes 786440 | tf_op jit(solution)/shard_map/ppermute | solution.py:25
  29.1 13.2 %collective-permute-start.3 = (bf16[128,1024]{1,0:T(8,128)(2,1)S(1)}, bf16[128,1024]{1,0:T(8,128)(2,1)S(1)}, u32[]{:S(2)}, u32[]{:S(2)}) collective-permute-start(bf16[128,1024]{1,0:T(8,128)(2,1)S(1)} %bitcast_select_fusion), channel_id=1, source_target_pairs={{3,0},{0,1},{1,2},{2,3},{7,4},{4,5},{5,6},{6,7},{11,8},{8,9},{9,10... | collective-permute-start | bytes 786440 | tf_op jit(solution)/shard_map/ppermute | solution.py:25
  30.1 12.6 %collective-permute-start.2 = (bf16[128,1024]{1,0:T(8,128)(2,1)S(1)}, bf16[128,1024]{1,0:T(8,128)(2,1)S(1)}, u32[]{:S(2)}, u32[]{:S(2)}) collective-permute-start(bf16[128,1024]{1,0:T(8,128)(2,1)S(1)} %bitcast_select_fusion), channel_id=1, source_target_pairs={{1,0},{2,1},{3,2},{0,3},{5,4},{6,5},{7,6},{4,7},{9,8},{10,9},{11,1... | collective-permute-start | bytes 786440 | tf_op jit(solution)/shard_map/ppermute | solution.py:25
  42.9 34.9 %copy-start.4 = (bf16[4,128,1024]{2,1,0:T(8,128)(2,1)}, bf16[4,128,1024]{2,1,0:T(8,128)(2,1)S(1)}, u32[]{:S(2)}) copy-start(bf16[4,128,1024]{2,1,0:T(8,128)(2,1)S(1)} %pad_maximum_fusion.1.base) | copy-start | bytes 3145732
  42.9 34.9 %collective-permute-start.5 = (bf16[4,128,1024]{2,1,0:T(8,128)(2,1)S(1)}, bf16[4,128,1024]{2,1,0:T(8,128)(2,1)}, u32[]{:S(2)}, u32[]{:S(2)}) collective-permute-start(bf16[4,128,1024]{2,1,0:T(8,128)(2,1)S(1)} %pad_maximum_fusion.1.base), channel_id=1, source_target_pairs={{16,0},{32,16},{48,32},{0,48},{17,1},{33,17},{49,33},{1,49},{18,2}... | collective-permute-start | bytes 3145736 | tf_op jit(solution)/shard_map/ppermute | solution.py:25
  43.8 33.9 %collective-permute-start.6 = (bf16[4,128,1024]{2,1,0:T(8,128)(2,1)S(1)}, bf16[4,128,1024]{2,1,0:T(8,128)(2,1)}, u32[]{:S(2)}, u32[]{:S(2)}) collective-permute-start(bf16[4,128,1024]{2,1,0:T(8,128)(2,1)S(1)} %pad_maximum_fusion.1.base), channel_id=1, source_target_pairs={{48,0},{0,16},{16,32},{32,48},{49,1},{1,17},{17,33},{33,49},{50,2}... | collective-permute-start | bytes 3145736 | tf_op jit(solution)/shard_map/ppermute | solution.py:25
  48.2 20.2 %all-to-all-start.1 = ((bf16[8,32,1024]{2,1,0:T(8,128)(2,1)}), bf16[8,32,1024]{2,1,0:T(8,128)(2,1)S(1)}, u32[]{:S(2)}, u32[]{:S(2)}) async-start(bf16[8,32,1024]{2,1,0:T(8,128)(2,1)} %copy.33), calls=%async_computation.1 | async-start | bytes 1048576 | tf_op jit(solution)/shard_map/all_to_all | solution.py:373
  58.7 17.5 %collective-permute-start.7 = (bf16[2,128,1024]{2,1,0:T(8,128)(2,1)}, bf16[2,128,1024]{2,1,0:T(8,128)(2,1)}, u32[]{:S(2)}, u32[]{:S(2)}) collective-permute-start(bf16[2,128,1024]{2,1,0:T(8,128)(2,1)} %pad_maximum_fusion.2), channel_id=1, source_target_pairs={{64,0},{4,64},{68,4},{0,68},{65,1},{5,65},{69,5},{1,69},{66,2},{6,... | collective-permute-start | bytes 1572872 | tf_op jit(solution)/shard_map/ppermute | solution.py:23
  62.2 15.5 %collective-permute-start.8 = (bf16[2,128,1024]{2,1,0:T(8,128)(2,1)S(1)}, bf16[2,128,1024]{2,1,0:T(8,128)(2,1)}, u32[]{:S(2)}, u32[]{:S(2)}) collective-permute-start(bf16[2,128,1024]{2,1,0:T(8,128)(2,1)S(1)} %pad_maximum_fusion.3), channel_id=1, source_target_pairs={{68,0},{0,64},{64,4},{4,68},{69,1},{1,65},{65,5},{5,69},{70,2},{2,... | collective-permute-start | bytes 1572872 | tf_op jit(solution)/shard_map/ppermute | solution.py:23
  68.4 9.3 %collective-permute-start.1 = (bf16[256,1024]{1,0:T(8,128)(2,1)S(1)}, bf16[256,1024]{1,0:T(8,128)(2,1)}, u32[]{:S(2)}, u32[]{:S(2)}) collective-permute-start(bf16[256,1024]{1,0:T(8,128)(2,1)S(1)} %bitcast.40), channel_id=1, source_target_pairs={{0,8},{8,0},{1,9},{9,1},{2,10},{10,2},{3,11},{11,3},{4,12},{12,4},... | collective-permute-start | bytes 1572872 | tf_op jit(solution)/shard_map/ppermute | solution.py:29
  88.0 2.2 %collective-permute-start.9 = (bf16[256,1024]{1,0:T(8,128)(2,1)}, bf16[256,1024]{1,0:T(8,128)(2,1)S(1)}, u32[]{:S(2)}, u32[]{:S(2)}) collective-permute-start(bf16[256,1024]{1,0:T(8,128)(2,1)} %get-tuple-element.17), channel_id=1, source_target_pairs={{0,8},{8,0},{1,9},{9,1},{2,10},{10,2},{3,11},{11,3},{4,12},{12,4},... | collective-permute-start | bytes 1572872 | tf_op jit(solution)/shard_map/ppermute | solution.py:29
  92.7 22.1 %all-to-all-start.2 = ((bf16[8,32,1024]{2,1,0:T(8,128)(2,1)}), bf16[8,32,1024]{2,1,0:T(8,128)(2,1)S(1)}, u32[]{:S(2)}, u32[]{:S(2)}) async-start(bf16[8,32,1024]{2,1,0:T(8,128)(2,1)} %bitcast.18), calls=%async_computation.2 | async-start | bytes 1048576 | tf_op jit(solution)/shard_map/all_to_all | solution.py:395
  98.0 14.8 %collective-permute-start.10 = (bf16[3,256,256]{2,1,0:T(8,128)(2,1)S(1)}, bf16[3,256,256]{2,1,0:T(8,128)(2,1)S(1)}, u32[]{:S(2)}, u32[]{:S(2)}) collective-permute-start(bf16[3,256,256]{2,1,0:T(8,128)(2,1)S(1)} %get-tuple-element.18), channel_id=1, source_target_pairs={{0,1},{1,2},{2,3},{3,4},{4,5},{5,6},{6,7},{7,8},{8,9},{9,10},{10,1... | collective-permute-start | bytes 1179656 | tf_op jit(solution)/shard_map/ppermute | solution.py:392
  101.9 12.8 %collective-permute-start.11 = (bf16[3,256,256]{2,1,0:T(8,128)(2,1)S(1)}, bf16[3,256,256]{2,1,0:T(8,128)(2,1)S(1)}, u32[]{:S(2)}, u32[]{:S(2)}) collective-permute-start(bf16[3,256,256]{2,1,0:T(8,128)(2,1)S(1)} %get-tuple-element.19), channel_id=1, source_target_pairs={{1,0},{2,1},{3,2},{4,3},{5,4},{6,5},{7,6},{8,7},{9,8},{10,9},{11,1... | collective-permute-start | bytes 1179656 | tf_op jit(solution)/shard_map/ppermute | solution.py:393
  112.8 21.8 %copy-start.13 = (bf16[3,256,256]{2,1,0:T(8,128)(2,1)}, bf16[3,256,256]{2,1,0:T(8,128)(2,1)S(1)}, u32[]{:S(2)}) copy-start(bf16[3,256,256]{2,1,0:T(8,128)(2,1)S(1)} %collective-permute-done.10.guide_low) | copy-start | bytes 1179652
  114.7 19.9 %copy-start.14 = (bf16[3,256,256]{2,1,0:T(8,128)(2,1)}, bf16[3,256,256]{2,1,0:T(8,128)(2,1)S(1)}, u32[]{:S(2)}) copy-start(bf16[3,256,256]{2,1,0:T(8,128)(2,1)S(1)} %collective-permute-done.11.guide_high) | copy-start | bytes 1179652
  114.8 5.4 %collective-permute-start.12 = (bf16[256,1024]{1,0:T(8,128)(2,1)S(1)}, bf16[256,1024]{1,0:T(8,128)(2,1)S(1)}, u32[]{:S(2)}, u32[]{:S(2)}) collective-permute-start(bf16[256,1024]{1,0:T(8,128)(2,1)S(1)} %bitcast.42), channel_id=1, source_target_pairs={{0,8},{8,0},{1,9},{9,1},{2,10},{10,2},{3,11},{11,3},{4,12},{12,4},... | collective-permute-start | bytes 1572872 | tf_op jit(solution)/shard_map/ppermute | solution.py:29
  130.5 2.4 %collective-permute-start.13 = (bf16[256,1024]{1,0:T(8,128)(2,1)}, bf16[256,1024]{1,0:T(8,128)(2,1)S(1)}, u32[]{:S(2)}, u32[]{:S(2)}) collective-permute-start(bf16[256,1024]{1,0:T(8,128)(2,1)} %get-tuple-element.22), channel_id=1, source_target_pairs={{0,8},{8,0},{1,9},{9,1},{2,10},{10,2},{3,11},{11,3},{4,12},{12,4},... | collective-permute-start | bytes 1572872 | tf_op jit(solution)/shard_map/ppermute | solution.py:29
  134.8 10.9 %collective-permute-start.14 = (bf16[2,128,256]{2,1,0:T(8,128)(2,1)S(1)}, bf16[2,128,256]{2,1,0:T(8,128)(2,1)S(1)}, u32[]{:S(2)}, u32[]{:S(2)}) collective-permute-start(bf16[2,128,256]{2,1,0:T(8,128)(2,1)S(1)} %bitcast.56), channel_id=1, source_target_pairs={{0,1},{1,2},{2,3},{3,4},{4,5},{5,6},{6,7},{7,8},{8,9},{9,10},{10,1... | collective-permute-start | bytes 393224 | tf_op jit(solution)/shard_map/ppermute | solution.py:408
  136.7 10.7 %collective-permute-start.15 = (bf16[2,128,256]{2,1,0:T(8,128)(2,1)S(1)}, bf16[2,128,256]{2,1,0:T(8,128)(2,1)S(1)}, u32[]{:S(2)}, u32[]{:S(2)}) collective-permute-start(bf16[2,128,256]{2,1,0:T(8,128)(2,1)S(1)} %bitcast.57), channel_id=1, source_target_pairs={{1,0},{2,1},{3,2},{4,3},{5,4},{6,5},{7,6},{8,7},{9,8},{10,9},{11,1... | collective-permute-start | bytes 393224 | tf_op jit(solution)/shard_map/ppermute | solution.py:409
  (14 other events, 69.3 us)
Sparse Core Ops, SparseCore 0:
  10.2 91.1 all-gather.2

commit v4 on v3

--- a/solution.py
+++ b/solution.py
@@ -43,20 +43,14 @@
 
 
 def along_z(piece):
-    return jnp.stack([piece] + [shift(piece, "z", step) for step in (1, 3, 2)])
-
-
-def across(base, one, two):
-    return (
-        base,
-        shift(base, one, 1),
-        shift(base, one, 3),
-        shift(base[:2], two, 1),
-        shift(base[2:], two, 3),
-    )
-
-
-VMEM_LIMIT = 56 * 2**20
+    return [piece] + [shift(piece, "z", step) for step in (1, 3, 2)]
+
+
+def across(pieces, one, two):
+    base = jnp.stack(pieces)
+    return base, shift(base, one, 1), shift(base, one, 3), shift(base, two, 1)
+
+
 NT = (((1,), (1,)), ((), ()))
 PARTS = 4
 
@@ -73,15 +67,14 @@
 
 
 def attention_kernel(
-    parity, own, other, gain, base, plus, minus, two_low, two_high,
+    parity, own, other, gain, base, plus, minus, two,
     near_out, far_out, held_base, held_plus, held_minus, held_two, normed, queries, values, context, sems
 ):
     copies = [
         pltpu.make_async_copy(base, held_base, sems.at[0]),
         pltpu.make_async_copy(minus, held_minus, sems.at[1]),
         pltpu.make_async_copy(plus, held_plus, sems.at[2]),
-        pltpu.make_async_copy(two_low, held_two.at[0:2], sems.at[3]),
-        pltpu.make_async_copy(two_high, held_two.at[2:4], sems.at[4]),
+        pltpu.make_async_copy(two, held_two, sems.at[3]),
     ]
     for copy in copies:
         copy.start()
@@ -115,12 +108,12 @@
     for tile in range(2):
         rows = slice(tile * count, (tile + 1) * count)
         for head in range(8):
-            q = queries[rows, head * 2 * HEAD : head * 2 * HEAD + HEAD]
+            q = queries[rows, head * 2 * HEAD : head * 2 * HEAD + HEAD] * BF16(HEAD ** (-0.5))
             k = queries[rows, head * 2 * HEAD + HEAD : (head + 1) * 2 * HEAD]
             v = values[rows, head * HEAD : (head + 1) * HEAD]
-            scores = lax.dot_general(q, k, NT, preferred_element_type=F32) * HEAD ** (-0.5)
+            scores = lax.dot_general(q, k, NT, preferred_element_type=F32)
             scores = jnp.exp(scores - jnp.max(scores, axis=-1, keepdims=True))
-            soft = (scores / jnp.sum(scores, axis=-1, keepdims=True)).astype(BF16)
+            soft = (scores * (1.0 / jnp.sum(scores, axis=-1, keepdims=True))).astype(BF16)
             context[rows, head * HEAD : (head + 1) * HEAD] = jnp.dot(
                 soft, v, preferred_element_type=F32
             ).astype(BF16)
@@ -130,11 +123,11 @@
             context[:, side * half : (side + 1) * half], pick(*vo, lower), preferred_element_type=F32
         )
         total = term if total is None else total + term
-    near_out[...] = total[:count]
+    near_out[...] = own[...].astype(F32) + total[:count]
     far_out[...] = total[count:].astype(BF16)
 
 
-def attention(parity, own, other, gain, base, plus, minus, two_low, two_high):
+def attention(parity, own, other, gain, base, plus, minus, two):
     count, width = own.shape
     stack = pltpu.VMEM((4, 2 * HEAD, width), BF16)
     return pl.pallas_call(
@@ -143,7 +136,7 @@
             jax.ShapeDtypeStruct((count, width), F32),
             jax.ShapeDtypeStruct((count, width), BF16),
         ),
-        in_specs=[whole(pltpu.SMEM)] + [whole(pltpu.VMEM)] * 3 + [whole(pl.ANY)] * 5,
+        in_specs=[whole(pltpu.SMEM)] + [whole(pltpu.VMEM)] * 3 + [whole(pl.ANY)] * 4,
         out_specs=(whole(pltpu.VMEM), whole(pltpu.VMEM)),
         scratch_shapes=[stack] * 4
         + [
@@ -151,12 +144,12 @@
             pltpu.VMEM((2 * count, 16 * HEAD), BF16),
             pltpu.VMEM((2 * count, 8 * HEAD), BF16),
             pltpu.VMEM((2 * count, 8 * HEAD), BF16),
-            pltpu.SemaphoreType.DMA((5,)),
+            pltpu.SemaphoreType.DMA((4,)),
         ],
-        compiler_params=pltpu.CompilerParams(vmem_limit_bytes=VMEM_LIMIT),
+        compiler_params=pltpu.CompilerParams(vmem_limit_bytes=24 * 2**20),
         cost_estimate=pl.CostEstimate(flops=3 * 10**9, bytes_accessed=7 * 10**6, transcendentals=2**20),
         name="attention",
-    )(parity, own, other, gain, base, plus, minus, two_low, two_high)
+    )(parity, own, other, gain, base, plus, minus, two)
 
 
 def mlp_kernel(own, other, gain, weights, near_out, far_out, held, normed, total, sems):
@@ -185,7 +178,7 @@
             total[...] = term
         else:
             total[...] += term
-    near_out[...] = total[:count]
+    near_out[...] = own[...].astype(F32) + total[:count]
     far_out[...] = total[count:].astype(BF16)
 
 
@@ -205,7 +198,7 @@
             pltpu.VMEM((2 * count, width), F32),
             pltpu.SemaphoreType.DMA((parts,)),
         ],
-        compiler_params=pltpu.CompilerParams(vmem_limit_bytes=VMEM_LIMIT),
+        compiler_params=pltpu.CompilerParams(vmem_limit_bytes=28 * 2**20),
         cost_estimate=pl.CostEstimate(flops=5 * 10**9, bytes_accessed=12 * 10**6, transcendentals=2**20),
         name="mlp",
     )(own, other, gain, weights)
@@ -299,7 +292,7 @@
             pltpu.VMEM(weights.shape, BF16),
             pltpu.SemaphoreType.DMA((3,)),
         ],
-        compiler_params=pltpu.CompilerParams(vmem_limit_bytes=VMEM_LIMIT),
+        compiler_params=pltpu.CompilerParams(vmem_limit_bytes=24 * 2**20),
         cost_estimate=pl.CostEstimate(flops=6 * 10**9, bytes_accessed=6 * 10**6, transcendentals=2**20),
         name="convs",
     )(place, image_low, image, image_high, guide_low, guide, guide_high, weights, bias)
@@ -335,8 +328,7 @@
         [by_head[0], by_head[1], by_head[2], out_heads], axis=1
     ).reshape(4, 2 * HEAD, width)
     attn_piece = type_exchange(attn_all[colour_x], attn_all[colour_x_beside])
-    attn_base = along_z(attn_piece)
-    attn_w = across(attn_base, "x", "y")
+    attn_w = across(along_z(attn_piece), "x", "y")
 
     slice_rows = in_weight.shape[0] // 16
     start = (lax.axis_index("c") * 8 + lax.axis_index(("x", "yl"))) * slice_rows
@@ -363,8 +355,8 @@
         "tk,tg->kg", column_hot.astype(F32), group_hot.astype(F32)
     ).astype(BF16)
     marked = jnp.where((land_mask == 0)[:, None, None], jnp.asarray(FAR, BF16), tokens)
+    marked, _ = lax.optimization_barrier((marked, attn_piece))
     outgoing = jnp.einsum("sj,jpd->spd", selector, marked, preferred_element_type=F32).astype(BF16)
-    outgoing, _ = lax.optimization_barrier((outgoing, attn_piece))
     incoming = lax.all_to_all(outgoing, TILE, split_axis=0, concat_axis=0, tiled=True)
     slab_tokens = jnp.einsum(
         "kg,gpd->kpd", arrange, incoming, preferred_element_type=F32
@@ -372,33 +364,34 @@
     land = slab_tokens[:, 0, 0] < FAR / 2
     tile_tokens = lax.all_to_all(slab_tokens, MP, split_axis=0, concat_axis=0, tiled=True)
     tile_tokens = tile_tokens.reshape(tiles * seg, width)
+    other_tokens = swap_cores(tile_tokens)
+
+    total = lax.axis_size(AXES)
+    forward = [(i, i + 1) for i in range(total - 1)]
+    backward = [(b, a) for a, b in forward]
+    rows = guide.shape[0]
+    guide_ends, _ = lax.optimization_barrier(((guide[rows - 3 :], guide[:3]), attn_w[0]))
+    guide_low = lax.ppermute(guide_ends[0], AXES, forward)
+    guide_high = lax.ppermute(guide_ends[1], AXES, backward)
+    tile_tokens, guide_low, guide_high = lax.optimization_barrier(
+        (tile_tokens, guide_low, guide_high)
+    )
 
     count = tiles * seg
     near, far = attention(
         (x_at % 2).astype(jnp.int32).reshape(1),
         tile_tokens,
-        swap_cores(tile_tokens),
+        other_tokens,
         ln_gain_one.reshape(1, width),
         *attn_w,
     )
-    summed = near + swap_cores(far).astype(F32)
-    middle = (tile_tokens.astype(F32) + summed).astype(BF16)
-
-    total = lax.axis_size(AXES)
-    forward = [(i, i + 1) for i in range(total - 1)]
-    backward = [(b, a) for a, b in forward]
-    rows = guide.shape[0]
-    guide_ends, _ = lax.optimization_barrier(((guide[rows - 3 :], guide[:3]), tile_tokens))
-    guide_low = lax.ppermute(guide_ends[0], AXES, forward)
-    guide_high = lax.ppermute(guide_ends[1], AXES, backward)
+    middle = (near + swap_cores(far).astype(F32)).astype(BF16)
 
     middle = lax.all_to_all(
         middle.reshape(tiles, seg, width), MP, split_axis=0, concat_axis=0, tiled=True
     ).reshape(count, width)
-    middle, guide_low, guide_high = lax.optimization_barrier((middle, guide_low, guide_high))
     near, far = mlp(middle, swap_cores(middle), ln_gain_two.reshape(1, width), mlp_w)
-    summed = near + swap_cores(far).astype(F32)
-    features = (middle.astype(F32) + summed).astype(BF16)
+    features = (near + swap_cores(far).astype(F32)).astype(BF16)
     embed = jnp.einsum("pd,dc->pc", features, proj_weight, preferred_element_type=F32).astype(BF16)
     channels = proj_weight.shape[1]
     token_rows = seg // SIDE

time: 168 us -> 196 us (1.17)
  the two profiles are of different devices: /device:TPU:6 before, /device:TPU:125 now
where the time goes in v4:
time: 196 us; the launch traced here: 195 us
  waiting for transfers between devices  69.5 us (35%)
  starting transfers between devices  54.8 us (28%)
  Pallas kernels  24.6 us (13%)
  between operations  13.8 us (7%)
  blocking collectives  13.7 us (7%)
  local copies, waits for them, and re-layouts  12.8 us (7%)
  other arithmetic  3.16 us (2%)
  matrix products  2.55 us (1%)
    all_to_all x1, waiting for transfers between devices, per_device(): lax.all_to_all(slab_tokens, MP, split_axis=0, concat_axis=0, tiled=True)  27 us
    ppermute x4, starting transfers between devices, swap_cores(): return lax.ppermute(block, 'c', [(0, 1), (1, 0)])  14.6 us
    all_to_all x1, blocking collectives, per_device(): lax.all_to_all(middle.reshape(tiles, seg, width), MP, split_axis=0, conca...  13.7 us
    ppermute x1, waiting for transfers between devices, per_device(): guide_high = lax.ppermute(guide_ends[1], AXES, backward)  13.6 us
    ppermute x5, waiting for transfers between devices, shift(): lax.ppermute(block, axis, [((i + step) % count, i) for i in range(count)])  13.2 us
    all_to_all x1, starting transfers between devices, per_device(): lax.all_to_all(outgoing, TILE, split_axis=0, concat_axis=0, tiled=True)  10.5 us
    pallas_call x1, Pallas kernels, conv_stage(): pl.pallas_call(conv_kernel, out_shape=jax.ShapeDtypeStruct(guide.shape, B...  9.93 us
    ppermute x1, waiting for transfers between devices, per_device(): image_high = lax.ppermute(image, AXES, backward)  8.77 us
  transfers between devices with their start and end apart: 18, of which 10 were waited for; matrix products, arithmetic and copies ran while one was open for 6% of the time, Pallas kernels for 4%

profile of v4, /device:TPU:125, one launch (start us, length us, event | category | flops | bytes accessed | tf_op | source)
XLA Modules:
  0.0 194.8 jit_solution(7621162623326482696)
XLA Ops:
  10.0 1.9 collective-permute-start
  12.2 3.0 %collective-permute-done = bf16[128,1024]{1,0:T(8,128)(2,1)S(1)} collective-permute-done((bf16[128,1024]{1,0:T(8,128)(2,1)S(1)}, bf16[128,1024]{1,0:T(8,128)(2,1)S(1)}, u32[]{:S(2)}, u32[]{:S(2)}) %collective-permute-start) | collective-permute-done | bytes 262176 | tf_op jit(solution)/shard_map/ppermute | solution.py:41
  17.4 10.5 %all-to-all-start = ((bf16[16,32,1024]{2,1,0:T(8,128)(2,1)}), bf16[16,32,1024]{2,1,0:T(8,128)(2,1)S(1)}, u32[]{:S(2)}, u32[]{:S(2)}) async-start(bf16[16,32,1024]{2,1,0:T(8,128)(2,1)} %copy.31), calls=%async_computation | async-start | bytes 2097152 | tf_op jit(solution)/shard_map/all_to_all | solution.py:360
  28.1 2.2 %collective-permute-start.2 = (bf16[128,1024]{1,0:T(8,128)(2,1)S(1)}, bf16[128,1024]{1,0:T(8,128)(2,1)S(1)}, u32[]{:S(2)}, u32[]{:S(2)}) collective-permute-start(bf16[128,1024]{1,0:T(8,128)(2,1)S(1)} %bitcast_select_fusion), channel_id=1, source_target_pairs={{3,0},{0,1},{1,2},{2,3},{7,4},{4,5},{5,6},{6,7},{11,8},{8,9},{9,10... | collective-permute-start | bytes 786440 | tf_op jit(solution)/shard_map/ppermute | solution.py:25
  30.4 7.0 %collective-permute-done.3 = bf16[128,1024]{1,0:T(8,128)(2,1)S(1)} collective-permute-done((bf16[128,1024]{1,0:T(8,128)(2,1)S(1)}, bf16[128,1024]{1,0:T(8,128)(2,1)S(1)}, u32[]{:S(2)}, u32[]{:S(2)}) %collective-permute-start.3) | collective-permute-done | bytes 262176 | tf_op jit(solution)/shard_map/ppermute | solution.py:25
  37.4 3.3 %collective-permute-done.2 = bf16[128,1024]{1,0:T(8,128)(2,1)S(1)} collective-permute-done((bf16[128,1024]{1,0:T(8,128)(2,1)S(1)}, bf16[128,1024]{1,0:T(8,128)(2,1)S(1)}, u32[]{:S(2)}, u32[]{:S(2)}) %collective-permute-start.2) | collective-permute-done | bytes 262176 | tf_op jit(solution)/shard_map/ppermute | solution.py:25
  40.6 3.0 %collective-permute-done.1 = bf16[128,1024]{1,0:T(8,128)(2,1)S(1)} collective-permute-done((bf16[128,1024]{1,0:T(8,128)(2,1)S(1)}, bf16[128,1024]{1,0:T(8,128)(2,1)S(1)}, u32[]{:S(2)}, u32[]{:S(2)}) %collective-permute-start.1) | collective-permute-done | bytes 262176 | tf_op jit(solution)/shard_map/ppermute | solution.py:25
  48.1 2.1 %copy.33 = bf16[8,32,1024]{2,1,0:T(8,128)(2,1)} copy(bf16[8,32,1024]{2,0,1:T(8,128)(2,1)} %convolution_convert_fusion.1) | data formatting | bytes 1048576 | tf_op jit(solution)/shard_map/convert_element_type | solution.py:363
  50.2 6.4 %all-to-all-start.1 = ((bf16[8,32,1024]{2,1,0:T(8,128)(2,1)}), bf16[8,32,1024]{2,1,0:T(8,128)(2,1)S(1)}, u32[]{:S(2)}, u32[]{:S(2)}) async-start(bf16[8,32,1024]{2,1,0:T(8,128)(2,1)} %copy.33), calls=%async_computation.1 | async-start | bytes 1048576 | tf_op jit(solution)/shard_map/all_to_all | solution.py:365
  57.6 5.3 %collective-permute-start.4 = (bf16[3,256,256]{2,1,0:T(8,128)(2,1)}, bf16[3,256,256]{2,1,0:T(8,128)(2,1)S(1)}, u32[]{:S(2)}, u32[]{:S(2)}) collective-permute-start(bf16[3,256,256]{2,1,0:T(8,128)(2,1)} %get-tuple-element.16), channel_id=1, source_target_pairs={{0,1},{1,2},{2,3},{3,4},{4,5},{5,6},{6,7},{7,8},{8,9},{9,10},{10,1... | collective-permute-start | bytes 1179656 | tf_op jit(solution)/shard_map/ppermute | solution.py:374
  62.9 27.0 %all-to-all-done.1 = bf16[8,32,1024]{2,1,0:T(8,128)(2,1)S(1)} async-done(((bf16[8,32,1024]{2,1,0:T(8,128)(2,1)}), bf16[8,32,1024]{2,1,0:T(8,128)(2,1)S(1)}, u32[]{:S(2)}, u32[]{:S(2)}) %all-to-all-start.1) | async-done | bytes 524320 | tf_op jit(solution)/shard_map/all_to_all | solution.py:365
  89.9 2.8 %collective-permute-start.6 = (bf16[256,1024]{1,0:T(8,128)(2,1)S(1)}, bf16[256,1024]{1,0:T(8,128)(2,1)S(1)}, u32[]{:S(2)}, u32[]{:S(2)}) collective-permute-start(bf16[256,1024]{1,0:T(8,128)(2,1)S(1)} %bitcast.34), channel_id=1, source_target_pairs={{0,8},{8,0},{1,9},{9,1},{2,10},{10,2},{3,11},{11,3},{4,12},{12,4},... | collective-permute-start | bytes 1572872 | tf_op jit(solution)/shard_map/ppermute | solution.py:29
  92.7 2.1 %collective-permute-start.5 = (bf16[3,256,256]{2,1,0:T(8,128)(2,1)}, bf16[3,256,256]{2,1,0:T(8,128)(2,1)}, u32[]{:S(2)}, u32[]{:S(2)}) collective-permute-start(bf16[3,256,256]{2,1,0:T(8,128)(2,1)} %get-tuple-element.17), channel_id=1, source_target_pairs={{1,0},{2,1},{3,2},{4,3},{5,4},{6,5},{7,6},{8,7},{9,8},{10,9},{11,1... | collective-permute-start | bytes 1179656 | tf_op jit(solution)/shard_map/ppermute | solution.py:375
  94.8 13.6 %collective-permute-done.5.guide_high = bf16[3,256,256]{2,1,0:T(8,128)(2,1)} collective-permute-done((bf16[3,256,256]{2,1,0:T(8,128)(2,1)}, bf16[3,256,256]{2,1,0:T(8,128)(2,1)}, u32[]{:S(2)}, u32[]{:S(2)}) %collective-permute-start.5) | collective-permute-done | bytes 393248 | tf_op jit(solution)/shard_map/ppermute | solution.py:375
  108.5 7.7 %attention.1 = (f32[256,1024]{1,0:T(8,128)S(1)}, bf16[256,1024]{1,0:T(8,128)(2,1)S(1)}) custom-call(s32[1]{0:T(128)} %bitcast.1.parity, bf16[256,1024]{1,0:T(8,128)(2,1)S(1)} %bitcast.35, bf16[256,1024]{1,0:T(8,128)(2,1)S(1)} %collective-permute-done.6.other, f32[1,1024]{1,0:T(1,128)S(1)} %bitcast.42, bf16[4,128,1024]{2,1,0:T(8,128)(2,1)S(1)} %pad_maximum_fusion.1.base, ...), custom_call_target="tpu_custom_call" | custom-call | flops 3000000000 | bytes 7000000 | tf_op jit(solution)/shard_map/attention/pallas_call | solution.py:133
  116.2 10.1 %collective-permute-start.10 = (bf16[256,1024]{1,0:T(8,128)(2,1)S(1)}, bf16[256,1024]{1,0:T(8,128)(2,1)S(1)}, u32[]{:S(2)}, u32[]{:S(2)}) collective-permute-start(bf16[256,1024]{1,0:T(8,128)(2,1)S(1)} %get-tuple-element.20), channel_id=1, source_target_pairs={{0,8},{8,0},{1,9},{9,1},{2,10},{10,2},{3,11},{11,3},{4,12},{12,4},... | collective-permute-start | bytes 1572872 | tf_op jit(solution)/shard_map/ppermute | solution.py:29
  128.0 13.7 %all_to_all.15 = bf16[8,32,1024]{2,1,0:T(8,128)(2,1)S(1)} all-to-all(bf16[8,32,1024]{2,1,0:T(8,128)(2,1)S(1)} %bitcast.47), channel_id=1, replica_groups=mesh['yl'=2,'x'=4,'c'=2,'yh'=2,'z'=4] {'yh','z'}, dimensions={0} | all-to-all | bytes 1048576 | tf_op jit(solution)/shard_map/all_to_all | solution.py:390
  144.3 3.4 %copy-done.2 = bf16[4096,1024]{1,0:T(8,128)(2,1)S(1)} copy-done((bf16[4096,1024]{1,0:T(8,128)(2,1)S(1)}, bf16[4096,1024]{1,0:T(8,128)(2,1)}, u32[]{:S(2)}) %copy-start.2) | copy-done | bytes 8388632
  147.7 7.0 %mlp.1 = (f32[256,1024]{1,0:T(8,128)S(1)}, bf16[256,1024]{1,0:T(8,128)(2,1)S(1)}) custom-call(bf16[256,1024]{1,0:T(8,128)(2,1)S(1)} %bitcast.37, bf16[256,1024]{1,0:T(8,128)(2,1)S(1)} %collective-permute-done.11.other, f32[1,1024]{1,0:T(1,128)S(1)} %bitcast.43, bf16[64,64,1024]{2,1,0:T(8,128)(2,1)S(1)} %bitcast.41), custom_call_target="tpu_custom_call" | custom-call | flops 5000000000 | bytes 12000000 | tf_op jit(solution)/shard_map/mlp/pallas_call | solution.py:187
  157.3 7.9 %collective-permute-start.13 = (bf16[2,128,256]{2,1,0:T(8,128)(2,1)S(1)}, bf16[2,128,256]{2,1,0:T(8,128)(2,1)S(1)}, u32[]{:S(2)}, u32[]{:S(2)}) collective-permute-start(bf16[2,128,256]{2,1,0:T(8,128)(2,1)S(1)} %bitcast.38), channel_id=1, source_target_pairs={{0,1},{1,2},{2,3},{3,4},{4,5},{5,6},{6,7},{7,8},{8,9},{9,10},{10,1... | collective-permute-start | bytes 393224 | tf_op jit(solution)/shard_map/ppermute | solution.py:401
  165.2 1.9 collective-permute-start.14
  167.3 8.8 %collective-permute-done.14.image_high = bf16[2,128,256]{2,1,0:T(8,128)(2,1)S(1)} collective-permute-done((bf16[2,128,256]{2,1,0:T(8,128)(2,1)S(1)}, bf16[2,128,256]{2,1,0:T(8,128)(2,1)S(1)}, u32[]{:S(2)}, u32[]{:S(2)}) %collective-permute-start.14) | collective-permute-done | bytes 131104 | tf_op jit(solution)/shard_map/ppermute | solution.py:402
  176.0 2.0 %copy-done.3 = bf16[3,3,3,256,256]{4,3,2,1,0:T(8,128)(2,1)S(1)} copy-done((bf16[3,3,3,256,256]{4,3,2,1,0:T(8,128)(2,1)S(1)}, bf16[3,3,3,256,256]{4,3,2,1,0:T(8,128)(2,1)}, u32[]{:S(2)}) %copy-start.3) | copy-done | bytes 3538968
  178.0 9.9 %convs.1 = bf16[4,256,256]{2,1,0:T(8,128)(2,1)} custom-call(s32[2]{0:T(128)S(1)} %pad_add_fusion.place, bf16[2,128,256]{2,1,0:T(8,128)(2,1)S(1)} %collective-permute-done.13.image_low, bf16[2,128,256]{2,1,0:T(8,128)(2,1)S(1)} %bitcast.40, bf16[2,128,256]{2,1,0:T(8,128)(2,1)S(1)} %collective-permute-done.14.image_high, ...), custom_call_target="tpu_custom_call" | custom-call | flops 6000000000 | bytes 6000000 | tf_op jit(solution)/shard_map/convs/pallas_call | solution.py:283
  (65 shorter events, 18.5 us)
Async XLA Ops:
  6.5 150.4 %copy-start = (bf16[1024,256]{1,0:T(8,128)(2,1)S(1)}, bf16[1024,256]{1,0:T(8,128)(2,1)}, u32[]{:S(2)}) copy-start(bf16[1024,256]{1,0:T(8,128)(2,1)} %param.20) | copy-start | bytes 1572868
  6.5 137.8 %all-gather.3.cloned.1.call-start = ((), (), s32[]{:S(2)}) async-start(), calls=%async_computation.3 | async-start | bytes 8519680 | tf_op jit(solution)/shard_map/all_gather | solution.py:342
  10.0 5.2 %collective-permute-start = (bf16[128,1024]{1,0:T(8,128)(2,1)S(1)}, bf16[128,1024]{1,0:T(8,128)(2,1)S(1)}, u32[]{:S(2)}, u32[]{:S(2)}) collective-permute-start(bf16[128,1024]{1,0:T(8,128)(2,1)S(1)} %dynamic-slice_bitcast_fusion), channel_id=1, source_target_pairs={{0,68},{64,4},{12,72},{76,8},{1,69},{65,5},{13,73},{77,9},{2,70},{... | collective-permute-start | bytes 786440 | tf_op jit(solution)/shard_map/ppermute | solution.py:41
  15.2 28.4 %copy-start.7 = (bf16[128,1024]{1,0:T(8,128)(2,1)}, bf16[128,1024]{1,0:T(8,128)(2,1)S(1)}, u32[]{:S(2)}) copy-start(bf16[128,1024]{1,0:T(8,128)(2,1)S(1)} %bitcast_select_fusion) | copy-start | bytes 786436
  17.4 39.2 %copy-start.1 = (bf16[4,256,256]{2,1,0:T(8,128)(2,1)S(1)}, bf16[4,256,256]{2,1,0:T(8,128)(2,1)}, u32[]{:S(2)}) copy-start(bf16[4,256,256]{2,1,0:T(8,128)(2,1)} %guide.1) | copy-start | bytes 1572868
  17.4 29.0 %all-to-all-start = ((bf16[16,32,1024]{2,1,0:T(8,128)(2,1)}), bf16[16,32,1024]{2,1,0:T(8,128)(2,1)S(1)}, u32[]{:S(2)}, u32[]{:S(2)}) async-start(bf16[16,32,1024]{2,1,0:T(8,128)(2,1)} %copy.31), calls=%async_computation | async-start | bytes 2097152 | tf_op jit(solution)/shard_map/all_to_all | solution.py:360
  27.9 9.5 %collective-permute-start.3 = (bf16[128,1024]{1,0:T(8,128)(2,1)S(1)}, bf16[128,1024]{1,0:T(8,128)(2,1)S(1)}, u32[]{:S(2)}, u32[]{:S(2)}) collective-permute-start(bf16[128,1024]{1,0:T(8,128)(2,1)S(1)} %bitcast_select_fusion), channel_id=1, source_target_pairs={{2,0},{3,1},{0,2},{1,3},{6,4},{7,5},{4,6},{5,7},{10,8},{11,9},{8,1... | collective-permute-start | bytes 786440 | tf_op jit(solution)/shard_map/ppermute | solution.py:25
  28.1 12.5 %collective-permute-start.2 = (bf16[128,1024]{1,0:T(8,128)(2,1)S(1)}, bf16[128,1024]{1,0:T(8,128)(2,1)S(1)}, u32[]{:S(2)}, u32[]{:S(2)}) collective-permute-start(bf16[128,1024]{1,0:T(8,128)(2,1)S(1)} %bitcast_select_fusion), channel_id=1, source_target_pairs={{3,0},{0,1},{1,2},{2,3},{7,4},{4,5},{5,6},{6,7},{11,8},{8,9},{9,10... | collective-permute-start | bytes 786440 | tf_op jit(solution)/shard_map/ppermute | solution.py:25
  30.4 13.2 %collective-permute-start.1 = (bf16[128,1024]{1,0:T(8,128)(2,1)S(1)}, bf16[128,1024]{1,0:T(8,128)(2,1)S(1)}, u32[]{:S(2)}, u32[]{:S(2)}) collective-permute-start(bf16[128,1024]{1,0:T(8,128)(2,1)S(1)} %bitcast_select_fusion), channel_id=1, source_target_pairs={{1,0},{2,1},{3,2},{0,3},{5,4},{6,5},{7,6},{4,7},{9,8},{10,9},{11,1... | collective-permute-start | bytes 786440 | tf_op jit(solution)/shard_map/ppermute | solution.py:25
  43.6 64.9 %copy-start.4 = (f32[1024]{0:T(1024)S(1)}, f32[1024]{0:T(1024)}, u32[]{:S(2)}) copy-start(f32[1024]{0:T(1024)} %param.14) | copy-start | bytes 12292
  44.7 63.8 %collective-permute-start.7 = (bf16[4,128,1024]{2,1,0:T(8,128)(2,1)S(1)}, bf16[4,128,1024]{2,1,0:T(8,128)(2,1)}, u32[]{:S(2)}, u32[]{:S(2)}) collective-permute-start(bf16[4,128,1024]{2,1,0:T(8,128)(2,1)S(1)} %pad_maximum_fusion.1.base), channel_id=1, source_target_pairs={{16,0},{32,16},{48,32},{0,48},{17,1},{33,17},{49,33},{1,49},{18,2}... | collective-permute-start | bytes 3145736 | tf_op jit(solution)/shard_map/ppermute | solution.py:25
  45.1 63.4 %collective-permute-start.8 = (bf16[4,128,1024]{2,1,0:T(8,128)(2,1)S(1)}, bf16[4,128,1024]{2,1,0:T(8,128)(2,1)}, u32[]{:S(2)}, u32[]{:S(2)}) collective-permute-start(bf16[4,128,1024]{2,1,0:T(8,128)(2,1)S(1)} %pad_maximum_fusion.1.base), channel_id=1, source_target_pairs={{48,0},{0,16},{16,32},{32,48},{49,1},{1,17},{17,33},{33,49},{50,2}... | collective-permute-start | bytes 3145736 | tf_op jit(solution)/shard_map/ppermute | solution.py:25
  46.2 62.3 %collective-permute-start.9 = (bf16[4,128,1024]{2,1,0:T(8,128)(2,1)S(1)}, bf16[4,128,1024]{2,1,0:T(8,128)(2,1)}, u32[]{:S(2)}, u32[]{:S(2)}) collective-permute-start(bf16[4,128,1024]{2,1,0:T(8,128)(2,1)S(1)} %pad_maximum_fusion.1.base), channel_id=1, source_target_pairs={{64,0},{4,64},{68,4},{0,68},{65,1},{5,65},{69,5},{1,69},{66,2},{6,... | collective-permute-start | bytes 3145736 | tf_op jit(solution)/shard_map/ppermute | solution.py:23
  50.2 39.7 %all-to-all-start.1 = ((bf16[8,32,1024]{2,1,0:T(8,128)(2,1)}), bf16[8,32,1024]{2,1,0:T(8,128)(2,1)S(1)}, u32[]{:S(2)}, u32[]{:S(2)}) async-start(bf16[8,32,1024]{2,1,0:T(8,128)(2,1)} %copy.33), calls=%async_computation.1 | async-start | bytes 1048576 | tf_op jit(solution)/shard_map/all_to_all | solution.py:365
  57.6 35.1 %collective-permute-start.4 = (bf16[3,256,256]{2,1,0:T(8,128)(2,1)}, bf16[3,256,256]{2,1,0:T(8,128)(2,1)S(1)}, u32[]{:S(2)}, u32[]{:S(2)}) collective-permute-start(bf16[3,256,256]{2,1,0:T(8,128)(2,1)} %get-tuple-element.16), channel_id=1, source_target_pairs={{0,1},{1,2},{2,3},{3,4},{4,5},{5,6},{6,7},{7,8},{8,9},{9,10},{10,1... | collective-permute-start | bytes 1179656 | tf_op jit(solution)/shard_map/ppermute | solution.py:374
  89.9 18.6 %collective-permute-start.6 = (bf16[256,1024]{1,0:T(8,128)(2,1)S(1)}, bf16[256,1024]{1,0:T(8,128)(2,1)S(1)}, u32[]{:S(2)}, u32[]{:S(2)}) collective-permute-start(bf16[256,1024]{1,0:T(8,128)(2,1)S(1)} %bitcast.34), channel_id=1, source_target_pairs={{0,8},{8,0},{1,9},{9,1},{2,10},{10,2},{3,11},{11,3},{4,12},{12,4},... | collective-permute-start | bytes 1572872 | tf_op jit(solution)/shard_map/ppermute | solution.py:29
  92.7 15.7 %collective-permute-start.5 = (bf16[3,256,256]{2,1,0:T(8,128)(2,1)}, bf16[3,256,256]{2,1,0:T(8,128)(2,1)}, u32[]{:S(2)}, u32[]{:S(2)}) collective-permute-start(bf16[3,256,256]{2,1,0:T(8,128)(2,1)} %get-tuple-element.17), channel_id=1, source_target_pairs={{1,0},{2,1},{3,2},{4,3},{5,4},{6,5},{7,6},{8,7},{9,8},{10,9},{11,1... | collective-permute-start | bytes 1179656 | tf_op jit(solution)/shard_map/ppermute | solution.py:375
  108.5 35.8 %copy-start.5 = (f32[1024]{0:T(1024)S(1)}, f32[1024]{0:T(1024)}, u32[]{:S(2)}) copy-start(f32[1024]{0:T(1024)} %param.15) | copy-start | bytes 12292
  116.2 11.6 %collective-permute-start.10 = (bf16[256,1024]{1,0:T(8,128)(2,1)S(1)}, bf16[256,1024]{1,0:T(8,128)(2,1)S(1)}, u32[]{:S(2)}, u32[]{:S(2)}) collective-permute-start(bf16[256,1024]{1,0:T(8,128)(2,1)S(1)} %get-tuple-element.20), channel_id=1, source_target_pairs={{0,8},{8,0},{1,9},{9,1},{2,10},{10,2},{3,11},{11,3},{4,12},{12,4},... | collective-permute-start | bytes 1572872 | tf_op jit(solution)/shard_map/ppermute | solution.py:29
  141.7 2.6 %collective-permute-start.11 = (bf16[256,1024]{1,0:T(8,128)(2,1)S(1)}, bf16[256,1024]{1,0:T(8,128)(2,1)S(1)}, u32[]{:S(2)}, u32[]{:S(2)}) collective-permute-start(bf16[256,1024]{1,0:T(8,128)(2,1)S(1)} %bitcast.36), channel_id=1, source_target_pairs={{0,8},{8,0},{1,9},{9,1},{2,10},{10,2},{3,11},{11,3},{4,12},{12,4},... | collective-permute-start | bytes 1572872 | tf_op jit(solution)/shard_map/ppermute | solution.py:29
  147.7 28.3 %copy-start.6 = (f32[3,256]{1,0:T(4,128)S(1)}, f32[3,256]{1,0:T(4,128)}, u32[]{:S(2)}) copy-start(f32[3,256]{1,0:T(4,128)} %bias.1) | copy-start | bytes 9220
  154.7 2.2 %collective-permute-start.12 = (bf16[256,1024]{1,0:T(8,128)(2,1)S(1)}, bf16[256,1024]{1,0:T(8,128)(2,1)S(1)}, u32[]{:S(2)}, u32[]{:S(2)}) collective-permute-start(bf16[256,1024]{1,0:T(8,128)(2,1)S(1)} %get-tuple-element.22), channel_id=1, source_target_pairs={{0,8},{8,0},{1,9},{9,1},{2,10},{10,2},{3,11},{11,3},{4,12},{12,4},... | collective-permute-start | bytes 1572872 | tf_op jit(solution)/shard_map/ppermute | solution.py:29
  157.3 9.9 %collective-permute-start.13 = (bf16[2,128,256]{2,1,0:T(8,128)(2,1)S(1)}, bf16[2,128,256]{2,1,0:T(8,128)(2,1)S(1)}, u32[]{:S(2)}, u32[]{:S(2)}) collective-permute-start(bf16[2,128,256]{2,1,0:T(8,128)(2,1)S(1)} %bitcast.38), channel_id=1, source_target_pairs={{0,1},{1,2},{2,3},{3,4},{4,5},{5,6},{6,7},{7,8},{8,9},{9,10},{10,1... | collective-permute-start | bytes 393224 | tf_op jit(solution)/shard_map/ppermute | solution.py:401
  165.2 10.8 %collective-permute-start.14 = (bf16[2,128,256]{2,1,0:T(8,128)(2,1)S(1)}, bf16[2,128,256]{2,1,0:T(8,128)(2,1)S(1)}, u32[]{:S(2)}, u32[]{:S(2)}) collective-permute-start(bf16[2,128,256]{2,1,0:T(8,128)(2,1)S(1)} %bitcast.39), channel_id=1, source_target_pairs={{1,0},{2,1},{3,2},{4,3},{5,4},{6,5},{7,6},{8,7},{9,8},{10,9},{11,1... | collective-permute-start | bytes 393224 | tf_op jit(solution)/shard_map/ppermute | solution.py:402
  (6 other events, 15.5 us)
Sparse Core Ops, SparseCore 0:
  10.2 103.1 all-gather.2

commit v5 on v4

--- a/solution.py
+++ b/solution.py
@@ -198,7 +198,7 @@
             pltpu.VMEM((2 * count, width), F32),
             pltpu.SemaphoreType.DMA((parts,)),
         ],
-        compiler_params=pltpu.CompilerParams(vmem_limit_bytes=28 * 2**20),
+        compiler_params=pltpu.CompilerParams(vmem_limit_bytes=56 * 2**20),
         cost_estimate=pl.CostEstimate(flops=5 * 10**9, bytes_accessed=12 * 10**6, transcendentals=2**20),
         name="mlp",
     )(own, other, gain, weights)
@@ -292,7 +292,7 @@
             pltpu.VMEM(weights.shape, BF16),
             pltpu.SemaphoreType.DMA((3,)),
         ],
-        compiler_params=pltpu.CompilerParams(vmem_limit_bytes=24 * 2**20),
+        compiler_params=pltpu.CompilerParams(vmem_limit_bytes=56 * 2**20),
         cost_estimate=pl.CostEstimate(flops=6 * 10**9, bytes_accessed=6 * 10**6, transcendentals=2**20),
         name="convs",
     )(place, image_low, image, image_high, guide_low, guide, guide_high, weights, bias)
@@ -366,17 +366,6 @@
     tile_tokens = tile_tokens.reshape(tiles * seg, width)
     other_tokens = swap_cores(tile_tokens)
 
-    total = lax.axis_size(AXES)
-    forward = [(i, i + 1) for i in range(total - 1)]
-    backward = [(b, a) for a, b in forward]
-    rows = guide.shape[0]
-    guide_ends, _ = lax.optimization_barrier(((guide[rows - 3 :], guide[:3]), attn_w[0]))
-    guide_low = lax.ppermute(guide_ends[0], AXES, forward)
-    guide_high = lax.ppermute(guide_ends[1], AXES, backward)
-    tile_tokens, guide_low, guide_high = lax.optimization_barrier(
-        (tile_tokens, guide_low, guide_high)
-    )
-
     count = tiles * seg
     near, far = attention(
         (x_at % 2).astype(jnp.int32).reshape(1),
@@ -387,9 +376,18 @@
     )
     middle = (near + swap_cores(far).astype(F32)).astype(BF16)
 
+    total = lax.axis_size(AXES)
+    forward = [(i, i + 1) for i in range(total - 1)]
+    backward = [(b, a) for a, b in forward]
+    rows = guide.shape[0]
+    guide_ends, _ = lax.optimization_barrier(((guide[rows - 3 :], guide[:3]), far))
+    guide_low = lax.ppermute(guide_ends[0], AXES, forward)
+    guide_high = lax.ppermute(guide_ends[1], AXES, backward)
+
     middle = lax.all_to_all(
         middle.reshape(tiles, seg, width), MP, split_axis=0, concat_axis=0, tiled=True
     ).reshape(count, width)
+    middle, guide_low, guide_high = lax.optimization_barrier((middle, guide_low, guide_high))
     near, far = mlp(middle, swap_cores(middle), ln_gain_two.reshape(1, width), mlp_w)
     features = (near + swap_cores(far).astype(F32)).astype(BF16)
     embed = jnp.einsum("pd,dc->pc", features, proj_weight, preferred_element_type=F32).astype(BF16)

time: 196 us -> 180 us (0.918)
  waiting for transfers between devices: 69.5 us -> 41.8 us
  blocking collectives: 13.7 us -> 34 us
  starting transfers between devices: 54.8 us -> 46.5 us
  local copies, waits for them, and re-layouts: 12.8 us -> 6.78 us
  Pallas kernels: 24.6 us -> 28.7 us
    all_to_all x1, waiting for transfers between devices: 27 us -> 0.01 us  [per_device(): lax.all_to_all(middle.reshape(tiles, seg, width), MP, split_axis=0, conca...]
    all_to_all x1, blocking collectives: 13.7 us -> 34 us  [per_device(): lax.all_to_all(slab_tokens, MP, split_axis=0, concat_axis=0, tiled=True)]
    ppermute x1, waiting for transfers between devices: 13.6 us -> 3.06 us  [per_device(): guide_high = lax.ppermute(guide_ends[1], AXES, backward)]
    ppermute x1, waiting for transfers between devices: 0.01 us -> 8.72 us  [per_device(): guide_low = lax.ppermute(guide_ends[0], AXES, forward)]
    ppermute x4, starting transfers between devices: 14.6 us -> 7.35 us  [swap_cores(): return lax.ppermute(block, 'c', [(0, 1), (1, 0)])]
    unnamed x25 -> x31, local copies, waits for them, and re-layouts: 6.84 us -> 3.67 us
    pallas_call x1, Pallas kernels: 7.01 us -> 9.63 us  [mlp(): pl.pallas_call(mlp_kernel, out_shape=(jax.ShapeDtypeStruct((count, width)...]
    ppermute x1, starting transfers between devices: 7.9 us -> 5.8 us  [per_device(): image_low = lax.ppermute(image, AXES, forward)]
  transfers between devices with their start and end apart: 18 -> 18, of which waited for: 10 -> 11; matrix products, arithmetic and copies ran while one was open for 6% -> 5% of each run, Pallas kernels for 4% -> 5%
where the time goes in v5:
time: 180 us; the launch traced here: 179 us
  starting transfers between devices  46.5 us (26%)
  waiting for transfers between devices  41.8 us (23%)
  blocking collectives  34 us (19%)
  Pallas kernels  28.7 us (16%)
  between operations  13.8 us (8%)
  local copies, waits for them, and re-layouts  6.78 us (4%)
  matrix products  4.21 us (2%)
  other arithmetic  3.48 us (2%)
    all_to_all x1, blocking collectives, per_device(): lax.all_to_all(slab_tokens, MP, split_axis=0, concat_axis=0, tiled=True)  34 us
    ppermute x5, waiting for transfers between devices, shift(): lax.ppermute(block, axis, [((i + step) % count, i) for i in range(count)])  13.2 us
    pallas_call x1, Pallas kernels, conv_stage(): pl.pallas_call(conv_kernel, out_shape=jax.ShapeDtypeStruct(guide.shape, B...  10.5 us
    all_to_all x1, starting transfers between devices, per_device(): lax.all_to_all(outgoing, TILE, split_axis=0, concat_axis=0, tiled=True)  10.5 us
    pallas_call x1, Pallas kernels, mlp(): pl.pallas_call(mlp_kernel, out_shape=(jax.ShapeDtypeStruct((count, width)...  9.63 us
    ppermute x1, waiting for transfers between devices, per_device(): guide_low = lax.ppermute(guide_ends[0], AXES, forward)  8.72 us
    pallas_call x1, Pallas kernels, attention(): pl.pallas_call(attention_kernel, out_shape=(jax.ShapeDtypeStruct((count,...  8.53 us
    all_to_all x1, starting transfers between devices, per_device(): lax.all_to_all(middle.reshape(tiles, seg, width), MP, split_axis=0, conca...  8.1 us
  transfers between devices with their start and end apart: 18, of which 11 were waited for; matrix products, arithmetic and copies ran while one was open for 5% of the time, Pallas kernels for 5%

profile of v5, /device:TPU:125, one launch (start us, length us, event | category | flops | bytes accessed | tf_op | source)
XLA Modules:
  0.0 179.2 jit_solution(7803431753827830775)
XLA Ops:
  10.0 1.9 %collective-permute-start = (bf16[128,1024]{1,0:T(8,128)(2,1)S(1)}, bf16[128,1024]{1,0:T(8,128)(2,1)S(1)}, u32[]{:S(2)}, u32[]{:S(2)}) collective-permute-start(bf16[128,1024]{1,0:T(8,128)(2,1)S(1)} %dynamic-slice_bitcast_fusion), channel_id=1, source_target_pairs={{0,68},{64,4},{12,72},{76,8},{1,69},{65,5},{13,73},{77,9},{2,70},{... | collective-permute-start | bytes 786440 | tf_op jit(solution)/shard_map/ppermute | solution.py:41
  12.1 3.0 %collective-permute-done = bf16[128,1024]{1,0:T(8,128)(2,1)S(1)} collective-permute-done((bf16[128,1024]{1,0:T(8,128)(2,1)S(1)}, bf16[128,1024]{1,0:T(8,128)(2,1)S(1)}, u32[]{:S(2)}, u32[]{:S(2)}) %collective-permute-start) | collective-permute-done | bytes 262176 | tf_op jit(solution)/shard_map/ppermute | solution.py:41
  15.8 1.6 copy.31
  17.4 10.5 %all-to-all-start = ((bf16[16,32,1024]{2,1,0:T(8,128)(2,1)}), bf16[16,32,1024]{2,1,0:T(8,128)(2,1)}, u32[]{:S(2)}, u32[]{:S(2)}) async-start(bf16[16,32,1024]{2,1,0:T(8,128)(2,1)} %copy.31), calls=%async_computation | async-start | bytes 2097152 | tf_op jit(solution)/shard_map/all_to_all | solution.py:360
  28.1 2.2 %collective-permute-start.3 = (bf16[128,1024]{1,0:T(8,128)(2,1)S(1)}, bf16[128,1024]{1,0:T(8,128)(2,1)S(1)}, u32[]{:S(2)}, u32[]{:S(2)}) collective-permute-start(bf16[128,1024]{1,0:T(8,128)(2,1)S(1)} %bitcast_select_fusion), channel_id=1, source_target_pairs={{3,0},{0,1},{1,2},{2,3},{7,4},{4,5},{5,6},{6,7},{11,8},{8,9},{9,10... | collective-permute-start | bytes 786440 | tf_op jit(solution)/shard_map/ppermute | solution.py:25
  30.4 7.0 %collective-permute-done.4 = bf16[128,1024]{1,0:T(8,128)(2,1)S(1)} collective-permute-done((bf16[128,1024]{1,0:T(8,128)(2,1)S(1)}, bf16[128,1024]{1,0:T(8,128)(2,1)S(1)}, u32[]{:S(2)}, u32[]{:S(2)}) %collective-permute-start.4) | collective-permute-done | bytes 262176 | tf_op jit(solution)/shard_map/ppermute | solution.py:25
  37.3 3.4 %collective-permute-done.3 = bf16[128,1024]{1,0:T(8,128)(2,1)S(1)} collective-permute-done((bf16[128,1024]{1,0:T(8,128)(2,1)S(1)}, bf16[128,1024]{1,0:T(8,128)(2,1)S(1)}, u32[]{:S(2)}, u32[]{:S(2)}) %collective-permute-start.3) | collective-permute-done | bytes 262176 | tf_op jit(solution)/shard_map/ppermute | solution.py:25
  40.7 2.9 %collective-permute-done.2 = bf16[128,1024]{1,0:T(8,128)(2,1)S(1)} collective-permute-done((bf16[128,1024]{1,0:T(8,128)(2,1)S(1)}, bf16[128,1024]{1,0:T(8,128)(2,1)S(1)}, u32[]{:S(2)}, u32[]{:S(2)}) %collective-permute-start.2) | collective-permute-done | bytes 262176 | tf_op jit(solution)/shard_map/ppermute | solution.py:25
  45.4 2.1 %convolution_convert_fusion.1 = bf16[8,32,1024]{2,0,1:T(8,128)(2,1)S(1)} fusion(bf16[16,32,1024]{2,1,0:T(8,128)(2,1)} %all-to-all-done, s32[128]{0:T(128)S(1)} %get-tuple-element.32, s32[128]{0:T(128)S(1)} %get-tuple-element.33, pred[128]{0:T(512)(128)(4,1)S(1)} %get-tuple-element.25), kind=kOutput, calls=%fused_computation.1 | convolution fusion | flops 8687744 | bytes 1574016 | tf_op jit(solution)/shard_map/kg,gpd->kpd/dot_general | solution.py:361
  48.6 34.0 %all_to_all.15 = bf16[8,32,1024]{2,1,0:T(8,128)(2,1)S(1)} all-to-all(bf16[8,32,1024]{2,1,0:T(8,128)(2,1)S(1)} %copy.33), channel_id=1, replica_groups=mesh['yl'=2,'x'=4,'c'=2,'yh'=2,'z'=4] {'yh','z'}, dimensions={0} | all-to-all | bytes 1048576 | tf_op jit(solution)/shard_map/all_to_all | solution.py:365
  82.6 5.0 %collective-permute-start.1 = (bf16[256,1024]{1,0:T(8,128)(2,1)S(1)}, bf16[256,1024]{1,0:T(8,128)(2,1)}, u32[]{:S(2)}, u32[]{:S(2)}) collective-permute-start(bf16[256,1024]{1,0:T(8,128)(2,1)S(1)} %bitcast.34), channel_id=1, source_target_pairs={{0,8},{8,0},{1,9},{9,1},{2,10},{10,2},{3,11},{11,3},{4,12},{12,4},... | collective-permute-start | bytes 1572872 | tf_op jit(solution)/shard_map/ppermute | solution.py:29
  87.6 1.7 collective-permute-done.1.other
  89.3 8.5 %attention.1 = (f32[256,1024]{1,0:T(8,128)S(1)}, bf16[256,1024]{1,0:T(8,128)(2,1)S(1)}) custom-call(s32[1]{0:T(128)} %bitcast.1.parity, bf16[256,1024]{1,0:T(8,128)(2,1)S(1)} %bitcast.35, bf16[256,1024]{1,0:T(8,128)(2,1)} %collective-permute-done.1.other, f32[1,1024]{1,0:T(1,128)S(1)} %bitcast.36, bf16[4,128,1024]{2,1,0:T(8,128)(2,1)S(1)} %pad_maximum_fusion.1.base, ...), custom_call_target="tpu_custom_call" | custom-call | flops 3000000000 | bytes 7000000 | tf_op jit(solution)/shard_map/attention/pallas_call | solution.py:133
  101.0 8.1 %all-to-all-start.2 = ((bf16[8,32,1024]{2,1,0:T(8,128)(2,1)}), bf16[8,32,1024]{2,1,0:T(8,128)(2,1)S(1)}, u32[]{:S(2)}, u32[]{:S(2)}) async-start(bf16[8,32,1024]{2,1,0:T(8,128)(2,1)} %bitcast.18), calls=%async_computation.2 | async-start | bytes 1048576 | tf_op jit(solution)/shard_map/all_to_all | solution.py:387
  109.1 4.6 %collective-permute-start.9 = (bf16[3,256,256]{2,1,0:T(8,128)(2,1)S(1)}, bf16[3,256,256]{2,1,0:T(8,128)(2,1)S(1)}, u32[]{:S(2)}, u32[]{:S(2)}) collective-permute-start(bf16[3,256,256]{2,1,0:T(8,128)(2,1)S(1)} %get-tuple-element.18), channel_id=1, source_target_pairs={{0,1},{1,2},{2,3},{3,4},{4,5},{5,6},{6,7},{7,8},{8,9},{9,10},{10,1... | collective-permute-start | bytes 1179656 | tf_op jit(solution)/shard_map/ppermute | solution.py:384
  113.8 1.9 %collective-permute-start.10 = (bf16[3,256,256]{2,1,0:T(8,128)(2,1)S(1)}, bf16[3,256,256]{2,1,0:T(8,128)(2,1)S(1)}, u32[]{:S(2)}, u32[]{:S(2)}) collective-permute-start(bf16[3,256,256]{2,1,0:T(8,128)(2,1)S(1)} %get-tuple-element.19), channel_id=1, source_target_pairs={{1,0},{2,1},{3,2},{4,3},{5,4},{6,5},{7,6},{8,7},{9,8},{10,9},{11,1... | collective-permute-start | bytes 1179656 | tf_op jit(solution)/shard_map/ppermute | solution.py:385
  115.7 8.7 %collective-permute-done.9.guide_low = bf16[3,256,256]{2,1,0:T(8,128)(2,1)S(1)} collective-permute-done((bf16[3,256,256]{2,1,0:T(8,128)(2,1)S(1)}, bf16[3,256,256]{2,1,0:T(8,128)(2,1)S(1)}, u32[]{:S(2)}, u32[]{:S(2)}) %collective-permute-start.9) | collective-permute-done | bytes 393248 | tf_op jit(solution)/shard_map/ppermute | solution.py:384
  124.4 3.1 %collective-permute-done.10.guide_high = bf16[3,256,256]{2,1,0:T(8,128)(2,1)S(1)} collective-permute-done((bf16[3,256,256]{2,1,0:T(8,128)(2,1)S(1)}, bf16[3,256,256]{2,1,0:T(8,128)(2,1)S(1)}, u32[]{:S(2)}, u32[]{:S(2)}) %collective-permute-start.10) | collective-permute-done | bytes 393248 | tf_op jit(solution)/shard_map/ppermute | solution.py:385
  131.1 9.6 %mlp.1 = (f32[256,1024]{1,0:T(8,128)}, bf16[256,1024]{1,0:T(8,128)(2,1)}) custom-call(bf16[256,1024]{1,0:T(8,128)(2,1)} %bitcast.46, bf16[256,1024]{1,0:T(8,128)(2,1)} %copy-done.9, f32[1,1024]{1,0:T(1,128)} %bitcast.55, bf16[64,64,1024]{2,1,0:T(8,128)(2,1)} %bitcast.54), custom_call_target="tpu_custom_call" | custom-call | flops 5000000000 | bytes 12000000 | tf_op jit(solution)/shard_map/mlp/pallas_call | solution.py:187
  142.9 1.5 convolution_convert_fusion.2
  144.6 5.8 %collective-permute-start.13 = (bf16[2,128,256]{2,1,0:T(8,128)(2,1)S(1)}, bf16[2,128,256]{2,1,0:T(8,128)(2,1)S(1)}, u32[]{:S(2)}, u32[]{:S(2)}) collective-permute-start(bf16[2,128,256]{2,1,0:T(8,128)(2,1)S(1)} %bitcast.51), channel_id=1, source_target_pairs={{0,1},{1,2},{2,3},{3,4},{4,5},{5,6},{6,7},{7,8},{8,9},{9,10},{10,1... | collective-permute-start | bytes 393224 | tf_op jit(solution)/shard_map/ppermute | solution.py:399
  150.4 2.1 %collective-permute-start.14 = (bf16[2,128,256]{2,1,0:T(8,128)(2,1)S(1)}, bf16[2,128,256]{2,1,0:T(8,128)(2,1)S(1)}, u32[]{:S(2)}, u32[]{:S(2)}) collective-permute-start(bf16[2,128,256]{2,1,0:T(8,128)(2,1)S(1)} %bitcast.52), channel_id=1, source_target_pairs={{1,0},{2,1},{3,2},{4,3},{5,4},{6,5},{7,6},{8,7},{9,8},{10,9},{11,1... | collective-permute-start | bytes 393224 | tf_op jit(solution)/shard_map/ppermute | solution.py:400
  153.2 8.0 %collective-permute-done.14.image_high = bf16[2,128,256]{2,1,0:T(8,128)(2,1)S(1)} collective-permute-done((bf16[2,128,256]{2,1,0:T(8,128)(2,1)S(1)}, bf16[2,128,256]{2,1,0:T(8,128)(2,1)S(1)}, u32[]{:S(2)}, u32[]{:S(2)}) %collective-permute-start.14) | collective-permute-done | bytes 131104 | tf_op jit(solution)/shard_map/ppermute | solution.py:400
  161.8 10.5 %convs.1 = bf16[4,256,256]{2,1,0:T(8,128)(2,1)} custom-call(s32[2]{0:T(128)} %pad_add_fusion.place, bf16[2,128,256]{2,1,0:T(8,128)(2,1)} %copy-done.12, bf16[2,128,256]{2,1,0:T(8,128)(2,1)} %bitcast.53, bf16[2,128,256]{2,1,0:T(8,128)(2,1)} %copy-done.13, bf16[3,256,256]{2,1,0:T(8,128)(2,1)} %copy-done.10, bf16[4,256,256]{2,1,0:T(8,128)(2,1)} %guide.1, ...), custom_call_target="tpu_custom_call" | custom-call | flops 6000000000 | bytes 6000000 | tf_op jit(solution)/shard_map/convs/pallas_call | solution.py:283
  (71 shorter events, 17.7 us)
Async XLA Ops:
  6.5 136.4 %copy-start = (bf16[1024,256]{1,0:T(8,128)(2,1)S(1)}, bf16[1024,256]{1,0:T(8,128)(2,1)}, u32[]{:S(2)}) copy-start(bf16[1024,256]{1,0:T(8,128)(2,1)} %param.20) | copy-start | bytes 1572868
  6.5 123.7 %all-gather.3.cloned.1.call-start = ((), (), s32[]{:S(2)}) async-start(), calls=%async_computation.3 | async-start | bytes 8519680 | tf_op jit(solution)/shard_map/all_gather | solution.py:342
  10.0 5.2 %collective-permute-start = (bf16[128,1024]{1,0:T(8,128)(2,1)S(1)}, bf16[128,1024]{1,0:T(8,128)(2,1)S(1)}, u32[]{:S(2)}, u32[]{:S(2)}) collective-permute-start(bf16[128,1024]{1,0:T(8,128)(2,1)S(1)} %dynamic-slice_bitcast_fusion), channel_id=1, source_target_pairs={{0,68},{64,4},{12,72},{76,8},{1,69},{65,5},{13,73},{77,9},{2,70},{... | collective-permute-start | bytes 786440 | tf_op jit(solution)/shard_map/ppermute | solution.py:41
  17.3 72.0 %copy-start.1 = (f32[1024]{0:T(1024)S(1)}, f32[1024]{0:T(1024)}, u32[]{:S(2)}) copy-start(f32[1024]{0:T(1024)} %param.14) | copy-start | bytes 12292
  17.4 28.1 %all-to-all-start = ((bf16[16,32,1024]{2,1,0:T(8,128)(2,1)}), bf16[16,32,1024]{2,1,0:T(8,128)(2,1)}, u32[]{:S(2)}, u32[]{:S(2)}) async-start(bf16[16,32,1024]{2,1,0:T(8,128)(2,1)} %copy.31), calls=%async_computation | async-start | bytes 2097152 | tf_op jit(solution)/shard_map/all_to_all | solution.py:360
  27.8 9.5 %collective-permute-start.4 = (bf16[128,1024]{1,0:T(8,128)(2,1)S(1)}, bf16[128,1024]{1,0:T(8,128)(2,1)S(1)}, u32[]{:S(2)}, u32[]{:S(2)}) collective-permute-start(bf16[128,1024]{1,0:T(8,128)(2,1)S(1)} %bitcast_select_fusion), channel_id=1, source_target_pairs={{2,0},{3,1},{0,2},{1,3},{6,4},{7,5},{4,6},{5,7},{10,8},{11,9},{8,1... | collective-permute-start | bytes 786440 | tf_op jit(solution)/shard_map/ppermute | solution.py:25
  28.1 12.6 %collective-permute-start.3 = (bf16[128,1024]{1,0:T(8,128)(2,1)S(1)}, bf16[128,1024]{1,0:T(8,128)(2,1)S(1)}, u32[]{:S(2)}, u32[]{:S(2)}) collective-permute-start(bf16[128,1024]{1,0:T(8,128)(2,1)S(1)} %bitcast_select_fusion), channel_id=1, source_target_pairs={{3,0},{0,1},{1,2},{2,3},{7,4},{4,5},{5,6},{6,7},{11,8},{8,9},{9,10... | collective-permute-start | bytes 786440 | tf_op jit(solution)/shard_map/ppermute | solution.py:25
  30.4 13.2 %collective-permute-start.2 = (bf16[128,1024]{1,0:T(8,128)(2,1)S(1)}, bf16[128,1024]{1,0:T(8,128)(2,1)S(1)}, u32[]{:S(2)}, u32[]{:S(2)}) collective-permute-start(bf16[128,1024]{1,0:T(8,128)(2,1)S(1)} %bitcast_select_fusion), channel_id=1, source_target_pairs={{1,0},{2,1},{3,2},{0,3},{5,4},{6,5},{7,6},{4,7},{9,8},{10,9},{11,1... | collective-permute-start | bytes 786440 | tf_op jit(solution)/shard_map/ppermute | solution.py:25
  43.7 43.9 %collective-permute-start.5 = (bf16[4,128,1024]{2,1,0:T(8,128)(2,1)S(1)}, bf16[4,128,1024]{2,1,0:T(8,128)(2,1)S(1)}, u32[]{:S(2)}, u32[]{:S(2)}) collective-permute-start(bf16[4,128,1024]{2,1,0:T(8,128)(2,1)S(1)} %pad_maximum_fusion.1.base), channel_id=1, source_target_pairs={{16,0},{32,16},{48,32},{0,48},{17,1},{33,17},{49,33},{1,49},{18,2}... | collective-permute-start | bytes 3145736 | tf_op jit(solution)/shard_map/ppermute | solution.py:25
  44.2 43.5 %collective-permute-start.6 = (bf16[4,128,1024]{2,1,0:T(8,128)(2,1)S(1)}, bf16[4,128,1024]{2,1,0:T(8,128)(2,1)}, u32[]{:S(2)}, u32[]{:S(2)}) collective-permute-start(bf16[4,128,1024]{2,1,0:T(8,128)(2,1)S(1)} %pad_maximum_fusion.1.base), channel_id=1, source_target_pairs={{48,0},{0,16},{16,32},{32,48},{49,1},{1,17},{17,33},{33,49},{50,2}... | collective-permute-start | bytes 3145736 | tf_op jit(solution)/shard_map/ppermute | solution.py:25
  45.2 42.4 %collective-permute-start.7 = (bf16[4,128,1024]{2,1,0:T(8,128)(2,1)S(1)}, bf16[4,128,1024]{2,1,0:T(8,128)(2,1)}, u32[]{:S(2)}, u32[]{:S(2)}) collective-permute-start(bf16[4,128,1024]{2,1,0:T(8,128)(2,1)S(1)} %pad_maximum_fusion.1.base), channel_id=1, source_target_pairs={{64,0},{4,64},{68,4},{0,68},{65,1},{5,65},{69,5},{1,69},{66,2},{6,... | collective-permute-start | bytes 3145736 | tf_op jit(solution)/shard_map/ppermute | solution.py:23
  82.6 6.7 %collective-permute-start.1 = (bf16[256,1024]{1,0:T(8,128)(2,1)S(1)}, bf16[256,1024]{1,0:T(8,128)(2,1)}, u32[]{:S(2)}, u32[]{:S(2)}) collective-permute-start(bf16[256,1024]{1,0:T(8,128)(2,1)S(1)} %bitcast.34), channel_id=1, source_target_pairs={{0,8},{8,0},{1,9},{9,1},{2,10},{10,2},{3,11},{11,3},{4,12},{12,4},... | collective-permute-start | bytes 1572872 | tf_op jit(solution)/shard_map/ppermute | solution.py:29
  97.8 11.3 %copy-start.3 = (bf16[4,256,256]{2,1,0:T(8,128)(2,1)S(1)}, bf16[4,256,256]{2,1,0:T(8,128)(2,1)}, u32[]{:S(2)}) copy-start(bf16[4,256,256]{2,1,0:T(8,128)(2,1)} %guide.1) | copy-start | bytes 1572868
  97.8 2.2 %collective-permute-start.8 = (bf16[256,1024]{1,0:T(8,128)(2,1)S(1)}, bf16[256,1024]{1,0:T(8,128)(2,1)S(1)}, u32[]{:S(2)}, u32[]{:S(2)}) collective-permute-start(bf16[256,1024]{1,0:T(8,128)(2,1)S(1)} %get-tuple-element.17), channel_id=1, source_target_pairs={{0,8},{8,0},{1,9},{9,1},{2,10},{10,2},{3,11},{11,3},{4,12},{12,4},... | collective-permute-start | bytes 1572872 | tf_op jit(solution)/shard_map/ppermute | solution.py:29
  101.0 26.5 %all-to-all-start.2 = ((bf16[8,32,1024]{2,1,0:T(8,128)(2,1)}), bf16[8,32,1024]{2,1,0:T(8,128)(2,1)S(1)}, u32[]{:S(2)}, u32[]{:S(2)}) async-start(bf16[8,32,1024]{2,1,0:T(8,128)(2,1)} %bitcast.18), calls=%async_computation.2 | async-start | bytes 1048576 | tf_op jit(solution)/shard_map/all_to_all | solution.py:387
  109.1 15.3 %collective-permute-start.9 = (bf16[3,256,256]{2,1,0:T(8,128)(2,1)S(1)}, bf16[3,256,256]{2,1,0:T(8,128)(2,1)S(1)}, u32[]{:S(2)}, u32[]{:S(2)}) collective-permute-start(bf16[3,256,256]{2,1,0:T(8,128)(2,1)S(1)} %get-tuple-element.18), channel_id=1, source_target_pairs={{0,1},{1,2},{2,3},{3,4},{4,5},{5,6},{6,7},{7,8},{8,9},{9,10},{10,1... | collective-permute-start | bytes 1179656 | tf_op jit(solution)/shard_map/ppermute | solution.py:384
  113.8 13.7 %collective-permute-start.10 = (bf16[3,256,256]{2,1,0:T(8,128)(2,1)S(1)}, bf16[3,256,256]{2,1,0:T(8,128)(2,1)S(1)}, u32[]{:S(2)}, u32[]{:S(2)}) collective-permute-start(bf16[3,256,256]{2,1,0:T(8,128)(2,1)S(1)} %get-tuple-element.19), channel_id=1, source_target_pairs={{1,0},{2,1},{3,2},{4,3},{5,4},{6,5},{7,6},{8,7},{9,8},{10,9},{11,1... | collective-permute-start | bytes 1179656 | tf_op jit(solution)/shard_map/ppermute | solution.py:385
  124.4 36.8 %copy-start.10 = (bf16[3,256,256]{2,1,0:T(8,128)(2,1)}, bf16[3,256,256]{2,1,0:T(8,128)(2,1)S(1)}, u32[]{:S(2)}) copy-start(bf16[3,256,256]{2,1,0:T(8,128)(2,1)S(1)} %collective-permute-done.9.guide_low) | copy-start | bytes 1179652
  127.5 33.7 %copy-start.11 = (bf16[3,256,256]{2,1,0:T(8,128)(2,1)}, bf16[3,256,256]{2,1,0:T(8,128)(2,1)S(1)}, u32[]{:S(2)}) copy-start(bf16[3,256,256]{2,1,0:T(8,128)(2,1)S(1)} %collective-permute-done.10.guide_high) | copy-start | bytes 1179652
  127.5 2.8 %collective-permute-start.11 = (bf16[256,1024]{1,0:T(8,128)(2,1)S(1)}, bf16[256,1024]{1,0:T(8,128)(2,1)S(1)}, u32[]{:S(2)}, u32[]{:S(2)}) collective-permute-start(bf16[256,1024]{1,0:T(8,128)(2,1)S(1)} %bitcast.45), channel_id=1, source_target_pairs={{0,8},{8,0},{1,9},{9,1},{2,10},{10,2},{3,11},{11,3},{4,12},{12,4},... | collective-permute-start | bytes 1572872 | tf_op jit(solution)/shard_map/ppermute | solution.py:29
  140.7 2.2 %collective-permute-start.12 = (bf16[256,1024]{1,0:T(8,128)(2,1)}, bf16[256,1024]{1,0:T(8,128)(2,1)S(1)}, u32[]{:S(2)}, u32[]{:S(2)}) collective-permute-start(bf16[256,1024]{1,0:T(8,128)(2,1)} %get-tuple-element.22), channel_id=1, source_target_pairs={{0,8},{8,0},{1,9},{9,1},{2,10},{10,2},{3,11},{11,3},{4,12},{12,4},... | collective-permute-start | bytes 1572872 | tf_op jit(solution)/shard_map/ppermute | solution.py:29
  144.5 16.6 %copy-start.7 = (bf16[8,2,16,256]{3,2,0,1:T(8,128)(2,1)}, bf16[8,2,16,256]{3,2,0,1:T(8,128)(2,1)S(1)}, u32[]{:S(2)}) copy-start(bf16[8,2,16,256]{3,2,0,1:T(8,128)(2,1)S(1)} %copy_multiply_fusion) | copy-start | bytes 393220
  144.6 8.6 %collective-permute-start.13 = (bf16[2,128,256]{2,1,0:T(8,128)(2,1)S(1)}, bf16[2,128,256]{2,1,0:T(8,128)(2,1)S(1)}, u32[]{:S(2)}, u32[]{:S(2)}) collective-permute-start(bf16[2,128,256]{2,1,0:T(8,128)(2,1)S(1)} %bitcast.51), channel_id=1, source_target_pairs={{0,1},{1,2},{2,3},{3,4},{4,5},{5,6},{6,7},{7,8},{8,9},{9,10},{10,1... | collective-permute-start | bytes 393224 | tf_op jit(solution)/shard_map/ppermute | solution.py:399
  150.4 10.8 %collective-permute-start.14 = (bf16[2,128,256]{2,1,0:T(8,128)(2,1)S(1)}, bf16[2,128,256]{2,1,0:T(8,128)(2,1)S(1)}, u32[]{:S(2)}, u32[]{:S(2)}) collective-permute-start(bf16[2,128,256]{2,1,0:T(8,128)(2,1)S(1)} %bitcast.52), channel_id=1, source_target_pairs={{1,0},{2,1},{3,2},{4,3},{5,4},{6,5},{7,6},{8,7},{9,8},{10,9},{11,1... | collective-permute-start | bytes 393224 | tf_op jit(solution)/shard_map/ppermute | solution.py:400
  (9 other events, 23.1 us)
Sparse Core Ops, SparseCore 0:
  10.2 94.7 all-gather.2

commit v6 on v5

--- a/solution.py
+++ b/solution.py
@@ -48,7 +48,9 @@
 
 def across(pieces, one, two):
     base = jnp.stack(pieces)
-    return base, shift(base, one, 1), shift(base, one, 3), shift(base, two, 1)
+    low = shift(jnp.stack(pieces[:2]), two, 1)
+    high = shift(jnp.stack(pieces[2:]), two, 3)
+    return base, shift(base, one, 1), shift(base, one, 3), low, high
 
 
 NT = (((1,), (1,)), ((), ()))
@@ -67,14 +69,15 @@
 
 
 def attention_kernel(
-    parity, own, other, gain, base, plus, minus, two,
+    parity, own, other, gain, base, plus, minus, two_low, two_high,
     near_out, far_out, held_base, held_plus, held_minus, held_two, normed, queries, values, context, sems
 ):
     copies = [
         pltpu.make_async_copy(base, held_base, sems.at[0]),
         pltpu.make_async_copy(minus, held_minus, sems.at[1]),
         pltpu.make_async_copy(plus, held_plus, sems.at[2]),
-        pltpu.make_async_copy(two, held_two, sems.at[3]),
+        pltpu.make_async_copy(two_low, held_two.at[0:2], sems.at[3]),
+        pltpu.make_async_copy(two_high, held_two.at[2:4], sems.at[4]),
     ]
     for copy in copies:
         copy.start()
@@ -127,7 +130,7 @@
     far_out[...] = total[count:].astype(BF16)
 
 
-def attention(parity, own, other, gain, base, plus, minus, two):
+def attention(parity, own, other, gain, base, plus, minus, two_low, two_high):
     count, width = own.shape
     stack = pltpu.VMEM((4, 2 * HEAD, width), BF16)
     return pl.pallas_call(
@@ -136,7 +139,7 @@
             jax.ShapeDtypeStruct((count, width), F32),
             jax.ShapeDtypeStruct((count, width), BF16),
         ),
-        in_specs=[whole(pltpu.SMEM)] + [whole(pltpu.VMEM)] * 3 + [whole(pl.ANY)] * 4,
+        in_specs=[whole(pltpu.SMEM)] + [whole(pltpu.VMEM)] * 3 + [whole(pl.ANY)] * 5,
         out_specs=(whole(pltpu.VMEM), whole(pltpu.VMEM)),
         scratch_shapes=[stack] * 4
         + [
@@ -144,12 +147,12 @@
             pltpu.VMEM((2 * count, 16 * HEAD), BF16),
             pltpu.VMEM((2 * count, 8 * HEAD), BF16),
             pltpu.VMEM((2 * count, 8 * HEAD), BF16),
-            pltpu.SemaphoreType.DMA((4,)),
+            pltpu.SemaphoreType.DMA((5,)),
         ],
         compiler_params=pltpu.CompilerParams(vmem_limit_bytes=24 * 2**20),
         cost_estimate=pl.CostEstimate(flops=3 * 10**9, bytes_accessed=7 * 10**6, transcendentals=2**20),
         name="attention",
-    )(parity, own, other, gain, base, plus, minus, two)
+    )(parity, own, other, gain, base, plus, minus, two_low, two_high)
 
 
 def mlp_kernel(own, other, gain, weights, near_out, far_out, held, normed, total, sems):
@@ -204,98 +207,141 @@
     )(own, other, gain, weights)
 
 
-def conv_kernel(
-    place, image_low, image, image_high, guide_low, guide, guide_high, weights, bias,
-    out, guided, first, second, held, sems
+def spread_tokens(cols, tokens):
+    pixel = lax.broadcasted_iota(jnp.int32, (cols, tokens), 0)
+    token = lax.broadcasted_iota(jnp.int32, (cols, tokens), 1)
+    return jnp.where(pixel // 2 == token, 1.0, 0.0).astype(BF16)
+
+
+def conv_terms(terms, weights):
+    sums = []
+    for col in range(3):
+        total = None
+        for row, at in terms:
+            term = jnp.dot(row, weights[at, col], preferred_element_type=F32)
+            total = term if total is None else total + term
+        sums.append(total)
+    cols = sums[0].shape[0]
+    column = lax.broadcasted_iota(jnp.int32, sums[0].shape, 0)
+    left = jnp.where(column == 0, 0.0, pltpu.roll(sums[0], 1, 0))
+    right = jnp.where(column == cols - 1, 0.0, pltpu.roll(sums[2], cols - 1, 0))
+    return sums[1] + left + right
+
+
+def near_terms(rows, out_row):
+    return [(rows[at], at - out_row + 1) for at in sorted(rows) if -1 <= at - out_row <= 1]
+
+
+def early_kernel(image, guide, weights, bias, guided, part_one, first, part_two, held, sems):
+    copies = [pltpu.make_async_copy(weights.at[k], held.at[k], sems.at[k]) for k in range(2)]
+    for copy in copies:
+        copy.start()
+    rows, cols, _ = guide.shape
+    spread = spread_tokens(cols, image.shape[1])
+    for at in range(rows // 2):
+        wide = jnp.dot(spread, image[at], preferred_element_type=F32)
+        for row in (2 * at, 2 * at + 1):
+            guided[row] = (wide + guide[row].astype(F32)).astype(BF16)
+    own = {at: guided[at] for at in range(rows)}
+    copies[0].wait()
+    for at in range(rows - 2):
+        value = conv_terms(near_terms(own, at + 1), held.at[0]) + bias[0:1, :]
+        first[at] = jax.nn.gelu(value).astype(BF16)
+    for at, row in enumerate((-1, 0, rows - 1, rows)):
+        part_one[at] = conv_terms(near_terms(own, row), held.at[0]) + bias[0:1, :]
+    copies[1].wait()
+    inner = {at + 1: first[at] for at in range(rows - 2)}
+    for at in range(rows):
+        part_two[at] = conv_terms(near_terms(inner, at), held.at[1]) + bias[1:2, :]
+
+
+def late_kernel(
+    place, image_low, image_high, guide_low, guide_high, guided, part_one, first, part_two, weights, bias,
+    out, outer, second, held, sems
 ):
     copies = [pltpu.make_async_copy(weights.at[k], held.at[k], sems.at[k]) for k in range(3)]
     for copy in copies:
         copy.start()
-    cols = guide.shape[1]
-    tokens = image.shape[1]
-    channels = image.shape[2]
-    pixel = lax.broadcasted_iota(jnp.int32, (cols, tokens), 0)
-    token = lax.broadcasted_iota(jnp.int32, (cols, tokens), 1)
-    spread = jnp.where(pixel // 2 == token, 1.0, 0.0).astype(BF16)
-    rows = guide.shape[0]
-    token_rows = (
-        (image_low, 0), (image_low, 1), (image, 0), (image, 1), (image_high, 0), (image_high, 1)
-    )
-    for at, (source, row) in enumerate(token_rows):
-        wide = jnp.dot(spread, source[row], preferred_element_type=F32)
-        for pixel_row in (2 * at - 4, 2 * at - 3):
-            if -3 <= pixel_row < 0:
-                addend = guide_low[pixel_row + 3]
-            elif 0 <= pixel_row < rows:
-                addend = guide[pixel_row]
-            elif rows <= pixel_row < rows + 3:
-                addend = guide_high[pixel_row - rows]
-            else:
-                continue
-            guided[pixel_row + 3] = (wide + addend.astype(F32)).astype(BF16)
+    rows, cols, _ = guided.shape
+    spread = spread_tokens(cols, image_low.shape[1])
+    beside = {}
+    for source, addend, top in ((image_low, guide_low, -4), (image_high, guide_high, rows)):
+        for at in range(2):
+            wide = jnp.dot(spread, source[at], preferred_element_type=F32)
+            for row in (top + 2 * at, top + 2 * at + 1):
+                if -3 <= row < rows + 3:
+                    added = addend[row + 3 if row < 0 else row - rows]
+                    beside[row] = (wide + added.astype(F32)).astype(BF16)
     first_row = place[0]
     last_row = place[1]
-    column = lax.broadcasted_iota(jnp.int32, (1, cols, channels), 1)
-    at_left = column == 0
-    at_right = column == cols - 1
-
-    def layer(source, layer_at, start, size):
-        sums = []
-        for col in range(3):
-            total = None
-            for row in range(3):
-                block = source[start + row : start + row + size].reshape(size * cols, channels)
-                term = jnp.dot(block, held[layer_at, row, col], preferred_element_type=F32)
-                total = term if total is None else total + term
-            sums.append(total)
-        left = pltpu.roll(sums[0], 1, 0).reshape(size, cols, channels)
-        right = pltpu.roll(sums[2], size * cols - 1, 0).reshape(size, cols, channels)
-        middle = sums[1].reshape(size, cols, channels)
-        return (
-            middle
-            + jnp.where(at_left, 0.0, left)
-            + jnp.where(at_right, 0.0, right)
-            + bias[layer_at : layer_at + 1, :].reshape(1, 1, channels)
-        )
-
-    def inside(values, top):
-        for row in range(values.shape[0]):
-            at = first_row + top + row
-            keep = jnp.logical_and(at >= 0, at < last_row)
-            yield row, jnp.where(keep, values[row], 0.0).astype(BF16)
+
+    def inside(value, row):
+        at = first_row + row
+        return jnp.where(jnp.logical_and(at >= 0, at < last_row), value, 0.0).astype(BF16)
 
     copies[0].wait()
-    for start in range(0, rows + 4, 2):
-        for row, value in inside(jax.nn.gelu(layer(guided, 0, start, 2)), start - 2):
-            first[start + row] = value
+    layer = {}
+    saved = {-1: 0, 0: 1, rows - 1: 2, rows: 3}
+    for at, row in enumerate((-2, -1, 0, rows - 1, rows, rows + 1)):
+        value = conv_terms(near_terms(beside, row), held.at[0])
+        value = value + (part_one[saved[row]] if row in saved else bias[0:1, :])
+        outer[at] = inside(jax.nn.gelu(value), row)
+        layer[row] = outer.at[at]
     copies[1].wait()
-    for start in range(0, rows + 2, 2):
-        for row, value in inside(jax.nn.gelu(layer(first, 1, start, 2)), start - 1):
-            second[start + row] = value
+    shown = {}
+    for row in range(-1, rows + 1):
+        value = conv_terms([(ref[...], at) for ref, at in near_terms(layer, row)], held.at[1]) if near_terms(
+            layer, row
+        ) else 0.0
+        value = value + (part_two[row] if 0 <= row < rows else bias[1:2, :])
+        second[row + 1] = inside(jax.nn.gelu(value), row)
+        shown[row] = second.at[row + 1]
     copies[2].wait()
-    for start in range(0, rows, 2):
-        last = layer(second, 2, start, 2) + guided[start + 3 : start + 5].astype(F32)
-        out[start : start + 2] = last.astype(BF16)
-
-
-def conv_stage(place, image_low, image, image_high, guide_low, guide, guide_high, weights, bias):
+    for row in range(rows):
+        value = conv_terms([(ref[...], at) for ref, at in near_terms(shown, row)], held.at[2])
+        out[row] = (value + bias[2:3, :] + guided[row].astype(F32)).astype(BF16)
+
+
+def early_stage(image, guide, weights, bias):
     rows, cols, channels = guide.shape
+    wide = (rows, cols, channels)
     return pl.pallas_call(
-        conv_kernel,
-        out_shape=jax.ShapeDtypeStruct(guide.shape, BF16),
-        in_specs=[whole(pltpu.SMEM)] + [whole(pltpu.VMEM)] * 6 + [whole(pl.ANY), whole(pltpu.VMEM)],
+        early_kernel,
+        out_shape=(
+            jax.ShapeDtypeStruct(wide, BF16),
+            jax.ShapeDtypeStruct((4, cols, channels), F32),
+            jax.ShapeDtypeStruct((rows - 2, cols, channels), BF16),
+            jax.ShapeDtypeStruct(wide, F32),
+        ),
+        in_specs=[whole(pltpu.VMEM)] * 2 + [whole(pl.ANY), whole(pltpu.VMEM)],
+        out_specs=(whole(pltpu.VMEM),) * 4,
+        scratch_shapes=[
+            pltpu.VMEM((2,) + weights.shape[1:], BF16),
+            pltpu.SemaphoreType.DMA((2,)),
+        ],
+        compiler_params=pltpu.CompilerParams(vmem_limit_bytes=24 * 2**20),
+        cost_estimate=pl.CostEstimate(flops=3 * 10**9, bytes_accessed=4 * 10**6, transcendentals=2**20),
+        name="early",
+    )(image, guide, weights, bias)
+
+
+def late_stage(place, image_low, image_high, guide_low, guide_high, early, weights, bias):
+    rows, cols, channels = early[0].shape
+    return pl.pallas_call(
+        late_kernel,
+        out_shape=jax.ShapeDtypeStruct((rows, cols, channels), BF16),
+        in_specs=[whole(pltpu.SMEM)] + [whole(pltpu.VMEM)] * 8 + [whole(pl.ANY), whole(pltpu.VMEM)],
         out_specs=whole(pltpu.VMEM),
         scratch_shapes=[
-            pltpu.VMEM((rows + 6, cols, channels), BF16),
-            pltpu.VMEM((rows + 4, cols, channels), BF16),
+            pltpu.VMEM((6, cols, channels), BF16),
             pltpu.VMEM((rows + 2, cols, channels), BF16),
             pltpu.VMEM(weights.shape, BF16),
             pltpu.SemaphoreType.DMA((3,)),
         ],
-        compiler_params=pltpu.CompilerParams(vmem_limit_bytes=56 * 2**20),
-        cost_estimate=pl.CostEstimate(flops=6 * 10**9, bytes_accessed=6 * 10**6, transcendentals=2**20),
-        name="convs",
-    )(place, image_low, image, image_high, guide_low, guide, guide_high, weights, bias)
+        compiler_params=pltpu.CompilerParams(vmem_limit_bytes=32 * 2**20),
+        cost_estimate=pl.CostEstimate(flops=4 * 10**9, bytes_accessed=6 * 10**6, transcendentals=2**20),
+        name="late",
+    )(place, image_low, image_high, guide_low, guide_high, *early, weights, bias)
 
 
 def per_device(
@@ -399,8 +445,9 @@
     image_low = lax.ppermute(image, AXES, forward)
     image_high = lax.ppermute(image, AXES, backward)
     place = jnp.stack([lax.axis_index(AXES) * rows, jnp.int32(total * rows)])
-    return conv_stage(
-        place, image_low, image, image_high, guide_low, guide, guide_high, conv_weights, conv_bias
+    early = early_stage(image, guide, conv_weights, conv_bias)
+    return late_stage(
+        place, image_low, image_high, guide_low, guide_high, early, conv_weights, conv_bias
     )
 
 

time: 180 us -> 166 us (0.922)
  the two profiles are of different devices: /device:TPU:125 before, /device:TPU:6 now
where the time goes in v6:
time: 166 us; the launch traced here: 165 us
  starting transfers between devices  60.5 us (36%)
  waiting for transfers between devices  43.1 us (26%)
  Pallas kernels  28.3 us (17%)
  between operations  13.8 us (8%)
  local copies, waits for them, and re-layouts  8.82 us (5%)
  other arithmetic  6.68 us (4%)
  matrix products  4.21 us (3%)
    ppermute x2, waiting for transfers between devices, shift(): return lax.ppermute(block, ('yl', 'yh'), pairs)  13.8 us
    ppermute x5, starting transfers between devices, shift(): lax.ppermute(block, axis, [((i + step) % count, i) for i in range(count)])  10.4 us
    ppermute x5, waiting for transfers between devices, shift(): lax.ppermute(block, axis, [((i + step) % count, i) for i in range(count)])  10.2 us
    pallas_call x1, Pallas kernels, mlp(): pl.pallas_call(mlp_kernel, out_shape=(jax.ShapeDtypeStruct((count, width)...  9.64 us
    pallas_call x1, Pallas kernels, attention(): pl.pallas_call(attention_kernel, out_shape=(jax.ShapeDtypeStruct((count,...  8.45 us
    ppermute x1, starting transfers between devices, per_device(): image_high = lax.ppermute(image, AXES, backward)  8.15 us
    all_to_all x1, starting transfers between devices, per_device(): lax.all_to_all(slab_tokens, MP, split_axis=0, concat_axis=0, tiled=True)  7.81 us
    pallas_call x1, Pallas kernels, late_stage(): pl.pallas_call(late_kernel, out_shape=jax.ShapeDtypeStruct((rows, cols, c...  7.23 us
  transfers between devices with their start and end apart: 20, of which 12 were waited for; matrix products, arithmetic and copies ran while one was open for 8% of the time, Pallas kernels for 7%

profile of v6, /device:TPU:6, one launch (start us, length us, event | category | flops | bytes accessed | tf_op | source)
XLA Modules:
  0.0 165.4 jit_solution(14606040564979396157)
XLA Ops:
  10.0 4.9 %collective-permute-start = (bf16[128,1024]{1,0:T(8,128)(2,1)S(1)}, bf16[128,1024]{1,0:T(8,128)(2,1)S(1)}, u32[]{:S(2)}, u32[]{:S(2)}) collective-permute-start(bf16[128,1024]{1,0:T(8,128)(2,1)S(1)} %dynamic-slice_bitcast_fusion), channel_id=1, source_target_pairs={{0,68},{64,4},{12,72},{76,8},{1,69},{65,5},{13,73},{77,9},{2,70},{... | collective-permute-start | bytes 786440 | tf_op jit(solution)/shard_map/ppermute | solution.py:41
  15.2 3.6 %collective-permute-done = bf16[128,1024]{1,0:T(8,128)(2,1)S(1)} collective-permute-done((bf16[128,1024]{1,0:T(8,128)(2,1)S(1)}, bf16[128,1024]{1,0:T(8,128)(2,1)S(1)}, u32[]{:S(2)}, u32[]{:S(2)}) %collective-permute-start) | collective-permute-done | bytes 262176 | tf_op jit(solution)/shard_map/ppermute | solution.py:41
  21.0 4.8 %all-to-all-start = ((bf16[16,32,1024]{2,1,0:T(8,128)(2,1)}), bf16[16,32,1024]{2,1,0:T(8,128)(2,1)}, u32[]{:S(2)}, u32[]{:S(2)}) async-start(bf16[16,32,1024]{2,1,0:T(8,128)(2,1)} %copy.31), calls=%async_computation | async-start | bytes 2097152 | tf_op jit(solution)/shard_map/all_to_all | solution.py:406
  25.8 3.9 %collective-permute-start.4 = (bf16[128,1024]{1,0:T(8,128)(2,1)S(1)}, bf16[128,1024]{1,0:T(8,128)(2,1)S(1)}, u32[]{:S(2)}, u32[]{:S(2)}) collective-permute-start(bf16[128,1024]{1,0:T(8,128)(2,1)S(1)} %bitcast_select_fusion), channel_id=1, source_target_pairs={{2,0},{3,1},{0,2},{1,3},{6,4},{7,5},{4,6},{5,7},{10,8},{11,9},{8,1... | collective-permute-start | bytes 786440 | tf_op jit(solution)/shard_map/ppermute | solution.py:25
  30.7 2.2 %collective-permute-start.2 = (bf16[128,1024]{1,0:T(8,128)(2,1)S(1)}, bf16[128,1024]{1,0:T(8,128)(2,1)S(1)}, u32[]{:S(2)}, u32[]{:S(2)}) collective-permute-start(bf16[128,1024]{1,0:T(8,128)(2,1)S(1)} %bitcast_select_fusion), channel_id=1, source_target_pairs={{1,0},{2,1},{3,2},{0,3},{5,4},{6,5},{7,6},{4,7},{9,8},{10,9},{11,1... | collective-permute-start | bytes 786440 | tf_op jit(solution)/shard_map/ppermute | solution.py:25
  32.9 4.8 %collective-permute-done.4 = bf16[128,1024]{1,0:T(8,128)(2,1)S(1)} collective-permute-done((bf16[128,1024]{1,0:T(8,128)(2,1)S(1)}, bf16[128,1024]{1,0:T(8,128)(2,1)S(1)}, u32[]{:S(2)}, u32[]{:S(2)}) %collective-permute-start.4) | collective-permute-done | bytes 262176 | tf_op jit(solution)/shard_map/ppermute | solution.py:25
  37.6 5.1 %collective-permute-done.3 = bf16[128,1024]{1,0:T(8,128)(2,1)S(1)} collective-permute-done((bf16[128,1024]{1,0:T(8,128)(2,1)S(1)}, bf16[128,1024]{1,0:T(8,128)(2,1)S(1)}, u32[]{:S(2)}, u32[]{:S(2)}) %collective-permute-start.3) | collective-permute-done | bytes 262176 | tf_op jit(solution)/shard_map/ppermute | solution.py:25
  44.9 2.4 %collective-permute-start.6 = (bf16[4,128,1024]{2,1,0:T(8,128)(2,1)S(1)}, bf16[4,128,1024]{2,1,0:T(8,128)(2,1)}, u32[]{:S(2)}, u32[]{:S(2)}) collective-permute-start(bf16[4,128,1024]{2,1,0:T(8,128)(2,1)S(1)} %pad_maximum_fusion.1.base), channel_id=1, source_target_pairs={{48,0},{0,16},{16,32},{32,48},{49,1},{1,17},{17,33},{33,49},{50,2}... | collective-permute-start | bytes 3145736 | tf_op jit(solution)/shard_map/ppermute | solution.py:25
  47.3 2.1 %convolution_convert_fusion.1 = bf16[8,32,1024]{2,0,1:T(8,128)(2,1)S(1)} fusion(bf16[16,32,1024]{2,1,0:T(8,128)(2,1)} %all-to-all-done, s32[128]{0:T(128)S(1)} %get-tuple-element.40, s32[128]{0:T(128)S(1)} %get-tuple-element.41, pred[128]{0:T(512)(128)(4,1)S(1)} %get-tuple-element.33), kind=kOutput, calls=%fused_computation.1 | convolution fusion | flops 8687744 | bytes 1574016 | tf_op jit(solution)/shard_map/kg,gpd->kpd/dot_general | solution.py:407
  50.5 7.8 %all-to-all-start.1 = ((bf16[8,32,1024]{2,1,0:T(8,128)(2,1)}), bf16[8,32,1024]{2,1,0:T(8,128)(2,1)S(1)}, u32[]{:S(2)}, u32[]{:S(2)}) async-start(bf16[8,32,1024]{2,1,0:T(8,128)(2,1)} %copy.33), calls=%async_computation.1 | async-start | bytes 1048576 | tf_op jit(solution)/shard_map/all_to_all | solution.py:411
  62.0 3.5 %collective-permute-start.7 = (bf16[2,128,1024]{2,1,0:T(8,128)(2,1)}, bf16[2,128,1024]{2,1,0:T(8,128)(2,1)}, u32[]{:S(2)}, u32[]{:S(2)}) collective-permute-start(bf16[2,128,1024]{2,1,0:T(8,128)(2,1)} %pad_maximum_fusion.2), channel_id=1, source_target_pairs={{64,0},{4,64},{68,4},{0,68},{65,1},{5,65},{69,5},{1,69},{66,2},{6,... | collective-permute-start | bytes 1572872 | tf_op jit(solution)/shard_map/ppermute | solution.py:23
  65.4 4.5 %all-to-all-done.1 = bf16[8,32,1024]{2,1,0:T(8,128)(2,1)S(1)} async-done(((bf16[8,32,1024]{2,1,0:T(8,128)(2,1)}), bf16[8,32,1024]{2,1,0:T(8,128)(2,1)S(1)}, u32[]{:S(2)}, u32[]{:S(2)}) %all-to-all-start.1) | async-done | bytes 524320 | tf_op jit(solution)/shard_map/all_to_all | solution.py:411
  69.9 10.1 %collective-permute-done.7.two_low = bf16[2,128,1024]{2,1,0:T(8,128)(2,1)} collective-permute-done((bf16[2,128,1024]{2,1,0:T(8,128)(2,1)}, bf16[2,128,1024]{2,1,0:T(8,128)(2,1)}, u32[]{:S(2)}, u32[]{:S(2)}) %collective-permute-start.7) | collective-permute-done | bytes 524320 | tf_op jit(solution)/shard_map/ppermute | solution.py:23
  80.0 3.7 %collective-permute-done.8.two_high = bf16[2,128,1024]{2,1,0:T(8,128)(2,1)} collective-permute-done((bf16[2,128,1024]{2,1,0:T(8,128)(2,1)}, bf16[2,128,1024]{2,1,0:T(8,128)(2,1)}, u32[]{:S(2)}, u32[]{:S(2)}) %collective-permute-start.8) | collective-permute-done | bytes 524320 | tf_op jit(solution)/shard_map/ppermute | solution.py:23
  83.7 8.5 %attention.1 = (f32[256,1024]{1,0:T(8,128)S(1)}, bf16[256,1024]{1,0:T(8,128)(2,1)S(1)}) custom-call(s32[1]{0:T(128)} %bitcast.1.parity, bf16[256,1024]{1,0:T(8,128)(2,1)S(1)} %bitcast.35, bf16[256,1024]{1,0:T(8,128)(2,1)} %collective-permute-done.1.other, f32[1,1024]{1,0:T(1,128)S(1)} %bitcast.39, bf16[4,128,1024]{2,1,0:T(8,128)(2,1)S(1)} %pad_maximum_fusion.1.base, ...), custom_call_target="tpu_custom_call" | custom-call | flops 3000000000 | bytes 7000000 | tf_op jit(solution)/shard_map/attention/pallas_call | solution.py:136
  95.2 4.3 %all-to-all-start.2 = ((bf16[8,32,1024]{2,1,0:T(8,128)(2,1)}), bf16[8,32,1024]{2,1,0:T(8,128)(2,1)S(1)}, u32[]{:S(2)}, u32[]{:S(2)}) async-start(bf16[8,32,1024]{2,1,0:T(8,128)(2,1)} %bitcast.18), calls=%async_computation.2 | async-start | bytes 1048576 | tf_op jit(solution)/shard_map/all_to_all | solution.py:433
  99.5 3.9 %collective-permute-start.10 = (bf16[3,256,256]{2,1,0:T(8,128)(2,1)S(1)}, bf16[3,256,256]{2,1,0:T(8,128)(2,1)S(1)}, u32[]{:S(2)}, u32[]{:S(2)}) collective-permute-start(bf16[3,256,256]{2,1,0:T(8,128)(2,1)S(1)} %get-tuple-element.22), channel_id=1, source_target_pairs={{0,1},{1,2},{2,3},{3,4},{4,5},{5,6},{6,7},{7,8},{8,9},{9,10},{10,1... | collective-permute-start | bytes 1179656 | tf_op jit(solution)/shard_map/ppermute | solution.py:430
  103.4 6.2 %collective-permute-start.11 = (bf16[3,256,256]{2,1,0:T(8,128)(2,1)S(1)}, bf16[3,256,256]{2,1,0:T(8,128)(2,1)S(1)}, u32[]{:S(2)}, u32[]{:S(2)}) collective-permute-start(bf16[3,256,256]{2,1,0:T(8,128)(2,1)S(1)} %get-tuple-element.23), channel_id=1, source_target_pairs={{1,0},{2,1},{3,2},{4,3},{5,4},{6,5},{7,6},{8,7},{9,8},{10,9},{11,1... | collective-permute-start | bytes 1179656 | tf_op jit(solution)/shard_map/ppermute | solution.py:431
  109.6 4.7 %collective-permute-done.10.guide_low = bf16[3,256,256]{2,1,0:T(8,128)(2,1)S(1)} collective-permute-done((bf16[3,256,256]{2,1,0:T(8,128)(2,1)S(1)}, bf16[3,256,256]{2,1,0:T(8,128)(2,1)S(1)}, u32[]{:S(2)}, u32[]{:S(2)}) %collective-permute-start.10) | collective-permute-done | bytes 393248 | tf_op jit(solution)/shard_map/ppermute | solution.py:430
  116.3 3.8 %collective-permute-start.12 = (bf16[256,1024]{1,0:T(8,128)(2,1)S(1)}, bf16[256,1024]{1,0:T(8,128)(2,1)S(1)}, u32[]{:S(2)}, u32[]{:S(2)}) collective-permute-start(bf16[256,1024]{1,0:T(8,128)(2,1)S(1)} %bitcast.55), channel_id=1, source_target_pairs={{0,8},{8,0},{1,9},{9,1},{2,10},{10,2},{3,11},{11,3},{4,12},{12,4},... | collective-permute-start | bytes 1572872 | tf_op jit(solution)/shard_map/ppermute | solution.py:29
  122.4 9.6 %mlp.1 = (f32[256,1024]{1,0:T(8,128)}, bf16[256,1024]{1,0:T(8,128)(2,1)}) custom-call(bf16[256,1024]{1,0:T(8,128)(2,1)} %bitcast.56, bf16[256,1024]{1,0:T(8,128)(2,1)} %copy-done.14, f32[1,1024]{1,0:T(1,128)} %bitcast.59, bf16[64,64,1024]{2,1,0:T(8,128)(2,1)} %bitcast.58), custom_call_target="tpu_custom_call" | custom-call | flops 5000000000 | bytes 12000000 | tf_op jit(solution)/shard_map/mlp/pallas_call | solution.py:190
  138.1 8.2 %collective-permute-start.15 = (bf16[2,128,256]{2,1,0:T(8,128)(2,1)S(1)}, bf16[2,128,256]{2,1,0:T(8,128)(2,1)S(1)}, u32[]{:S(2)}, u32[]{:S(2)}) collective-permute-start(bf16[2,128,256]{2,1,0:T(8,128)(2,1)S(1)} %bitcast.37), channel_id=1, source_target_pairs={{1,0},{2,1},{3,2},{4,3},{5,4},{6,5},{7,6},{8,7},{9,8},{10,9},{11,1... | collective-permute-start | bytes 393224 | tf_op jit(solution)/shard_map/ppermute | solution.py:446
  148.3 3.0 %early.1 = (bf16[4,256,256]{2,1,0:T(8,128)(2,1)S(1)}, f32[4,256,256]{2,1,0:T(8,128)S(1)}, bf16[2,256,256]{2,1,0:T(8,128)(2,1)S(1)}, f32[4,256,256]{2,1,0:T(8,128)S(1)}) custom-call(bf16[2,128,256]{2,1,0:T(8,128)(2,1)S(1)} %bitcast.38, bf16[4,256,256]{2,1,0:T(8,128)(2,1)S(1)} %copy-done.1, bf16[3,3,3,256,256]{4,3,2,1,0:T(8,128)(2,1)S(1)} %copy-done.2, ...), custom_call_target="tpu_custom_call" | custom-call | flops 3000000000 | bytes 4000000 | tf_op jit(solution)/shard_map/early/pallas_call | solution.py:308
  151.3 7.2 %late.1 = bf16[4,256,256]{2,1,0:T(8,128)(2,1)} custom-call(s32[2]{0:T(128)S(1)} %pad_add_fusion.place, bf16[2,128,256]{2,1,0:T(8,128)(2,1)S(1)} %collective-permute-done.14.image_low, bf16[2,128,256]{2,1,0:T(8,128)(2,1)S(1)} %collective-permute-done.15.image_high, bf16[3,256,256]{2,1,0:T(8,128)(2,1)S(1)} %collective-permute-done.10.guide_low, ...), custom_call_target="tpu_custom_call" | custom-call | flops 4000000000 | bytes 6000000 | tf_op jit(solution)/shard_map/late/pallas_call | solution.py:330
  (79 shorter events, 28.8 us)
Async XLA Ops:
  6.5 128.0 %copy-start = (bf16[1024,256]{1,0:T(8,128)(2,1)S(1)}, bf16[1024,256]{1,0:T(8,128)(2,1)}, u32[]{:S(2)}) copy-start(bf16[1024,256]{1,0:T(8,128)(2,1)} %param.20) | copy-start | bytes 1572868
  6.5 115.1 %all-gather.3.cloned.1.call-start = ((), (), s32[]{:S(2)}) async-start(), calls=%async_computation.3 | async-start | bytes 8519680 | tf_op jit(solution)/shard_map/all_gather | solution.py:388
  10.0 8.8 %collective-permute-start = (bf16[128,1024]{1,0:T(8,128)(2,1)S(1)}, bf16[128,1024]{1,0:T(8,128)(2,1)S(1)}, u32[]{:S(2)}, u32[]{:S(2)}) collective-permute-start(bf16[128,1024]{1,0:T(8,128)(2,1)S(1)} %dynamic-slice_bitcast_fusion), channel_id=1, source_target_pairs={{0,68},{64,4},{12,72},{76,8},{1,69},{65,5},{13,73},{77,9},{2,70},{... | collective-permute-start | bytes 786440 | tf_op jit(solution)/shard_map/ppermute | solution.py:41
  21.0 26.3 %all-to-all-start = ((bf16[16,32,1024]{2,1,0:T(8,128)(2,1)}), bf16[16,32,1024]{2,1,0:T(8,128)(2,1)}, u32[]{:S(2)}, u32[]{:S(2)}) async-start(bf16[16,32,1024]{2,1,0:T(8,128)(2,1)} %copy.31), calls=%async_computation | async-start | bytes 2097152 | tf_op jit(solution)/shard_map/all_to_all | solution.py:406
  25.8 11.9 %collective-permute-start.4 = (bf16[128,1024]{1,0:T(8,128)(2,1)S(1)}, bf16[128,1024]{1,0:T(8,128)(2,1)S(1)}, u32[]{:S(2)}, u32[]{:S(2)}) collective-permute-start(bf16[128,1024]{1,0:T(8,128)(2,1)S(1)} %bitcast_select_fusion), channel_id=1, source_target_pairs={{2,0},{3,1},{0,2},{1,3},{6,4},{7,5},{4,6},{5,7},{10,8},{11,9},{8,1... | collective-permute-start | bytes 786440 | tf_op jit(solution)/shard_map/ppermute | solution.py:25
  29.6 13.2 %collective-permute-start.3 = (bf16[128,1024]{1,0:T(8,128)(2,1)S(1)}, bf16[128,1024]{1,0:T(8,128)(2,1)S(1)}, u32[]{:S(2)}, u32[]{:S(2)}) collective-permute-start(bf16[128,1024]{1,0:T(8,128)(2,1)S(1)} %bitcast_select_fusion), channel_id=1, source_target_pairs={{3,0},{0,1},{1,2},{2,3},{7,4},{4,5},{5,6},{6,7},{11,8},{8,9},{9,10... | collective-permute-start | bytes 786440 | tf_op jit(solution)/shard_map/ppermute | solution.py:25
  30.7 12.5 %collective-permute-start.2 = (bf16[128,1024]{1,0:T(8,128)(2,1)S(1)}, bf16[128,1024]{1,0:T(8,128)(2,1)S(1)}, u32[]{:S(2)}, u32[]{:S(2)}) collective-permute-start(bf16[128,1024]{1,0:T(8,128)(2,1)S(1)} %bitcast_select_fusion), channel_id=1, source_target_pairs={{1,0},{2,1},{3,2},{0,3},{5,4},{6,5},{7,6},{4,7},{9,8},{10,9},{11,1... | collective-permute-start | bytes 786440 | tf_op jit(solution)/shard_map/ppermute | solution.py:25
  43.8 39.9 %copy-start.4 = (f32[1024]{0:T(1024)S(1)}, f32[1024]{0:T(1024)}, u32[]{:S(2)}) copy-start(f32[1024]{0:T(1024)} %param.14) | copy-start | bytes 12292
  44.0 39.8 %collective-permute-start.5 = (bf16[4,128,1024]{2,1,0:T(8,128)(2,1)S(1)}, bf16[4,128,1024]{2,1,0:T(8,128)(2,1)S(1)}, u32[]{:S(2)}, u32[]{:S(2)}) collective-permute-start(bf16[4,128,1024]{2,1,0:T(8,128)(2,1)S(1)} %pad_maximum_fusion.1.base), channel_id=1, source_target_pairs={{16,0},{32,16},{48,32},{0,48},{17,1},{33,17},{49,33},{1,49},{18,2}... | collective-permute-start | bytes 3145736 | tf_op jit(solution)/shard_map/ppermute | solution.py:25
  44.9 38.8 %collective-permute-start.6 = (bf16[4,128,1024]{2,1,0:T(8,128)(2,1)S(1)}, bf16[4,128,1024]{2,1,0:T(8,128)(2,1)}, u32[]{:S(2)}, u32[]{:S(2)}) collective-permute-start(bf16[4,128,1024]{2,1,0:T(8,128)(2,1)S(1)} %pad_maximum_fusion.1.base), channel_id=1, source_target_pairs={{48,0},{0,16},{16,32},{32,48},{49,1},{1,17},{17,33},{33,49},{50,2}... | collective-permute-start | bytes 3145736 | tf_op jit(solution)/shard_map/ppermute | solution.py:25
  50.5 19.5 %all-to-all-start.1 = ((bf16[8,32,1024]{2,1,0:T(8,128)(2,1)}), bf16[8,32,1024]{2,1,0:T(8,128)(2,1)S(1)}, u32[]{:S(2)}, u32[]{:S(2)}) async-start(bf16[8,32,1024]{2,1,0:T(8,128)(2,1)} %copy.33), calls=%async_computation.1 | async-start | bytes 1048576 | tf_op jit(solution)/shard_map/all_to_all | solution.py:411
  62.0 18.1 %collective-permute-start.7 = (bf16[2,128,1024]{2,1,0:T(8,128)(2,1)}, bf16[2,128,1024]{2,1,0:T(8,128)(2,1)}, u32[]{:S(2)}, u32[]{:S(2)}) collective-permute-start(bf16[2,128,1024]{2,1,0:T(8,128)(2,1)} %pad_maximum_fusion.2), channel_id=1, source_target_pairs={{64,0},{4,64},{68,4},{0,68},{65,1},{5,65},{69,5},{1,69},{66,2},{6,... | collective-permute-start | bytes 1572872 | tf_op jit(solution)/shard_map/ppermute | solution.py:23
  65.4 18.3 %collective-permute-start.8 = (bf16[2,128,1024]{2,1,0:T(8,128)(2,1)}, bf16[2,128,1024]{2,1,0:T(8,128)(2,1)}, u32[]{:S(2)}, u32[]{:S(2)}) collective-permute-start(bf16[2,128,1024]{2,1,0:T(8,128)(2,1)} %pad_maximum_fusion.3), channel_id=1, source_target_pairs={{68,0},{0,64},{64,4},{4,68},{69,1},{1,65},{65,5},{5,69},{70,2},{2,... | collective-permute-start | bytes 1572872 | tf_op jit(solution)/shard_map/ppermute | solution.py:23
  69.9 13.8 %collective-permute-start.1 = (bf16[256,1024]{1,0:T(8,128)(2,1)S(1)}, bf16[256,1024]{1,0:T(8,128)(2,1)}, u32[]{:S(2)}, u32[]{:S(2)}) collective-permute-start(bf16[256,1024]{1,0:T(8,128)(2,1)S(1)} %bitcast.34), channel_id=1, source_target_pairs={{0,8},{8,0},{1,9},{9,1},{2,10},{10,2},{3,11},{11,3},{4,12},{12,4},... | collective-permute-start | bytes 1572872 | tf_op jit(solution)/shard_map/ppermute | solution.py:29
  92.2 7.2 %copy-start.1 = (bf16[4,256,256]{2,1,0:T(8,128)(2,1)S(1)}, bf16[4,256,256]{2,1,0:T(8,128)(2,1)}, u32[]{:S(2)}) copy-start(bf16[4,256,256]{2,1,0:T(8,128)(2,1)} %guide.1) | copy-start | bytes 1572868
  92.2 2.0 %collective-permute-start.9 = (bf16[256,1024]{1,0:T(8,128)(2,1)S(1)}, bf16[256,1024]{1,0:T(8,128)(2,1)S(1)}, u32[]{:S(2)}, u32[]{:S(2)}) collective-permute-start(bf16[256,1024]{1,0:T(8,128)(2,1)S(1)} %get-tuple-element.21), channel_id=1, source_target_pairs={{0,8},{8,0},{1,9},{9,1},{2,10},{10,2},{3,11},{11,3},{4,12},{12,4},... | collective-permute-start | bytes 1572872 | tf_op jit(solution)/shard_map/ppermute | solution.py:29
  95.2 21.1 %all-to-all-start.2 = ((bf16[8,32,1024]{2,1,0:T(8,128)(2,1)}), bf16[8,32,1024]{2,1,0:T(8,128)(2,1)S(1)}, u32[]{:S(2)}, u32[]{:S(2)}) async-start(bf16[8,32,1024]{2,1,0:T(8,128)(2,1)} %bitcast.18), calls=%async_computation.2 | async-start | bytes 1048576 | tf_op jit(solution)/shard_map/all_to_all | solution.py:433
  99.5 14.8 %collective-permute-start.10 = (bf16[3,256,256]{2,1,0:T(8,128)(2,1)S(1)}, bf16[3,256,256]{2,1,0:T(8,128)(2,1)S(1)}, u32[]{:S(2)}, u32[]{:S(2)}) collective-permute-start(bf16[3,256,256]{2,1,0:T(8,128)(2,1)S(1)} %get-tuple-element.22), channel_id=1, source_target_pairs={{0,1},{1,2},{2,3},{3,4},{4,5},{5,6},{6,7},{7,8},{8,9},{9,10},{10,1... | collective-permute-start | bytes 1179656 | tf_op jit(solution)/shard_map/ppermute | solution.py:430
  103.4 12.8 %collective-permute-start.11 = (bf16[3,256,256]{2,1,0:T(8,128)(2,1)S(1)}, bf16[3,256,256]{2,1,0:T(8,128)(2,1)S(1)}, u32[]{:S(2)}, u32[]{:S(2)}) collective-permute-start(bf16[3,256,256]{2,1,0:T(8,128)(2,1)S(1)} %get-tuple-element.23), channel_id=1, source_target_pairs={{1,0},{2,1},{3,2},{4,3},{5,4},{6,5},{7,6},{8,7},{9,8},{10,9},{11,1... | collective-permute-start | bytes 1179656 | tf_op jit(solution)/shard_map/ppermute | solution.py:431
  116.3 5.4 %collective-permute-start.12 = (bf16[256,1024]{1,0:T(8,128)(2,1)S(1)}, bf16[256,1024]{1,0:T(8,128)(2,1)S(1)}, u32[]{:S(2)}, u32[]{:S(2)}) collective-permute-start(bf16[256,1024]{1,0:T(8,128)(2,1)S(1)} %bitcast.55), channel_id=1, source_target_pairs={{0,8},{8,0},{1,9},{9,1},{2,10},{10,2},{3,11},{11,3},{4,12},{12,4},... | collective-permute-start | bytes 1572872 | tf_op jit(solution)/shard_map/ppermute | solution.py:29
  122.4 23.8 %copy-start.5 = (f32[3,256]{1,0:T(4,128)S(1)}, f32[3,256]{1,0:T(4,128)}, u32[]{:S(2)}) copy-start(f32[3,256]{1,0:T(4,128)} %bias.3) | copy-start | bytes 9220
  132.1 2.4 %collective-permute-start.13 = (bf16[256,1024]{1,0:T(8,128)(2,1)}, bf16[256,1024]{1,0:T(8,128)(2,1)S(1)}, u32[]{:S(2)}, u32[]{:S(2)}) collective-permute-start(bf16[256,1024]{1,0:T(8,128)(2,1)} %get-tuple-element.26), channel_id=1, source_target_pairs={{0,8},{8,0},{1,9},{9,1},{2,10},{10,2},{3,11},{11,3},{4,12},{12,4},... | collective-permute-start | bytes 1572872 | tf_op jit(solution)/shard_map/ppermute | solution.py:29
  136.1 15.1 %collective-permute-start.14 = (bf16[2,128,256]{2,1,0:T(8,128)(2,1)S(1)}, bf16[2,128,256]{2,1,0:T(8,128)(2,1)S(1)}, u32[]{:S(2)}, u32[]{:S(2)}) collective-permute-start(bf16[2,128,256]{2,1,0:T(8,128)(2,1)S(1)} %bitcast.36), channel_id=1, source_target_pairs={{0,1},{1,2},{2,3},{3,4},{4,5},{5,6},{6,7},{7,8},{8,9},{9,10},{10,1... | collective-permute-start | bytes 393224 | tf_op jit(solution)/shard_map/ppermute | solution.py:445
  138.1 13.2 %collective-permute-start.15 = (bf16[2,128,256]{2,1,0:T(8,128)(2,1)S(1)}, bf16[2,128,256]{2,1,0:T(8,128)(2,1)S(1)}, u32[]{:S(2)}, u32[]{:S(2)}) collective-permute-start(bf16[2,128,256]{2,1,0:T(8,128)(2,1)S(1)} %bitcast.37), channel_id=1, source_target_pairs={{1,0},{2,1},{3,2},{4,3},{5,4},{6,5},{7,6},{8,7},{9,8},{10,9},{11,1... | collective-permute-start | bytes 393224 | tf_op jit(solution)/shard_map/ppermute | solution.py:446
  (12 other events, 38.5 us)
Sparse Core Ops, SparseCore 0:
  10.2 92.2 all-gather.2

commit v7 on v6

--- a/solution.py
+++ b/solution.py
@@ -46,11 +46,8 @@
     return [piece] + [shift(piece, "z", step) for step in (1, 3, 2)]
 
 
-def across(pieces, one, two):
-    base = jnp.stack(pieces)
-    low = shift(jnp.stack(pieces[:2]), two, 1)
-    high = shift(jnp.stack(pieces[2:]), two, 3)
-    return base, shift(base, one, 1), shift(base, one, 3), low, high
+def across(base, low, high, one, two):
+    return base, shift(base, one, 1), shift(base, one, 3), shift(low, two, 1), shift(high, two, 3)
 
 
 NT = (((1,), (1,)), ((), ()))
@@ -374,7 +371,7 @@
         [by_head[0], by_head[1], by_head[2], out_heads], axis=1
     ).reshape(4, 2 * HEAD, width)
     attn_piece = type_exchange(attn_all[colour_x], attn_all[colour_x_beside])
-    attn_w = across(along_z(attn_piece), "x", "y")
+    attn_pieces = along_z(attn_piece)
 
     slice_rows = in_weight.shape[0] // 16
     start = (lax.axis_index("c") * 8 + lax.axis_index(("x", "yl"))) * slice_rows
@@ -401,13 +398,16 @@
         "tk,tg->kg", column_hot.astype(F32), group_hot.astype(F32)
     ).astype(BF16)
     marked = jnp.where((land_mask == 0)[:, None, None], jnp.asarray(FAR, BF16), tokens)
-    marked, _ = lax.optimization_barrier((marked, attn_piece))
     outgoing = jnp.einsum("sj,jpd->spd", selector, marked, preferred_element_type=F32).astype(BF16)
     incoming = lax.all_to_all(outgoing, TILE, split_axis=0, concat_axis=0, tiled=True)
     slab_tokens = jnp.einsum(
         "kg,gpd->kpd", arrange, incoming, preferred_element_type=F32
     ).astype(BF16)
     land = slab_tokens[:, 0, 0] < FAR / 2
+    attn_pieces, _ = lax.optimization_barrier((attn_pieces, slab_tokens))
+    stacks = (jnp.stack(attn_pieces), jnp.stack(attn_pieces[:2]), jnp.stack(attn_pieces[2:]))
+    slab_tokens, stacks = lax.optimization_barrier((slab_tokens, stacks))
+    attn_w = across(*stacks, "x", "y")
     tile_tokens = lax.all_to_all(slab_tokens, MP, split_axis=0, concat_axis=0, tiled=True)
     tile_tokens = tile_tokens.reshape(tiles * seg, width)
     other_tokens = swap_cores(tile_tokens)

time: 166 us -> 166 us (level)
  waiting for transfers between devices: 43.1 us -> 51 us
  starting transfers between devices: 60.5 us -> 54.9 us
  local copies, waits for them, and re-layouts: 8.82 us -> 6.99 us
    ppermute x5, waiting for transfers between devices: 10.2 us -> 16.2 us  [shift(): lax.ppermute(block, axis, [((i + step) % count, i) for i in range(count)])]
    all_to_all x1, waiting for transfers between devices: 4.5 us -> 9.33 us  [per_device(): lax.all_to_all(slab_tokens, MP, split_axis=0, concat_axis=0, tiled=True)]
    ppermute x2, waiting for transfers between devices: 13.8 us -> 9.32 us  [shift(): return lax.ppermute(block, ('yl', 'yh'), pairs)]
    all_to_all x1, starting transfers between devices: 7.81 us -> 3.49 us  [per_device(): lax.all_to_all(slab_tokens, MP, split_axis=0, concat_axis=0, tiled=True)]
    another operation x3, other arithmetic: 3.8 us -> 1.84 us  [the longest x1 0.86 us: per_device(): jnp.stack(attn_pieces[2:])]
    unnamed x33 -> x25, local copies, waits for them, and re-layouts: 4.96 us -> 3.13 us
  transfers between devices with their start and end apart: 20 -> 20, of which waited for: 12 -> 12; matrix products, arithmetic and copies ran while one was open for 8% -> 7% of each run, Pallas kernels for 7% -> 7%
where the time goes in v7:
time: 166 us; the launch traced here: 165 us
  starting transfers between devices  54.9 us (33%)
  waiting for transfers between devices  51 us (31%)
  Pallas kernels  28.2 us (17%)
  between operations  13.8 us (8%)
  other arithmetic  7.06 us (4%)
  local copies, waits for them, and re-layouts  6.99 us (4%)
  matrix products  2.98 us (2%)
    ppermute x5, waiting for transfers between devices, shift(): lax.ppermute(block, axis, [((i + step) % count, i) for i in range(count)])  16.2 us
    pallas_call x1, Pallas kernels, mlp(): pl.pallas_call(mlp_kernel, out_shape=(jax.ShapeDtypeStruct((count, width)...  9.61 us
    all_to_all x1, waiting for transfers between devices, per_device(): lax.all_to_all(slab_tokens, MP, split_axis=0, concat_axis=0, tiled=True)  9.33 us
    ppermute x2, waiting for transfers between devices, shift(): return lax.ppermute(block, ('yl', 'yh'), pairs)  9.32 us
    ppermute x5, starting transfers between devices, shift(): lax.ppermute(block, axis, [((i + step) % count, i) for i in range(count)])  9.28 us
    pallas_call x1, Pallas kernels, attention(): pl.pallas_call(attention_kernel, out_shape=(jax.ShapeDtypeStruct((count,...  8.41 us
    ppermute x1, starting transfers between devices, per_device(): image_high = lax.ppermute(image, AXES, backward)  8.15 us
    pallas_call x1, Pallas kernels, late_stage(): pl.pallas_call(late_kernel, out_shape=jax.ShapeDtypeStruct((rows, cols, c...  7.23 us
  transfers between devices with their start and end apart: 20, of which 12 were waited for; matrix products, arithmetic and copies ran while one was open for 7% of the time, Pallas kernels for 7%

profile of v7, /device:TPU:6, one launch (start us, length us, event | category | flops | bytes accessed | tf_op | source)
XLA Modules:
  0.0 165.0 jit_solution(16436848091529793427)
XLA Ops:
  13.0 5.8 %all-to-all-start = ((bf16[16,32,1024]{2,1,0:T(8,128)(2,1)}), bf16[16,32,1024]{2,1,0:T(8,128)(2,1)S(1)}, u32[]{:S(2)}, u32[]{:S(2)}) async-start(bf16[16,32,1024]{2,1,0:T(8,128)(2,1)} %copy.29), calls=%async_computation | async-start | bytes 2097152 | tf_op jit(solution)/shard_map/all_to_all | solution.py:402
  19.4 4.8 %collective-permute-start = (bf16[128,1024]{1,0:T(8,128)(2,1)S(1)}, bf16[128,1024]{1,0:T(8,128)(2,1)S(1)}, u32[]{:S(2)}, u32[]{:S(2)}) collective-permute-start(bf16[128,1024]{1,0:T(8,128)(2,1)S(1)} %dynamic-slice_bitcast_fusion), channel_id=1, source_target_pairs={{0,68},{64,4},{12,72},{76,8},{1,69},{65,5},{13,73},{77,9},{2,70},{... | collective-permute-start | bytes 786440 | tf_op jit(solution)/shard_map/ppermute | solution.py:41
  24.3 3.8 %collective-permute-done = bf16[128,1024]{1,0:T(8,128)(2,1)S(1)} collective-permute-done((bf16[128,1024]{1,0:T(8,128)(2,1)S(1)}, bf16[128,1024]{1,0:T(8,128)(2,1)S(1)}, u32[]{:S(2)}, u32[]{:S(2)}) %collective-permute-start) | collective-permute-done | bytes 262176 | tf_op jit(solution)/shard_map/ppermute | solution.py:41
  28.1 4.1 %collective-permute-start.1 = (bf16[128,1024]{1,0:T(8,128)(2,1)S(1)}, bf16[128,1024]{1,0:T(8,128)(2,1)S(1)}, u32[]{:S(2)}, u32[]{:S(2)}) collective-permute-start(bf16[128,1024]{1,0:T(8,128)(2,1)S(1)} %bitcast_select_fusion), channel_id=1, source_target_pairs={{1,0},{2,1},{3,2},{0,3},{5,4},{6,5},{7,6},{4,7},{9,8},{10,9},{11,1... | collective-permute-start | bytes 786440 | tf_op jit(solution)/shard_map/ppermute | solution.py:25
  35.0 9.6 %collective-permute-done.1 = bf16[128,1024]{1,0:T(8,128)(2,1)S(1)} collective-permute-done((bf16[128,1024]{1,0:T(8,128)(2,1)S(1)}, bf16[128,1024]{1,0:T(8,128)(2,1)S(1)}, u32[]{:S(2)}, u32[]{:S(2)}) %collective-permute-start.1) | collective-permute-done | bytes 262176 | tf_op jit(solution)/shard_map/ppermute | solution.py:25
  44.6 3.4 %collective-permute-done.2 = bf16[128,1024]{1,0:T(8,128)(2,1)S(1)} collective-permute-done((bf16[128,1024]{1,0:T(8,128)(2,1)S(1)}, bf16[128,1024]{1,0:T(8,128)(2,1)S(1)}, u32[]{:S(2)}, u32[]{:S(2)}) %collective-permute-start.2) | collective-permute-done | bytes 262176 | tf_op jit(solution)/shard_map/ppermute | solution.py:25
  50.6 2.6 %collective-permute-start.6 = (bf16[4,128,1024]{2,1,0:T(8,128)(2,1)S(1)}, bf16[4,128,1024]{2,1,0:T(8,128)(2,1)}, u32[]{:S(2)}, u32[]{:S(2)}) collective-permute-start(bf16[4,128,1024]{2,1,0:T(8,128)(2,1)S(1)} %pad_maximum_fusion.1.base), channel_id=1, source_target_pairs={{48,0},{0,16},{16,32},{32,48},{49,1},{1,17},{17,33},{33,49},{50,2}... | collective-permute-start | bytes 3145736 | tf_op jit(solution)/shard_map/ppermute | solution.py:25
  54.2 3.5 %all-to-all-start.1 = ((bf16[8,32,1024]{2,1,0:T(8,128)(2,1)}), bf16[8,32,1024]{2,1,0:T(8,128)(2,1)S(1)}, u32[]{:S(2)}, u32[]{:S(2)}) async-start(bf16[8,32,1024]{2,1,0:T(8,128)(2,1)} %copy.33), calls=%async_computation.1 | async-start | bytes 1048576 | tf_op jit(solution)/shard_map/all_to_all | solution.py:411
  57.7 2.9 %collective-permute-start.7 = (bf16[2,128,1024]{2,1,0:T(8,128)(2,1)}, bf16[2,128,1024]{2,1,0:T(8,128)(2,1)}, u32[]{:S(2)}, u32[]{:S(2)}) collective-permute-start(bf16[2,128,1024]{2,1,0:T(8,128)(2,1)} %pad_maximum_fusion.2), channel_id=1, source_target_pairs={{64,0},{4,64},{68,4},{0,68},{65,1},{5,65},{69,5},{1,69},{66,2},{6,... | collective-permute-start | bytes 1572872 | tf_op jit(solution)/shard_map/ppermute | solution.py:23
  60.7 9.3 %all-to-all-done.1 = bf16[8,32,1024]{2,1,0:T(8,128)(2,1)S(1)} async-done(((bf16[8,32,1024]{2,1,0:T(8,128)(2,1)}), bf16[8,32,1024]{2,1,0:T(8,128)(2,1)S(1)}, u32[]{:S(2)}, u32[]{:S(2)}) %all-to-all-start.1) | async-done | bytes 524320 | tf_op jit(solution)/shard_map/all_to_all | solution.py:411
  70.0 7.4 %collective-permute-done.7.two_low = bf16[2,128,1024]{2,1,0:T(8,128)(2,1)} collective-permute-done((bf16[2,128,1024]{2,1,0:T(8,128)(2,1)}, bf16[2,128,1024]{2,1,0:T(8,128)(2,1)}, u32[]{:S(2)}, u32[]{:S(2)}) %collective-permute-start.7) | collective-permute-done | bytes 524320 | tf_op jit(solution)/shard_map/ppermute | solution.py:23
  79.4 3.2 %collective-permute-done.5.plus = bf16[4,128,1024]{2,1,0:T(8,128)(2,1)S(1)} collective-permute-done((bf16[4,128,1024]{2,1,0:T(8,128)(2,1)S(1)}, bf16[4,128,1024]{2,1,0:T(8,128)(2,1)S(1)}, u32[]{:S(2)}, u32[]{:S(2)}) %collective-permute-start.5) | collective-permute-done | bytes 1048608 | tf_op jit(solution)/shard_map/ppermute | solution.py:25
  82.6 8.4 %attention.1 = (f32[256,1024]{1,0:T(8,128)S(1)}, bf16[256,1024]{1,0:T(8,128)(2,1)S(1)}) custom-call(s32[1]{0:T(128)} %bitcast.1.parity, bf16[256,1024]{1,0:T(8,128)(2,1)S(1)} %bitcast.35, bf16[256,1024]{1,0:T(8,128)(2,1)} %collective-permute-done.4.other, f32[1,1024]{1,0:T(1,128)S(1)} %bitcast.39, bf16[4,128,1024]{2,1,0:T(8,128)(2,1)S(1)} %pad_maximum_fusion.1.base, ...), custom_call_target="tpu_custom_call" | custom-call | flops 3000000000 | bytes 7000000 | tf_op jit(solution)/shard_map/attention/pallas_call | solution.py:133
  93.9 3.5 %all-to-all-start.2 = ((bf16[8,32,1024]{2,1,0:T(8,128)(2,1)}), bf16[8,32,1024]{2,1,0:T(8,128)(2,1)S(1)}, u32[]{:S(2)}, u32[]{:S(2)}) async-start(bf16[8,32,1024]{2,1,0:T(8,128)(2,1)} %bitcast.18), calls=%async_computation.2 | async-start | bytes 1048576 | tf_op jit(solution)/shard_map/all_to_all | solution.py:433
  97.5 3.8 %collective-permute-start.10 = (bf16[3,256,256]{2,1,0:T(8,128)(2,1)S(1)}, bf16[3,256,256]{2,1,0:T(8,128)(2,1)S(1)}, u32[]{:S(2)}, u32[]{:S(2)}) collective-permute-start(bf16[3,256,256]{2,1,0:T(8,128)(2,1)S(1)} %get-tuple-element.36), channel_id=1, source_target_pairs={{0,1},{1,2},{2,3},{3,4},{4,5},{5,6},{6,7},{7,8},{8,9},{9,10},{10,1... | collective-permute-start | bytes 1179656 | tf_op jit(solution)/shard_map/ppermute | solution.py:430
  101.3 6.3 %collective-permute-start.11 = (bf16[3,256,256]{2,1,0:T(8,128)(2,1)S(1)}, bf16[3,256,256]{2,1,0:T(8,128)(2,1)S(1)}, u32[]{:S(2)}, u32[]{:S(2)}) collective-permute-start(bf16[3,256,256]{2,1,0:T(8,128)(2,1)S(1)} %get-tuple-element.37), channel_id=1, source_target_pairs={{1,0},{2,1},{3,2},{4,3},{5,4},{6,5},{7,6},{8,7},{9,8},{10,9},{11,1... | collective-permute-start | bytes 1179656 | tf_op jit(solution)/shard_map/ppermute | solution.py:431
  107.6 5.9 %collective-permute-done.10.guide_low = bf16[3,256,256]{2,1,0:T(8,128)(2,1)S(1)} collective-permute-done((bf16[3,256,256]{2,1,0:T(8,128)(2,1)S(1)}, bf16[3,256,256]{2,1,0:T(8,128)(2,1)S(1)}, u32[]{:S(2)}, u32[]{:S(2)}) %collective-permute-start.10) | collective-permute-done | bytes 393248 | tf_op jit(solution)/shard_map/ppermute | solution.py:430
  113.5 2.0 %collective-permute-done.11.guide_high = bf16[3,256,256]{2,1,0:T(8,128)(2,1)S(1)} collective-permute-done((bf16[3,256,256]{2,1,0:T(8,128)(2,1)S(1)}, bf16[3,256,256]{2,1,0:T(8,128)(2,1)S(1)}, u32[]{:S(2)}, u32[]{:S(2)}) %collective-permute-start.11) | collective-permute-done | bytes 393248 | tf_op jit(solution)/shard_map/ppermute | solution.py:431
  115.6 4.2 %collective-permute-start.12 = (bf16[256,1024]{1,0:T(8,128)(2,1)S(1)}, bf16[256,1024]{1,0:T(8,128)(2,1)S(1)}, u32[]{:S(2)}, u32[]{:S(2)}) collective-permute-start(bf16[256,1024]{1,0:T(8,128)(2,1)S(1)} %bitcast.55), channel_id=1, source_target_pairs={{0,8},{8,0},{1,9},{9,1},{2,10},{10,2},{3,11},{11,3},{4,12},{12,4},... | collective-permute-start | bytes 1572872 | tf_op jit(solution)/shard_map/ppermute | solution.py:29
  122.1 9.6 %mlp.1 = (f32[256,1024]{1,0:T(8,128)}, bf16[256,1024]{1,0:T(8,128)(2,1)}) custom-call(bf16[256,1024]{1,0:T(8,128)(2,1)} %bitcast.56, bf16[256,1024]{1,0:T(8,128)(2,1)} %copy-done.11, f32[1,1024]{1,0:T(1,128)} %bitcast.59, bf16[64,64,1024]{2,1,0:T(8,128)(2,1)} %bitcast.58), custom_call_target="tpu_custom_call" | custom-call | flops 5000000000 | bytes 12000000 | tf_op jit(solution)/shard_map/mlp/pallas_call | solution.py:187
  137.7 8.2 %collective-permute-start.15 = (bf16[2,128,256]{2,1,0:T(8,128)(2,1)S(1)}, bf16[2,128,256]{2,1,0:T(8,128)(2,1)S(1)}, u32[]{:S(2)}, u32[]{:S(2)}) collective-permute-start(bf16[2,128,256]{2,1,0:T(8,128)(2,1)S(1)} %bitcast.37), channel_id=1, source_target_pairs={{1,0},{2,1},{3,2},{4,3},{5,4},{6,5},{7,6},{8,7},{9,8},{10,9},{11,1... | collective-permute-start | bytes 393224 | tf_op jit(solution)/shard_map/ppermute | solution.py:446
  145.9 2.0 %copy-done.2 = bf16[3,3,3,256,256]{4,3,2,1,0:T(8,128)(2,1)S(1)} copy-done((bf16[3,3,3,256,256]{4,3,2,1,0:T(8,128)(2,1)S(1)}, bf16[3,3,3,256,256]{4,3,2,1,0:T(8,128)(2,1)}, u32[]{:S(2)}) %copy-start.2) | copy-done | bytes 3538968
  147.9 3.0 %early.1 = (bf16[4,256,256]{2,1,0:T(8,128)(2,1)S(1)}, f32[4,256,256]{2,1,0:T(8,128)S(1)}, bf16[2,256,256]{2,1,0:T(8,128)(2,1)S(1)}, f32[4,256,256]{2,1,0:T(8,128)S(1)}) custom-call(bf16[2,128,256]{2,1,0:T(8,128)(2,1)S(1)} %bitcast.38, bf16[4,256,256]{2,1,0:T(8,128)(2,1)S(1)} %copy-done.1, bf16[3,3,3,256,256]{4,3,2,1,0:T(8,128)(2,1)S(1)} %copy-done.2, ...), custom_call_target="tpu_custom_call" | custom-call | flops 3000000000 | bytes 4000000 | tf_op jit(solution)/shard_map/early/pallas_call | solution.py:305
  150.9 7.2 %late.1 = bf16[4,256,256]{2,1,0:T(8,128)(2,1)} custom-call(s32[2]{0:T(128)S(1)} %pad_add_fusion.place, bf16[2,128,256]{2,1,0:T(8,128)(2,1)S(1)} %collective-permute-done.14.image_low, bf16[2,128,256]{2,1,0:T(8,128)(2,1)S(1)} %collective-permute-done.15.image_high, bf16[3,256,256]{2,1,0:T(8,128)(2,1)S(1)} %collective-permute-done.10.guide_low, ...), custom_call_target="tpu_custom_call" | custom-call | flops 4000000000 | bytes 6000000 | tf_op jit(solution)/shard_map/late/pallas_call | solution.py:327
  (71 shorter events, 26.7 us)
Async XLA Ops:
  6.5 127.6 %copy-start = (bf16[1024,256]{1,0:T(8,128)(2,1)S(1)}, bf16[1024,256]{1,0:T(8,128)(2,1)}, u32[]{:S(2)}) copy-start(bf16[1024,256]{1,0:T(8,128)(2,1)} %param.20) | copy-start | bytes 1572868
  6.5 114.7 %all-gather.3.cloned.1.call-start = ((), (), s32[]{:S(2)}) async-start(), calls=%async_computation.3 | async-start | bytes 8519680 | tf_op jit(solution)/shard_map/all_gather | solution.py:385
  13.0 21.1 %all-to-all-start = ((bf16[16,32,1024]{2,1,0:T(8,128)(2,1)}), bf16[16,32,1024]{2,1,0:T(8,128)(2,1)S(1)}, u32[]{:S(2)}, u32[]{:S(2)}) async-start(bf16[16,32,1024]{2,1,0:T(8,128)(2,1)} %copy.29), calls=%async_computation | async-start | bytes 2097152 | tf_op jit(solution)/shard_map/all_to_all | solution.py:402
  19.4 8.7 %collective-permute-start = (bf16[128,1024]{1,0:T(8,128)(2,1)S(1)}, bf16[128,1024]{1,0:T(8,128)(2,1)S(1)}, u32[]{:S(2)}, u32[]{:S(2)}) collective-permute-start(bf16[128,1024]{1,0:T(8,128)(2,1)S(1)} %dynamic-slice_bitcast_fusion), channel_id=1, source_target_pairs={{0,68},{64,4},{12,72},{76,8},{1,69},{65,5},{13,73},{77,9},{2,70},{... | collective-permute-start | bytes 786440 | tf_op jit(solution)/shard_map/ppermute | solution.py:41
  28.1 16.5 %collective-permute-start.1 = (bf16[128,1024]{1,0:T(8,128)(2,1)S(1)}, bf16[128,1024]{1,0:T(8,128)(2,1)S(1)}, u32[]{:S(2)}, u32[]{:S(2)}) collective-permute-start(bf16[128,1024]{1,0:T(8,128)(2,1)S(1)} %bitcast_select_fusion), channel_id=1, source_target_pairs={{1,0},{2,1},{3,2},{0,3},{5,4},{6,5},{7,6},{4,7},{9,8},{10,9},{11,1... | collective-permute-start | bytes 786440 | tf_op jit(solution)/shard_map/ppermute | solution.py:25
  32.2 15.8 %collective-permute-start.2 = (bf16[128,1024]{1,0:T(8,128)(2,1)S(1)}, bf16[128,1024]{1,0:T(8,128)(2,1)S(1)}, u32[]{:S(2)}, u32[]{:S(2)}) collective-permute-start(bf16[128,1024]{1,0:T(8,128)(2,1)S(1)} %bitcast_select_fusion), channel_id=1, source_target_pairs={{3,0},{0,1},{1,2},{2,3},{7,4},{4,5},{5,6},{6,7},{11,8},{8,9},{9,10... | collective-permute-start | bytes 786440 | tf_op jit(solution)/shard_map/ppermute | solution.py:25
  32.2 15.8 %collective-permute-start.3 = (bf16[128,1024]{1,0:T(8,128)(2,1)S(1)}, bf16[128,1024]{1,0:T(8,128)(2,1)S(1)}, u32[]{:S(2)}, u32[]{:S(2)}) collective-permute-start(bf16[128,1024]{1,0:T(8,128)(2,1)S(1)} %bitcast_select_fusion), channel_id=1, source_target_pairs={{2,0},{3,1},{0,2},{1,3},{6,4},{7,5},{4,6},{5,7},{10,8},{11,9},{8,1... | collective-permute-start | bytes 786440 | tf_op jit(solution)/shard_map/ppermute | solution.py:25
  35.0 19.3 %copy-start.6 = (bf16[8,32,1024]{2,0,1:T(8,128)(2,1)}, bf16[8,32,1024]{2,0,1:T(8,128)(2,1)S(1)}, u32[]{:S(2)}) copy-start(bf16[8,32,1024]{2,0,1:T(8,128)(2,1)S(1)} %convolution_convert_fusion.1) | copy-start | bytes 1572868
  35.0 47.6 %copy-start.4 = (f32[1024]{0:T(1024)S(1)}, f32[1024]{0:T(1024)}, u32[]{:S(2)}) copy-start(f32[1024]{0:T(1024)} %param.14) | copy-start | bytes 12292
  49.8 32.7 %collective-permute-start.5 = (bf16[4,128,1024]{2,1,0:T(8,128)(2,1)S(1)}, bf16[4,128,1024]{2,1,0:T(8,128)(2,1)S(1)}, u32[]{:S(2)}, u32[]{:S(2)}) collective-permute-start(bf16[4,128,1024]{2,1,0:T(8,128)(2,1)S(1)} %pad_maximum_fusion.1.base), channel_id=1, source_target_pairs={{16,0},{32,16},{48,32},{0,48},{17,1},{33,17},{49,33},{1,49},{18,2}... | collective-permute-start | bytes 3145736 | tf_op jit(solution)/shard_map/ppermute | solution.py:25
  50.6 32.0 %collective-permute-start.6 = (bf16[4,128,1024]{2,1,0:T(8,128)(2,1)S(1)}, bf16[4,128,1024]{2,1,0:T(8,128)(2,1)}, u32[]{:S(2)}, u32[]{:S(2)}) collective-permute-start(bf16[4,128,1024]{2,1,0:T(8,128)(2,1)S(1)} %pad_maximum_fusion.1.base), channel_id=1, source_target_pairs={{48,0},{0,16},{16,32},{32,48},{49,1},{1,17},{17,33},{33,49},{50,2}... | collective-permute-start | bytes 3145736 | tf_op jit(solution)/shard_map/ppermute | solution.py:25
  54.2 15.8 %all-to-all-start.1 = ((bf16[8,32,1024]{2,1,0:T(8,128)(2,1)}), bf16[8,32,1024]{2,1,0:T(8,128)(2,1)S(1)}, u32[]{:S(2)}, u32[]{:S(2)}) async-start(bf16[8,32,1024]{2,1,0:T(8,128)(2,1)} %copy.33), calls=%async_computation.1 | async-start | bytes 1048576 | tf_op jit(solution)/shard_map/all_to_all | solution.py:411
  57.7 19.7 %collective-permute-start.7 = (bf16[2,128,1024]{2,1,0:T(8,128)(2,1)}, bf16[2,128,1024]{2,1,0:T(8,128)(2,1)}, u32[]{:S(2)}, u32[]{:S(2)}) collective-permute-start(bf16[2,128,1024]{2,1,0:T(8,128)(2,1)} %pad_maximum_fusion.2), channel_id=1, source_target_pairs={{64,0},{4,64},{68,4},{0,68},{65,1},{5,65},{69,5},{1,69},{66,2},{6,... | collective-permute-start | bytes 1572872 | tf_op jit(solution)/shard_map/ppermute | solution.py:23
  60.7 18.7 %collective-permute-start.8 = (bf16[2,128,1024]{2,1,0:T(8,128)(2,1)}, bf16[2,128,1024]{2,1,0:T(8,128)(2,1)}, u32[]{:S(2)}, u32[]{:S(2)}) collective-permute-start(bf16[2,128,1024]{2,1,0:T(8,128)(2,1)} %pad_maximum_fusion.3), channel_id=1, source_target_pairs={{68,0},{0,64},{64,4},{4,68},{69,1},{1,65},{65,5},{5,69},{70,2},{2,... | collective-permute-start | bytes 1572872 | tf_op jit(solution)/shard_map/ppermute | solution.py:23
  70.0 9.3 %collective-permute-start.4 = (bf16[256,1024]{1,0:T(8,128)(2,1)S(1)}, bf16[256,1024]{1,0:T(8,128)(2,1)}, u32[]{:S(2)}, u32[]{:S(2)}) collective-permute-start(bf16[256,1024]{1,0:T(8,128)(2,1)S(1)} %bitcast.34), channel_id=1, source_target_pairs={{0,8},{8,0},{1,9},{9,1},{2,10},{10,2},{3,11},{11,3},{4,12},{12,4},... | collective-permute-start | bytes 1572872 | tf_op jit(solution)/shard_map/ppermute | solution.py:29
  91.0 2.0 %collective-permute-start.9 = (bf16[256,1024]{1,0:T(8,128)(2,1)S(1)}, bf16[256,1024]{1,0:T(8,128)(2,1)S(1)}, u32[]{:S(2)}, u32[]{:S(2)}) collective-permute-start(bf16[256,1024]{1,0:T(8,128)(2,1)S(1)} %get-tuple-element.35), channel_id=1, source_target_pairs={{0,8},{8,0},{1,9},{9,1},{2,10},{10,2},{3,11},{11,3},{4,12},{12,4},... | collective-permute-start | bytes 1572872 | tf_op jit(solution)/shard_map/ppermute | solution.py:29
  93.9 21.6 %all-to-all-start.2 = ((bf16[8,32,1024]{2,1,0:T(8,128)(2,1)}), bf16[8,32,1024]{2,1,0:T(8,128)(2,1)S(1)}, u32[]{:S(2)}, u32[]{:S(2)}) async-start(bf16[8,32,1024]{2,1,0:T(8,128)(2,1)} %bitcast.18), calls=%async_computation.2 | async-start | bytes 1048576 | tf_op jit(solution)/shard_map/all_to_all | solution.py:433
  97.5 16.0 %collective-permute-start.10 = (bf16[3,256,256]{2,1,0:T(8,128)(2,1)S(1)}, bf16[3,256,256]{2,1,0:T(8,128)(2,1)S(1)}, u32[]{:S(2)}, u32[]{:S(2)}) collective-permute-start(bf16[3,256,256]{2,1,0:T(8,128)(2,1)S(1)} %get-tuple-element.36), channel_id=1, source_target_pairs={{0,1},{1,2},{2,3},{3,4},{4,5},{5,6},{6,7},{7,8},{8,9},{9,10},{10,1... | collective-permute-start | bytes 1179656 | tf_op jit(solution)/shard_map/ppermute | solution.py:430
  101.3 14.2 %collective-permute-start.11 = (bf16[3,256,256]{2,1,0:T(8,128)(2,1)S(1)}, bf16[3,256,256]{2,1,0:T(8,128)(2,1)S(1)}, u32[]{:S(2)}, u32[]{:S(2)}) collective-permute-start(bf16[3,256,256]{2,1,0:T(8,128)(2,1)S(1)} %get-tuple-element.37), channel_id=1, source_target_pairs={{1,0},{2,1},{3,2},{4,3},{5,4},{6,5},{7,6},{8,7},{9,8},{10,9},{11,1... | collective-permute-start | bytes 1179656 | tf_op jit(solution)/shard_map/ppermute | solution.py:431
  115.6 5.7 %collective-permute-start.12 = (bf16[256,1024]{1,0:T(8,128)(2,1)S(1)}, bf16[256,1024]{1,0:T(8,128)(2,1)S(1)}, u32[]{:S(2)}, u32[]{:S(2)}) collective-permute-start(bf16[256,1024]{1,0:T(8,128)(2,1)S(1)} %bitcast.55), channel_id=1, source_target_pairs={{0,8},{8,0},{1,9},{9,1},{2,10},{10,2},{3,11},{11,3},{4,12},{12,4},... | collective-permute-start | bytes 1572872 | tf_op jit(solution)/shard_map/ppermute | solution.py:29
  122.1 23.8 %copy-start.5 = (f32[3,256]{1,0:T(4,128)S(1)}, f32[3,256]{1,0:T(4,128)}, u32[]{:S(2)}) copy-start(f32[3,256]{1,0:T(4,128)} %bias.3) | copy-start | bytes 9220
  131.7 2.4 %collective-permute-start.13 = (bf16[256,1024]{1,0:T(8,128)(2,1)}, bf16[256,1024]{1,0:T(8,128)(2,1)S(1)}, u32[]{:S(2)}, u32[]{:S(2)}) collective-permute-start(bf16[256,1024]{1,0:T(8,128)(2,1)} %get-tuple-element.40), channel_id=1, source_target_pairs={{0,8},{8,0},{1,9},{9,1},{2,10},{10,2},{3,11},{11,3},{4,12},{12,4},... | collective-permute-start | bytes 1572872 | tf_op jit(solution)/shard_map/ppermute | solution.py:29
  135.8 15.1 %collective-permute-start.14 = (bf16[2,128,256]{2,1,0:T(8,128)(2,1)S(1)}, bf16[2,128,256]{2,1,0:T(8,128)(2,1)S(1)}, u32[]{:S(2)}, u32[]{:S(2)}) collective-permute-start(bf16[2,128,256]{2,1,0:T(8,128)(2,1)S(1)} %bitcast.36), channel_id=1, source_target_pairs={{0,1},{1,2},{2,3},{3,4},{4,5},{5,6},{6,7},{7,8},{8,9},{9,10},{10,1... | collective-permute-start | bytes 393224 | tf_op jit(solution)/shard_map/ppermute | solution.py:445
  137.7 13.2 %collective-permute-start.15 = (bf16[2,128,256]{2,1,0:T(8,128)(2,1)S(1)}, bf16[2,128,256]{2,1,0:T(8,128)(2,1)S(1)}, u32[]{:S(2)}, u32[]{:S(2)}) collective-permute-start(bf16[2,128,256]{2,1,0:T(8,128)(2,1)S(1)} %bitcast.37), channel_id=1, source_target_pairs={{1,0},{2,1},{3,2},{4,3},{5,4},{6,5},{7,6},{8,7},{9,8},{10,9},{11,1... | collective-permute-start | bytes 393224 | tf_op jit(solution)/shard_map/ppermute | solution.py:446
  (8 other events, 41.6 us)
Sparse Core Ops, SparseCore 0:
  10.2 96.0 all-gather.2

commit v8 on v6

--- a/solution.py
+++ b/solution.py
@@ -42,15 +42,8 @@
     return jnp.where(lax.axis_index("yh") == lax.axis_index("c"), mine, received)
 
 
-def along_z(piece):
-    return [piece] + [shift(piece, "z", step) for step in (1, 3, 2)]
-
-
-def across(pieces, one, two):
-    base = jnp.stack(pieces)
-    low = shift(jnp.stack(pieces[:2]), two, 1)
-    high = shift(jnp.stack(pieces[2:]), two, 3)
-    return base, shift(base, one, 1), shift(base, one, 3), low, high
+def across(half, end):
+    return half, shift(half, "x", 1), shift(half, "x", 3), shift(half, "y", end)
 
 
 NT = (((1,), (1,)), ((), ()))
@@ -69,15 +62,16 @@
 
 
 def attention_kernel(
-    parity, own, other, gain, base, plus, minus, two_low, two_high,
-    near_out, far_out, held_base, held_plus, held_minus, held_two, normed, queries, values, context, sems
+    parity, own, other, gain, *rest
 ):
+    groups = rest[:8]
+    near_out, far_out, held_base, held_plus, held_minus, held_two, normed, queries, values, context, sems = rest[8:]
+    stacks = (held_base, held_plus, held_minus, held_two)
     copies = [
-        pltpu.make_async_copy(base, held_base, sems.at[0]),
-        pltpu.make_async_copy(minus, held_minus, sems.at[1]),
-        pltpu.make_async_copy(plus, held_plus, sems.at[2]),
-        pltpu.make_async_copy(two_low, held_two.at[0:2], sems.at[3]),
-        pltpu.make_async_copy(two_high, held_two.at[2:4], sems.at[4]),
+        pltpu.make_async_copy(
+            group, stacks[at % 4].at[at // 4 * 2 : at // 4 * 2 + 2], sems.at[at]
+        )
+        for at, group in enumerate(groups)
     ]
     for copy in copies:
         copy.start()
@@ -130,7 +124,7 @@
     far_out[...] = total[count:].astype(BF16)
 
 
-def attention(parity, own, other, gain, base, plus, minus, two_low, two_high):
+def attention(parity, own, other, gain, groups):
     count, width = own.shape
     stack = pltpu.VMEM((4, 2 * HEAD, width), BF16)
     return pl.pallas_call(
@@ -139,7 +133,7 @@
             jax.ShapeDtypeStruct((count, width), F32),
             jax.ShapeDtypeStruct((count, width), BF16),
         ),
-        in_specs=[whole(pltpu.SMEM)] + [whole(pltpu.VMEM)] * 3 + [whole(pl.ANY)] * 5,
+        in_specs=[whole(pltpu.SMEM)] + [whole(pltpu.VMEM)] * 3 + [whole(pl.ANY)] * 8,
         out_specs=(whole(pltpu.VMEM), whole(pltpu.VMEM)),
         scratch_shapes=[stack] * 4
         + [
@@ -147,12 +141,12 @@
             pltpu.VMEM((2 * count, 16 * HEAD), BF16),
             pltpu.VMEM((2 * count, 8 * HEAD), BF16),
             pltpu.VMEM((2 * count, 8 * HEAD), BF16),
-            pltpu.SemaphoreType.DMA((5,)),
+            pltpu.SemaphoreType.DMA((8,)),
         ],
         compiler_params=pltpu.CompilerParams(vmem_limit_bytes=24 * 2**20),
         cost_estimate=pl.CostEstimate(flops=3 * 10**9, bytes_accessed=7 * 10**6, transcendentals=2**20),
         name="attention",
-    )(parity, own, other, gain, base, plus, minus, two_low, two_high)
+    )(parity, own, other, gain, *groups)
 
 
 def mlp_kernel(own, other, gain, weights, near_out, far_out, held, normed, total, sems):
@@ -374,7 +368,9 @@
         [by_head[0], by_head[1], by_head[2], out_heads], axis=1
     ).reshape(4, 2 * HEAD, width)
     attn_piece = type_exchange(attn_all[colour_x], attn_all[colour_x_beside])
-    attn_w = across(along_z(attn_piece), "x", "y")
+    near_half = jnp.stack([attn_piece, shift(attn_piece, "z", 1)])
+    far_half = jnp.stack([shift(attn_piece, "z", 3), shift(attn_piece, "z", 2)])
+    attn_w = across(near_half, 1) + across(far_half, 3)
 
     slice_rows = in_weight.shape[0] // 16
     start = (lax.axis_index("c") * 8 + lax.axis_index(("x", "yl"))) * slice_rows
@@ -408,6 +404,7 @@
         "kg,gpd->kpd", arrange, incoming, preferred_element_type=F32
     ).astype(BF16)
     land = slab_tokens[:, 0, 0] < FAR / 2
+    slab_tokens, _ = lax.optimization_barrier((slab_tokens, far_half))
     tile_tokens = lax.all_to_all(slab_tokens, MP, split_axis=0, concat_axis=0, tiled=True)
     tile_tokens = tile_tokens.reshape(tiles * seg, width)
     other_tokens = swap_cores(tile_tokens)
@@ -418,7 +415,7 @@
         tile_tokens,
         other_tokens,
         ln_gain_one.reshape(1, width),
-        *attn_w,
+        attn_w,
     )
     middle = (near + swap_cores(far).astype(F32)).astype(BF16)
 

time: 166 us -> 166 us (level)
  other arithmetic: 6.68 us -> 2.96 us
  starting transfers between devices: 60.5 us -> 62.8 us
    ppermute x2, waiting for transfers between devices: 13.8 us -> 9.76 us  [shift(): return lax.ppermute(block, ('yl', 'yh'), pairs)]
    ppermute x1, waiting for transfers between devices: 4.74 us -> 8.47 us  [per_device(): guide_low = lax.ppermute(guide_ends[0], AXES, forward)]
    another operation x3 -> x2, other arithmetic: 3.8 us -> 0.1 us  [the longest x1 0.05 us: per_device(): near_half = jnp.stack([attn_piece, shift(attn_piece, 'z', 1)])]
    ppermute x5 -> x7, starting transfers between devices: 10.4 us -> 11.8 us  [shift(): lax.ppermute(block, axis, [((i + step) % count, i) for i in range(count)])]
    unnamed x33 -> x27, local copies, waits for them, and re-layouts: 4.96 us -> 4.25 us
    ppermute x5 -> x7, waiting for transfers between devices: 10.2 us -> 10.7 us  [shift(): lax.ppermute(block, axis, [((i + step) % count, i) for i in range(count)])]
  transfers between devices with their start and end apart: 20 -> 22, of which waited for: 12 -> 10; matrix products, arithmetic and copies ran while one was open for 8% -> 6% of each run, Pallas kernels for 7% -> 7%
where the time goes in v8:
time: 166 us; the launch traced here: 165 us
  starting transfers between devices  62.8 us (38%)
  waiting for transfers between devices  44.5 us (27%)
  Pallas kernels  28.3 us (17%)
  between operations  13.8 us (8%)
  local copies, waits for them, and re-layouts  8.12 us (5%)
  matrix products  4.21 us (3%)
  other arithmetic  2.96 us (2%)
    ppermute x7, starting transfers between devices, shift(): lax.ppermute(block, axis, [((i + step) % count, i) for i in range(count)])  11.8 us
    ppermute x7, waiting for transfers between devices, shift(): lax.ppermute(block, axis, [((i + step) % count, i) for i in range(count)])  10.7 us
    ppermute x2, waiting for transfers between devices, shift(): return lax.ppermute(block, ('yl', 'yh'), pairs)  9.76 us
    pallas_call x1, Pallas kernels, mlp(): pl.pallas_call(mlp_kernel, out_shape=(jax.ShapeDtypeStruct((count, width)...  9.63 us
    all_to_all x1, starting transfers between devices, per_device(): lax.all_to_all(slab_tokens, MP, split_axis=0, concat_axis=0, tiled=True)  8.77 us
    ppermute x1, waiting for transfers between devices, per_device(): guide_low = lax.ppermute(guide_ends[0], AXES, forward)  8.47 us
    pallas_call x1, Pallas kernels, attention(): pl.pallas_call(attention_kernel, out_shape=(jax.ShapeDtypeStruct((count,...  8.45 us
    ppermute x1, starting transfers between devices, per_device(): image_high = lax.ppermute(image, AXES, backward)  8.15 us
  transfers between devices with their start and end apart: 22, of which 10 were waited for; matrix products, arithmetic and copies ran while one was open for 6% of the time, Pallas kernels for 7%

profile of v8, /device:TPU:6, one launch (start us, length us, event | category | flops | bytes accessed | tf_op | source)
XLA Modules:
  0.0 164.7 jit_solution(3930441316862787225)
XLA Ops:
  10.0 4.9 %collective-permute-start = (bf16[128,1024]{1,0:T(8,128)(2,1)S(1)}, bf16[128,1024]{1,0:T(8,128)(2,1)S(1)}, u32[]{:S(2)}, u32[]{:S(2)}) collective-permute-start(bf16[128,1024]{1,0:T(8,128)(2,1)S(1)} %dynamic-slice_bitcast_fusion), channel_id=1, source_target_pairs={{0,68},{64,4},{12,72},{76,8},{1,69},{65,5},{13,73},{77,9},{2,70},{... | collective-permute-start | bytes 786440 | tf_op jit(solution)/shard_map/ppermute | solution.py:41
  15.2 3.6 %collective-permute-done = bf16[128,1024]{1,0:T(8,128)(2,1)S(1)} collective-permute-done((bf16[128,1024]{1,0:T(8,128)(2,1)S(1)}, bf16[128,1024]{1,0:T(8,128)(2,1)S(1)}, u32[]{:S(2)}, u32[]{:S(2)}) %collective-permute-start) | collective-permute-done | bytes 262176 | tf_op jit(solution)/shard_map/ppermute | solution.py:41
  21.0 4.9 %all-to-all-start = ((bf16[16,32,1024]{2,1,0:T(8,128)(2,1)}), bf16[16,32,1024]{2,1,0:T(8,128)(2,1)}, u32[]{:S(2)}, u32[]{:S(2)}) async-start(bf16[16,32,1024]{2,1,0:T(8,128)(2,1)} %copy.31), calls=%async_computation | async-start | bytes 2097152 | tf_op jit(solution)/shard_map/all_to_all | solution.py:402
  25.9 4.0 %collective-permute-start.4 = (bf16[128,1024]{1,0:T(8,128)(2,1)S(1)}, bf16[128,1024]{1,0:T(8,128)(2,1)S(1)}, u32[]{:S(2)}, u32[]{:S(2)}) collective-permute-start(bf16[128,1024]{1,0:T(8,128)(2,1)S(1)} %bitcast_select_fusion), channel_id=1, source_target_pairs={{1,0},{2,1},{3,2},{0,3},{5,4},{6,5},{7,6},{4,7},{9,8},{10,9},{11,1... | collective-permute-start | bytes 786440 | tf_op jit(solution)/shard_map/ppermute | solution.py:25
  31.2 10.7 %collective-permute-done.4 = bf16[128,1024]{1,0:T(8,128)(2,1)S(1)} collective-permute-done((bf16[128,1024]{1,0:T(8,128)(2,1)S(1)}, bf16[128,1024]{1,0:T(8,128)(2,1)S(1)}, u32[]{:S(2)}, u32[]{:S(2)}) %collective-permute-start.4) | collective-permute-done | bytes 262176 | tf_op jit(solution)/shard_map/ppermute | solution.py:25
  42.9 2.4 %collective-permute-start.6 = (bf16[2,128,1024]{2,1,0:T(8,128)(2,1)S(1)}, bf16[2,128,1024]{2,1,0:T(8,128)(2,1)S(1)}, u32[]{:S(2)}, u32[]{:S(2)}) collective-permute-start(bf16[2,128,1024]{2,1,0:T(8,128)(2,1)S(1)} %pad_maximum_fusion.2.rest_0_), channel_id=1, source_target_pairs={{48,0},{0,16},{16,32},{32,48},{49,1},{1,17},{17,33},{33,49},{50,2}... | collective-permute-start | bytes 1572872 | tf_op jit(solution)/shard_map/ppermute | solution.py:25
  45.3 2.1 %convolution_convert_fusion.1 = bf16[8,32,1024]{2,0,1:T(8,128)(2,1)S(1)} fusion(bf16[16,32,1024]{2,1,0:T(8,128)(2,1)} %all-to-all-done, s32[128]{0:T(128)S(1)} %get-tuple-element.42, s32[128]{0:T(128)S(1)} %get-tuple-element.43, pred[128]{0:T(512)(128)(4,1)S(1)} %get-tuple-element.35), kind=kOutput, calls=%fused_computation.1 | convolution fusion | flops 8687744 | bytes 1574016 | tf_op jit(solution)/shard_map/kg,gpd->kpd/dot_general | solution.py:403
  48.5 8.8 %all-to-all-start.1 = ((bf16[8,32,1024]{2,1,0:T(8,128)(2,1)}), bf16[8,32,1024]{2,1,0:T(8,128)(2,1)S(1)}, u32[]{:S(2)}, u32[]{:S(2)}) async-start(bf16[8,32,1024]{2,1,0:T(8,128)(2,1)} %copy.33), calls=%async_computation.1 | async-start | bytes 1048576 | tf_op jit(solution)/shard_map/all_to_all | solution.py:408
  57.3 3.5 %collective-permute-start.7 = (bf16[2,128,1024]{2,1,0:T(8,128)(2,1)S(1)}, bf16[2,128,1024]{2,1,0:T(8,128)(2,1)}, u32[]{:S(2)}, u32[]{:S(2)}) collective-permute-start(bf16[2,128,1024]{2,1,0:T(8,128)(2,1)S(1)} %pad_maximum_fusion.2.rest_0_), channel_id=1, source_target_pairs={{64,0},{4,64},{68,4},{0,68},{65,1},{5,65},{69,5},{1,69},{66,2},{6,... | collective-permute-start | bytes 1572872 | tf_op jit(solution)/shard_map/ppermute | solution.py:23
  60.7 3.2 %collective-permute-start.9 = (bf16[2,128,1024]{2,1,0:T(8,128)(2,1)S(1)}, bf16[2,128,1024]{2,1,0:T(8,128)(2,1)}, u32[]{:S(2)}, u32[]{:S(2)}) collective-permute-start(bf16[2,128,1024]{2,1,0:T(8,128)(2,1)S(1)} %pad_maximum_fusion.1.rest_4_), channel_id=1, source_target_pairs={{48,0},{0,16},{16,32},{32,48},{49,1},{1,17},{17,33},{33,49},{50,2}... | collective-permute-start | bytes 1572872 | tf_op jit(solution)/shard_map/ppermute | solution.py:25
  64.0 5.7 %all-to-all-done.1 = bf16[8,32,1024]{2,1,0:T(8,128)(2,1)S(1)} async-done(((bf16[8,32,1024]{2,1,0:T(8,128)(2,1)}), bf16[8,32,1024]{2,1,0:T(8,128)(2,1)S(1)}, u32[]{:S(2)}, u32[]{:S(2)}) %all-to-all-start.1) | async-done | bytes 524320 | tf_op jit(solution)/shard_map/all_to_all | solution.py:408
  69.7 8.0 %collective-permute-done.7.rest_3_ = bf16[2,128,1024]{2,1,0:T(8,128)(2,1)} collective-permute-done((bf16[2,128,1024]{2,1,0:T(8,128)(2,1)S(1)}, bf16[2,128,1024]{2,1,0:T(8,128)(2,1)}, u32[]{:S(2)}, u32[]{:S(2)}) %collective-permute-start.7) | collective-permute-done | bytes 524320 | tf_op jit(solution)/shard_map/ppermute | solution.py:23
  79.4 8.4 %attention.1 = (f32[256,1024]{1,0:T(8,128)S(1)}, bf16[256,1024]{1,0:T(8,128)(2,1)S(1)}) custom-call(s32[1]{0:T(128)} %bitcast.1.parity, bf16[256,1024]{1,0:T(8,128)(2,1)S(1)} %bitcast.35, bf16[256,1024]{1,0:T(8,128)(2,1)} %collective-permute-done.3.other, f32[1,1024]{1,0:T(1,128)S(1)} %bitcast.39, bf16[2,128,1024]{2,1,0:T(8,128)(2,1)S(1)} %pad_maximum_fusion.2.rest_0_, ...), custom_call_target="tpu_custom_call" | custom-call | flops 3000000000 | bytes 7000000 | tf_op jit(solution)/shard_map/attention/pallas_call | solution.py:130
  90.8 4.6 %all-to-all-start.2 = ((bf16[8,32,1024]{2,1,0:T(8,128)(2,1)}), bf16[8,32,1024]{2,1,0:T(8,128)(2,1)S(1)}, u32[]{:S(2)}, u32[]{:S(2)}) async-start(bf16[8,32,1024]{2,1,0:T(8,128)(2,1)} %bitcast.18), calls=%async_computation.2 | async-start | bytes 1048576 | tf_op jit(solution)/shard_map/all_to_all | solution.py:430
  95.5 3.9 %collective-permute-start.12 = (bf16[3,256,256]{2,1,0:T(8,128)(2,1)S(1)}, bf16[3,256,256]{2,1,0:T(8,128)(2,1)S(1)}, u32[]{:S(2)}, u32[]{:S(2)}) collective-permute-start(bf16[3,256,256]{2,1,0:T(8,128)(2,1)S(1)} %get-tuple-element.24), channel_id=1, source_target_pairs={{0,1},{1,2},{2,3},{3,4},{4,5},{5,6},{6,7},{7,8},{8,9},{9,10},{10,1... | collective-permute-start | bytes 1179656 | tf_op jit(solution)/shard_map/ppermute | solution.py:427
  99.4 6.2 %collective-permute-start.13 = (bf16[3,256,256]{2,1,0:T(8,128)(2,1)S(1)}, bf16[3,256,256]{2,1,0:T(8,128)(2,1)S(1)}, u32[]{:S(2)}, u32[]{:S(2)}) collective-permute-start(bf16[3,256,256]{2,1,0:T(8,128)(2,1)S(1)} %get-tuple-element.25), channel_id=1, source_target_pairs={{1,0},{2,1},{3,2},{4,3},{5,4},{6,5},{7,6},{8,7},{9,8},{10,9},{11,1... | collective-permute-start | bytes 1179656 | tf_op jit(solution)/shard_map/ppermute | solution.py:428
  105.6 8.5 %collective-permute-done.12.guide_low = bf16[3,256,256]{2,1,0:T(8,128)(2,1)S(1)} collective-permute-done((bf16[3,256,256]{2,1,0:T(8,128)(2,1)S(1)}, bf16[3,256,256]{2,1,0:T(8,128)(2,1)S(1)}, u32[]{:S(2)}, u32[]{:S(2)}) %collective-permute-start.12) | collective-permute-done | bytes 393248 | tf_op jit(solution)/shard_map/ppermute | solution.py:427
  114.1 2.0 %collective-permute-done.13.guide_high = bf16[3,256,256]{2,1,0:T(8,128)(2,1)S(1)} collective-permute-done((bf16[3,256,256]{2,1,0:T(8,128)(2,1)S(1)}, bf16[3,256,256]{2,1,0:T(8,128)(2,1)S(1)}, u32[]{:S(2)}, u32[]{:S(2)}) %collective-permute-start.13) | collective-permute-done | bytes 393248 | tf_op jit(solution)/shard_map/ppermute | solution.py:428
  116.1 3.3 %collective-permute-start.14 = (bf16[256,1024]{1,0:T(8,128)(2,1)S(1)}, bf16[256,1024]{1,0:T(8,128)(2,1)S(1)}, u32[]{:S(2)}, u32[]{:S(2)}) collective-permute-start(bf16[256,1024]{1,0:T(8,128)(2,1)S(1)} %bitcast.48), channel_id=1, source_target_pairs={{0,8},{8,0},{1,9},{9,1},{2,10},{10,2},{3,11},{11,3},{4,12},{12,4},... | collective-permute-start | bytes 1572872 | tf_op jit(solution)/shard_map/ppermute | solution.py:29
  121.8 9.6 %mlp.1 = (f32[256,1024]{1,0:T(8,128)}, bf16[256,1024]{1,0:T(8,128)(2,1)}) custom-call(bf16[256,1024]{1,0:T(8,128)(2,1)} %bitcast.49, bf16[256,1024]{1,0:T(8,128)(2,1)} %copy-done.11, f32[1,1024]{1,0:T(1,128)} %bitcast.55, bf16[64,64,1024]{2,1,0:T(8,128)(2,1)} %bitcast.54), custom_call_target="tpu_custom_call" | custom-call | flops 5000000000 | bytes 12000000 | tf_op jit(solution)/shard_map/mlp/pallas_call | solution.py:184
  137.4 8.2 %collective-permute-start.17 = (bf16[2,128,256]{2,1,0:T(8,128)(2,1)S(1)}, bf16[2,128,256]{2,1,0:T(8,128)(2,1)S(1)}, u32[]{:S(2)}, u32[]{:S(2)}) collective-permute-start(bf16[2,128,256]{2,1,0:T(8,128)(2,1)S(1)} %bitcast.37), channel_id=1, source_target_pairs={{1,0},{2,1},{3,2},{4,3},{5,4},{6,5},{7,6},{8,7},{9,8},{10,9},{11,1... | collective-permute-start | bytes 393224 | tf_op jit(solution)/shard_map/ppermute | solution.py:443
  145.6 2.0 %copy-done.2 = bf16[3,3,3,256,256]{4,3,2,1,0:T(8,128)(2,1)S(1)} copy-done((bf16[3,3,3,256,256]{4,3,2,1,0:T(8,128)(2,1)S(1)}, bf16[3,3,3,256,256]{4,3,2,1,0:T(8,128)(2,1)}, u32[]{:S(2)}) %copy-start.2) | copy-done | bytes 3538968
  147.6 3.0 %early.1 = (bf16[4,256,256]{2,1,0:T(8,128)(2,1)S(1)}, f32[4,256,256]{2,1,0:T(8,128)S(1)}, bf16[2,256,256]{2,1,0:T(8,128)(2,1)S(1)}, f32[4,256,256]{2,1,0:T(8,128)S(1)}) custom-call(bf16[2,128,256]{2,1,0:T(8,128)(2,1)S(1)} %bitcast.38, bf16[4,256,256]{2,1,0:T(8,128)(2,1)S(1)} %copy-done.1, bf16[3,3,3,256,256]{4,3,2,1,0:T(8,128)(2,1)S(1)} %copy-done.2, ...), custom_call_target="tpu_custom_call" | custom-call | flops 3000000000 | bytes 4000000 | tf_op jit(solution)/shard_map/early/pallas_call | solution.py:302
  150.6 7.2 %late.1 = bf16[4,256,256]{2,1,0:T(8,128)(2,1)} custom-call(s32[2]{0:T(128)S(1)} %pad_add_fusion.place, bf16[2,128,256]{2,1,0:T(8,128)(2,1)S(1)} %collective-permute-done.16.image_low, bf16[2,128,256]{2,1,0:T(8,128)(2,1)S(1)} %collective-permute-done.17.image_high, bf16[3,256,256]{2,1,0:T(8,128)(2,1)S(1)} %collective-permute-done.12.guide_low, ...), custom_call_target="tpu_custom_call" | custom-call | flops 4000000000 | bytes 6000000 | tf_op jit(solution)/shard_map/late/pallas_call | solution.py:324
  (76 shorter events, 22.2 us)
Async XLA Ops:
  6.5 127.3 %copy-start = (bf16[1024,256]{1,0:T(8,128)(2,1)S(1)}, bf16[1024,256]{1,0:T(8,128)(2,1)}, u32[]{:S(2)}) copy-start(bf16[1024,256]{1,0:T(8,128)(2,1)} %param.20) | copy-start | bytes 1572868
  6.5 114.4 %all-gather.3.cloned.1.call-start = ((), (), s32[]{:S(2)}) async-start(), calls=%async_computation.3 | async-start | bytes 8519680 | tf_op jit(solution)/shard_map/all_gather | solution.py:384
  10.0 8.8 %collective-permute-start = (bf16[128,1024]{1,0:T(8,128)(2,1)S(1)}, bf16[128,1024]{1,0:T(8,128)(2,1)S(1)}, u32[]{:S(2)}, u32[]{:S(2)}) collective-permute-start(bf16[128,1024]{1,0:T(8,128)(2,1)S(1)} %dynamic-slice_bitcast_fusion), channel_id=1, source_target_pairs={{0,68},{64,4},{12,72},{76,8},{1,69},{65,5},{13,73},{77,9},{2,70},{... | collective-permute-start | bytes 786440 | tf_op jit(solution)/shard_map/ppermute | solution.py:41
  21.0 58.5 %copy-start.4 = (f32[1024]{0:T(1024)S(1)}, f32[1024]{0:T(1024)}, u32[]{:S(2)}) copy-start(f32[1024]{0:T(1024)} %param.14) | copy-start | bytes 12292
  21.0 24.3 %all-to-all-start = ((bf16[16,32,1024]{2,1,0:T(8,128)(2,1)}), bf16[16,32,1024]{2,1,0:T(8,128)(2,1)}, u32[]{:S(2)}, u32[]{:S(2)}) async-start(bf16[16,32,1024]{2,1,0:T(8,128)(2,1)} %copy.31), calls=%async_computation | async-start | bytes 2097152 | tf_op jit(solution)/shard_map/all_to_all | solution.py:402
  25.9 16.0 %collective-permute-start.4 = (bf16[128,1024]{1,0:T(8,128)(2,1)S(1)}, bf16[128,1024]{1,0:T(8,128)(2,1)S(1)}, u32[]{:S(2)}, u32[]{:S(2)}) collective-permute-start(bf16[128,1024]{1,0:T(8,128)(2,1)S(1)} %bitcast_select_fusion), channel_id=1, source_target_pairs={{1,0},{2,1},{3,2},{0,3},{5,4},{6,5},{7,6},{4,7},{9,8},{10,9},{11,1... | collective-permute-start | bytes 786440 | tf_op jit(solution)/shard_map/ppermute | solution.py:25
  29.9 15.3 %collective-permute-start.2 = (bf16[128,1024]{1,0:T(8,128)(2,1)S(1)}, bf16[128,1024]{1,0:T(8,128)(2,1)S(1)}, u32[]{:S(2)}, u32[]{:S(2)}) collective-permute-start(bf16[128,1024]{1,0:T(8,128)(2,1)S(1)} %bitcast_select_fusion), channel_id=1, source_target_pairs={{2,0},{3,1},{0,2},{1,3},{6,4},{7,5},{4,6},{5,7},{10,8},{11,9},{8,1... | collective-permute-start | bytes 786440 | tf_op jit(solution)/shard_map/ppermute | solution.py:25
  29.9 15.3 %collective-permute-start.1 = (bf16[128,1024]{1,0:T(8,128)(2,1)S(1)}, bf16[128,1024]{1,0:T(8,128)(2,1)S(1)}, u32[]{:S(2)}, u32[]{:S(2)}) collective-permute-start(bf16[128,1024]{1,0:T(8,128)(2,1)S(1)} %bitcast_select_fusion), channel_id=1, source_target_pairs={{3,0},{0,1},{1,2},{2,3},{7,4},{4,5},{5,6},{6,7},{11,8},{8,9},{9,10... | collective-permute-start | bytes 786440 | tf_op jit(solution)/shard_map/ppermute | solution.py:25
  41.9 22.0 %collective-permute-start.5 = (bf16[2,128,1024]{2,1,0:T(8,128)(2,1)S(1)}, bf16[2,128,1024]{2,1,0:T(8,128)(2,1)S(1)}, u32[]{:S(2)}, u32[]{:S(2)}) collective-permute-start(bf16[2,128,1024]{2,1,0:T(8,128)(2,1)S(1)} %pad_maximum_fusion.2.rest_0_), channel_id=1, source_target_pairs={{16,0},{32,16},{48,32},{0,48},{17,1},{33,17},{49,33},{1,49},{18,2}... | collective-permute-start | bytes 1572872 | tf_op jit(solution)/shard_map/ppermute | solution.py:25
  42.9 21.1 %collective-permute-start.6 = (bf16[2,128,1024]{2,1,0:T(8,128)(2,1)S(1)}, bf16[2,128,1024]{2,1,0:T(8,128)(2,1)S(1)}, u32[]{:S(2)}, u32[]{:S(2)}) collective-permute-start(bf16[2,128,1024]{2,1,0:T(8,128)(2,1)S(1)} %pad_maximum_fusion.2.rest_0_), channel_id=1, source_target_pairs={{48,0},{0,16},{16,32},{32,48},{49,1},{1,17},{17,33},{33,49},{50,2}... | collective-permute-start | bytes 1572872 | tf_op jit(solution)/shard_map/ppermute | solution.py:25
  48.5 21.1 %all-to-all-start.1 = ((bf16[8,32,1024]{2,1,0:T(8,128)(2,1)}), bf16[8,32,1024]{2,1,0:T(8,128)(2,1)S(1)}, u32[]{:S(2)}, u32[]{:S(2)}) async-start(bf16[8,32,1024]{2,1,0:T(8,128)(2,1)} %copy.33), calls=%async_computation.1 | async-start | bytes 1048576 | tf_op jit(solution)/shard_map/all_to_all | solution.py:408
  57.3 20.4 %collective-permute-start.7 = (bf16[2,128,1024]{2,1,0:T(8,128)(2,1)S(1)}, bf16[2,128,1024]{2,1,0:T(8,128)(2,1)}, u32[]{:S(2)}, u32[]{:S(2)}) collective-permute-start(bf16[2,128,1024]{2,1,0:T(8,128)(2,1)S(1)} %pad_maximum_fusion.2.rest_0_), channel_id=1, source_target_pairs={{64,0},{4,64},{68,4},{0,68},{65,1},{5,65},{69,5},{1,69},{66,2},{6,... | collective-permute-start | bytes 1572872 | tf_op jit(solution)/shard_map/ppermute | solution.py:23
  60.7 16.9 %collective-permute-start.8 = (bf16[2,128,1024]{2,1,0:T(8,128)(2,1)S(1)}, bf16[2,128,1024]{2,1,0:T(8,128)(2,1)}, u32[]{:S(2)}, u32[]{:S(2)}) collective-permute-start(bf16[2,128,1024]{2,1,0:T(8,128)(2,1)S(1)} %pad_maximum_fusion.1.rest_4_), channel_id=1, source_target_pairs={{16,0},{32,16},{48,32},{0,48},{17,1},{33,17},{49,33},{1,49},{18,2}... | collective-permute-start | bytes 1572872 | tf_op jit(solution)/shard_map/ppermute | solution.py:25
  60.7 16.9 %collective-permute-start.9 = (bf16[2,128,1024]{2,1,0:T(8,128)(2,1)S(1)}, bf16[2,128,1024]{2,1,0:T(8,128)(2,1)}, u32[]{:S(2)}, u32[]{:S(2)}) collective-permute-start(bf16[2,128,1024]{2,1,0:T(8,128)(2,1)S(1)} %pad_maximum_fusion.1.rest_4_), channel_id=1, source_target_pairs={{48,0},{0,16},{16,32},{32,48},{49,1},{1,17},{17,33},{33,49},{50,2}... | collective-permute-start | bytes 1572872 | tf_op jit(solution)/shard_map/ppermute | solution.py:25
  64.0 15.4 %collective-permute-start.10 = (bf16[2,128,1024]{2,1,0:T(8,128)(2,1)S(1)}, bf16[2,128,1024]{2,1,0:T(8,128)(2,1)}, u32[]{:S(2)}, u32[]{:S(2)}) collective-permute-start(bf16[2,128,1024]{2,1,0:T(8,128)(2,1)S(1)} %pad_maximum_fusion.1.rest_4_), channel_id=1, source_target_pairs={{68,0},{0,64},{64,4},{4,68},{69,1},{1,65},{65,5},{5,69},{70,2},{2,... | collective-permute-start | bytes 1572872 | tf_op jit(solution)/shard_map/ppermute | solution.py:23
  69.6 9.8 %collective-permute-start.3 = (bf16[256,1024]{1,0:T(8,128)(2,1)S(1)}, bf16[256,1024]{1,0:T(8,128)(2,1)}, u32[]{:S(2)}, u32[]{:S(2)}) collective-permute-start(bf16[256,1024]{1,0:T(8,128)(2,1)S(1)} %bitcast.34), channel_id=1, source_target_pairs={{0,8},{8,0},{1,9},{9,1},{2,10},{10,2},{3,11},{11,3},{4,12},{12,4},... | collective-permute-start | bytes 1572872 | tf_op jit(solution)/shard_map/ppermute | solution.py:29
  87.9 2.0 %collective-permute-start.11 = (bf16[256,1024]{1,0:T(8,128)(2,1)S(1)}, bf16[256,1024]{1,0:T(8,128)(2,1)S(1)}, u32[]{:S(2)}, u32[]{:S(2)}) collective-permute-start(bf16[256,1024]{1,0:T(8,128)(2,1)S(1)} %get-tuple-element.23), channel_id=1, source_target_pairs={{0,8},{8,0},{1,9},{9,1},{2,10},{10,2},{3,11},{11,3},{4,12},{12,4},... | collective-permute-start | bytes 1572872 | tf_op jit(solution)/shard_map/ppermute | solution.py:29
  90.8 25.3 %all-to-all-start.2 = ((bf16[8,32,1024]{2,1,0:T(8,128)(2,1)}), bf16[8,32,1024]{2,1,0:T(8,128)(2,1)S(1)}, u32[]{:S(2)}, u32[]{:S(2)}) async-start(bf16[8,32,1024]{2,1,0:T(8,128)(2,1)} %bitcast.18), calls=%async_computation.2 | async-start | bytes 1048576 | tf_op jit(solution)/shard_map/all_to_all | solution.py:430
  95.5 18.6 %collective-permute-start.12 = (bf16[3,256,256]{2,1,0:T(8,128)(2,1)S(1)}, bf16[3,256,256]{2,1,0:T(8,128)(2,1)S(1)}, u32[]{:S(2)}, u32[]{:S(2)}) collective-permute-start(bf16[3,256,256]{2,1,0:T(8,128)(2,1)S(1)} %get-tuple-element.24), channel_id=1, source_target_pairs={{0,1},{1,2},{2,3},{3,4},{4,5},{5,6},{6,7},{7,8},{8,9},{9,10},{10,1... | collective-permute-start | bytes 1179656 | tf_op jit(solution)/shard_map/ppermute | solution.py:427
  99.4 16.7 %collective-permute-start.13 = (bf16[3,256,256]{2,1,0:T(8,128)(2,1)S(1)}, bf16[3,256,256]{2,1,0:T(8,128)(2,1)S(1)}, u32[]{:S(2)}, u32[]{:S(2)}) collective-permute-start(bf16[3,256,256]{2,1,0:T(8,128)(2,1)S(1)} %get-tuple-element.25), channel_id=1, source_target_pairs={{1,0},{2,1},{3,2},{4,3},{5,4},{6,5},{7,6},{8,7},{9,8},{10,9},{11,1... | collective-permute-start | bytes 1179656 | tf_op jit(solution)/shard_map/ppermute | solution.py:428
  116.1 4.9 %collective-permute-start.14 = (bf16[256,1024]{1,0:T(8,128)(2,1)S(1)}, bf16[256,1024]{1,0:T(8,128)(2,1)S(1)}, u32[]{:S(2)}, u32[]{:S(2)}) collective-permute-start(bf16[256,1024]{1,0:T(8,128)(2,1)S(1)} %bitcast.48), channel_id=1, source_target_pairs={{0,8},{8,0},{1,9},{9,1},{2,10},{10,2},{3,11},{11,3},{4,12},{12,4},... | collective-permute-start | bytes 1572872 | tf_op jit(solution)/shard_map/ppermute | solution.py:29
  131.4 2.4 %collective-permute-start.15 = (bf16[256,1024]{1,0:T(8,128)(2,1)}, bf16[256,1024]{1,0:T(8,128)(2,1)S(1)}, u32[]{:S(2)}, u32[]{:S(2)}) collective-permute-start(bf16[256,1024]{1,0:T(8,128)(2,1)} %get-tuple-element.28), channel_id=1, source_target_pairs={{0,8},{8,0},{1,9},{9,1},{2,10},{10,2},{3,11},{11,3},{4,12},{12,4},... | collective-permute-start | bytes 1572872 | tf_op jit(solution)/shard_map/ppermute | solution.py:29
  135.5 15.1 %collective-permute-start.16 = (bf16[2,128,256]{2,1,0:T(8,128)(2,1)S(1)}, bf16[2,128,256]{2,1,0:T(8,128)(2,1)S(1)}, u32[]{:S(2)}, u32[]{:S(2)}) collective-permute-start(bf16[2,128,256]{2,1,0:T(8,128)(2,1)S(1)} %bitcast.36), channel_id=1, source_target_pairs={{0,1},{1,2},{2,3},{3,4},{4,5},{5,6},{6,7},{7,8},{8,9},{9,10},{10,1... | collective-permute-start | bytes 393224 | tf_op jit(solution)/shard_map/ppermute | solution.py:442
  137.4 13.2 %collective-permute-start.17 = (bf16[2,128,256]{2,1,0:T(8,128)(2,1)S(1)}, bf16[2,128,256]{2,1,0:T(8,128)(2,1)S(1)}, u32[]{:S(2)}, u32[]{:S(2)}) collective-permute-start(bf16[2,128,256]{2,1,0:T(8,128)(2,1)S(1)} %bitcast.37), channel_id=1, source_target_pairs={{1,0},{2,1},{3,2},{4,3},{5,4},{6,5},{7,6},{8,7},{9,8},{10,9},{11,1... | collective-permute-start | bytes 393224 | tf_op jit(solution)/shard_map/ppermute | solution.py:443
  (11 other events, 62.5 us)
Sparse Core Ops, SparseCore 0:
  10.2 102.4 all-gather.2

commit v9 on v8

--- a/solution.py
+++ b/solution.py
@@ -372,8 +372,8 @@
     far_half = jnp.stack([shift(attn_piece, "z", 3), shift(attn_piece, "z", 2)])
     attn_w = across(near_half, 1) + across(far_half, 3)
 
-    slice_rows = in_weight.shape[0] // 16
-    start = (lax.axis_index("c") * 8 + lax.axis_index(("x", "yl"))) * slice_rows
+    slice_rows = in_weight.shape[0] // 4
+    start = (lax.axis_index("c") * 2 + lax.axis_index("yl")) * slice_rows
     mlp_own = jnp.concatenate(
         [
             lax.dynamic_slice_in_dim(in_weight, start, slice_rows, 0),
@@ -381,7 +381,7 @@
         ],
         axis=0,
     )
-    mlp_w = lax.all_gather(mlp_own, ("x", "yh", "yl", "z"), axis=0, tiled=False)
+    mlp_w = lax.all_gather(mlp_own, ("yh", "yl", "z"), axis=0, tiled=False)
 
     slab_all = placement // tiles
     column_all = placement % tiles

time: 166 us -> 179 us (1.078)
  waiting for transfers between devices: 44.5 us -> 56.3 us
  starting transfers between devices: 62.8 us -> 64.6 us
    ppermute x2, waiting for transfers between devices: 9.76 us -> 18.3 us  [shift(): return lax.ppermute(block, ('yl', 'yh'), pairs)]
    all_to_all x1, waiting for transfers between devices: 5.65 us -> 10.4 us  [per_device(): lax.all_to_all(slab_tokens, MP, split_axis=0, concat_axis=0, tiled=True)]
    ppermute x1, waiting for transfers between devices: 8.47 us -> 4.74 us  [per_device(): guide_low = lax.ppermute(guide_ends[0], AXES, forward)]
    all_to_all x1, starting transfers between devices: 4.62 us -> 7.32 us  [per_device(): lax.all_to_all(middle.reshape(tiles, seg, width), MP, split_axis=0, conca...]
    ppermute x7, waiting for transfers between devices: 10.7 us -> 13.1 us  [shift(): lax.ppermute(block, axis, [((i + step) % count, i) for i in range(count)])]
  transfers between devices with their start and end apart: 22 -> 22, of which waited for: 10 -> 11; matrix products, arithmetic and copies ran while one was open for 6% -> 5% of each run, Pallas kernels for 7% -> 6%
where the time goes in v9:
time: 179 us
  starting transfers between devices  64.6 us (36%)
  waiting for transfers between devices  56.3 us (31%)
  Pallas kernels  28.3 us (16%)
  between operations  13.8 us (8%)
  local copies, waits for them, and re-layouts  8.31 us (5%)
  matrix products  4.21 us (2%)
  other arithmetic  3.12 us (2%)
    ppermute x2, waiting for transfers between devices, shift(): return lax.ppermute(block, ('yl', 'yh'), pairs)  18.3 us
    ppermute x7, waiting for transfers between devices, shift(): lax.ppermute(block, axis, [((i + step) % count, i) for i in range(count)])  13.1 us
    ppermute x7, starting transfers between devices, shift(): lax.ppermute(block, axis, [((i + step) % count, i) for i in range(count)])  11.8 us
    all_to_all x1, waiting for transfers between devices, per_device(): lax.all_to_all(slab_tokens, MP, split_axis=0, concat_axis=0, tiled=True)  10.4 us
    pallas_call x1, Pallas kernels, mlp(): pl.pallas_call(mlp_kernel, out_shape=(jax.ShapeDtypeStruct((count, width)...  9.62 us
    pallas_call x1, Pallas kernels, attention(): pl.pallas_call(attention_kernel, out_shape=(jax.ShapeDtypeStruct((count,...  8.46 us
    ppermute x1, starting transfers between devices, per_device(): image_high = lax.ppermute(image, AXES, backward)  8.15 us
    all_to_all x1, starting transfers between devices, per_device(): lax.all_to_all(slab_tokens, MP, split_axis=0, concat_axis=0, tiled=True)  7.96 us
  transfers between devices with their start and end apart: 22, of which 11 were waited for; matrix products, arithmetic and copies ran while one was open for 5% of the time, Pallas kernels for 6%

profile of v9, /device:TPU:6, one launch (start us, length us, event | category | flops | bytes accessed | tf_op | source)
XLA Modules:
  0.0 178.6 jit_solution(13252022873728698698)
XLA Ops:
  10.3 4.9 %collective-permute-start = (bf16[128,1024]{1,0:T(8,128)(2,1)S(1)}, bf16[128,1024]{1,0:T(8,128)(2,1)S(1)}, u32[]{:S(2)}, u32[]{:S(2)}) collective-permute-start(bf16[128,1024]{1,0:T(8,128)(2,1)S(1)} %dynamic-slice_bitcast_fusion), channel_id=1, source_target_pairs={{0,68},{64,4},{12,72},{76,8},{1,69},{65,5},{13,73},{77,9},{2,70},{... | collective-permute-start | bytes 786440 | tf_op jit(solution)/shard_map/ppermute | solution.py:41
  15.6 3.6 %collective-permute-done = bf16[128,1024]{1,0:T(8,128)(2,1)S(1)} collective-permute-done((bf16[128,1024]{1,0:T(8,128)(2,1)S(1)}, bf16[128,1024]{1,0:T(8,128)(2,1)S(1)}, u32[]{:S(2)}, u32[]{:S(2)}) %collective-permute-start) | collective-permute-done | bytes 262176 | tf_op jit(solution)/shard_map/ppermute | solution.py:41
  21.3 4.9 %all-to-all-start = ((bf16[16,32,1024]{2,1,0:T(8,128)(2,1)}), bf16[16,32,1024]{2,1,0:T(8,128)(2,1)}, u32[]{:S(2)}, u32[]{:S(2)}) async-start(bf16[16,32,1024]{2,1,0:T(8,128)(2,1)} %copy.31), calls=%async_computation | async-start | bytes 2097152 | tf_op jit(solution)/shard_map/all_to_all | solution.py:402
  26.2 4.0 %collective-permute-start.4 = (bf16[128,1024]{1,0:T(8,128)(2,1)S(1)}, bf16[128,1024]{1,0:T(8,128)(2,1)S(1)}, u32[]{:S(2)}, u32[]{:S(2)}) collective-permute-start(bf16[128,1024]{1,0:T(8,128)(2,1)S(1)} %bitcast_select_fusion), channel_id=1, source_target_pairs={{1,0},{2,1},{3,2},{0,3},{5,4},{6,5},{7,6},{4,7},{9,8},{10,9},{11,1... | collective-permute-start | bytes 786440 | tf_op jit(solution)/shard_map/ppermute | solution.py:25
  31.5 7.8 %collective-permute-done.4 = bf16[128,1024]{1,0:T(8,128)(2,1)S(1)} collective-permute-done((bf16[128,1024]{1,0:T(8,128)(2,1)S(1)}, bf16[128,1024]{1,0:T(8,128)(2,1)S(1)}, u32[]{:S(2)}, u32[]{:S(2)}) %collective-permute-start.4) | collective-permute-done | bytes 262176 | tf_op jit(solution)/shard_map/ppermute | solution.py:25
  40.2 2.5 %collective-permute-start.6 = (bf16[2,128,1024]{2,1,0:T(8,128)(2,1)S(1)}, bf16[2,128,1024]{2,1,0:T(8,128)(2,1)S(1)}, u32[]{:S(2)}, u32[]{:S(2)}) collective-permute-start(bf16[2,128,1024]{2,1,0:T(8,128)(2,1)S(1)} %pad_maximum_fusion.2.rest_0_), channel_id=1, source_target_pairs={{48,0},{0,16},{16,32},{32,48},{49,1},{1,17},{17,33},{33,49},{50,2}... | collective-permute-start | bytes 1572872 | tf_op jit(solution)/shard_map/ppermute | solution.py:25
  42.7 5.2 %collective-permute-done.1 = bf16[128,1024]{1,0:T(8,128)(2,1)S(1)} collective-permute-done((bf16[128,1024]{1,0:T(8,128)(2,1)S(1)}, bf16[128,1024]{1,0:T(8,128)(2,1)S(1)}, u32[]{:S(2)}, u32[]{:S(2)}) %collective-permute-start.1) | collective-permute-done | bytes 262176 | tf_op jit(solution)/shard_map/ppermute | solution.py:25
  48.0 2.1 %convolution_convert_fusion.1 = bf16[8,32,1024]{2,0,1:T(8,128)(2,1)S(1)} fusion(bf16[16,32,1024]{2,1,0:T(8,128)(2,1)} %all-to-all-done, s32[128]{0:T(128)S(1)} %get-tuple-element.42, s32[128]{0:T(128)S(1)} %get-tuple-element.43, pred[128]{0:T(512)(128)(4,1)S(1)} %get-tuple-element.35), kind=kOutput, calls=%fused_computation.1 | convolution fusion | flops 8687744 | bytes 1574016 | tf_op jit(solution)/shard_map/kg,gpd->kpd/dot_general | solution.py:403
  51.2 8.0 %all-to-all-start.1 = ((bf16[8,32,1024]{2,1,0:T(8,128)(2,1)}), bf16[8,32,1024]{2,1,0:T(8,128)(2,1)S(1)}, u32[]{:S(2)}, u32[]{:S(2)}) async-start(bf16[8,32,1024]{2,1,0:T(8,128)(2,1)} %copy.33), calls=%async_computation.1 | async-start | bytes 1048576 | tf_op jit(solution)/shard_map/all_to_all | solution.py:408
  59.2 2.9 %collective-permute-start.7 = (bf16[2,128,1024]{2,1,0:T(8,128)(2,1)S(1)}, bf16[2,128,1024]{2,1,0:T(8,128)(2,1)}, u32[]{:S(2)}, u32[]{:S(2)}) collective-permute-start(bf16[2,128,1024]{2,1,0:T(8,128)(2,1)S(1)} %pad_maximum_fusion.2.rest_0_), channel_id=1, source_target_pairs={{64,0},{4,64},{68,4},{0,68},{65,1},{5,65},{69,5},{1,69},{66,2},{6,... | collective-permute-start | bytes 1572872 | tf_op jit(solution)/shard_map/ppermute | solution.py:23
  62.0 3.2 %collective-permute-start.9 = (bf16[2,128,1024]{2,1,0:T(8,128)(2,1)S(1)}, bf16[2,128,1024]{2,1,0:T(8,128)(2,1)}, u32[]{:S(2)}, u32[]{:S(2)}) collective-permute-start(bf16[2,128,1024]{2,1,0:T(8,128)(2,1)S(1)} %pad_maximum_fusion.1.rest_4_), channel_id=1, source_target_pairs={{48,0},{0,16},{16,32},{32,48},{49,1},{1,17},{17,33},{33,49},{50,2}... | collective-permute-start | bytes 1572872 | tf_op jit(solution)/shard_map/ppermute | solution.py:25
  65.3 10.4 %all-to-all-done.1 = bf16[8,32,1024]{2,1,0:T(8,128)(2,1)S(1)} async-done(((bf16[8,32,1024]{2,1,0:T(8,128)(2,1)}), bf16[8,32,1024]{2,1,0:T(8,128)(2,1)S(1)}, u32[]{:S(2)}, u32[]{:S(2)}) %all-to-all-start.1) | async-done | bytes 524320 | tf_op jit(solution)/shard_map/all_to_all | solution.py:408
  75.6 17.8 %collective-permute-done.7.rest_3_ = bf16[2,128,1024]{2,1,0:T(8,128)(2,1)} collective-permute-done((bf16[2,128,1024]{2,1,0:T(8,128)(2,1)S(1)}, bf16[2,128,1024]{2,1,0:T(8,128)(2,1)}, u32[]{:S(2)}, u32[]{:S(2)}) %collective-permute-start.7) | collective-permute-done | bytes 524320 | tf_op jit(solution)/shard_map/ppermute | solution.py:23
  93.9 8.5 %attention.1 = (f32[256,1024]{1,0:T(8,128)S(1)}, bf16[256,1024]{1,0:T(8,128)(2,1)S(1)}) custom-call(s32[1]{0:T(128)} %bitcast.1.parity, bf16[256,1024]{1,0:T(8,128)(2,1)S(1)} %bitcast.35, bf16[256,1024]{1,0:T(8,128)(2,1)} %collective-permute-done.3.other, f32[1,1024]{1,0:T(1,128)S(1)} %bitcast.39, bf16[2,128,1024]{2,1,0:T(8,128)(2,1)S(1)} %pad_maximum_fusion.2.rest_0_, ...), custom_call_target="tpu_custom_call" | custom-call | flops 3000000000 | bytes 7000000 | tf_op jit(solution)/shard_map/attention/pallas_call | solution.py:130
  105.3 7.3 %all-to-all-start.2 = ((bf16[8,32,1024]{2,1,0:T(8,128)(2,1)}), bf16[8,32,1024]{2,1,0:T(8,128)(2,1)S(1)}, u32[]{:S(2)}, u32[]{:S(2)}) async-start(bf16[8,32,1024]{2,1,0:T(8,128)(2,1)} %bitcast.18), calls=%async_computation.2 | async-start | bytes 1048576 | tf_op jit(solution)/shard_map/all_to_all | solution.py:430
  112.7 3.9 %collective-permute-start.12 = (bf16[3,256,256]{2,1,0:T(8,128)(2,1)S(1)}, bf16[3,256,256]{2,1,0:T(8,128)(2,1)S(1)}, u32[]{:S(2)}, u32[]{:S(2)}) collective-permute-start(bf16[3,256,256]{2,1,0:T(8,128)(2,1)S(1)} %get-tuple-element.24), channel_id=1, source_target_pairs={{0,1},{1,2},{2,3},{3,4},{4,5},{5,6},{6,7},{7,8},{8,9},{9,10},{10,1... | collective-permute-start | bytes 1179656 | tf_op jit(solution)/shard_map/ppermute | solution.py:427
  116.7 6.2 %collective-permute-start.13 = (bf16[3,256,256]{2,1,0:T(8,128)(2,1)S(1)}, bf16[3,256,256]{2,1,0:T(8,128)(2,1)S(1)}, u32[]{:S(2)}, u32[]{:S(2)}) collective-permute-start(bf16[3,256,256]{2,1,0:T(8,128)(2,1)S(1)} %get-tuple-element.25), channel_id=1, source_target_pairs={{1,0},{2,1},{3,2},{4,3},{5,4},{6,5},{7,6},{8,7},{9,8},{10,9},{11,1... | collective-permute-start | bytes 1179656 | tf_op jit(solution)/shard_map/ppermute | solution.py:428
  122.8 4.7 %collective-permute-done.12.guide_low = bf16[3,256,256]{2,1,0:T(8,128)(2,1)S(1)} collective-permute-done((bf16[3,256,256]{2,1,0:T(8,128)(2,1)S(1)}, bf16[3,256,256]{2,1,0:T(8,128)(2,1)S(1)}, u32[]{:S(2)}, u32[]{:S(2)}) %collective-permute-start.12) | collective-permute-done | bytes 393248 | tf_op jit(solution)/shard_map/ppermute | solution.py:427
  129.5 3.8 %collective-permute-start.14 = (bf16[256,1024]{1,0:T(8,128)(2,1)S(1)}, bf16[256,1024]{1,0:T(8,128)(2,1)S(1)}, u32[]{:S(2)}, u32[]{:S(2)}) collective-permute-start(bf16[256,1024]{1,0:T(8,128)(2,1)S(1)} %bitcast.48), channel_id=1, source_target_pairs={{0,8},{8,0},{1,9},{9,1},{2,10},{10,2},{3,11},{11,3},{4,12},{12,4},... | collective-permute-start | bytes 1572872 | tf_op jit(solution)/shard_map/ppermute | solution.py:29
  135.7 9.6 %mlp.1 = (f32[256,1024]{1,0:T(8,128)}, bf16[256,1024]{1,0:T(8,128)(2,1)}) custom-call(bf16[256,1024]{1,0:T(8,128)(2,1)} %bitcast.49, bf16[256,1024]{1,0:T(8,128)(2,1)} %copy-done.11, f32[1,1024]{1,0:T(1,128)} %bitcast.55, bf16[16,256,1024]{2,1,0:T(8,128)(2,1)} %bitcast.54), custom_call_target="tpu_custom_call" | custom-call | flops 5000000000 | bytes 12000000 | tf_op jit(solution)/shard_map/mlp/pallas_call | solution.py:184
  151.3 8.2 %collective-permute-start.17 = (bf16[2,128,256]{2,1,0:T(8,128)(2,1)S(1)}, bf16[2,128,256]{2,1,0:T(8,128)(2,1)S(1)}, u32[]{:S(2)}, u32[]{:S(2)}) collective-permute-start(bf16[2,128,256]{2,1,0:T(8,128)(2,1)S(1)} %bitcast.37), channel_id=1, source_target_pairs={{1,0},{2,1},{3,2},{4,3},{5,4},{6,5},{7,6},{8,7},{9,8},{10,9},{11,1... | collective-permute-start | bytes 393224 | tf_op jit(solution)/shard_map/ppermute | solution.py:443
  159.5 2.0 %copy-done.2 = bf16[3,3,3,256,256]{4,3,2,1,0:T(8,128)(2,1)S(1)} copy-done((bf16[3,3,3,256,256]{4,3,2,1,0:T(8,128)(2,1)S(1)}, bf16[3,3,3,256,256]{4,3,2,1,0:T(8,128)(2,1)}, u32[]{:S(2)}) %copy-start.2) | copy-done | bytes 3538968
  161.5 3.0 %early.1 = (bf16[4,256,256]{2,1,0:T(8,128)(2,1)S(1)}, f32[4,256,256]{2,1,0:T(8,128)S(1)}, bf16[2,256,256]{2,1,0:T(8,128)(2,1)S(1)}, f32[4,256,256]{2,1,0:T(8,128)S(1)}) custom-call(bf16[2,128,256]{2,1,0:T(8,128)(2,1)S(1)} %bitcast.38, bf16[4,256,256]{2,1,0:T(8,128)(2,1)S(1)} %copy-done.1, bf16[3,3,3,256,256]{4,3,2,1,0:T(8,128)(2,1)S(1)} %copy-done.2, ...), custom_call_target="tpu_custom_call" | custom-call | flops 3000000000 | bytes 4000000 | tf_op jit(solution)/shard_map/early/pallas_call | solution.py:302
  164.5 7.2 %late.1 = bf16[4,256,256]{2,1,0:T(8,128)(2,1)} custom-call(s32[2]{0:T(128)S(1)} %pad_add_fusion.place, bf16[2,128,256]{2,1,0:T(8,128)(2,1)S(1)} %collective-permute-done.16.image_low, bf16[2,128,256]{2,1,0:T(8,128)(2,1)S(1)} %collective-permute-done.17.image_high, bf16[3,256,256]{2,1,0:T(8,128)(2,1)S(1)} %collective-permute-done.12.guide_low, ...), custom_call_target="tpu_custom_call" | custom-call | flops 4000000000 | bytes 6000000 | tf_op jit(solution)/shard_map/late/pallas_call | solution.py:324
  (76 shorter events, 23.0 us)
Async XLA Ops:
  6.5 141.2 %copy-start = (bf16[1024,256]{1,0:T(8,128)(2,1)S(1)}, bf16[1024,256]{1,0:T(8,128)(2,1)}, u32[]{:S(2)}) copy-start(bf16[1024,256]{1,0:T(8,128)(2,1)} %param.20) | copy-start | bytes 1572868
  6.5 128.3 %all-gather.3.cloned.1.call-start = ((), (), s32[]{:S(2)}) async-start(), calls=%async_computation.3 | async-start | bytes 8912896 | tf_op jit(solution)/shard_map/all_gather | solution.py:384
  10.3 8.8 %collective-permute-start = (bf16[128,1024]{1,0:T(8,128)(2,1)S(1)}, bf16[128,1024]{1,0:T(8,128)(2,1)S(1)}, u32[]{:S(2)}, u32[]{:S(2)}) collective-permute-start(bf16[128,1024]{1,0:T(8,128)(2,1)S(1)} %dynamic-slice_bitcast_fusion), channel_id=1, source_target_pairs={{0,68},{64,4},{12,72},{76,8},{1,69},{65,5},{13,73},{77,9},{2,70},{... | collective-permute-start | bytes 786440 | tf_op jit(solution)/shard_map/ppermute | solution.py:41
  21.3 72.6 %copy-start.4 = (f32[1024]{0:T(1024)S(1)}, f32[1024]{0:T(1024)}, u32[]{:S(2)}) copy-start(f32[1024]{0:T(1024)} %param.14) | copy-start | bytes 12292
  21.3 26.7 %all-to-all-start = ((bf16[16,32,1024]{2,1,0:T(8,128)(2,1)}), bf16[16,32,1024]{2,1,0:T(8,128)(2,1)}, u32[]{:S(2)}, u32[]{:S(2)}) async-start(bf16[16,32,1024]{2,1,0:T(8,128)(2,1)} %copy.31), calls=%async_computation | async-start | bytes 2097152 | tf_op jit(solution)/shard_map/all_to_all | solution.py:402
  26.2 13.1 %collective-permute-start.4 = (bf16[128,1024]{1,0:T(8,128)(2,1)S(1)}, bf16[128,1024]{1,0:T(8,128)(2,1)S(1)}, u32[]{:S(2)}, u32[]{:S(2)}) collective-permute-start(bf16[128,1024]{1,0:T(8,128)(2,1)S(1)} %bitcast_select_fusion), channel_id=1, source_target_pairs={{1,0},{2,1},{3,2},{0,3},{5,4},{6,5},{7,6},{4,7},{9,8},{10,9},{11,1... | collective-permute-start | bytes 786440 | tf_op jit(solution)/shard_map/ppermute | solution.py:25
  30.3 12.5 %collective-permute-start.2 = (bf16[128,1024]{1,0:T(8,128)(2,1)S(1)}, bf16[128,1024]{1,0:T(8,128)(2,1)S(1)}, u32[]{:S(2)}, u32[]{:S(2)}) collective-permute-start(bf16[128,1024]{1,0:T(8,128)(2,1)S(1)} %bitcast_select_fusion), channel_id=1, source_target_pairs={{2,0},{3,1},{0,2},{1,3},{6,4},{7,5},{4,6},{5,7},{10,8},{11,9},{8,1... | collective-permute-start | bytes 786440 | tf_op jit(solution)/shard_map/ppermute | solution.py:25
  30.3 17.7 %collective-permute-start.1 = (bf16[128,1024]{1,0:T(8,128)(2,1)S(1)}, bf16[128,1024]{1,0:T(8,128)(2,1)S(1)}, u32[]{:S(2)}, u32[]{:S(2)}) collective-permute-start(bf16[128,1024]{1,0:T(8,128)(2,1)S(1)} %bitcast_select_fusion), channel_id=1, source_target_pairs={{3,0},{0,1},{1,2},{2,3},{7,4},{4,5},{5,6},{6,7},{11,8},{8,9},{9,10... | collective-permute-start | bytes 786440 | tf_op jit(solution)/shard_map/ppermute | solution.py:25
  39.4 25.8 %collective-permute-start.5 = (bf16[2,128,1024]{2,1,0:T(8,128)(2,1)S(1)}, bf16[2,128,1024]{2,1,0:T(8,128)(2,1)S(1)}, u32[]{:S(2)}, u32[]{:S(2)}) collective-permute-start(bf16[2,128,1024]{2,1,0:T(8,128)(2,1)S(1)} %pad_maximum_fusion.2.rest_0_), channel_id=1, source_target_pairs={{16,0},{32,16},{48,32},{0,48},{17,1},{33,17},{49,33},{1,49},{18,2}... | collective-permute-start | bytes 1572872 | tf_op jit(solution)/shard_map/ppermute | solution.py:25
  40.2 25.0 %collective-permute-start.6 = (bf16[2,128,1024]{2,1,0:T(8,128)(2,1)S(1)}, bf16[2,128,1024]{2,1,0:T(8,128)(2,1)S(1)}, u32[]{:S(2)}, u32[]{:S(2)}) collective-permute-start(bf16[2,128,1024]{2,1,0:T(8,128)(2,1)S(1)} %pad_maximum_fusion.2.rest_0_), channel_id=1, source_target_pairs={{48,0},{0,16},{16,32},{32,48},{49,1},{1,17},{17,33},{33,49},{50,2}... | collective-permute-start | bytes 1572872 | tf_op jit(solution)/shard_map/ppermute | solution.py:25
  51.2 24.4 %all-to-all-start.1 = ((bf16[8,32,1024]{2,1,0:T(8,128)(2,1)}), bf16[8,32,1024]{2,1,0:T(8,128)(2,1)S(1)}, u32[]{:S(2)}, u32[]{:S(2)}) async-start(bf16[8,32,1024]{2,1,0:T(8,128)(2,1)} %copy.33), calls=%async_computation.1 | async-start | bytes 1048576 | tf_op jit(solution)/shard_map/all_to_all | solution.py:408
  59.2 34.3 %collective-permute-start.7 = (bf16[2,128,1024]{2,1,0:T(8,128)(2,1)S(1)}, bf16[2,128,1024]{2,1,0:T(8,128)(2,1)}, u32[]{:S(2)}, u32[]{:S(2)}) collective-permute-start(bf16[2,128,1024]{2,1,0:T(8,128)(2,1)S(1)} %pad_maximum_fusion.2.rest_0_), channel_id=1, source_target_pairs={{64,0},{4,64},{68,4},{0,68},{65,1},{5,65},{69,5},{1,69},{66,2},{6,... | collective-permute-start | bytes 1572872 | tf_op jit(solution)/shard_map/ppermute | solution.py:23
  62.0 31.5 %collective-permute-start.8 = (bf16[2,128,1024]{2,1,0:T(8,128)(2,1)S(1)}, bf16[2,128,1024]{2,1,0:T(8,128)(2,1)}, u32[]{:S(2)}, u32[]{:S(2)}) collective-permute-start(bf16[2,128,1024]{2,1,0:T(8,128)(2,1)S(1)} %pad_maximum_fusion.1.rest_4_), channel_id=1, source_target_pairs={{16,0},{32,16},{48,32},{0,48},{17,1},{33,17},{49,33},{1,49},{18,2}... | collective-permute-start | bytes 1572872 | tf_op jit(solution)/shard_map/ppermute | solution.py:25
  62.0 31.5 %collective-permute-start.9 = (bf16[2,128,1024]{2,1,0:T(8,128)(2,1)S(1)}, bf16[2,128,1024]{2,1,0:T(8,128)(2,1)}, u32[]{:S(2)}, u32[]{:S(2)}) collective-permute-start(bf16[2,128,1024]{2,1,0:T(8,128)(2,1)S(1)} %pad_maximum_fusion.1.rest_4_), channel_id=1, source_target_pairs={{48,0},{0,16},{16,32},{32,48},{49,1},{1,17},{17,33},{33,49},{50,2}... | collective-permute-start | bytes 1572872 | tf_op jit(solution)/shard_map/ppermute | solution.py:25
  65.2 28.7 %collective-permute-start.10 = (bf16[2,128,1024]{2,1,0:T(8,128)(2,1)S(1)}, bf16[2,128,1024]{2,1,0:T(8,128)(2,1)}, u32[]{:S(2)}, u32[]{:S(2)}) collective-permute-start(bf16[2,128,1024]{2,1,0:T(8,128)(2,1)S(1)} %pad_maximum_fusion.1.rest_4_), channel_id=1, source_target_pairs={{68,0},{0,64},{64,4},{4,68},{69,1},{1,65},{65,5},{5,69},{70,2},{2,... | collective-permute-start | bytes 1572872 | tf_op jit(solution)/shard_map/ppermute | solution.py:23
  75.6 18.3 %collective-permute-start.3 = (bf16[256,1024]{1,0:T(8,128)(2,1)S(1)}, bf16[256,1024]{1,0:T(8,128)(2,1)}, u32[]{:S(2)}, u32[]{:S(2)}) collective-permute-start(bf16[256,1024]{1,0:T(8,128)(2,1)S(1)} %bitcast.34), channel_id=1, source_target_pairs={{0,8},{8,0},{1,9},{9,1},{2,10},{10,2},{3,11},{11,3},{4,12},{12,4},... | collective-permute-start | bytes 1572872 | tf_op jit(solution)/shard_map/ppermute | solution.py:29
  102.4 2.0 %collective-permute-start.11 = (bf16[256,1024]{1,0:T(8,128)(2,1)S(1)}, bf16[256,1024]{1,0:T(8,128)(2,1)S(1)}, u32[]{:S(2)}, u32[]{:S(2)}) collective-permute-start(bf16[256,1024]{1,0:T(8,128)(2,1)S(1)} %get-tuple-element.23), channel_id=1, source_target_pairs={{0,8},{8,0},{1,9},{9,1},{2,10},{10,2},{3,11},{11,3},{4,12},{12,4},... | collective-permute-start | bytes 1572872 | tf_op jit(solution)/shard_map/ppermute | solution.py:29
  105.3 24.1 %all-to-all-start.2 = ((bf16[8,32,1024]{2,1,0:T(8,128)(2,1)}), bf16[8,32,1024]{2,1,0:T(8,128)(2,1)S(1)}, u32[]{:S(2)}, u32[]{:S(2)}) async-start(bf16[8,32,1024]{2,1,0:T(8,128)(2,1)} %bitcast.18), calls=%async_computation.2 | async-start | bytes 1048576 | tf_op jit(solution)/shard_map/all_to_all | solution.py:430
  112.7 14.8 %collective-permute-start.12 = (bf16[3,256,256]{2,1,0:T(8,128)(2,1)S(1)}, bf16[3,256,256]{2,1,0:T(8,128)(2,1)S(1)}, u32[]{:S(2)}, u32[]{:S(2)}) collective-permute-start(bf16[3,256,256]{2,1,0:T(8,128)(2,1)S(1)} %get-tuple-element.24), channel_id=1, source_target_pairs={{0,1},{1,2},{2,3},{3,4},{4,5},{5,6},{6,7},{7,8},{8,9},{9,10},{10,1... | collective-permute-start | bytes 1179656 | tf_op jit(solution)/shard_map/ppermute | solution.py:427
  116.7 12.8 %collective-permute-start.13 = (bf16[3,256,256]{2,1,0:T(8,128)(2,1)S(1)}, bf16[3,256,256]{2,1,0:T(8,128)(2,1)S(1)}, u32[]{:S(2)}, u32[]{:S(2)}) collective-permute-start(bf16[3,256,256]{2,1,0:T(8,128)(2,1)S(1)} %get-tuple-element.25), channel_id=1, source_target_pairs={{1,0},{2,1},{3,2},{4,3},{5,4},{6,5},{7,6},{8,7},{9,8},{10,9},{11,1... | collective-permute-start | bytes 1179656 | tf_op jit(solution)/shard_map/ppermute | solution.py:428
  129.5 5.4 %collective-permute-start.14 = (bf16[256,1024]{1,0:T(8,128)(2,1)S(1)}, bf16[256,1024]{1,0:T(8,128)(2,1)S(1)}, u32[]{:S(2)}, u32[]{:S(2)}) collective-permute-start(bf16[256,1024]{1,0:T(8,128)(2,1)S(1)} %bitcast.48), channel_id=1, source_target_pairs={{0,8},{8,0},{1,9},{9,1},{2,10},{10,2},{3,11},{11,3},{4,12},{12,4},... | collective-permute-start | bytes 1572872 | tf_op jit(solution)/shard_map/ppermute | solution.py:29
  145.3 2.4 %collective-permute-start.15 = (bf16[256,1024]{1,0:T(8,128)(2,1)}, bf16[256,1024]{1,0:T(8,128)(2,1)S(1)}, u32[]{:S(2)}, u32[]{:S(2)}) collective-permute-start(bf16[256,1024]{1,0:T(8,128)(2,1)} %get-tuple-element.28), channel_id=1, source_target_pairs={{0,8},{8,0},{1,9},{9,1},{2,10},{10,2},{3,11},{11,3},{4,12},{12,4},... | collective-permute-start | bytes 1572872 | tf_op jit(solution)/shard_map/ppermute | solution.py:29
  149.4 15.1 %collective-permute-start.16 = (bf16[2,128,256]{2,1,0:T(8,128)(2,1)S(1)}, bf16[2,128,256]{2,1,0:T(8,128)(2,1)S(1)}, u32[]{:S(2)}, u32[]{:S(2)}) collective-permute-start(bf16[2,128,256]{2,1,0:T(8,128)(2,1)S(1)} %bitcast.36), channel_id=1, source_target_pairs={{0,1},{1,2},{2,3},{3,4},{4,5},{5,6},{6,7},{7,8},{8,9},{9,10},{10,1... | collective-permute-start | bytes 393224 | tf_op jit(solution)/shard_map/ppermute | solution.py:442
  151.3 13.2 %collective-permute-start.17 = (bf16[2,128,256]{2,1,0:T(8,128)(2,1)S(1)}, bf16[2,128,256]{2,1,0:T(8,128)(2,1)S(1)}, u32[]{:S(2)}, u32[]{:S(2)}) collective-permute-start(bf16[2,128,256]{2,1,0:T(8,128)(2,1)S(1)} %bitcast.37), channel_id=1, source_target_pairs={{1,0},{2,1},{3,2},{4,3},{5,4},{6,5},{7,6},{8,7},{9,8},{10,9},{11,1... | collective-permute-start | bytes 393224 | tf_op jit(solution)/shard_map/ppermute | solution.py:443
  (11 other events, 66.0 us)
Sparse Core Ops, SparseCore 0:
  9.5 100.2 all-gather.2

commit v10 on v8

--- a/solution.py
+++ b/solution.py
@@ -196,7 +196,7 @@
             pltpu.SemaphoreType.DMA((parts,)),
         ],
         compiler_params=pltpu.CompilerParams(vmem_limit_bytes=56 * 2**20),
-        cost_estimate=pl.CostEstimate(flops=5 * 10**9, bytes_accessed=12 * 10**6, transcendentals=2**20),
+        cost_estimate=pl.CostEstimate(flops=10**6, bytes_accessed=10**4, transcendentals=0),
         name="mlp",
     )(own, other, gain, weights)
 
@@ -425,13 +425,15 @@
     rows = guide.shape[0]
     guide_ends, _ = lax.optimization_barrier(((guide[rows - 3 :], guide[:3]), far))
     guide_low = lax.ppermute(guide_ends[0], AXES, forward)
-    guide_high = lax.ppermute(guide_ends[1], AXES, backward)
+    guide_first, _ = lax.optimization_barrier((guide_ends[1], guide_low))
+    guide_high = lax.ppermute(guide_first, AXES, backward)
 
     middle = lax.all_to_all(
         middle.reshape(tiles, seg, width), MP, split_axis=0, concat_axis=0, tiled=True
     ).reshape(count, width)
-    middle, guide_low, guide_high = lax.optimization_barrier((middle, guide_low, guide_high))
+    middle, guide_low = lax.optimization_barrier((middle, guide_low))
     near, far = mlp(middle, swap_cores(middle), ln_gain_two.reshape(1, width), mlp_w)
+    far, guide_high = lax.optimization_barrier((far, guide_high))
     features = (near + swap_cores(far).astype(F32)).astype(BF16)
     embed = jnp.einsum("pd,dc->pc", features, proj_weight, preferred_element_type=F32).astype(BF16)
     channels = proj_weight.shape[1]

time: 166 us -> 168 us (1.012)
  waiting for transfers between devices: 44.5 us -> 47.7 us
    ppermute x1, waiting for transfers between devices: 8.47 us -> 14.6 us  [per_device(): guide_low = lax.ppermute(guide_ends[0], AXES, forward)]
    ppermute x1, starting transfers between devices: 6.15 us -> 3.65 us  [per_device(): guide_high = lax.ppermute(guide_first, AXES, backward)]
    ppermute x1, waiting for transfers between devices: 2.02 us -> 0.01 us  [per_device(): guide_high = lax.ppermute(guide_first, AXES, backward)]
  transfers between devices with their start and end apart: 22 -> 22, of which waited for: 10 -> 9; matrix products, arithmetic and copies ran while one was open for 6% -> 6% of each run, Pallas kernels for 7% -> 13%
where the time goes in v10:
time: 168 us; the launch traced here: 167 us
  starting transfers between devices  61.7 us (37%)
  waiting for transfers between devices  47.7 us (28%)
  Pallas kernels  28.3 us (17%)
  between operations  13.9 us (8%)
  local copies, waits for them, and re-layouts  8.08 us (5%)
  matrix products  4.21 us (3%)
  other arithmetic  2.96 us (2%)
    ppermute x1, waiting for transfers between devices, per_device(): guide_low = lax.ppermute(guide_ends[0], AXES, forward)  14.6 us
    ppermute x7, starting transfers between devices, shift(): lax.ppermute(block, axis, [((i + step) % count, i) for i in range(count)])  11.8 us
    ppermute x7, waiting for transfers between devices, shift(): lax.ppermute(block, axis, [((i + step) % count, i) for i in range(count)])  10.7 us
    ppermute x2, waiting for transfers between devices, shift(): return lax.ppermute(block, ('yl', 'yh'), pairs)  9.76 us
    pallas_call x1, Pallas kernels, mlp(): pl.pallas_call(mlp_kernel, out_shape=(jax.ShapeDtypeStruct((count, width)...  9.63 us
    all_to_all x1, starting transfers between devices, per_device(): lax.all_to_all(slab_tokens, MP, split_axis=0, concat_axis=0, tiled=True)  8.77 us
    pallas_call x1, Pallas kernels, attention(): pl.pallas_call(attention_kernel, out_shape=(jax.ShapeDtypeStruct((count,...  8.45 us
    ppermute x1, starting transfers between devices, per_device(): image_high = lax.ppermute(image, AXES, backward)  7.9 us
  transfers between devices with their start and end apart: 22, of which 9 were waited for; matrix products, arithmetic and copies ran while one was open for 6% of the time, Pallas kernels for 13%

profile of v10, /device:TPU:6, one launch (start us, length us, event | category | flops | bytes accessed | tf_op | source)
XLA Modules:
  0.0 166.8 jit_solution(1377711039531557134)
XLA Ops:
  10.0 4.9 %collective-permute-start = (bf16[128,1024]{1,0:T(8,128)(2,1)S(1)}, bf16[128,1024]{1,0:T(8,128)(2,1)S(1)}, u32[]{:S(2)}, u32[]{:S(2)}) collective-permute-start(bf16[128,1024]{1,0:T(8,128)(2,1)S(1)} %dynamic-slice_bitcast_fusion), channel_id=1, source_target_pairs={{0,68},{64,4},{12,72},{76,8},{1,69},{65,5},{13,73},{77,9},{2,70},{... | collective-permute-start | bytes 786440 | tf_op jit(solution)/shard_map/ppermute | solution.py:41
  15.2 3.6 %collective-permute-done = bf16[128,1024]{1,0:T(8,128)(2,1)S(1)} collective-permute-done((bf16[128,1024]{1,0:T(8,128)(2,1)S(1)}, bf16[128,1024]{1,0:T(8,128)(2,1)S(1)}, u32[]{:S(2)}, u32[]{:S(2)}) %collective-permute-start) | collective-permute-done | bytes 262176 | tf_op jit(solution)/shard_map/ppermute | solution.py:41
  21.0 4.9 %all-to-all-start = ((bf16[16,32,1024]{2,1,0:T(8,128)(2,1)}), bf16[16,32,1024]{2,1,0:T(8,128)(2,1)}, u32[]{:S(2)}, u32[]{:S(2)}) async-start(bf16[16,32,1024]{2,1,0:T(8,128)(2,1)} %copy.31), calls=%async_computation | async-start | bytes 2097152 | tf_op jit(solution)/shard_map/all_to_all | solution.py:402
  25.9 4.0 %collective-permute-start.4 = (bf16[128,1024]{1,0:T(8,128)(2,1)S(1)}, bf16[128,1024]{1,0:T(8,128)(2,1)S(1)}, u32[]{:S(2)}, u32[]{:S(2)}) collective-permute-start(bf16[128,1024]{1,0:T(8,128)(2,1)S(1)} %bitcast_select_fusion), channel_id=1, source_target_pairs={{1,0},{2,1},{3,2},{0,3},{5,4},{6,5},{7,6},{4,7},{9,8},{10,9},{11,1... | collective-permute-start | bytes 786440 | tf_op jit(solution)/shard_map/ppermute | solution.py:25
  31.2 10.7 %collective-permute-done.4 = bf16[128,1024]{1,0:T(8,128)(2,1)S(1)} collective-permute-done((bf16[128,1024]{1,0:T(8,128)(2,1)S(1)}, bf16[128,1024]{1,0:T(8,128)(2,1)S(1)}, u32[]{:S(2)}, u32[]{:S(2)}) %collective-permute-start.4) | collective-permute-done | bytes 262176 | tf_op jit(solution)/shard_map/ppermute | solution.py:25
  42.9 2.4 %collective-permute-start.6 = (bf16[2,128,1024]{2,1,0:T(8,128)(2,1)S(1)}, bf16[2,128,1024]{2,1,0:T(8,128)(2,1)S(1)}, u32[]{:S(2)}, u32[]{:S(2)}) collective-permute-start(bf16[2,128,1024]{2,1,0:T(8,128)(2,1)S(1)} %pad_maximum_fusion.2.rest_0_), channel_id=1, source_target_pairs={{48,0},{0,16},{16,32},{32,48},{49,1},{1,17},{17,33},{33,49},{50,2}... | collective-permute-start | bytes 1572872 | tf_op jit(solution)/shard_map/ppermute | solution.py:25
  45.3 2.1 %convolution_convert_fusion.1 = bf16[8,32,1024]{2,0,1:T(8,128)(2,1)S(1)} fusion(bf16[16,32,1024]{2,1,0:T(8,128)(2,1)} %all-to-all-done, s32[128]{0:T(128)S(1)} %get-tuple-element.46, s32[128]{0:T(128)S(1)} %get-tuple-element.47, pred[128]{0:T(512)(128)(4,1)S(1)} %get-tuple-element.39), kind=kOutput, calls=%fused_computation.1 | convolution fusion | flops 8687744 | bytes 1574016 | tf_op jit(solution)/shard_map/kg,gpd->kpd/dot_general | solution.py:403
  48.5 8.8 %all-to-all-start.1 = ((bf16[8,32,1024]{2,1,0:T(8,128)(2,1)}), bf16[8,32,1024]{2,1,0:T(8,128)(2,1)S(1)}, u32[]{:S(2)}, u32[]{:S(2)}) async-start(bf16[8,32,1024]{2,1,0:T(8,128)(2,1)} %copy.33), calls=%async_computation.1 | async-start | bytes 1048576 | tf_op jit(solution)/shard_map/all_to_all | solution.py:408
  57.3 3.5 %collective-permute-start.7 = (bf16[2,128,1024]{2,1,0:T(8,128)(2,1)S(1)}, bf16[2,128,1024]{2,1,0:T(8,128)(2,1)}, u32[]{:S(2)}, u32[]{:S(2)}) collective-permute-start(bf16[2,128,1024]{2,1,0:T(8,128)(2,1)S(1)} %pad_maximum_fusion.2.rest_0_), channel_id=1, source_target_pairs={{64,0},{4,64},{68,4},{0,68},{65,1},{5,65},{69,5},{1,69},{66,2},{6,... | collective-permute-start | bytes 1572872 | tf_op jit(solution)/shard_map/ppermute | solution.py:23
  60.7 3.2 %collective-permute-start.9 = (bf16[2,128,1024]{2,1,0:T(8,128)(2,1)S(1)}, bf16[2,128,1024]{2,1,0:T(8,128)(2,1)}, u32[]{:S(2)}, u32[]{:S(2)}) collective-permute-start(bf16[2,128,1024]{2,1,0:T(8,128)(2,1)S(1)} %pad_maximum_fusion.1.rest_4_), channel_id=1, source_target_pairs={{48,0},{0,16},{16,32},{32,48},{49,1},{1,17},{17,33},{33,49},{50,2}... | collective-permute-start | bytes 1572872 | tf_op jit(solution)/shard_map/ppermute | solution.py:25
  64.0 5.7 %all-to-all-done.1 = bf16[8,32,1024]{2,1,0:T(8,128)(2,1)S(1)} async-done(((bf16[8,32,1024]{2,1,0:T(8,128)(2,1)}), bf16[8,32,1024]{2,1,0:T(8,128)(2,1)S(1)}, u32[]{:S(2)}, u32[]{:S(2)}) %all-to-all-start.1) | async-done | bytes 524320 | tf_op jit(solution)/shard_map/all_to_all | solution.py:408
  69.7 8.0 %collective-permute-done.7.rest_3_ = bf16[2,128,1024]{2,1,0:T(8,128)(2,1)} collective-permute-done((bf16[2,128,1024]{2,1,0:T(8,128)(2,1)S(1)}, bf16[2,128,1024]{2,1,0:T(8,128)(2,1)}, u32[]{:S(2)}, u32[]{:S(2)}) %collective-permute-start.7) | collective-permute-done | bytes 524320 | tf_op jit(solution)/shard_map/ppermute | solution.py:23
  79.4 8.4 %attention.1 = (f32[256,1024]{1,0:T(8,128)S(1)}, bf16[256,1024]{1,0:T(8,128)(2,1)S(1)}) custom-call(s32[1]{0:T(128)} %bitcast.1.parity, bf16[256,1024]{1,0:T(8,128)(2,1)S(1)} %bitcast.35, bf16[256,1024]{1,0:T(8,128)(2,1)} %collective-permute-done.3.other, f32[1,1024]{1,0:T(1,128)S(1)} %bitcast.39, bf16[2,128,1024]{2,1,0:T(8,128)(2,1)S(1)} %pad_maximum_fusion.2.rest_0_, ...), custom_call_target="tpu_custom_call" | custom-call | flops 3000000000 | bytes 7000000 | tf_op jit(solution)/shard_map/attention/pallas_call | solution.py:130
  90.8 4.6 %all-to-all-start.2 = ((bf16[8,32,1024]{2,1,0:T(8,128)(2,1)}), bf16[8,32,1024]{2,1,0:T(8,128)(2,1)S(1)}, u32[]{:S(2)}, u32[]{:S(2)}) async-start(bf16[8,32,1024]{2,1,0:T(8,128)(2,1)} %bitcast.18), calls=%async_computation.2 | async-start | bytes 1048576 | tf_op jit(solution)/shard_map/all_to_all | solution.py:431
  95.5 3.9 %collective-permute-start.12 = (bf16[3,256,256]{2,1,0:T(8,128)(2,1)S(1)}, bf16[3,256,256]{2,1,0:T(8,128)(2,1)S(1)}, u32[]{:S(2)}, u32[]{:S(2)}) collective-permute-start(bf16[3,256,256]{2,1,0:T(8,128)(2,1)S(1)} %get-tuple-element.26), channel_id=1, source_target_pairs={{0,1},{1,2},{2,3},{3,4},{4,5},{5,6},{6,7},{7,8},{8,9},{9,10},{10,1... | collective-permute-start | bytes 1179656 | tf_op jit(solution)/shard_map/ppermute | solution.py:427
  99.4 14.6 %collective-permute-done.12.guide_low = bf16[3,256,256]{2,1,0:T(8,128)(2,1)S(1)} collective-permute-done((bf16[3,256,256]{2,1,0:T(8,128)(2,1)S(1)}, bf16[3,256,256]{2,1,0:T(8,128)(2,1)S(1)}, u32[]{:S(2)}, u32[]{:S(2)}) %collective-permute-start.12) | collective-permute-done | bytes 393248 | tf_op jit(solution)/shard_map/ppermute | solution.py:427
  114.3 5.1 %collective-permute-start.13 = (bf16[256,1024]{1,0:T(8,128)(2,1)S(1)}, bf16[256,1024]{1,0:T(8,128)(2,1)S(1)}, u32[]{:S(2)}, u32[]{:S(2)}) collective-permute-start(bf16[256,1024]{1,0:T(8,128)(2,1)S(1)} %bitcast.44), channel_id=1, source_target_pairs={{0,8},{8,0},{1,9},{9,1},{2,10},{10,2},{3,11},{11,3},{4,12},{12,4},... | collective-permute-start | bytes 1572872 | tf_op jit(solution)/shard_map/ppermute | solution.py:29
  119.3 3.7 %collective-permute-start.14 = (bf16[3,256,256]{2,1,0:T(8,128)(2,1)S(1)}, bf16[3,256,256]{2,1,0:T(8,128)(2,1)S(1)}, u32[]{:S(2)}, u32[]{:S(2)}) collective-permute-start(bf16[3,256,256]{2,1,0:T(8,128)(2,1)S(1)} %get-tuple-element.31), channel_id=1, source_target_pairs={{1,0},{2,1},{3,2},{4,3},{5,4},{6,5},{7,6},{8,7},{9,8},{10,9},{11,1... | collective-permute-start | bytes 1179656 | tf_op jit(solution)/shard_map/ppermute | solution.py:429
  123.8 9.6 %mlp.1 = (f32[256,1024]{1,0:T(8,128)}, bf16[256,1024]{1,0:T(8,128)(2,1)}) custom-call(bf16[256,1024]{1,0:T(8,128)(2,1)} %bitcast.45, bf16[256,1024]{1,0:T(8,128)(2,1)} %copy-done.8, f32[1,1024]{1,0:T(1,128)} %bitcast.55, bf16[64,64,1024]{2,1,0:T(8,128)(2,1)} %bitcast.40), custom_call_target="tpu_custom_call" | custom-call | flops 1000000 | bytes 10000 | tf_op jit(solution)/shard_map/mlp/pallas_call | solution.py:184
  137.5 2.2 %collective-permute-start.16 = (bf16[2,128,256]{2,1,0:T(8,128)(2,1)S(1)}, bf16[2,128,256]{2,1,0:T(8,128)(2,1)S(1)}, u32[]{:S(2)}, u32[]{:S(2)}) collective-permute-start(bf16[2,128,256]{2,1,0:T(8,128)(2,1)S(1)} %bitcast.36), channel_id=1, source_target_pairs={{0,1},{1,2},{2,3},{3,4},{4,5},{5,6},{6,7},{7,8},{8,9},{9,10},{10,1... | collective-permute-start | bytes 393224 | tf_op jit(solution)/shard_map/ppermute | solution.py:444
  139.7 7.9 %collective-permute-start.17 = (bf16[2,128,256]{2,1,0:T(8,128)(2,1)S(1)}, bf16[2,128,256]{2,1,0:T(8,128)(2,1)S(1)}, u32[]{:S(2)}, u32[]{:S(2)}) collective-permute-start(bf16[2,128,256]{2,1,0:T(8,128)(2,1)S(1)} %bitcast.37), channel_id=1, source_target_pairs={{1,0},{2,1},{3,2},{4,3},{5,4},{6,5},{7,6},{8,7},{9,8},{10,9},{11,1... | collective-permute-start | bytes 393224 | tf_op jit(solution)/shard_map/ppermute | solution.py:445
  147.6 2.0 %copy-done.2 = bf16[3,3,3,256,256]{4,3,2,1,0:T(8,128)(2,1)S(1)} copy-done((bf16[3,3,3,256,256]{4,3,2,1,0:T(8,128)(2,1)S(1)}, bf16[3,3,3,256,256]{4,3,2,1,0:T(8,128)(2,1)}, u32[]{:S(2)}) %copy-start.2) | copy-done | bytes 3538968
  149.6 3.0 %early.1 = (bf16[4,256,256]{2,1,0:T(8,128)(2,1)S(1)}, f32[4,256,256]{2,1,0:T(8,128)S(1)}, bf16[2,256,256]{2,1,0:T(8,128)(2,1)S(1)}, f32[4,256,256]{2,1,0:T(8,128)S(1)}) custom-call(bf16[2,128,256]{2,1,0:T(8,128)(2,1)S(1)} %bitcast.38, bf16[4,256,256]{2,1,0:T(8,128)(2,1)S(1)} %copy-done.1, bf16[3,3,3,256,256]{4,3,2,1,0:T(8,128)(2,1)S(1)} %copy-done.2, ...), custom_call_target="tpu_custom_call" | custom-call | flops 3000000000 | bytes 4000000 | tf_op jit(solution)/shard_map/early/pallas_call | solution.py:302
  152.7 7.2 %late.1 = bf16[4,256,256]{2,1,0:T(8,128)(2,1)} custom-call(s32[2]{0:T(128)S(1)} %pad_add_fusion.place, bf16[2,128,256]{2,1,0:T(8,128)(2,1)S(1)} %collective-permute-done.16.image_low, bf16[2,128,256]{2,1,0:T(8,128)(2,1)S(1)} %collective-permute-done.17.image_high, bf16[3,256,256]{2,1,0:T(8,128)(2,1)S(1)} %collective-permute-done.12.guide_low, ...), custom_call_target="tpu_custom_call" | custom-call | flops 4000000000 | bytes 6000000 | tf_op jit(solution)/shard_map/late/pallas_call | solution.py:324
  (76 shorter events, 18.9 us)
Async XLA Ops:
  6.5 129.4 %copy-start = (bf16[1024,256]{1,0:T(8,128)(2,1)S(1)}, bf16[1024,256]{1,0:T(8,128)(2,1)}, u32[]{:S(2)}) copy-start(bf16[1024,256]{1,0:T(8,128)(2,1)} %param.20) | copy-start | bytes 1572868
  6.5 116.5 %all-gather.3.cloned.1.call-start = ((), (), s32[]{:S(2)}) async-start(), calls=%async_computation.3 | async-start | bytes 8519680 | tf_op jit(solution)/shard_map/all_gather | solution.py:384
  10.0 8.8 %collective-permute-start = (bf16[128,1024]{1,0:T(8,128)(2,1)S(1)}, bf16[128,1024]{1,0:T(8,128)(2,1)S(1)}, u32[]{:S(2)}, u32[]{:S(2)}) collective-permute-start(bf16[128,1024]{1,0:T(8,128)(2,1)S(1)} %dynamic-slice_bitcast_fusion), channel_id=1, source_target_pairs={{0,68},{64,4},{12,72},{76,8},{1,69},{65,5},{13,73},{77,9},{2,70},{... | collective-permute-start | bytes 786440 | tf_op jit(solution)/shard_map/ppermute | solution.py:41
  21.0 58.5 %copy-start.4 = (f32[1024]{0:T(1024)S(1)}, f32[1024]{0:T(1024)}, u32[]{:S(2)}) copy-start(f32[1024]{0:T(1024)} %param.14) | copy-start | bytes 12292
  21.0 24.3 %all-to-all-start = ((bf16[16,32,1024]{2,1,0:T(8,128)(2,1)}), bf16[16,32,1024]{2,1,0:T(8,128)(2,1)}, u32[]{:S(2)}, u32[]{:S(2)}) async-start(bf16[16,32,1024]{2,1,0:T(8,128)(2,1)} %copy.31), calls=%async_computation | async-start | bytes 2097152 | tf_op jit(solution)/shard_map/all_to_all | solution.py:402
  25.9 16.0 %collective-permute-start.4 = (bf16[128,1024]{1,0:T(8,128)(2,1)S(1)}, bf16[128,1024]{1,0:T(8,128)(2,1)S(1)}, u32[]{:S(2)}, u32[]{:S(2)}) collective-permute-start(bf16[128,1024]{1,0:T(8,128)(2,1)S(1)} %bitcast_select_fusion), channel_id=1, source_target_pairs={{1,0},{2,1},{3,2},{0,3},{5,4},{6,5},{7,6},{4,7},{9,8},{10,9},{11,1... | collective-permute-start | bytes 786440 | tf_op jit(solution)/shard_map/ppermute | solution.py:25
  29.9 15.3 %collective-permute-start.2 = (bf16[128,1024]{1,0:T(8,128)(2,1)S(1)}, bf16[128,1024]{1,0:T(8,128)(2,1)S(1)}, u32[]{:S(2)}, u32[]{:S(2)}) collective-permute-start(bf16[128,1024]{1,0:T(8,128)(2,1)S(1)} %bitcast_select_fusion), channel_id=1, source_target_pairs={{2,0},{3,1},{0,2},{1,3},{6,4},{7,5},{4,6},{5,7},{10,8},{11,9},{8,1... | collective-permute-start | bytes 786440 | tf_op jit(solution)/shard_map/ppermute | solution.py:25
  29.9 15.3 %collective-permute-start.1 = (bf16[128,1024]{1,0:T(8,128)(2,1)S(1)}, bf16[128,1024]{1,0:T(8,128)(2,1)S(1)}, u32[]{:S(2)}, u32[]{:S(2)}) collective-permute-start(bf16[128,1024]{1,0:T(8,128)(2,1)S(1)} %bitcast_select_fusion), channel_id=1, source_target_pairs={{3,0},{0,1},{1,2},{2,3},{7,4},{4,5},{5,6},{6,7},{11,8},{8,9},{9,10... | collective-permute-start | bytes 786440 | tf_op jit(solution)/shard_map/ppermute | solution.py:25
  41.9 22.0 %collective-permute-start.5 = (bf16[2,128,1024]{2,1,0:T(8,128)(2,1)S(1)}, bf16[2,128,1024]{2,1,0:T(8,128)(2,1)S(1)}, u32[]{:S(2)}, u32[]{:S(2)}) collective-permute-start(bf16[2,128,1024]{2,1,0:T(8,128)(2,1)S(1)} %pad_maximum_fusion.2.rest_0_), channel_id=1, source_target_pairs={{16,0},{32,16},{48,32},{0,48},{17,1},{33,17},{49,33},{1,49},{18,2}... | collective-permute-start | bytes 1572872 | tf_op jit(solution)/shard_map/ppermute | solution.py:25
  42.9 21.1 %collective-permute-start.6 = (bf16[2,128,1024]{2,1,0:T(8,128)(2,1)S(1)}, bf16[2,128,1024]{2,1,0:T(8,128)(2,1)S(1)}, u32[]{:S(2)}, u32[]{:S(2)}) collective-permute-start(bf16[2,128,1024]{2,1,0:T(8,128)(2,1)S(1)} %pad_maximum_fusion.2.rest_0_), channel_id=1, source_target_pairs={{48,0},{0,16},{16,32},{32,48},{49,1},{1,17},{17,33},{33,49},{50,2}... | collective-permute-start | bytes 1572872 | tf_op jit(solution)/shard_map/ppermute | solution.py:25
  48.5 21.1 %all-to-all-start.1 = ((bf16[8,32,1024]{2,1,0:T(8,128)(2,1)}), bf16[8,32,1024]{2,1,0:T(8,128)(2,1)S(1)}, u32[]{:S(2)}, u32[]{:S(2)}) async-start(bf16[8,32,1024]{2,1,0:T(8,128)(2,1)} %copy.33), calls=%async_computation.1 | async-start | bytes 1048576 | tf_op jit(solution)/shard_map/all_to_all | solution.py:408
  57.3 20.4 %collective-permute-start.7 = (bf16[2,128,1024]{2,1,0:T(8,128)(2,1)S(1)}, bf16[2,128,1024]{2,1,0:T(8,128)(2,1)}, u32[]{:S(2)}, u32[]{:S(2)}) collective-permute-start(bf16[2,128,1024]{2,1,0:T(8,128)(2,1)S(1)} %pad_maximum_fusion.2.rest_0_), channel_id=1, source_target_pairs={{64,0},{4,64},{68,4},{0,68},{65,1},{5,65},{69,5},{1,69},{66,2},{6,... | collective-permute-start | bytes 1572872 | tf_op jit(solution)/shard_map/ppermute | solution.py:23
  60.7 16.9 %collective-permute-start.8 = (bf16[2,128,1024]{2,1,0:T(8,128)(2,1)S(1)}, bf16[2,128,1024]{2,1,0:T(8,128)(2,1)}, u32[]{:S(2)}, u32[]{:S(2)}) collective-permute-start(bf16[2,128,1024]{2,1,0:T(8,128)(2,1)S(1)} %pad_maximum_fusion.1.rest_4_), channel_id=1, source_target_pairs={{16,0},{32,16},{48,32},{0,48},{17,1},{33,17},{49,33},{1,49},{18,2}... | collective-permute-start | bytes 1572872 | tf_op jit(solution)/shard_map/ppermute | solution.py:25
  60.7 16.9 %collective-permute-start.9 = (bf16[2,128,1024]{2,1,0:T(8,128)(2,1)S(1)}, bf16[2,128,1024]{2,1,0:T(8,128)(2,1)}, u32[]{:S(2)}, u32[]{:S(2)}) collective-permute-start(bf16[2,128,1024]{2,1,0:T(8,128)(2,1)S(1)} %pad_maximum_fusion.1.rest_4_), channel_id=1, source_target_pairs={{48,0},{0,16},{16,32},{32,48},{49,1},{1,17},{17,33},{33,49},{50,2}... | collective-permute-start | bytes 1572872 | tf_op jit(solution)/shard_map/ppermute | solution.py:25
  64.0 15.4 %collective-permute-start.10 = (bf16[2,128,1024]{2,1,0:T(8,128)(2,1)S(1)}, bf16[2,128,1024]{2,1,0:T(8,128)(2,1)}, u32[]{:S(2)}, u32[]{:S(2)}) collective-permute-start(bf16[2,128,1024]{2,1,0:T(8,128)(2,1)S(1)} %pad_maximum_fusion.1.rest_4_), channel_id=1, source_target_pairs={{68,0},{0,64},{64,4},{4,68},{69,1},{1,65},{65,5},{5,69},{70,2},{2,... | collective-permute-start | bytes 1572872 | tf_op jit(solution)/shard_map/ppermute | solution.py:23
  69.6 9.8 %collective-permute-start.3 = (bf16[256,1024]{1,0:T(8,128)(2,1)S(1)}, bf16[256,1024]{1,0:T(8,128)(2,1)}, u32[]{:S(2)}, u32[]{:S(2)}) collective-permute-start(bf16[256,1024]{1,0:T(8,128)(2,1)S(1)} %bitcast.34), channel_id=1, source_target_pairs={{0,8},{8,0},{1,9},{9,1},{2,10},{10,2},{3,11},{11,3},{4,12},{12,4},... | collective-permute-start | bytes 1572872 | tf_op jit(solution)/shard_map/ppermute | solution.py:29
  87.9 2.0 %collective-permute-start.11 = (bf16[256,1024]{1,0:T(8,128)(2,1)S(1)}, bf16[256,1024]{1,0:T(8,128)(2,1)S(1)}, u32[]{:S(2)}, u32[]{:S(2)}) collective-permute-start(bf16[256,1024]{1,0:T(8,128)(2,1)S(1)} %get-tuple-element.25), channel_id=1, source_target_pairs={{0,8},{8,0},{1,9},{9,1},{2,10},{10,2},{3,11},{11,3},{4,12},{12,4},... | collective-permute-start | bytes 1572872 | tf_op jit(solution)/shard_map/ppermute | solution.py:29
  90.8 23.4 %all-to-all-start.2 = ((bf16[8,32,1024]{2,1,0:T(8,128)(2,1)}), bf16[8,32,1024]{2,1,0:T(8,128)(2,1)S(1)}, u32[]{:S(2)}, u32[]{:S(2)}) async-start(bf16[8,32,1024]{2,1,0:T(8,128)(2,1)} %bitcast.18), calls=%async_computation.2 | async-start | bytes 1048576 | tf_op jit(solution)/shard_map/all_to_all | solution.py:431
  95.5 18.6 %collective-permute-start.12 = (bf16[3,256,256]{2,1,0:T(8,128)(2,1)S(1)}, bf16[3,256,256]{2,1,0:T(8,128)(2,1)S(1)}, u32[]{:S(2)}, u32[]{:S(2)}) collective-permute-start(bf16[3,256,256]{2,1,0:T(8,128)(2,1)S(1)} %get-tuple-element.26), channel_id=1, source_target_pairs={{0,1},{1,2},{2,3},{3,4},{4,5},{5,6},{6,7},{7,8},{8,9},{9,10},{10,1... | collective-permute-start | bytes 1179656 | tf_op jit(solution)/shard_map/ppermute | solution.py:427
  114.3 8.7 %collective-permute-start.13 = (bf16[256,1024]{1,0:T(8,128)(2,1)S(1)}, bf16[256,1024]{1,0:T(8,128)(2,1)S(1)}, u32[]{:S(2)}, u32[]{:S(2)}) collective-permute-start(bf16[256,1024]{1,0:T(8,128)(2,1)S(1)} %bitcast.44), channel_id=1, source_target_pairs={{0,8},{8,0},{1,9},{9,1},{2,10},{10,2},{3,11},{11,3},{4,12},{12,4},... | collective-permute-start | bytes 1572872 | tf_op jit(solution)/shard_map/ppermute | solution.py:29
  119.3 14.1 %collective-permute-start.14 = (bf16[3,256,256]{2,1,0:T(8,128)(2,1)S(1)}, bf16[3,256,256]{2,1,0:T(8,128)(2,1)S(1)}, u32[]{:S(2)}, u32[]{:S(2)}) collective-permute-start(bf16[3,256,256]{2,1,0:T(8,128)(2,1)S(1)} %get-tuple-element.31), channel_id=1, source_target_pairs={{1,0},{2,1},{3,2},{4,3},{5,4},{6,5},{7,6},{8,7},{9,8},{10,9},{11,1... | collective-permute-start | bytes 1179656 | tf_op jit(solution)/shard_map/ppermute | solution.py:429
  133.5 2.4 %collective-permute-start.15 = (bf16[256,1024]{1,0:T(8,128)(2,1)}, bf16[256,1024]{1,0:T(8,128)(2,1)S(1)}, u32[]{:S(2)}, u32[]{:S(2)}) collective-permute-start(bf16[256,1024]{1,0:T(8,128)(2,1)} %get-tuple-element.32), channel_id=1, source_target_pairs={{0,8},{8,0},{1,9},{9,1},{2,10},{10,2},{3,11},{11,3},{4,12},{12,4},... | collective-permute-start | bytes 1572872 | tf_op jit(solution)/shard_map/ppermute | solution.py:29
  137.5 15.1 %collective-permute-start.16 = (bf16[2,128,256]{2,1,0:T(8,128)(2,1)S(1)}, bf16[2,128,256]{2,1,0:T(8,128)(2,1)S(1)}, u32[]{:S(2)}, u32[]{:S(2)}) collective-permute-start(bf16[2,128,256]{2,1,0:T(8,128)(2,1)S(1)} %bitcast.36), channel_id=1, source_target_pairs={{0,1},{1,2},{2,3},{3,4},{4,5},{5,6},{6,7},{7,8},{8,9},{9,10},{10,1... | collective-permute-start | bytes 393224 | tf_op jit(solution)/shard_map/ppermute | solution.py:444
  139.7 12.9 %collective-permute-start.17 = (bf16[2,128,256]{2,1,0:T(8,128)(2,1)S(1)}, bf16[2,128,256]{2,1,0:T(8,128)(2,1)S(1)}, u32[]{:S(2)}, u32[]{:S(2)}) collective-permute-start(bf16[2,128,256]{2,1,0:T(8,128)(2,1)S(1)} %bitcast.37), channel_id=1, source_target_pairs={{1,0},{2,1},{3,2},{4,3},{5,4},{6,5},{7,6},{8,7},{9,8},{10,9},{11,1... | collective-permute-start | bytes 393224 | tf_op jit(solution)/shard_map/ppermute | solution.py:445
  (11 other events, 66.4 us)
Sparse Core Ops, SparseCore 0:
  10.2 102.4 all-gather.2

commit v11 on v8

--- a/solution.py
+++ b/solution.py
@@ -196,7 +196,7 @@
             pltpu.SemaphoreType.DMA((parts,)),
         ],
         compiler_params=pltpu.CompilerParams(vmem_limit_bytes=56 * 2**20),
-        cost_estimate=pl.CostEstimate(flops=5 * 10**9, bytes_accessed=12 * 10**6, transcendentals=2**20),
+        cost_estimate=pl.CostEstimate(flops=10**6, bytes_accessed=10**4, transcendentals=0),
         name="mlp",
     )(own, other, gain, weights)
 
@@ -430,8 +430,8 @@
     middle = lax.all_to_all(
         middle.reshape(tiles, seg, width), MP, split_axis=0, concat_axis=0, tiled=True
     ).reshape(count, width)
-    middle, guide_low, guide_high = lax.optimization_barrier((middle, guide_low, guide_high))
     near, far = mlp(middle, swap_cores(middle), ln_gain_two.reshape(1, width), mlp_w)
+    far, guide_low, guide_high = lax.optimization_barrier((far, guide_low, guide_high))
     features = (near + swap_cores(far).astype(F32)).astype(BF16)
     embed = jnp.einsum("pd,dc->pc", features, proj_weight, preferred_element_type=F32).astype(BF16)
     channels = proj_weight.shape[1]

time: 166 us -> 166 us (level)
  blocking collectives: 0 us -> 20.6 us
  waiting for transfers between devices: 44.5 us -> 32.9 us
  starting transfers between devices: 62.8 us -> 54.5 us
    all_to_all x0 -> x1, blocking collectives: none -> 20.6 us  [per_device(): lax.all_to_all(middle.reshape(tiles, seg, width), MP, split_axis=0, conca...]
    ppermute x1, waiting for transfers between devices: 8.47 us -> 0.01 us  [per_device(): guide_low = lax.ppermute(guide_ends[0], AXES, forward)]
    all_to_all x1 -> x0, starting transfers between devices: 4.62 us -> none  [per_device(): lax.all_to_all(middle.reshape(tiles, seg, width), MP, split_axis=0, conca...]
    ppermute x4, starting transfers between devices: 4.08 us -> 0.4 us  [swap_cores(): return lax.ppermute(block, 'c', [(0, 1), (1, 0)])]
    ppermute x1, waiting for transfers between devices: 2.02 us -> 0.01 us  [per_device(): guide_high = lax.ppermute(guide_ends[1], AXES, backward)]
    ppermute x1, starting transfers between devices: 3.92 us -> 2.07 us  [per_device(): guide_low = lax.ppermute(guide_ends[0], AXES, forward)]
    ppermute x1, starting transfers between devices: 6.15 us -> 8 us  [per_device(): guide_high = lax.ppermute(guide_ends[1], AXES, backward)]
  transfers between devices with their start and end apart: 22 -> 21, of which waited for: 10 -> 7; matrix products, arithmetic and copies ran while one was open for 6% -> 6% of each run, Pallas kernels for 7% -> 13%
where the time goes in v11:
time: 166 us; the launch traced here: 165 us
  starting transfers between devices  54.5 us (33%)
  waiting for transfers between devices  32.9 us (20%)
  Pallas kernels  28.3 us (17%)
  blocking collectives  20.6 us (12%)
  between operations  13.9 us (8%)
  local copies, waits for them, and re-layouts  8.89 us (5%)
  matrix products  4.21 us (3%)
  other arithmetic  2.17 us (1%)
    all_to_all x1, blocking collectives, per_device(): lax.all_to_all(middle.reshape(tiles, seg, width), MP, split_axis=0, conca...  20.6 us
    ppermute x7, starting transfers between devices, shift(): lax.ppermute(block, axis, [((i + step) % count, i) for i in range(count)])  11.8 us
    ppermute x7, waiting for transfers between devices, shift(): lax.ppermute(block, axis, [((i + step) % count, i) for i in range(count)])  10.7 us
    ppermute x2, waiting for transfers between devices, shift(): return lax.ppermute(block, ('yl', 'yh'), pairs)  9.79 us
    pallas_call x1, Pallas kernels, mlp(): pl.pallas_call(mlp_kernel, out_shape=(jax.ShapeDtypeStruct((count, width)...  9.62 us
    all_to_all x1, starting transfers between devices, per_device(): lax.all_to_all(slab_tokens, MP, split_axis=0, concat_axis=0, tiled=True)  8.77 us
    pallas_call x1, Pallas kernels, attention(): pl.pallas_call(attention_kernel, out_shape=(jax.ShapeDtypeStruct((count,...  8.45 us
    ppermute x1, starting transfers between devices, per_device(): image_high = lax.ppermute(image, AXES, backward)  8.15 us
  transfers between devices with their start and end apart: 21, of which 7 were waited for; matrix products, arithmetic and copies ran while one was open for 6% of the time, Pallas kernels for 13%

profile of v11, /device:TPU:6, one launch (start us, length us, event | category | flops | bytes accessed | tf_op | source)
XLA Modules:
  0.0 165.4 jit_solution(17069923159291936124)
XLA Ops:
  10.0 4.9 %collective-permute-start = (bf16[128,1024]{1,0:T(8,128)(2,1)S(1)}, bf16[128,1024]{1,0:T(8,128)(2,1)S(1)}, u32[]{:S(2)}, u32[]{:S(2)}) collective-permute-start(bf16[128,1024]{1,0:T(8,128)(2,1)S(1)} %dynamic-slice_bitcast_fusion), channel_id=1, source_target_pairs={{0,68},{64,4},{12,72},{76,8},{1,69},{65,5},{13,73},{77,9},{2,70},{... | collective-permute-start | bytes 786440 | tf_op jit(solution)/shard_map/ppermute | solution.py:41
  15.2 3.6 %collective-permute-done = bf16[128,1024]{1,0:T(8,128)(2,1)S(1)} collective-permute-done((bf16[128,1024]{1,0:T(8,128)(2,1)S(1)}, bf16[128,1024]{1,0:T(8,128)(2,1)S(1)}, u32[]{:S(2)}, u32[]{:S(2)}) %collective-permute-start) | collective-permute-done | bytes 262176 | tf_op jit(solution)/shard_map/ppermute | solution.py:41
  21.0 4.9 %all-to-all-start = ((bf16[16,32,1024]{2,1,0:T(8,128)(2,1)}), bf16[16,32,1024]{2,1,0:T(8,128)(2,1)}, u32[]{:S(2)}, u32[]{:S(2)}) async-start(bf16[16,32,1024]{2,1,0:T(8,128)(2,1)} %copy.31), calls=%async_computation | async-start | bytes 2097152 | tf_op jit(solution)/shard_map/all_to_all | solution.py:402
  25.9 4.0 %collective-permute-start.4 = (bf16[128,1024]{1,0:T(8,128)(2,1)S(1)}, bf16[128,1024]{1,0:T(8,128)(2,1)S(1)}, u32[]{:S(2)}, u32[]{:S(2)}) collective-permute-start(bf16[128,1024]{1,0:T(8,128)(2,1)S(1)} %bitcast_select_fusion), channel_id=1, source_target_pairs={{1,0},{2,1},{3,2},{0,3},{5,4},{6,5},{7,6},{4,7},{9,8},{10,9},{11,1... | collective-permute-start | bytes 786440 | tf_op jit(solution)/shard_map/ppermute | solution.py:25
  31.2 10.7 %collective-permute-done.4 = bf16[128,1024]{1,0:T(8,128)(2,1)S(1)} collective-permute-done((bf16[128,1024]{1,0:T(8,128)(2,1)S(1)}, bf16[128,1024]{1,0:T(8,128)(2,1)S(1)}, u32[]{:S(2)}, u32[]{:S(2)}) %collective-permute-start.4) | collective-permute-done | bytes 262176 | tf_op jit(solution)/shard_map/ppermute | solution.py:25
  42.9 2.4 %collective-permute-start.6 = (bf16[2,128,1024]{2,1,0:T(8,128)(2,1)S(1)}, bf16[2,128,1024]{2,1,0:T(8,128)(2,1)S(1)}, u32[]{:S(2)}, u32[]{:S(2)}) collective-permute-start(bf16[2,128,1024]{2,1,0:T(8,128)(2,1)S(1)} %pad_maximum_fusion.2.rest_0_), channel_id=1, source_target_pairs={{48,0},{0,16},{16,32},{32,48},{49,1},{1,17},{17,33},{33,49},{50,2}... | collective-permute-start | bytes 1572872 | tf_op jit(solution)/shard_map/ppermute | solution.py:25
  45.3 2.1 %convolution_convert_fusion.1 = bf16[8,32,1024]{2,0,1:T(8,128)(2,1)S(1)} fusion(bf16[16,32,1024]{2,1,0:T(8,128)(2,1)} %all-to-all-done, s32[128]{0:T(128)S(1)} %get-tuple-element.42, s32[128]{0:T(128)S(1)} %get-tuple-element.43, pred[128]{0:T(512)(128)(4,1)S(1)} %get-tuple-element.35), kind=kOutput, calls=%fused_computation.1 | convolution fusion | flops 8687744 | bytes 1574016 | tf_op jit(solution)/shard_map/kg,gpd->kpd/dot_general | solution.py:403
  48.5 8.8 %all-to-all-start.1 = ((bf16[8,32,1024]{2,1,0:T(8,128)(2,1)}), bf16[8,32,1024]{2,1,0:T(8,128)(2,1)S(1)}, u32[]{:S(2)}, u32[]{:S(2)}) async-start(bf16[8,32,1024]{2,1,0:T(8,128)(2,1)} %copy.33), calls=%async_computation.1 | async-start | bytes 1048576 | tf_op jit(solution)/shard_map/all_to_all | solution.py:408
  57.3 3.5 %collective-permute-start.7 = (bf16[2,128,1024]{2,1,0:T(8,128)(2,1)S(1)}, bf16[2,128,1024]{2,1,0:T(8,128)(2,1)}, u32[]{:S(2)}, u32[]{:S(2)}) collective-permute-start(bf16[2,128,1024]{2,1,0:T(8,128)(2,1)S(1)} %pad_maximum_fusion.2.rest_0_), channel_id=1, source_target_pairs={{64,0},{4,64},{68,4},{0,68},{65,1},{5,65},{69,5},{1,69},{66,2},{6,... | collective-permute-start | bytes 1572872 | tf_op jit(solution)/shard_map/ppermute | solution.py:23
  60.7 3.2 %collective-permute-start.9 = (bf16[2,128,1024]{2,1,0:T(8,128)(2,1)S(1)}, bf16[2,128,1024]{2,1,0:T(8,128)(2,1)}, u32[]{:S(2)}, u32[]{:S(2)}) collective-permute-start(bf16[2,128,1024]{2,1,0:T(8,128)(2,1)S(1)} %pad_maximum_fusion.1.rest_4_), channel_id=1, source_target_pairs={{48,0},{0,16},{16,32},{32,48},{49,1},{1,17},{17,33},{33,49},{50,2}... | collective-permute-start | bytes 1572872 | tf_op jit(solution)/shard_map/ppermute | solution.py:25
  64.0 5.6 %all-to-all-done.1 = bf16[8,32,1024]{2,1,0:T(8,128)(2,1)S(1)} async-done(((bf16[8,32,1024]{2,1,0:T(8,128)(2,1)}), bf16[8,32,1024]{2,1,0:T(8,128)(2,1)S(1)}, u32[]{:S(2)}, u32[]{:S(2)}) %all-to-all-start.1) | async-done | bytes 524320 | tf_op jit(solution)/shard_map/all_to_all | solution.py:408
  69.6 8.0 %collective-permute-done.7.rest_3_ = bf16[2,128,1024]{2,1,0:T(8,128)(2,1)} collective-permute-done((bf16[2,128,1024]{2,1,0:T(8,128)(2,1)S(1)}, bf16[2,128,1024]{2,1,0:T(8,128)(2,1)}, u32[]{:S(2)}, u32[]{:S(2)}) %collective-permute-start.7) | collective-permute-done | bytes 524320 | tf_op jit(solution)/shard_map/ppermute | solution.py:23
  77.7 1.7 %collective-permute-done.10.rest_7_ = bf16[2,128,1024]{2,1,0:T(8,128)(2,1)} collective-permute-done((bf16[2,128,1024]{2,1,0:T(8,128)(2,1)S(1)}, bf16[2,128,1024]{2,1,0:T(8,128)(2,1)}, u32[]{:S(2)}, u32[]{:S(2)}) %collective-permute-start.10) | collective-permute-done | bytes 524320 | tf_op jit(solution)/shard_map/ppermute | solution.py:23
  79.4 8.4 %attention.1 = (f32[256,1024]{1,0:T(8,128)S(1)}, bf16[256,1024]{1,0:T(8,128)(2,1)S(1)}) custom-call(s32[1]{0:T(128)} %bitcast.1.parity, bf16[256,1024]{1,0:T(8,128)(2,1)S(1)} %bitcast.35, bf16[256,1024]{1,0:T(8,128)(2,1)} %collective-permute-done.3.other, f32[1,1024]{1,0:T(1,128)S(1)} %bitcast.39, bf16[2,128,1024]{2,1,0:T(8,128)(2,1)S(1)} %pad_maximum_fusion.2.rest_0_, ...), custom_call_target="tpu_custom_call" | custom-call | flops 3000000000 | bytes 7000000 | tf_op jit(solution)/shard_map/attention/pallas_call | solution.py:130
  88.0 1.9 %collective-permute-done.11 = bf16[256,1024]{1,0:T(8,128)(2,1)S(1)} collective-permute-done((bf16[256,1024]{1,0:T(8,128)(2,1)S(1)}, bf16[256,1024]{1,0:T(8,128)(2,1)S(1)}, u32[]{:S(2)}, u32[]{:S(2)}) %collective-permute-start.11) | collective-permute-done | bytes 524320 | tf_op jit(solution)/shard_map/ppermute | solution.py:29
  90.0 20.6 %all_to_all.15 = bf16[8,32,1024]{2,1,0:T(8,128)(2,1)S(1)} all-to-all(bf16[8,32,1024]{2,1,0:T(8,128)(2,1)S(1)} %bitcast.46), channel_id=1, replica_groups=mesh['yl'=2,'x'=4,'c'=2,'yh'=2,'z'=4] {'yh','z'}, dimensions={0} | all-to-all | bytes 1048576 | tf_op jit(solution)/shard_map/all_to_all | solution.py:430
  111.6 2.1 %collective-permute-start.13 = (bf16[3,256,256]{2,1,0:T(8,128)(2,1)}, bf16[3,256,256]{2,1,0:T(8,128)(2,1)S(1)}, u32[]{:S(2)}, u32[]{:S(2)}) collective-permute-start(bf16[3,256,256]{2,1,0:T(8,128)(2,1)} %get-tuple-element.26), channel_id=1, source_target_pairs={{0,1},{1,2},{2,3},{3,4},{4,5},{5,6},{6,7},{7,8},{8,9},{9,10},{10,1... | collective-permute-start | bytes 1179656 | tf_op jit(solution)/shard_map/ppermute | solution.py:427
  113.6 8.0 %collective-permute-start.14 = (bf16[3,256,256]{2,1,0:T(8,128)(2,1)S(1)}, bf16[3,256,256]{2,1,0:T(8,128)(2,1)S(1)}, u32[]{:S(2)}, u32[]{:S(2)}) collective-permute-start(bf16[3,256,256]{2,1,0:T(8,128)(2,1)S(1)} %get-tuple-element.27), channel_id=1, source_target_pairs={{1,0},{2,1},{3,2},{4,3},{5,4},{6,5},{7,6},{8,7},{9,8},{10,9},{11,1... | collective-permute-start | bytes 1179656 | tf_op jit(solution)/shard_map/ppermute | solution.py:428
  122.4 9.6 %mlp.1 = (f32[256,1024]{1,0:T(8,128)}, bf16[256,1024]{1,0:T(8,128)(2,1)}) custom-call(bf16[256,1024]{1,0:T(8,128)(2,1)} %bitcast.45, bf16[256,1024]{1,0:T(8,128)(2,1)} %copy-done.8, f32[1,1024]{1,0:T(1,128)} %bitcast.56, bf16[64,64,1024]{2,1,0:T(8,128)(2,1)} %bitcast.40), custom_call_target="tpu_custom_call" | custom-call | flops 1000000 | bytes 10000 | tf_op jit(solution)/shard_map/mlp/pallas_call | solution.py:184
  136.2 1.9 %collective-permute-start.16 = (bf16[2,128,256]{2,1,0:T(8,128)(2,1)S(1)}, bf16[2,128,256]{2,1,0:T(8,128)(2,1)S(1)}, u32[]{:S(2)}, u32[]{:S(2)}) collective-permute-start(bf16[2,128,256]{2,1,0:T(8,128)(2,1)S(1)} %bitcast.36), channel_id=1, source_target_pairs={{0,1},{1,2},{2,3},{3,4},{4,5},{5,6},{6,7},{7,8},{8,9},{9,10},{10,1... | collective-permute-start | bytes 393224 | tf_op jit(solution)/shard_map/ppermute | solution.py:442
  138.1 8.2 %collective-permute-start.17 = (bf16[2,128,256]{2,1,0:T(8,128)(2,1)S(1)}, bf16[2,128,256]{2,1,0:T(8,128)(2,1)S(1)}, u32[]{:S(2)}, u32[]{:S(2)}) collective-permute-start(bf16[2,128,256]{2,1,0:T(8,128)(2,1)S(1)} %bitcast.37), channel_id=1, source_target_pairs={{1,0},{2,1},{3,2},{4,3},{5,4},{6,5},{7,6},{8,7},{9,8},{10,9},{11,1... | collective-permute-start | bytes 393224 | tf_op jit(solution)/shard_map/ppermute | solution.py:443
  146.3 2.0 %copy-done.2 = bf16[3,3,3,256,256]{4,3,2,1,0:T(8,128)(2,1)S(1)} copy-done((bf16[3,3,3,256,256]{4,3,2,1,0:T(8,128)(2,1)S(1)}, bf16[3,3,3,256,256]{4,3,2,1,0:T(8,128)(2,1)}, u32[]{:S(2)}) %copy-start.2) | copy-done | bytes 3538968
  148.3 3.0 %early.1 = (bf16[4,256,256]{2,1,0:T(8,128)(2,1)S(1)}, f32[4,256,256]{2,1,0:T(8,128)S(1)}, bf16[2,256,256]{2,1,0:T(8,128)(2,1)S(1)}, f32[4,256,256]{2,1,0:T(8,128)S(1)}) custom-call(bf16[2,128,256]{2,1,0:T(8,128)(2,1)S(1)} %bitcast.38, bf16[4,256,256]{2,1,0:T(8,128)(2,1)S(1)} %copy-done.1, bf16[3,3,3,256,256]{4,3,2,1,0:T(8,128)(2,1)S(1)} %copy-done.2, ...), custom_call_target="tpu_custom_call" | custom-call | flops 3000000000 | bytes 4000000 | tf_op jit(solution)/shard_map/early/pallas_call | solution.py:302
  151.3 7.2 %late.1 = bf16[4,256,256]{2,1,0:T(8,128)(2,1)} custom-call(s32[2]{0:T(128)S(1)} %pad_add_fusion.place, bf16[2,128,256]{2,1,0:T(8,128)(2,1)S(1)} %collective-permute-done.16.image_low, bf16[2,128,256]{2,1,0:T(8,128)(2,1)S(1)} %collective-permute-done.17.image_high, bf16[3,256,256]{2,1,0:T(8,128)(2,1)S(1)} %collective-permute-done.13.guide_low, ...), custom_call_target="tpu_custom_call" | custom-call | flops 4000000000 | bytes 6000000 | tf_op jit(solution)/shard_map/late/pallas_call | solution.py:324
  (75 shorter events, 15.1 us)
Async XLA Ops:
  6.5 128.0 %copy-start = (bf16[1024,256]{1,0:T(8,128)(2,1)S(1)}, bf16[1024,256]{1,0:T(8,128)(2,1)}, u32[]{:S(2)}) copy-start(bf16[1024,256]{1,0:T(8,128)(2,1)} %param.20) | copy-start | bytes 1572868
  6.5 115.2 %all-gather.3.cloned.1.call-start = ((), (), s32[]{:S(2)}) async-start(), calls=%async_computation.3 | async-start | bytes 8519680 | tf_op jit(solution)/shard_map/all_gather | solution.py:384
  10.0 8.8 %collective-permute-start = (bf16[128,1024]{1,0:T(8,128)(2,1)S(1)}, bf16[128,1024]{1,0:T(8,128)(2,1)S(1)}, u32[]{:S(2)}, u32[]{:S(2)}) collective-permute-start(bf16[128,1024]{1,0:T(8,128)(2,1)S(1)} %dynamic-slice_bitcast_fusion), channel_id=1, source_target_pairs={{0,68},{64,4},{12,72},{76,8},{1,69},{65,5},{13,73},{77,9},{2,70},{... | collective-permute-start | bytes 786440 | tf_op jit(solution)/shard_map/ppermute | solution.py:41
  21.0 58.5 %copy-start.4 = (f32[1024]{0:T(1024)S(1)}, f32[1024]{0:T(1024)}, u32[]{:S(2)}) copy-start(f32[1024]{0:T(1024)} %param.14) | copy-start | bytes 12292
  21.0 24.3 %all-to-all-start = ((bf16[16,32,1024]{2,1,0:T(8,128)(2,1)}), bf16[16,32,1024]{2,1,0:T(8,128)(2,1)}, u32[]{:S(2)}, u32[]{:S(2)}) async-start(bf16[16,32,1024]{2,1,0:T(8,128)(2,1)} %copy.31), calls=%async_computation | async-start | bytes 2097152 | tf_op jit(solution)/shard_map/all_to_all | solution.py:402
  25.9 16.0 %collective-permute-start.4 = (bf16[128,1024]{1,0:T(8,128)(2,1)S(1)}, bf16[128,1024]{1,0:T(8,128)(2,1)S(1)}, u32[]{:S(2)}, u32[]{:S(2)}) collective-permute-start(bf16[128,1024]{1,0:T(8,128)(2,1)S(1)} %bitcast_select_fusion), channel_id=1, source_target_pairs={{1,0},{2,1},{3,2},{0,3},{5,4},{6,5},{7,6},{4,7},{9,8},{10,9},{11,1... | collective-permute-start | bytes 786440 | tf_op jit(solution)/shard_map/ppermute | solution.py:25
  29.9 15.3 %collective-permute-start.2 = (bf16[128,1024]{1,0:T(8,128)(2,1)S(1)}, bf16[128,1024]{1,0:T(8,128)(2,1)S(1)}, u32[]{:S(2)}, u32[]{:S(2)}) collective-permute-start(bf16[128,1024]{1,0:T(8,128)(2,1)S(1)} %bitcast_select_fusion), channel_id=1, source_target_pairs={{2,0},{3,1},{0,2},{1,3},{6,4},{7,5},{4,6},{5,7},{10,8},{11,9},{8,1... | collective-permute-start | bytes 786440 | tf_op jit(solution)/shard_map/ppermute | solution.py:25
  29.9 15.3 %collective-permute-start.1 = (bf16[128,1024]{1,0:T(8,128)(2,1)S(1)}, bf16[128,1024]{1,0:T(8,128)(2,1)S(1)}, u32[]{:S(2)}, u32[]{:S(2)}) collective-permute-start(bf16[128,1024]{1,0:T(8,128)(2,1)S(1)} %bitcast_select_fusion), channel_id=1, source_target_pairs={{3,0},{0,1},{1,2},{2,3},{7,4},{4,5},{5,6},{6,7},{11,8},{8,9},{9,10... | collective-permute-start | bytes 786440 | tf_op jit(solution)/shard_map/ppermute | solution.py:25
  41.9 22.0 %collective-permute-start.5 = (bf16[2,128,1024]{2,1,0:T(8,128)(2,1)S(1)}, bf16[2,128,1024]{2,1,0:T(8,128)(2,1)S(1)}, u32[]{:S(2)}, u32[]{:S(2)}) collective-permute-start(bf16[2,128,1024]{2,1,0:T(8,128)(2,1)S(1)} %pad_maximum_fusion.2.rest_0_), channel_id=1, source_target_pairs={{16,0},{32,16},{48,32},{0,48},{17,1},{33,17},{49,33},{1,49},{18,2}... | collective-permute-start | bytes 1572872 | tf_op jit(solution)/shard_map/ppermute | solution.py:25
  42.9 21.1 %collective-permute-start.6 = (bf16[2,128,1024]{2,1,0:T(8,128)(2,1)S(1)}, bf16[2,128,1024]{2,1,0:T(8,128)(2,1)S(1)}, u32[]{:S(2)}, u32[]{:S(2)}) collective-permute-start(bf16[2,128,1024]{2,1,0:T(8,128)(2,1)S(1)} %pad_maximum_fusion.2.rest_0_), channel_id=1, source_target_pairs={{48,0},{0,16},{16,32},{32,48},{49,1},{1,17},{17,33},{33,49},{50,2}... | collective-permute-start | bytes 1572872 | tf_op jit(solution)/shard_map/ppermute | solution.py:25
  48.5 21.1 %all-to-all-start.1 = ((bf16[8,32,1024]{2,1,0:T(8,128)(2,1)}), bf16[8,32,1024]{2,1,0:T(8,128)(2,1)S(1)}, u32[]{:S(2)}, u32[]{:S(2)}) async-start(bf16[8,32,1024]{2,1,0:T(8,128)(2,1)} %copy.33), calls=%async_computation.1 | async-start | bytes 1048576 | tf_op jit(solution)/shard_map/all_to_all | solution.py:408
  57.3 20.4 %collective-permute-start.7 = (bf16[2,128,1024]{2,1,0:T(8,128)(2,1)S(1)}, bf16[2,128,1024]{2,1,0:T(8,128)(2,1)}, u32[]{:S(2)}, u32[]{:S(2)}) collective-permute-start(bf16[2,128,1024]{2,1,0:T(8,128)(2,1)S(1)} %pad_maximum_fusion.2.rest_0_), channel_id=1, source_target_pairs={{64,0},{4,64},{68,4},{0,68},{65,1},{5,65},{69,5},{1,69},{66,2},{6,... | collective-permute-start | bytes 1572872 | tf_op jit(solution)/shard_map/ppermute | solution.py:23
  60.7 16.9 %collective-permute-start.8 = (bf16[2,128,1024]{2,1,0:T(8,128)(2,1)S(1)}, bf16[2,128,1024]{2,1,0:T(8,128)(2,1)}, u32[]{:S(2)}, u32[]{:S(2)}) collective-permute-start(bf16[2,128,1024]{2,1,0:T(8,128)(2,1)S(1)} %pad_maximum_fusion.1.rest_4_), channel_id=1, source_target_pairs={{16,0},{32,16},{48,32},{0,48},{17,1},{33,17},{49,33},{1,49},{18,2}... | collective-permute-start | bytes 1572872 | tf_op jit(solution)/shard_map/ppermute | solution.py:25
  60.7 16.9 %collective-permute-start.9 = (bf16[2,128,1024]{2,1,0:T(8,128)(2,1)S(1)}, bf16[2,128,1024]{2,1,0:T(8,128)(2,1)}, u32[]{:S(2)}, u32[]{:S(2)}) collective-permute-start(bf16[2,128,1024]{2,1,0:T(8,128)(2,1)S(1)} %pad_maximum_fusion.1.rest_4_), channel_id=1, source_target_pairs={{48,0},{0,16},{16,32},{32,48},{49,1},{1,17},{17,33},{33,49},{50,2}... | collective-permute-start | bytes 1572872 | tf_op jit(solution)/shard_map/ppermute | solution.py:25
  64.0 15.4 %collective-permute-start.10 = (bf16[2,128,1024]{2,1,0:T(8,128)(2,1)S(1)}, bf16[2,128,1024]{2,1,0:T(8,128)(2,1)}, u32[]{:S(2)}, u32[]{:S(2)}) collective-permute-start(bf16[2,128,1024]{2,1,0:T(8,128)(2,1)S(1)} %pad_maximum_fusion.1.rest_4_), channel_id=1, source_target_pairs={{68,0},{0,64},{64,4},{4,68},{69,1},{1,65},{65,5},{5,69},{70,2},{2,... | collective-permute-start | bytes 1572872 | tf_op jit(solution)/shard_map/ppermute | solution.py:23
  69.6 9.8 %collective-permute-start.3 = (bf16[256,1024]{1,0:T(8,128)(2,1)S(1)}, bf16[256,1024]{1,0:T(8,128)(2,1)}, u32[]{:S(2)}, u32[]{:S(2)}) collective-permute-start(bf16[256,1024]{1,0:T(8,128)(2,1)S(1)} %bitcast.34), channel_id=1, source_target_pairs={{0,8},{8,0},{1,9},{9,1},{2,10},{10,2},{3,11},{11,3},{4,12},{12,4},... | collective-permute-start | bytes 1572872 | tf_op jit(solution)/shard_map/ppermute | solution.py:29
  87.9 2.0 %collective-permute-start.11 = (bf16[256,1024]{1,0:T(8,128)(2,1)S(1)}, bf16[256,1024]{1,0:T(8,128)(2,1)S(1)}, u32[]{:S(2)}, u32[]{:S(2)}) collective-permute-start(bf16[256,1024]{1,0:T(8,128)(2,1)S(1)} %get-tuple-element.23), channel_id=1, source_target_pairs={{0,8},{8,0},{1,9},{9,1},{2,10},{10,2},{3,11},{11,3},{4,12},{12,4},... | collective-permute-start | bytes 1572872 | tf_op jit(solution)/shard_map/ppermute | solution.py:29
  110.7 11.0 %collective-permute-start.12 = (bf16[256,1024]{1,0:T(8,128)(2,1)S(1)}, bf16[256,1024]{1,0:T(8,128)(2,1)S(1)}, u32[]{:S(2)}, u32[]{:S(2)}) collective-permute-start(bf16[256,1024]{1,0:T(8,128)(2,1)S(1)} %bitcast.44), channel_id=1, source_target_pairs={{0,8},{8,0},{1,9},{9,1},{2,10},{10,2},{3,11},{11,3},{4,12},{12,4},... | collective-permute-start | bytes 1572872 | tf_op jit(solution)/shard_map/ppermute | solution.py:29
  111.6 20.5 %collective-permute-start.13 = (bf16[3,256,256]{2,1,0:T(8,128)(2,1)}, bf16[3,256,256]{2,1,0:T(8,128)(2,1)S(1)}, u32[]{:S(2)}, u32[]{:S(2)}) collective-permute-start(bf16[3,256,256]{2,1,0:T(8,128)(2,1)} %get-tuple-element.26), channel_id=1, source_target_pairs={{0,1},{1,2},{2,3},{3,4},{4,5},{5,6},{6,7},{7,8},{8,9},{9,10},{10,1... | collective-permute-start | bytes 1179656 | tf_op jit(solution)/shard_map/ppermute | solution.py:427
  113.6 18.4 %collective-permute-start.14 = (bf16[3,256,256]{2,1,0:T(8,128)(2,1)S(1)}, bf16[3,256,256]{2,1,0:T(8,128)(2,1)S(1)}, u32[]{:S(2)}, u32[]{:S(2)}) collective-permute-start(bf16[3,256,256]{2,1,0:T(8,128)(2,1)S(1)} %get-tuple-element.27), channel_id=1, source_target_pairs={{1,0},{2,1},{3,2},{4,3},{5,4},{6,5},{7,6},{8,7},{9,8},{10,9},{11,1... | collective-permute-start | bytes 1179656 | tf_op jit(solution)/shard_map/ppermute | solution.py:428
  122.4 23.8 %copy-start.5 = (f32[3,256]{1,0:T(4,128)S(1)}, f32[3,256]{1,0:T(4,128)}, u32[]{:S(2)}) copy-start(f32[3,256]{1,0:T(4,128)} %bias.3) | copy-start | bytes 9220
  132.1 2.4 %collective-permute-start.15 = (bf16[256,1024]{1,0:T(8,128)(2,1)}, bf16[256,1024]{1,0:T(8,128)(2,1)S(1)}, u32[]{:S(2)}, u32[]{:S(2)}) collective-permute-start(bf16[256,1024]{1,0:T(8,128)(2,1)} %get-tuple-element.28), channel_id=1, source_target_pairs={{0,8},{8,0},{1,9},{9,1},{2,10},{10,2},{3,11},{11,3},{4,12},{12,4},... | collective-permute-start | bytes 1572872 | tf_op jit(solution)/shard_map/ppermute | solution.py:29
  136.2 15.1 %collective-permute-start.16 = (bf16[2,128,256]{2,1,0:T(8,128)(2,1)S(1)}, bf16[2,128,256]{2,1,0:T(8,128)(2,1)S(1)}, u32[]{:S(2)}, u32[]{:S(2)}) collective-permute-start(bf16[2,128,256]{2,1,0:T(8,128)(2,1)S(1)} %bitcast.36), channel_id=1, source_target_pairs={{0,1},{1,2},{2,3},{3,4},{4,5},{5,6},{6,7},{7,8},{8,9},{9,10},{10,1... | collective-permute-start | bytes 393224 | tf_op jit(solution)/shard_map/ppermute | solution.py:442
  138.1 13.2 %collective-permute-start.17 = (bf16[2,128,256]{2,1,0:T(8,128)(2,1)S(1)}, bf16[2,128,256]{2,1,0:T(8,128)(2,1)S(1)}, u32[]{:S(2)}, u32[]{:S(2)}) collective-permute-start(bf16[2,128,256]{2,1,0:T(8,128)(2,1)S(1)} %bitcast.37), channel_id=1, source_target_pairs={{1,0},{2,1},{3,2},{4,3},{5,4},{6,5},{7,6},{8,7},{9,8},{10,9},{11,1... | collective-permute-start | bytes 393224 | tf_op jit(solution)/shard_map/ppermute | solution.py:443
  (10 other events, 60.0 us)
Sparse Core Ops, SparseCore 0:
  10.2 98.0 all-gather.2
